TPU v7x, 32 devices: a whole 2x2x4 slice. The times are simulated.
32 devices in a mesh: batch: 16 (over z, y, x), head: 2 (over core).
Axes of the slice: x: 2, y: 2, z: 4, core: 2. Of those that a mesh axis runs over, the one named last changes fastest.
Arguments:
- tokens: bfloat16 [128, 640, 384], P(('batch', 'head')), may hold values from -6 to 6
- cotangent: bfloat16 [128, 640, 384], P(('batch', 'head')), may hold values from -9 to 9
- lengths: int32 [128], P('batch'), may hold values from 1 to 577, 49237 in all
- key_masks: int32 [128, 640], P('batch'), may hold values 0 or 1
- qkv_master: float32 [384, 3, 384], P('batch', None, 'head'), may hold values from -0.3125 to 0.3125
- out_master: float32 [384, 384], P('head', 'batch'), may hold values from -1.25 to 1.25
- up_master: float32 [384, 1536], P('batch', 'head'), may hold values from -0.3125 to 0.3125
- down_master: float32 [1536, 384], P('head', 'batch'), may hold values from -0.15625 to 0.15625
- norm_master: float32 [1536], P(('batch', 'head')), may hold values from -2 to 3
- qkv_moments: float32 [2, 384, 3, 384], P(None, 'batch', None, 'head'), may hold values from -9 to 31, as said below
- out_moments: float32 [2, 384, 384], P(None, 'head', 'batch'), may hold values from -9 to 31, as said below
- up_moments: float32 [2, 384, 1536], P(None, 'batch', 'head'), may hold values from -9 to 31, as said below
- down_moments: float32 [2, 1536, 384], P(None, 'head', 'batch'), may hold values from -9 to 31, as said below
- norm_moments: float32 [2, 1536], P(None, ('batch', 'head')), may hold values from -34 to 490, as said below
Outputs:
- block_out: bfloat16 [128, 640, 384], P(('batch', 'head'))
- input_grad: float32 [128, 640, 384], P(('batch', 'head'))
- grad_norm: float32 [], replicated
- qkv_next: float32 [384, 3, 384], P('batch', None, 'head')
- out_next: float32 [384, 384], P('head', 'batch')
- up_next: float32 [384, 1536], P('batch', 'head')
- down_next: float32 [1536, 384], P('head', 'batch')
- norm_next: float32 [1536], P(('batch', 'head'))
- qkv_states: float32 [2, 384, 3, 384], P(None, 'batch', None, 'head')
- out_states: float32 [2, 384, 384], P(None, 'head', 'batch')
- up_states: float32 [2, 384, 1536], P(None, 'batch', 'head')
- down_states: float32 [2, 1536, 384], P(None, 'head', 'batch')
- norm_states: float32 [2, 1536], P(None, ('batch', 'head'))
- norm_grads: float32 [1536], P(('batch', 'head'))
Inputs may be any that keep to these rules, and one draw needn't show every extreme that they name: `lengths`: at least one sequence has 577 live rows. `qkv_moments`: first moments, then second moments (positive). `out_moments`: first moments, then second moments (positive). `up_moments`: first moments, then second moments (positive). `down_moments`: first moments, then second moments (positive). `norm_moments`: first moments, then second moments (positive).
All inputs are finite; a program needn't handle non-finite values. No bound on the sum of `lengths` or of `key_masks` on one device may be relied on, other than what follows from the above.
Results may differ from a plain program's by a relative error of at most 0.017.
Values may be sent and summed in bfloat16 or wider, within the bound.
No kernel may reach another device: no remote copies, remote signals or barrier semaphores. Data moves between devices by JAX's collectives and lax.ppermute only.
A program may use at most 192 MiB of HBM per device.

v0:
```python
import jax
import jax.numpy as jnp
from jax import lax
from jax.sharding import PartitionSpec as P

HD = 64
STEP = 10


NORM_EPS = 1e-06
CLIP_NORM = 1000.0
BETA_ONE = 0.5
BETA_TWO = 0.5
ADAM_EPS = 1e-08
RATE_LIST = (0.06, 0.25, 0.06, 0.03, 0.5)
DECAY_LIST = (0.04, 0.04, 0.04, 0.04, 0.0)


def layer_norm(values, norm_gain, norm_bias):
    row_mean = jnp.mean(values, axis=-1, keepdims=True)
    centred = values - row_mean
    variance = jnp.mean(centred * centred, axis=-1, keepdims=True)
    return centred * lax.rsqrt(variance + NORM_EPS) * norm_gain + norm_bias


def exact_gelu(values):
    return jax.nn.gelu(values, approximate=False)


def adamw(master, gradient, moments, rate, decay):
    moment = BETA_ONE * moments[0] + (1.0 - BETA_ONE) * gradient
    second = BETA_TWO * moments[1] + (1.0 - BETA_TWO) * gradient * gradient
    step_size = (
        moment / (1.0 - BETA_ONE**STEP) / (jnp.sqrt(second / (1.0 - BETA_TWO**STEP)) + ADAM_EPS)
    )
    return (master - rate * (step_size + decay * master), jnp.stack([moment, second]))


def masked_scores(queries, key_rows, visible):
    score_scale = queries.shape[-1] ** (-0.5)
    scores = (
        jnp.einsum("qhe,khe->hqk", queries, key_rows, preferred_element_type=jnp.float32)
        * score_scale
    )
    return (jnp.where(visible[None, None, :], scores, -1e30), score_scale)


def attend_forward(member):
    projected, visible = member
    queries, key_rows, values = (projected[:, 0], projected[:, 1], projected[:, 2])
    scores, score_scale = masked_scores(queries, key_rows, visible)
    row_top = jnp.max(scores, axis=-1, keepdims=True)
    powers = jnp.exp(scores - row_top)
    row_sum = jnp.sum(powers, axis=-1, keepdims=True)
    attn_prob = (powers / row_sum).astype(jnp.bfloat16)
    attended = jnp.einsum("hqk,khe->qhe", attn_prob, values, preferred_element_type=jnp.float32)
    return (attended.astype(jnp.bfloat16), row_top + jnp.log(row_sum))


def attend_backward(member):
    projected, visible, log_total, grad_attended = member
    queries, key_rows, values = (projected[:, 0], projected[:, 1], projected[:, 2])
    scores, score_scale = masked_scores(queries, key_rows, visible)
    attn_prob = jnp.exp(scores - log_total)
    grad_values = jnp.einsum(
        "hqk,qhe->khe",
        attn_prob.astype(jnp.bfloat16),
        grad_attended,
        preferred_element_type=jnp.float32,
    )
    grad_prob = jnp.einsum(
        "qhe,khe->hqk", grad_attended, values, preferred_element_type=jnp.float32
    )
    row_inner = jnp.sum(attn_prob * grad_prob, axis=-1, keepdims=True)
    grad_scores = (attn_prob * (grad_prob - row_inner)).astype(jnp.bfloat16)
    grad_queries = (
        jnp.einsum("hqk,khe->qhe", grad_scores, key_rows, preferred_element_type=jnp.float32)
        * score_scale
    )
    grad_keys = (
        jnp.einsum("hqk,qhe->khe", grad_scores, queries, preferred_element_type=jnp.float32)
        * score_scale
    )
    return jnp.stack([grad_queries, grad_keys, grad_values], axis=1)


def spread_heads(values):
    return lax.all_gather(values, "head", axis=0, tiled=True)


def total_heads(terms):
    return lax.psum_scatter(
        terms.astype(jnp.bfloat16), "head", scatter_dimension=0, tiled=True
    ).astype(jnp.float32)


def spread_hidden(values):
    return lax.all_gather(values, "head", axis=0, tiled=True)


def total_hidden(terms):
    return lax.psum_scatter(
        terms.astype(jnp.bfloat16), "head", scatter_dimension=0, tiled=True
    ).astype(jnp.float32)


def per_device(
    tokens,
    cotangent,
    lengths,
    key_masks,
    qkv_master,
    out_master,
    up_master,
    down_master,
    norm_master,
    qkv_moments,
    out_moments,
    up_moments,
    down_moments,
    norm_moments,
):
    half_seqs, slot_rows, width = tokens.shape
    head_side = lax.axis_index("head")
    positions = jnp.arange(slot_rows, dtype=jnp.int32)
    visible = (positions[None, :] < lengths[:, None]) & (
        (key_masks == 1) | (positions[None, :] == 0)
    )
    own_lengths = lax.dynamic_slice_in_dim(lengths, head_side * half_seqs, half_seqs)
    live_rows = (positions[None, :] < own_lengths[:, None]).astype(jnp.float32)[:, :, None]
    norms_all = lax.all_gather(norm_master, ("batch", "head"), axis=0, tiled=True).reshape(4, width)
    qkv_full, out_full, up_full, down_full = (
        lax.all_gather(qkv_master.astype(jnp.bfloat16), "batch", axis=0, tiled=True),
        lax.all_gather(out_master.astype(jnp.bfloat16), "batch", axis=1, tiled=True),
        lax.all_gather(up_master.astype(jnp.bfloat16), "batch", axis=0, tiled=True),
        lax.all_gather(down_master.astype(jnp.bfloat16), "batch", axis=1, tiled=True),
    )
    inputs = tokens.astype(jnp.float32)
    normed_one = layer_norm(inputs, norms_all[0], norms_all[1]).astype(jnp.bfloat16)
    query_key_value_stack, output_weight_stack, up_weight_stack, down_weight_stack = (
        qkv_full,
        out_full,
        up_full,
        down_full,
    )
    normalized_full_rows = spread_heads(normed_one)
    head_width = query_key_value_stack.shape[2]
    local_heads = head_width // HD
    row_count = normalized_full_rows.shape[0]
    projected = jnp.einsum(
        "mzp,pvb->mzvb",
        normalized_full_rows,
        query_key_value_stack,
        preferred_element_type=jnp.float32,
    ).astype(jnp.bfloat16)
    projected = projected.reshape(row_count, slot_rows, 3, local_heads, HD)
    attended, log_total = lax.map(attend_forward, (projected, visible))
    attention_output_rows = attended.reshape(row_count, slot_rows, head_width)
    attn_terms = jnp.einsum(
        "wyv,vf->wyf",
        attention_output_rows,
        output_weight_stack,
        preferred_element_type=jnp.float32,
    )
    attn_branch = total_heads(attn_terms)
    middle = inputs + attn_branch
    normed_two = layer_norm(middle, norms_all[2], norms_all[3]).astype(jnp.bfloat16)
    hidden_preactivation = spread_hidden(normed_two)
    hidden_rows = jnp.einsum(
        "jzt,tq->jzq", hidden_preactivation, up_weight_stack, preferred_element_type=jnp.float32
    )
    gelu_output = exact_gelu(hidden_rows).astype(jnp.bfloat16)
    down_product_rows = jnp.einsum(
        "hbt,tp->hbp", gelu_output, down_weight_stack, preferred_element_type=jnp.float32
    )
    ffn_branch = total_hidden(down_product_rows)
    block_out = (middle + ffn_branch).astype(jnp.bfloat16)
    upstream = cotangent.astype(jnp.float32) * live_rows
    grad_branch = upstream.astype(jnp.bfloat16)
    branch_gradient_stack = spread_hidden(grad_branch)
    grad_down = jnp.einsum(
        "rkv,rkp->vp", gelu_output, branch_gradient_stack, preferred_element_type=jnp.float32
    )
    grad_act = jnp.einsum(
        "tpc,oc->tpo", branch_gradient_stack, down_weight_stack, preferred_element_type=jnp.float32
    )
    unused_value, gelu_back = jax.vjp(exact_gelu, hidden_rows)
    hidden_gradient = gelu_back(grad_act)[0].astype(jnp.bfloat16)
    grad_up = jnp.einsum(
        "tkm,tkg->mg", hidden_preactivation, hidden_gradient, preferred_element_type=jnp.float32
    )
    normalized_gradient = jnp.einsum(
        "xtm,nm->xtn", hidden_gradient, up_weight_stack, preferred_element_type=jnp.float32
    )
    grad_two = total_hidden(normalized_gradient)
    unused_two, second_back = jax.vjp(layer_norm, middle, norms_all[2], norms_all[3])
    grad_mid, grad_gain_two, grad_bias_two = second_back(grad_two)
    grad_middle = upstream + grad_mid
    mixed_gradient_stack = spread_heads(grad_middle.astype(jnp.bfloat16))
    grad_out = jnp.einsum(
        "opi,opt->it",
        attention_output_rows,
        mixed_gradient_stack,
        preferred_element_type=jnp.float32,
    )
    grad_attended = jnp.einsum(
        "gbz,kz->gbk", mixed_gradient_stack, output_weight_stack, preferred_element_type=jnp.float32
    ).astype(jnp.bfloat16)
    grad_attended = grad_attended.reshape(row_count, slot_rows, local_heads, HD)
    projection_gradient = lax.map(attend_backward, (projected, visible, log_total, grad_attended))
    projection_gradient = projection_gradient.astype(jnp.bfloat16).reshape(
        row_count, slot_rows, 3, head_width
    )
    grad_qkv = jnp.einsum(
        "gjn,gjro->nro",
        normalized_full_rows,
        projection_gradient,
        preferred_element_type=jnp.float32,
    )
    one_terms = jnp.einsum(
        "bavk,nvk->ban",
        projection_gradient,
        query_key_value_stack,
        preferred_element_type=jnp.float32,
    )
    grad_one = total_heads(one_terms)
    unused_one, first_back = jax.vjp(layer_norm, inputs, norms_all[0], norms_all[1])
    grad_in, grad_gain_one, grad_bias_one = first_back(grad_one)
    input_grad = grad_middle + grad_in
    qkv_shard, out_shard, up_shard, down_shard = (
        lax.psum_scatter(grad_qkv, "batch", scatter_dimension=0, tiled=True),
        lax.psum_scatter(grad_out, "batch", scatter_dimension=1, tiled=True),
        lax.psum_scatter(grad_up, "batch", scatter_dimension=0, tiled=True),
        lax.psum_scatter(grad_down, "batch", scatter_dimension=1, tiled=True),
    )
    norm_terms = jnp.concatenate([grad_gain_one, grad_bias_one, grad_gain_two, grad_bias_two])
    norm_shard = lax.psum_scatter(norm_terms, ("batch", "head"), scatter_dimension=0, tiled=True)
    shards = (qkv_shard, out_shard, up_shard, down_shard, norm_shard)
    local_squares = sum((jnp.sum(piece * piece) for piece in shards))
    grad_norm = jnp.sqrt(lax.psum(local_squares, ("batch", "head")))
    factor = jnp.minimum(1.0, CLIP_NORM / (grad_norm + 1e-06))
    norm_grads = factor * norm_shard
    qkv_next, qkv_states = adamw(
        qkv_master, factor * qkv_shard, qkv_moments, RATE_LIST[0], DECAY_LIST[0]
    )
    out_next, out_states = adamw(
        out_master, factor * out_shard, out_moments, RATE_LIST[1], DECAY_LIST[1]
    )
    up_next, up_states = adamw(
        up_master, factor * up_shard, up_moments, RATE_LIST[2], DECAY_LIST[2]
    )
    down_next, down_states = adamw(
        down_master, factor * down_shard, down_moments, RATE_LIST[3], DECAY_LIST[3]
    )
    norm_next, norm_states = adamw(
        norm_master, norm_grads, norm_moments, RATE_LIST[4], DECAY_LIST[4]
    )
    return (
        block_out,
        input_grad,
        grad_norm,
        qkv_next,
        out_next,
        up_next,
        down_next,
        norm_next,
        qkv_states,
        out_states,
        up_states,
        down_states,
        norm_states,
        norm_grads,
    )


def solution(mesh):
    return jax.shard_map(
        per_device,
        mesh=mesh,
        in_specs=(
            P(("batch", "head"), None, None),
            P(("batch", "head"), None, None),
            P("batch"),
            P("batch", None),
            P("batch", None, "head"),
            P("head", "batch"),
            P("batch", "head"),
            P("head", "batch"),
            P(("batch", "head")),
            P(None, "batch", None, "head"),
            P(None, "head", "batch"),
            P(None, "batch", "head"),
            P(None, "head", "batch"),
            P(None, ("batch", "head")),
        ),
        out_specs=(
            P(("batch", "head"), None, None),
            P(("batch", "head"), None, None),
            P(),
            P("batch", None, "head"),
            P("head", "batch"),
            P("batch", "head"),
            P("head", "batch"),
            P(("batch", "head")),
            P(None, "batch", None, "head"),
            P(None, "head", "batch"),
            P(None, "batch", "head"),
            P(None, "head", "batch"),
            P(None, ("batch", "head")),
            P(("batch", "head")),
        ),
        check_vma=False,
    )
```

profile of v0, /device:TPU:0, one launch (start us, length us, event | category | flops | bytes accessed | tf_op | source)
XLA Modules:
  0.0 1052.1 jit_solution(3459986605919117316)
XLA Ops:
  12.8 42.0 %all-reduce = f32[1536]{0:T(1024)S(1)} all-reduce(f32[1536]{0:T(1024)S(1)} %dynamic-update-slice), channel_id=1, replica_groups=mesh['batch'=16,'head'=2] {'batch','head'}, use_global_device_ids=true, to_apply=%add | all-reduce | flops 1536 | bytes 12288
  56.9 40.6 %all_gather.30 = bf16[192,384]{0,1:T(8,128)(2,1)S(1)} all-gather(bf16[192,24]{0,1:T(8,128)(2,1)S(1)} %convert_element_type.98), channel_id=1, replica_groups=mesh['batch'=16,'head'=2] {'batch'}, dimensions={1}, use_global_device_ids=true | all-gather | bytes 156672 | tf_op jit(solution)/shard_map/all_gather | solution.py:134
  97.5 38.8 %all_gather.29 = bf16[384,3,192]{2,0,1:T(8,128)(2,1)S(1)} all-gather(bf16[24,3,192]{2,0,1:T(8,128)(2,1)S(1)} %convert_element_type.96), channel_id=1, replica_groups=mesh['batch'=16,'head'=2] {'batch'}, dimensions={0}, use_global_device_ids=true | all-gather | bytes 470016 | tf_op jit(solution)/shard_map/all_gather | solution.py:133
  136.4 8.0 fusion.59
  144.3 44.2 %while.22 = (s32[]{:T(128)}, bf16[8,640,3,64]{1,3,2,0:T(8,128)(2,1)}, f32[8,3,640,1]{2,1,3,0:T(4,128)S(1)}, bf16[8,640,3,3,64]{1,4,3,2,0:T(8,128)(2,1)}, pred[8,640]{1,0:T(8,128)(4,1)S(1)}, /*index=5*/s32[]{:T(128)}) while((s32[]{:T(128)}, bf16[8,640,3,64]{1,3,2,0:T(8,128)(2,1)}, f32[8,3,640,1]{2,1,3,0:T(4,128)S(1)}, ...), condition=%wide.region_5.6_spmd, body=%wide.region_2.5_spmd.sunk | while | flops 329439360 | bytes 17282000 | solution.py:157
  188.5 5.1 convolution_convert_fusion.2
  193.9 9.8 reduce-scatter.9.cloned.1.call-done
  209.6 3.2 fusion.54
  212.9 46.4 %all_gather.32 = bf16[384,768]{1,0:T(8,128)(2,1)} all-gather(bf16[24,768]{1,0:T(8,128)(2,1)S(1)} %convert_element_type.102), channel_id=1, replica_groups=mesh['batch'=16,'head'=2] {'batch'}, dimensions={0}, use_global_device_ids=true | all-gather | bytes 626688 | tf_op jit(solution)/shard_map/all_gather | solution.py:135
  259.3 39.0 %all_gather.33 = bf16[768,384]{0,1:T(8,128)(2,1)S(1)} all-gather(bf16[768,24]{0,1:T(8,128)(2,1)S(1)} %convert_element_type.104), channel_id=1, replica_groups=mesh['batch'=16,'head'=2] {'batch'}, dimensions={1}, use_global_device_ids=true | all-gather | bytes 626688 | tf_op jit(solution)/shard_map/all_gather | solution.py:136
  298.4 10.4 fusion.56
  308.7 5.5 copy-done.6
  314.3 36.4 %multiply_convert_fusion.1 = (bf16[8,640,768]{2,1,0:T(8,128)(2,1)}, f32[8,640,768]{2,1,0:T(8,128)}) fusion(f32[8,640,768]{2,1,0:T(8,128)S(1)} %get-tuple-element.135, u8[640,768]{1,0:T(8,128)(4,1)S(1)} %get-tuple-element.78, u8[640,768]{1,0:T(8,128)(4,1)S(1)} %get-tuple-element.77), kind=kLoop, calls=%fused_computation.55 | loop fusion | flops 275251200 | bytes 40304640 | tf_op jit(solution)/shard_map/convert_element_type | solution.py:172
  350.7 17.8 %add_convert_fusion = bf16[8,640,768]{2,1,0:T(8,128)(2,1)} fusion(f32[8,640,768]{2,1,0:T(8,128)} %get-tuple-element.110, f32[8,640,768]{2,1,0:T(8,128)} %copy-done.6, bf16[8,640,384]{2,1,0:T(8,128)(2,1)} %all-gather.9.cloned.1.call-done, bf16[768,384]{0,1:T(8,128)(2,1)S(1)} %all_gather.33), kind=kOutput, calls=%fused_computation.54 | convolution fusion | flops 3074949120 | bytes 43843584 | tf_op jit(solution)/shard_map/tpc,oc->tpo/dot_general | solution.py:184
  368.5 9.4 convolution_convert_fusion
  378.4 9.5 reduce-scatter.13.cloned.1.call-done
  393.8 3.7 fusion.63
  397.5 8.7 convolution_bitcast_fusion.1
  406.4 9.8 convolution_bitcast_fusion
  416.4 4.9 convolution_convert_fusion.3
  421.3 86.6 %while.23 = (s32[]{:T(128)}, bf16[8,640,3,3,64]{1,4,3,2,0:T(8,128)(2,1)}, bf16[8,640,3,3,64]{1,4,3,2,0:T(8,128)(2,1)}, pred[8,640]{1,0:T(8,128)(4,1)S(1)}, f32[8...) while((s32[]{:T(128)}, bf16[8,640,3,3,64]{1,4,3,2,0:T(8,128)(2,1)}, ...), condition=%wide.region_15.16_spmd, body=%wide.region_13.15_spmd.sunk | while | flops 807565440 | bytes 42332248 | solution.py:210
  507.9 5.1 convolution_bitcast_fusion.2
  513.3 8.2 fusion.64
  521.6 9.0 bitcast_convert_fusion
  530.9 9.4 convolution_convert_fusion.1
  544.1 126.7 %reduce-scatter.23.cloned.1.call-done = f32[768,24]{0,1:T(8,128)} async-done(((f32[768,384]{0,1:T(8,128)}), f32[768,24]{0,1:T(8,128)}) %reduce-scatter.23.cloned.1.call-update) | async-done | bytes 73744 | tf_op jit(solution)/shard_map/reduce_scatter | solution.py:234
  672.3 123.8 %reduce-scatter.19.cloned.1.call-done = f32[192,24]{0,1:T(8,128)} async-done(((f32[192,384]{0,1:T(8,128)}), f32[192,24]{0,1:T(8,128)}) %reduce-scatter.19.cloned.1.call-update) | async-done | bytes 18448 | tf_op jit(solution)/shard_map/reduce_scatter | solution.py:232
  797.4 127.2 %reduce-scatter.17.cloned.1.call-done = f32[24,3,192]{2,0,1:T(8,128)} async-done(((f32[384,3,192]{2,0,1:T(8,128)}), f32[24,3,192]{2,0,1:T(8,128)}) %reduce-scatter.17.cloned.1.call-update) | async-done | bytes 55312 | tf_op jit(solution)/shard_map/reduce_scatter | solution.py:231
  928.8 9.5 reduce-scatter.15.cloned.1.call-done
  943.7 40.6 %all-reduce.1 = f32[1536]{0:T(1024)S(1)} all-reduce(f32[1536]{0:T(1024)S(1)} %pad_maximum_fusion.4), channel_id=10, replica_groups=mesh['batch'=16,'head'=2] {'batch','head'}, use_global_device_ids=true, to_apply=%region_31.32.clone | all-reduce | flops 1536 | bytes 12288
  985.6 40.0 %psum.7 = f32[]{:T(128)} all-reduce(f32[]{:T(128)S(6)} %add.198), channel_id=1, replica_groups=mesh['batch'=16,'head'=2] {'batch','head'}, use_global_device_ids=true, to_apply=%region_33.34 | all-reduce | flops 1 | bytes 8 | tf_op jit(solution)/shard_map/psum | solution.py:240
  1033.0 10.7 %add_add_fusion.2 = (f32[4,640,384]{2,1,0:T(8,128)}, bf16[4,640,384]{2,1,0:T(8,128)(2,1)}) fusion(bf16[4,640,384]{2,1,0:T(8,128)(2,1)S(1)} %copy-done, bf16[4,640,384]{2,1,0:T(8,128)(2,1)} %reduce-scatter.15.cloned.1.call-done, bf16[4,640,384]{2,1,0:T(8,128)(2,1)} %param.19, f32[4,640]{1,0:T(4,128)S(1)} %negate_multiply_fusion.1, ...), kind=kLoop, calls=%fused_computation.99 | loop fusion | flops 25559040 | bytes 17789952 | tf_op jit(solution)/shard_map/add | solution.py:229
  (286 shorter events, 172.2 us)
Async XLA Ops:
  7.2 129.2 %all-gather.5.cloned.1.call-start = ((), (), s32[]{:S(2)}) async-start(), calls=%async_computation.8 | async-start | bytes 5898240 | tf_op jit(solution)/shard_map/all_gather | solution.py:88
  12.5 123.8 %copy-start.34 = (s32[8,640]{1,0:T(8,128)S(1)}, s32[8,640]{1,0:T(8,128)}, u32[]{:S(2)}) copy-start(s32[8,640]{1,0:T(8,128)} %param.21) | copy-start | bytes 61444
  12.5 123.8 %copy-start.37 = (s32[8]{0:T(128)S(1)}, s32[8]{0:T(128)}, u32[]{:S(2)}) copy-start(s32[8]{0:T(128)} %param.20) | copy-start | bytes 100
  56.8 146.9 %reduce-scatter.9.cloned.1.call-start = ((), (), s32[]{:S(2)}) async-start(), calls=%async_computation.9 | async-start | bytes 5898240 | tf_op jit(solution)/shard_map/reduce_scatter | solution.py:92
  193.6 104.8 %all-gather.7.cloned.1.call-start = ((), (), s32[]{:S(2)}) async-start(), calls=%async_computation.10 | async-start | bytes 5898240 | tf_op jit(solution)/shard_map/all_gather | solution.py:98
  209.4 141.3 %all-gather.9.cloned.1.call-start = ((), (), s32[]{:S(2)}) async-start(), calls=%async_computation.12 | async-start | bytes 5898240 | tf_op jit(solution)/shard_map/all_gather | solution.py:98
  212.8 175.1 %reduce-scatter.13.cloned.1.call-start = ((), (), s32[]{:S(2)}) async-start(), calls=%async_computation.13 | async-start | bytes 5898240 | tf_op jit(solution)/shard_map/reduce_scatter | solution.py:102
  378.0 38.4 %all-gather.11.cloned.1.call-start = ((), (), s32[]{:S(2)}) async-start(), calls=%async_computation.14 | async-start | bytes 5898240 | tf_op jit(solution)/shard_map/all_gather | solution.py:88
  397.5 145.1 %reduce-scatter.21.cloned.1.call-start = ((), (), s32[]{:S(2)}) async-start(), calls=%async_computation.18 | async-start | bytes 1253376 | tf_op jit(solution)/shard_map/reduce_scatter | solution.py:233
  406.3 264.5 %reduce-scatter.23.cloned.1.call-start = ((), (), s32[]{:S(2)}) async-start(), calls=%async_computation.19 | async-start | bytes 1253376 | tf_op jit(solution)/shard_map/reduce_scatter | solution.py:234
  416.2 379.9 %reduce-scatter.19.cloned.1.call-start = ((), (), s32[]{:S(2)}) async-start(), calls=%async_computation.17 | async-start | bytes 417792 | tf_op jit(solution)/shard_map/reduce_scatter | solution.py:232
  513.0 411.6 %reduce-scatter.17.cloned.1.call-start = ((), (), s32[]{:S(2)}) async-start(), calls=%async_computation.16 | async-start | bytes 1253376 | tf_op jit(solution)/shard_map/reduce_scatter | solution.py:231
  521.5 416.8 %reduce-scatter.15.cloned.1.call-start = ((), (), s32[]{:S(2)}) async-start(), calls=%async_computation.15 | async-start | bytes 5898240 | tf_op jit(solution)/shard_map/reduce_scatter | solution.py:92
  530.6 502.4 %reduce-scatter.11.cloned.1.call-start = ((), (), s32[]{:S(2)}) async-start(), calls=%async_computation.11 | async-start | bytes 5898240 | tf_op jit(solution)/shard_map/reduce_scatter | solution.py:102
  540.3 398.1 %copy-start.11 = (f32[4,640]{1,0:T(4,128)S(1)}, f32[4,640]{1,0:T(4,128)}, u32[]{:S(2)}) copy-start(f32[4,640]{1,0:T(4,128)} %copy-done.10) | copy-start | bytes 30724
  540.3 398.1 %copy-start.32 = (f32[384]{0:T(512)S(1)}, f32[384]{0:T(512)}, u32[]{:S(2)}) copy-start(f32[384]{0:T(512)} %copy-done.31) | copy-start | bytes 4612
  540.3 400.9 %copy-start.30 = (f32[4,640]{1,0:T(4,128)S(1)}, f32[4,640]{1,0:T(4,128)}, u32[]{:S(2)}) copy-start(f32[4,640]{1,0:T(4,128)} %copy-done.29) | copy-start | bytes 30724
  540.3 400.9 %copy-start.22 = (f32[4,640]{1,0:T(4,128)S(1)}, f32[4,640]{1,0:T(4,128)}, u32[]{:S(2)}) copy-start(f32[4,640]{1,0:T(4,128)} %copy-done.21) | copy-start | bytes 30724
  928.7 97.7 %copy-start.35 = (f32[2,48]{1,0:T(2,128)S(1)}, f32[2,48]{1,0:T(2,128)}, u32[]{:S(2)}) copy-start(f32[2,48]{1,0:T(2,128)} %param.31) | copy-start | bytes 1156
  928.7 97.8 %copy-start.39 = (f32[48]{0:T(128)S(1)}, f32[48]{0:T(128)}, u32[]{:S(2)}) copy-start(f32[48]{0:T(128)} %param.26) | copy-start | bytes 580
  928.7 98.9 %copy-start.27 = (f32[192,24]{0,1:T(8,128)S(1)}, f32[192,24]{0,1:T(8,128)}, u32[]{:S(2)}) copy-start(f32[192,24]{0,1:T(8,128)} %param.23) | copy-start | bytes 55300
  928.7 98.8 %copy-start.28 = (f32[192,24]{0,1:T(8,128)S(1)}, f32[192,24]{0,1:T(8,128)}, u32[]{:S(2)}) copy-start(f32[192,24]{0,1:T(8,128)} %reduce-scatter.19.cloned.1.call-done) | copy-start | bytes 55300
  928.7 98.8 %copy-start.33 = (f32[2,192,24]{1,2,0:T(8,128)S(1)}, f32[2,192,24]{1,2,0:T(8,128)}, u32[]{:S(2)}) copy-start(f32[2,192,24]{1,2,0:T(8,128)} %param.28) | copy-start | bytes 110596
  928.7 100.1 %copy-start.13 = (f32[768,24]{0,1:T(8,128)S(1)}, f32[768,24]{0,1:T(8,128)}, u32[]{:S(2)}) copy-start(f32[768,24]{0,1:T(8,128)} %param.25) | copy-start | bytes 221188
  928.7 100.1 %copy-start.19 = (f32[768,24]{0,1:T(8,128)S(1)}, f32[768,24]{0,1:T(8,128)}, u32[]{:S(2)}) copy-start(f32[768,24]{0,1:T(8,128)} %reduce-scatter.23.cloned.1.call-done) | copy-start | bytes 221188
  928.8 100.1 %copy-start.23 = (f32[2,768,24]{1,2,0:T(8,128)S(1)}, f32[2,768,24]{1,2,0:T(8,128)}, u32[]{:S(2)}) copy-start(f32[2,768,24]{1,2,0:T(8,128)} %param.30) | copy-start | bytes 442372
  928.8 101.5 %copy-start.15 = (f32[24,768]{1,0:T(8,128)S(1)}, f32[24,768]{1,0:T(8,128)}, u32[]{:S(2)}) copy-start(f32[24,768]{1,0:T(8,128)} %param.24) | copy-start | bytes 221188
  928.8 101.4 %copy-start.18 = (f32[24,768]{1,0:T(8,128)S(1)}, f32[24,768]{1,0:T(8,128)}, u32[]{:S(2)}) copy-start(f32[24,768]{1,0:T(8,128)} %reduce-scatter.21.cloned.1.call-done) | copy-start | bytes 221188
  928.8 101.4 %copy-start.24 = (f32[2,24,768]{2,1,0:T(8,128)S(1)}, f32[2,24,768]{2,1,0:T(8,128)}, u32[]{:S(2)}) copy-start(f32[2,24,768]{2,1,0:T(8,128)} %param.29) | copy-start | bytes 442372
  941.1 90.5 %copy-start.17 = (f32[24,3,192]{2,0,1:T(8,128)S(1)}, f32[24,3,192]{2,0,1:T(8,128)}, u32[]{:S(2)}) copy-start(f32[24,3,192]{2,0,1:T(8,128)} %param.22) | copy-start | bytes 165892
  941.1 90.5 %copy-start.20 = (f32[24,3,192]{2,0,1:T(8,128)S(1)}, f32[24,3,192]{2,0,1:T(8,128)}, u32[]{:S(2)}) copy-start(f32[24,3,192]{2,0,1:T(8,128)} %reduce-scatter.17.cloned.1.call-done) | copy-start | bytes 165892
  941.2 90.5 %copy-start.25 = (f32[2,24,3,192]{3,1,2,0:T(8,128)S(1)}, f32[2,24,3,192]{3,1,2,0:T(8,128)}, u32[]{:S(2)}) copy-start(f32[2,24,3,192]{3,1,2,0:T(8,128)} %param.27) | copy-start | bytes 331780
  (20 other events, 367.4 us)
Sparse Core Ops, SparseCore 0:
  56.9 13.1 all-gather.4
  193.7 9.9 reduce-scatter.8
  209.5 14.4 all-gather.6
  225.4 14.4 all-gather.8
  378.1 9.8 reduce-scatter.12
  397.6 14.5 all-gather.10
  416.9 125.5 reduce-scatter.20
  547.3 123.4 reduce-scatter.22
  675.4 120.5 reduce-scatter.18
  802.0 122.5 reduce-scatter.16
  927.5 10.8 reduce-scatter.14
  940.4 13.0 reduce-scatter.10
where the time goes:
time: 1060 us; the launch traced here: 1050 us
  waiting for transfers between devices  409 us (39%)
  blocking collectives  287 us (27%)
  matrix products  188 us (18%)
  other arithmetic  119 us (11%)
  local copies, waits for them, and re-layouts  26.2 us (2%)
  between operations  20.3 us (2%)
    reduce_scatter x1, waiting for transfers between devices, per_device(): lax.psum_scatter(grad_qkv, 'batch', scatter_dimension=0, tiled=True)  127 us
    reduce_scatter x1, waiting for transfers between devices, per_device(): lax.psum_scatter(grad_down, 'batch', scatter_dimension=1, tiled=True)  127 us
    reduce_scatter x1, waiting for transfers between devices, per_device(): lax.psum_scatter(grad_out, 'batch', scatter_dimension=1, tiled=True)  124 us
    unnamed x2, blocking collectives  82.6 us
    all_gather x1, blocking collectives, per_device(): lax.all_gather(up_master.astype(jnp.bfloat16), 'batch', axis=0, tiled=True)  46.4 us
    all_gather x1, blocking collectives, per_device(): lax.all_gather(out_master.astype(jnp.bfloat16), 'batch', axis=1, tiled=True)  40.6 us
    psum x1, blocking collectives, per_device(): grad_norm = jnp.sqrt(lax.psum(local_squares, ('batch', 'head')))  40 us
    all_gather x1, blocking collectives, per_device(): lax.all_gather(down_master.astype(jnp.bfloat16), 'batch', axis=1, tiled=T...  39 us
  transfers between devices with their start and end apart: 12, of which 7 were waited for; matrix products, arithmetic and copies ran while one was open for 20% of the time, Pallas kernels for 0%

commit v1 on v0

v1 whole, which is shorter than its diff:
```python
import functools

import jax
import jax.numpy as jnp
from jax import lax
from jax.experimental import pallas as pl
from jax.experimental.pallas import tpu as pltpu
from jax.sharding import PartitionSpec as P

HD = 64
STEP = 10
NORM_EPS = 1e-06
CLIP_NORM = 1000.0
BETA_ONE = 0.5
BETA_TWO = 0.5
ADAM_EPS = 1e-08
RATE_LIST = (0.06, 0.25, 0.06, 0.03, 0.5)
DECAY_LIST = (0.04, 0.04, 0.04, 0.04, 0.0)

F32 = jnp.float32
BF16 = jnp.bfloat16
NN = (((1,), (0,)), ((), ()))
NT = (((1,), (1,)), ((), ()))
TN = (((0,), (0,)), ((), ()))
QB = 128
FB = 512
FC = 256
PAIR = 2 * HD
VMEM = pltpu.CompilerParams(vmem_limit_bytes=56 * 2**20)


def cost(microseconds):
    return pl.CostEstimate(flops=microseconds * 1_000_000_000, bytes_accessed=1_000_000, transcendentals=0)


def mm(left, right, dims=NN):
    return lax.dot_general(left, right, dims, preferred_element_type=F32)


def normalize(values):
    centred = values - jnp.mean(values, axis=-1, keepdims=True)
    variance = jnp.mean(centred * centred, axis=-1, keepdims=True)
    rs = lax.rsqrt(variance + NORM_EPS)
    return centred * rs, rs


def norm_backward(normal, rs, gained):
    inner = jnp.mean(gained * normal, axis=-1, keepdims=True)
    return rs * (gained - jnp.mean(gained, axis=-1, keepdims=True) - normal * inner)


def gelu_parts(h):
    gauss = jnp.exp(h * h * -0.5)
    t = 1.0 / (1.0 + (0.3275911 * 0.7071067811865476) * jnp.abs(h))
    poly = t * (
        0.127414796
        + t * (-0.142248368 + t * (0.7107068705 + t * (-0.7265760135 + t * 0.5307027145)))
    )
    tail = poly * gauss
    return jnp.where(h < 0.0, tail, 1.0 - tail), gauss


def split_pairs(own, other, per_pair):
    wide, narrow = 2 * per_pair, per_pair
    singles = []
    for part in range(per_pair // HD):
        cols = slice(wide + part * HD, wide + (part + 1) * HD)
        singles += [own[:, cols], other[:, cols]]
    return own[:, :wide], jnp.concatenate(singles, axis=1), other[:, :wide]


def join_pairs(first, second, third, per_pair):
    parts = [
        [second[:, p * PAIR + side * HD : p * PAIR + (side + 1) * HD] for p in range(per_pair // HD)]
        for side in range(2)
    ]
    return [first] + parts[0], [third] + parts[1]


def forward_kernel(
    tok_ref, bias_ref, own_ref, other_ref, norms_ref, n1t_ref, qkv_ref, att_ref, p_ref, w_ref
):
    rows, width = tok_ref.shape

    @pl.when(pl.program_id(0) == 0)
    def _():
        cols = 9 * HD
        for i, part in enumerate(split_pairs(own_ref[:, :cols], other_ref[:, :cols], 3 * HD)):
            w_ref[i] = part

    x = tok_ref[...].astype(F32)
    normal, _ = normalize(x)
    n1 = (normal * norms_ref[0:1, :] + norms_ref[1:2, :]).astype(BF16)
    n1t_ref[...] = n1.T
    bias = bias_ref[...]
    lane = lax.broadcasted_iota(jnp.int32, (QB, PAIR), 1)
    for pair in range(width // PAIR):
        part = mm(n1, w_ref[pair])
        qkv_ref[pair, :, :PAIR] = (part[:, :PAIR].astype(BF16).astype(F32) * (HD**-0.5)).astype(BF16)
        qkv_ref[pair, :, PAIR:] = part[:, PAIR:].astype(BF16)
        kp = qkv_ref[pair, :, PAIR : 2 * PAIR]
        vp = qkv_ref[pair, :, 2 * PAIR :]
        for qb in range(rows // QB):
            sl = slice(qb * QB, (qb + 1) * QB)
            qp = qkv_ref[pair, sl, :PAIR]
            outs = []
            for half in range(2):
                qm = jnp.where((lane < HD) == (half == 0), qp, jnp.zeros_like(qp))
                s = mm(qm, kp, NT) + bias
                e = jnp.exp(s - jnp.max(s, axis=-1, keepdims=True))
                p = (e * (1.0 / jnp.sum(e, axis=-1, keepdims=True))).astype(BF16)
                p_ref[pair * 2 + half, sl, :] = p
                outs.append(mm(p, vp))
            att_ref[sl, pair * PAIR : (pair + 1) * PAIR] = jnp.where(
                lane < HD, outs[0], outs[1]
            ).astype(BF16)


def forward(tokens, bias, own, other, norms):
    seqs, rows, width = tokens.shape
    heads, pairs = width // HD, width // PAIR
    sq = pl.squeezed
    shape = jax.ShapeDtypeStruct
    whole = lambda *dims: pl.BlockSpec(dims, lambda s: (0,) * len(dims))
    return pl.pallas_call(
        forward_kernel,
        grid=(seqs,),
        in_specs=[
            pl.BlockSpec((sq, rows, width), lambda s: (s, 0, 0)),
            pl.BlockSpec((sq, 1, rows), lambda s: (s, 0, 0)),
            whole(*own.shape),
            whole(*other.shape),
            whole(4, width),
        ],
        out_specs=[
            pl.BlockSpec((sq, width, rows), lambda s: (s, 0, 0)),
            pl.BlockSpec((sq, pairs, rows, 3 * PAIR), lambda s: (s, 0, 0, 0)),
            pl.BlockSpec((sq, rows, width), lambda s: (s, 0, 0)),
            pl.BlockSpec((sq, heads, rows, rows), lambda s: (s, 0, 0, 0)),
            whole(pairs, width, 3 * PAIR),
        ],
        out_shape=[
            shape((seqs, width, rows), BF16),
            shape((seqs, pairs, rows, 3 * PAIR), BF16),
            shape((seqs, rows, width), BF16),
            shape((seqs, heads, rows, rows), BF16),
            shape((pairs, width, 3 * PAIR), BF16),
        ],
        compiler_params=VMEM,
        cost_estimate=cost(50),
        name="attention_forward",
    )(tokens, bias, own, other, norms)


def middle_kernel(
    seq_rows, units, len_ref, tok_ref, cot_ref, att_ref, own_ref, other_ref, norms_ref,
    out_ref, gmid_ref, gatt_ref, gown_ref, gother_ref, gnorm_ref,
    wo_ref, gout_ref, gup_ref, gdown_ref,
):
    step = pl.program_id(0)
    rows, width = tok_ref.shape
    halves = (own_ref, other_ref)

    @pl.when(step == 0)
    def _():
        gout_ref[...] = jnp.zeros_like(gout_ref)
        gup_ref[...] = jnp.zeros_like(gup_ref)
        gdown_ref[...] = jnp.zeros_like(gdown_ref)
        gnorm_ref[...] = jnp.zeros_like(gnorm_ref)
        cols = slice(2 * units, 2 * units + 3 * HD)
        parts = split_pairs(own_ref[:, cols], other_ref[:, cols], HD)
        for i, part in enumerate(parts):
            wo_ref[:, i * PAIR : (i + 1) * PAIR] = part

    first = step * rows
    row = first + lax.broadcasted_iota(jnp.int32, (rows, 1), 0)
    live = row < 0
    last = len_ref.shape[0] - 1
    for near in range(-(-rows // seq_rows) + 1):
        s = first // seq_rows + near
        bound = jnp.where(s <= last, len_ref[jnp.minimum(s, last)], 0)
        live = live | ((row >= s * seq_rows) & (row < s * seq_rows + bound))

    x = tok_ref[...].astype(F32)
    att = att_ref[...]
    mid = x + mm(att, wo_ref[...], NT)
    normal, rs = normalize(mid)
    gain, shift = norms_ref[2:3, :], norms_ref[3:4, :]
    n2 = (normal * gain + shift).astype(BF16)
    n2t = n2.T
    up = jnp.where(live, cot_ref[...].astype(F32), 0.0)
    gb = up.astype(BF16)
    gbt = gb.T
    bo = mid
    gtwo = jnp.zeros_like(mid)
    for half in range(2):
        for c in range(units // FC):
            cols = slice(c * FC, (c + 1) * FC)
            wu = halves[half][:, c * FC : (c + 1) * FC]
            wd = halves[half][:, units + c * FC : units + (c + 1) * FC]
            h = mm(n2, wu)
            ga = mm(gb, wd)
            cdf, gauss = gelu_parts(h)
            act = (h * cdf).astype(BF16)
            gh = (ga * (cdf + h * (gauss * 0.3989422804014327))).astype(BF16)
            bo = bo + mm(act, wd, NT)
            gtwo = gtwo + mm(gh, wu, NT)
            gup_ref[half, :, cols] += mm(n2t, gh)
            gdown_ref[half, :, cols] += mm(gbt, act)
    out_ref[...] = bo.astype(BF16)
    gnorm_ref[0:8, :] += jnp.sum((gtwo * normal).reshape(rows // 8, 8, width), axis=0)
    gnorm_ref[8:16, :] += jnp.sum(gtwo.reshape(rows // 8, 8, width), axis=0)
    gmid = up + norm_backward(normal, rs, gtwo * gain)
    gmid_ref[...] = gmid
    gm = gmid.astype(BF16)
    gout_ref[...] += mm(gm, att, TN)
    gatt_ref[...] = mm(gm, wo_ref[...]).astype(BF16)

    @pl.when(step == pl.num_programs(0) - 1)
    def _():
        total = gout_ref[...]
        sides = join_pairs(
            total[:, :PAIR], total[:, PAIR : 2 * PAIR], total[:, 2 * PAIR :], HD
        )
        for half, ref in enumerate((gown_ref, gother_ref)):
            ref[:, :units] = gup_ref[half].astype(BF16)
            ref[:, units : 2 * units] = gdown_ref[half].astype(BF16)
            blank = jnp.zeros((total.shape[0], HD), F32)
            ref[:, 2 * units :] = jnp.concatenate(sides[half] + [blank], axis=1).astype(BF16)


def middle(lengths, tokens, cotangent, attended, own, other, norms):
    seqs, seq_rows, width = tokens.shape
    total = seqs * seq_rows
    packed = own.shape[1]
    units = (packed - 4 * HD) // 2
    flat = lambda a: a.reshape(total, width)
    rowspec = pl.BlockSpec((FB, width), lambda s: (s, 0))
    whole = lambda *dims: pl.BlockSpec(dims, lambda s: (0,) * len(dims))
    shape = jax.ShapeDtypeStruct
    return pl.pallas_call(
        functools.partial(middle_kernel, seq_rows, units),
        grid=(total // FB,),
        in_specs=[
            pl.BlockSpec(memory_space=pltpu.SMEM),
            rowspec,
            rowspec,
            rowspec,
            whole(*own.shape),
            whole(*other.shape),
            whole(4, width),
        ],
        out_specs=[rowspec] * 3 + [whole(*own.shape), whole(*own.shape), whole(16, width)],
        out_shape=[
            shape((total, width), BF16),
            shape((total, width), F32),
            shape((total, width), BF16),
            shape(own.shape, BF16),
            shape(own.shape, BF16),
            shape((16, width), F32),
        ],
        scratch_shapes=[
            pltpu.VMEM((width, width), BF16),
            pltpu.VMEM((width, width), F32),
            pltpu.VMEM((2, width, units), F32),
            pltpu.VMEM((2, width, units), F32),
        ],
        compiler_params=VMEM,
        cost_estimate=cost(50),
        name="feed_forward",
    )(lengths, flat(tokens), flat(cotangent), flat(attended), own, other, norms)


def backward_kernel(
    n1t_ref, qkv_ref, p_ref, gatt_ref, att_ref, gp_ref, gown_ref, gother_ref, gqkv_ref
):
    seq, pair = pl.program_id(0), pl.program_id(1)
    rows = qkv_ref.shape[0]
    qp, kp, vp = qkv_ref[:, :PAIR], qkv_ref[:, PAIR : 2 * PAIR], qkv_ref[:, 2 * PAIR :]
    ga = gatt_ref[...]
    prod = ga.astype(F32) * att_ref[...].astype(F32)
    lane = lax.broadcasted_iota(jnp.int32, (QB, PAIR), 1)
    gat, qt = ga.T, qp.T
    zero = jnp.zeros((QB, PAIR), BF16)
    gq = [[], []]
    gkt, gvt = [], []
    for half in range(2):
        ds_all = []
        mask = (lane < HD) == (half == 0)
        for qb in range(rows // QB):
            sl = slice(qb * QB, (qb + 1) * QB)
            dp = mm(jnp.where(mask, ga[sl], zero), vp, NT)
            inner = jnp.sum(jnp.where(mask, prod[sl], 0.0), axis=-1, keepdims=True)
            ds = (p_ref[half, sl, :].astype(F32) * (dp - inner)).astype(BF16)
            ds_all.append(ds)
            gq[half].append(mm(ds, kp))
        ds = jnp.concatenate(ds_all, axis=0)
        hs = slice(half * HD, half * HD + HD)
        gkt.append(mm(qt[hs], ds))
        gvt.append(mm(gat[hs], p_ref[half]))
    for qb in range(rows // QB):
        sl = slice(qb * QB, (qb + 1) * QB)
        joined = jnp.where(lane < HD, gq[0][qb], gq[1][qb])
        gp_ref[sl, :PAIR] = (joined * (HD**-0.5)).astype(BF16)
    gp_ref[:, PAIR : 2 * PAIR] = jnp.concatenate(gkt, axis=0).astype(BF16).T
    gp_ref[:, 2 * PAIR :] = jnp.concatenate(gvt, axis=0).astype(BF16).T
    new = mm(n1t_ref[...], gp_ref[...])

    @pl.when(seq == 0)
    def _():
        gqkv_ref[pair] = new

    @pl.when(seq > 0)
    def _():
        gqkv_ref[pair] += new

    @pl.when((seq == pl.num_programs(0) - 1) & (pair == pl.num_programs(1) - 1))
    def _():
        sides = join_pairs(gqkv_ref[0], gqkv_ref[1], gqkv_ref[2], 3 * HD)
        blank = jnp.zeros((gqkv_ref.shape[1], HD), F32)
        for columns, ref in zip(sides, (gown_ref, gother_ref)):
            ref[...] = jnp.concatenate(columns + [blank], axis=1).astype(BF16)


def backward(n1t, qkv, probs, gatt, attended):
    seqs, rows, width = attended.shape
    pairs = width // PAIR
    sq = pl.squeezed
    pairspec = pl.BlockSpec((sq, rows, PAIR), lambda s, p: (s, 0, p))
    groupspec = pl.BlockSpec((sq, sq, rows, 3 * PAIR), lambda s, p: (s, p, 0, 0))
    whole = lambda *dims: pl.BlockSpec(dims, lambda s, p: (0,) * len(dims))
    shape = jax.ShapeDtypeStruct
    packed = (width, 10 * HD)
    return pl.pallas_call(
        backward_kernel,
        grid=(seqs, pairs),
        in_specs=[
            pl.BlockSpec((sq, width, rows), lambda s, p: (s, 0, 0)),
            groupspec,
            pl.BlockSpec((sq, 2, rows, rows), lambda s, p: (s, p, 0, 0)),
            pairspec,
            pairspec,
        ],
        out_specs=[groupspec, whole(*packed), whole(*packed)],
        out_shape=[shape(qkv.shape, BF16), shape(packed, BF16), shape(packed, BF16)],
        scratch_shapes=[pltpu.VMEM((pairs, width, 3 * PAIR), F32)],
        compiler_params=VMEM,
        cost_estimate=cost(50),
        name="attention_backward",
    )(n1t, qkv, probs, gatt, attended)


def input_kernel(tok_ref, gp_ref, gmid_ref, w_ref, norms_ref, two_ref, gin_ref, terms_ref):
    rows, width = tok_ref.shape
    gone = mm(gp_ref[0], w_ref[0], NT)
    for pair in range(1, w_ref.shape[0]):
        gone = gone + mm(gp_ref[pair], w_ref[pair], NT)
    normal, rs = normalize(tok_ref[...].astype(F32))

    @pl.when(pl.program_id(0) == 0)
    def _():
        terms_ref[...] = jnp.zeros_like(terms_ref)
        terms_ref[2:3, :] = jnp.sum(two_ref[0:8, :], axis=0, keepdims=True)
        terms_ref[3:4, :] = jnp.sum(two_ref[8:16, :], axis=0, keepdims=True)

    terms_ref[0:1, :] += jnp.sum(gone * normal, axis=0, keepdims=True)
    terms_ref[1:2, :] += jnp.sum(gone, axis=0, keepdims=True)
    gin_ref[...] = gmid_ref[...] + norm_backward(normal, rs, gone * norms_ref[0:1, :])


def input_gradient(tokens, gp, gmid, wpairs, norms, gnorm_two):
    seqs, rows, width = tokens.shape
    pairs = width // PAIR
    sq = pl.squeezed
    full = pl.BlockSpec((sq, rows, width), lambda s: (s, 0, 0))
    whole = lambda *dims: pl.BlockSpec(dims, lambda s: (0,) * len(dims))
    shape = jax.ShapeDtypeStruct
    return pl.pallas_call(
        input_kernel,
        grid=(seqs,),
        in_specs=[
            full,
            pl.BlockSpec((sq, pairs, rows, 3 * PAIR), lambda s: (s, 0, 0, 0)),
            full,
            whole(pairs, width, 3 * PAIR),
            whole(4, width),
            whole(16, width),
        ],
        out_specs=[full, whole(8, width)],
        out_shape=[shape((seqs, rows, width), F32), shape((8, width), F32)],
        compiler_params=VMEM,
        cost_estimate=cost(12),
        name="input_gradient",
    )(tokens, gp, gmid, wpairs, norms, gnorm_two)


def pack_kernel(qkv_ref, out_ref, up_ref, down_ref, norm_ref, lead_ref, rest_ref):
    chips, rows, _ = lead_ref.shape
    part = norm_ref.shape[1]
    norm = norm_ref[...]
    high = norm.astype(BF16).astype(F32)
    row = lax.broadcasted_iota(jnp.int32, (rows, part), 0)
    extra = jnp.where(row == 0, high, jnp.where(row == 1, norm - high, 0.0))
    columns = [qkv_ref[c, :, :PAIR] for c in range(3)] + [qkv_ref[c, :, PAIR:] for c in range(3)]
    blank = jnp.zeros((rows, HD - part), F32)
    lead_ref[...] = jnp.broadcast_to(
        jnp.concatenate(columns + [extra, blank], axis=1).astype(BF16)[None], lead_ref.shape
    )
    blank = jnp.zeros((rows, HD), F32)
    rest_ref[...] = jnp.concatenate([up_ref[...], down_ref[...], out_ref[...], blank], axis=1).astype(BF16)


def sum_kernel(parts_ref, rest_ref, terms_ref, lead_ref, message_ref):
    parts = parts_ref[...].astype(F32)
    lead = jnp.sum(parts, axis=0)
    lead_ref[...] = lead
    rest = rest_ref[...].astype(F32)
    lanes = message_ref.shape[1]
    total = jnp.zeros((lead.shape[0], PAIR), F32)
    for values in (lead, rest):
        for start in range(0, values.shape[1], PAIR):
            piece = values[:, start : start + PAIR]
            total = total + piece * piece
    message_ref[...] = terms_ref[...]
    message_ref[4:5, :PAIR] = jnp.sum(total, axis=0, keepdims=True)


def adamw(master, gradient, moments, rate, decay):
    moment = BETA_ONE * moments[0] + (1.0 - BETA_ONE) * gradient
    second = BETA_TWO * moments[1] + (1.0 - BETA_TWO) * gradient * gradient
    step_size = (
        moment / (1.0 - BETA_ONE**STEP) / (jnp.sqrt(second / (1.0 - BETA_TWO**STEP)) + ADAM_EPS)
    )
    return master - rate * (step_size + decay * master), moment, second


def update_kernel(
    message_ref, mine_ref, lead_ref, rest_ref,
    qkv_ref, out_ref, up_ref, down_ref, norm_ref,
    qkv_m_ref, out_m_ref, up_m_ref, down_m_ref, norm_m_ref,
    gn_ref, qkv_n_ref, out_n_ref, up_n_ref, down_n_ref, norm_n_ref,
    qkv_s_ref, out_s_ref, up_s_ref, down_s_ref, norm_s_ref, grads_ref,
):
    units = up_ref.shape[1]
    terms = message_ref[0:4, :]
    squares = jnp.sum(terms * terms, axis=(0, 1), keepdims=True) + jnp.sum(
        message_ref[4:5, :], axis=(0, 1), keepdims=True
    )
    grad_norm = jnp.sqrt(squares)
    gn_ref[...] = grad_norm
    factor = jnp.minimum(1.0, CLIP_NORM / (grad_norm + 1e-06))
    for c in range(3):
        wide = lead_ref[:, c * PAIR : (c + 1) * PAIR]
        narrow = lead_ref[:, 3 * PAIR + c * HD : 3 * PAIR + (c + 1) * HD]
        for cols, grad in ((slice(0, PAIR), wide), (slice(PAIR, PAIR + HD), narrow)):
            new, moment, second = adamw(
                qkv_ref[c, :, cols], factor * grad, qkv_m_ref[:, c, :, cols], RATE_LIST[0], DECAY_LIST[0]
            )
            qkv_n_ref[c, :, cols] = new
            qkv_s_ref[0, c, :, cols] = moment
            qkv_s_ref[1, c, :, cols] = second
    norm_grads = factor * mine_ref[...]
    grads_ref[...] = norm_grads
    plain = (
        (out_ref, rest_ref[:, 2 * units : 2 * units + 3 * HD], out_m_ref, out_n_ref, out_s_ref, 1),
        (up_ref, rest_ref[:, :units], up_m_ref, up_n_ref, up_s_ref, 2),
        (down_ref, rest_ref[:, units : 2 * units], down_m_ref, down_n_ref, down_s_ref, 3),
    )
    for master, grad, moments, next_ref, state_ref, i in plain:
        next_ref[...], state_ref[0], state_ref[1] = adamw(
            master[...], factor * grad.astype(F32), moments[...], RATE_LIST[i], DECAY_LIST[i]
        )
    norm_n_ref[...], norm_s_ref[0:1, :], norm_s_ref[1:2, :] = adamw(
        norm_ref[...], norm_grads, (norm_m_ref[0:1, :], norm_m_ref[1:2, :]), RATE_LIST[4], DECAY_LIST[4]
    )


def small_call(kernel, name, out_shape, *operands):
    return pl.pallas_call(kernel, out_shape=out_shape, compiler_params=VMEM, cost_estimate=cost(3), name=name)(
        *operands
    )


def swap(values):
    return lax.ppermute(values, "head", [(0, 1), (1, 0)])


def per_device(
    groups,
    tokens,
    cotangent,
    lengths,
    key_masks,
    qkv_master,
    out_master,
    up_master,
    down_master,
    norm_master,
    qkv_moments,
    out_moments,
    up_moments,
    down_moments,
    norm_moments,
):
    seqs, slot_rows, width = tokens.shape
    chips = groups[2]
    shard_rows = qkv_master.shape[0]
    norm_part = norm_master.shape[0]
    units = up_master.shape[1]
    side = lax.axis_index("head")
    own_first = side == 0

    qkv_rows = qkv_master.transpose(1, 0, 2)
    masters = (qkv_rows, out_master.T, up_master, down_master.T, norm_master[None])
    shape = jax.ShapeDtypeStruct
    lead, rest = small_call(
        pack_kernel,
        "pack_weights",
        [shape((chips, shard_rows, 10 * HD), BF16), shape((shard_rows, 2 * units + 4 * HD), BF16)],
        *masters,
    )
    lead_own = lax.all_to_all(lead, "batch", 0, 0)
    rest_own = lax.all_gather(rest, "batch", axis=0, tiled=True)
    lead_other = swap(lead_own)

    def norms_of(gathered):
        parts = gathered[:, :2, 9 * HD : 9 * HD + norm_part].astype(F32)
        return parts[:, 0] + parts[:, 1]

    norms_own, norms_other = norms_of(lead_own), norms_of(lead_other)
    norms = jnp.stack(
        [jnp.where(own_first, norms_own, norms_other), jnp.where(own_first, norms_other, norms_own)], axis=1
    ).reshape(4, width)

    positions = jnp.arange(slot_rows, dtype=jnp.int32)
    own_lengths = lax.dynamic_slice_in_dim(lengths, side * seqs, seqs)
    own_masks = lax.dynamic_slice_in_dim(key_masks, side * seqs, seqs)
    visible = (positions[None, :] < own_lengths[:, None]) & ((own_masks == 1) | (positions[None, :] == 0))
    bias = jnp.where(visible, 0.0, -1e30).astype(F32)[:, None, :]

    flat = lambda a: a.reshape(chips * shard_rows, a.shape[-1])
    n1t, qkv, attended, probs, wpairs = forward(tokens, bias, flat(lead_own), flat(lead_other), norms)
    rest_own, attended = lax.optimization_barrier((rest_own, attended))
    rest_other = swap(rest_own)
    block_out, gmid, gatt, grest_own, grest_other, gnorm_two = middle(
        own_lengths, tokens, cotangent, attended, rest_own, rest_other, norms
    )
    per_seq = lambda a: a.reshape(seqs, slot_rows, width)
    rest_sum = (grest_own.astype(F32) + swap(grest_other).astype(F32)).astype(BF16)
    rest_part = lax.psum_scatter(
        rest_sum, "batch", scatter_dimension=0, tiled=True, axis_index_groups=groups[0]
    )
    gp, glead_own, glead_other = backward(n1t, qkv, probs, per_seq(gatt), attended)
    rest_part, glead_own, glead_other = lax.optimization_barrier((rest_part, glead_own, glead_other))
    rest_shard = lax.psum_scatter(
        rest_part, "batch", scatter_dimension=0, tiled=True, axis_index_groups=groups[1]
    )
    lead_sum = (glead_own.astype(F32) + swap(glead_other).astype(F32)).astype(BF16)
    lead_parts = lax.all_to_all(lead_sum.reshape(chips, shard_rows, 10 * HD), "batch", 0, 0)
    input_grad, terms = input_gradient(tokens, gp, per_seq(gmid), wpairs, norms, gnorm_two)
    lead_shard, message = small_call(
        sum_kernel,
        "sum_parts",
        [shape((shard_rows, 10 * HD), F32), shape(terms.shape, F32)],
        lead_parts,
        rest_shard,
        terms,
    )
    message = message + swap(message)
    stride = 1
    while stride < chips:
        message = message + lax.ppermute(message, "batch", [(i, i ^ stride) for i in range(chips)])
        stride *= 2
    place = (lax.axis_index("batch") * 2 + side) * norm_part
    mine = lax.dynamic_slice_in_dim(message[:4].reshape(1, 4 * width), place, norm_part, axis=1)
    like = lambda a: shape(a.shape, F32)
    moments = (
        qkv_moments.transpose(0, 2, 1, 3),
        out_moments.transpose(0, 2, 1),
        up_moments,
        down_moments.transpose(0, 2, 1),
        norm_moments,
    )
    results = small_call(
        update_kernel,
        "update_weights",
        [shape((1, 1), F32)] + [like(a) for a in masters + moments] + [like(mine)],
        message,
        mine,
        lead_shard,
        rest_shard,
        *masters,
        *moments,
    )
    grad_norm, qkv_next, out_next, up_next, down_next, norm_next = results[:6]
    qkv_states, out_states, up_states, down_states, norm_states, norm_grads = results[6:]
    return (
        per_seq(block_out),
        input_grad,
        grad_norm.reshape(()),
        qkv_next.transpose(1, 0, 2),
        out_next.T,
        up_next,
        down_next.T,
        norm_next[0],
        qkv_states.transpose(0, 2, 1, 3),
        out_states.transpose(0, 2, 1),
        up_states,
        down_states.transpose(0, 2, 1),
        norm_states,
        norm_grads[0],
    )


def solution(mesh):
    chips = mesh.shape["batch"]
    near = 4
    outer = [[c + near * z for z in range(chips // near)] for c in range(near)]
    inner = [[near * z + c for c in range(near)] for z in range(chips // near)]
    return jax.shard_map(
        functools.partial(per_device, (outer, inner, chips)),
        mesh=mesh,
        in_specs=(
            P(("batch", "head"), None, None),
            P(("batch", "head"), None, None),
            P("batch"),
            P("batch", None),
            P("batch", None, "head"),
            P("head", "batch"),
            P("batch", "head"),
            P("head", "batch"),
            P(("batch", "head")),
            P(None, "batch", None, "head"),
            P(None, "head", "batch"),
            P(None, "batch", "head"),
            P(None, "head", "batch"),
            P(None, ("batch", "head")),
        ),
        out_specs=(
            P(("batch", "head"), None, None),
            P(("batch", "head"), None, None),
            P(),
            P("batch", None, "head"),
            P("head", "batch"),
            P("batch", "head"),
            P("head", "batch"),
            P(("batch", "head")),
            P(None, "batch", None, "head"),
            P(None, "head", "batch"),
            P(None, "batch", "head"),
            P(None, "head", "batch"),
            P(None, ("batch", "head")),
            P(("batch", "head")),
        ),
        check_vma=False,
    )
```

time: 1060 us -> 246 us (0.23)
  waiting for transfers between devices: 409 us -> 40.4 us
  blocking collectives: 287 us -> 0 us
  matrix products: 188 us -> 0 us
  Pallas kernels: 0 us -> 162 us
  other arithmetic: 119 us -> 5.75 us
  local copies, waits for them, and re-layouts: 26.2 us -> 4.02 us
  starting transfers between devices: 1.75 us -> 19.5 us
    reduce_scatter x8 -> x1, waiting for transfers between devices: 409 us -> 0.01 us  [per_device(): lax.psum_scatter(rest_sum, 'batch', scatter_dimension=0, tiled=True, axis...]
    dot_general x68 -> x0, matrix products: 188 us -> none  [the longest x8 20.2 us: attend_backward(): jnp.einsum('qhe,khe->hqk', grad_attended, values, preferred_element_type=...]
    all_gather x4 -> x0, blocking collectives: 165 us -> none  [the longest x1 46.4 us: per_device(): lax.all_gather(up_master.astype(jnp.bfloat16), 'batch', axis=0, tiled=True)]
    pallas_call x0 -> x7, Pallas kernels: none -> 162 us  [the longest x1 59.7 us: forward(): pl.pallas_call(forward_kernel, grid=(seqs,), in_specs=[pl.BlockSpec((sq,...]
    unnamed x2 -> x0, blocking collectives: 82.6 us -> none
    convert_element_type x18 -> x4, other arithmetic: 59.9 us -> 4.9 us  [the longest x1 2.79 us: per_device(): (grest_own.astype(F32) + swap(grest_other).astype(F32)).astype(BF16)]
    psum x1 -> x0, blocking collectives: 40 us -> none  [per_device(): grad_norm = jnp.sqrt(lax.psum(local_squares, ('batch', 'head')))]
    reduce_sum x21 -> x0, other arithmetic: 33.9 us -> none  [the longest x4 10.9 us: layer_norm(): return centred * lax.rsqrt(variance + NORM_EPS) * norm_gain + norm_bias]
  transfers between devices with their start and end apart: 12 -> 14, of which waited for: 7 -> 11; matrix products, arithmetic and copies ran while one was open for 20% -> 1% of each run, Pallas kernels for 0% -> 45%
where the time goes in v1:
time: 246 us; the launch traced here: 245 us
  Pallas kernels  162 us (66%)
  waiting for transfers between devices  40.4 us (16%)
  starting transfers between devices  19.5 us (8%)
  between operations  13.9 us (6%)
  other arithmetic  5.75 us (2%)
  local copies, waits for them, and re-layouts  4.02 us (2%)
    pallas_call x1, Pallas kernels, forward(): pl.pallas_call(forward_kernel, grid=(seqs,), in_specs=[pl.BlockSpec((sq,...  59.7 us
    pallas_call x1, Pallas kernels, middle(): pl.pallas_call(functools.partial(middle_kernel, seq_rows, units), grid=(t...  45.3 us
    pallas_call x1, Pallas kernels, backward(): pl.pallas_call(backward_kernel, grid=(seqs, pairs), in_specs=[pl.BlockSpe...  40.2 us
    all_to_all x1, waiting for transfers between devices, per_device(): lead_own = lax.all_to_all(lead, 'batch', 0, 0)  13.7 us
    ppermute x5, waiting for transfers between devices, swap(): return lax.ppermute(values, 'head', [(0, 1), (1, 0)])  10.7 us
    pallas_call x1, Pallas kernels, input_gradient(): pl.pallas_call(input_kernel, grid=(seqs,), in_specs=[full, pl.BlockSpec((...  10.5 us
    ppermute x4, waiting for transfers between devices, per_device(): lax.ppermute(message, 'batch', [(i, i ^ stride) for i in range(chips)])  9.04 us
    all_to_all x1, starting transfers between devices, per_device(): lead_own = lax.all_to_all(lead, 'batch', 0, 0)  8.31 us
  transfers between devices with their start and end apart: 14, of which 11 were waited for; matrix products, arithmetic and copies ran while one was open for 1% of the time, Pallas kernels for 45%

profile of v1, /device:TPU:0, one launch (start us, length us, event | category | flops | bytes accessed | tf_op | source)
XLA Modules:
  0.0 245.3 jit_solution(10534092133925640423)
XLA Ops:
  7.2 1.9 pack_weights.1
  9.1 8.3 %all-to-all-start = ((bf16[16,24,640]{2,1,0:T(8,128)(2,1)}), bf16[16,24,640]{2,1,0:T(8,128)(2,1)S(1)}, u32[]{:S(2)}, u32[]{:S(2)}) async-start(bf16[16,24,640]{2,1,0:T(8,128)(2,1)} %get-tuple-element.52), calls=%async_computation | async-start | bytes 983040 | tf_op jit(solution)/shard_map/all_to_all | solution.py:522
  17.4 0.7 all-gather.2.cloned.1.call-update
  18.2 13.7 %all-to-all-done = bf16[16,24,640]{2,1,0:T(8,128)(2,1)S(1)} async-done(((bf16[16,24,640]{2,1,0:T(8,128)(2,1)}), bf16[16,24,640]{2,1,0:T(8,128)(2,1)S(1)}, u32[]{:S(2)}, u32[]{:S(2)}) %all-to-all-start) | async-done | bytes 491552 | tf_op jit(solution)/shard_map/all_to_all | solution.py:522
  32.8 1.0 collective-permute-done
  33.9 0.7 reshape.74.norms_ref
  34.6 59.7 %attention_forward.1 = (bf16[4,384,640]{2,1,0:T(8,128)(2,1)}, bf16[4,3,640,384]{3,2,1,0:T(8,128)(2,1)}, bf16[4,640,384]{2,1,0:T(8,128)(2,1)}, bf16[4,6,640,640]{3,2,1,0:T(8,128)(2,1)}, bf16[3,384,384]{2,1,0:T(8,128)(2,1)}) custom-call(bf16[4,640,384]{2,1,0:T(8,128)(2,1)} %tok_ref.3, f32[4,1,640]{2,1,0:T(1,128)} %broadcast_in_dim.20.bias_ref, ...), custom_call_target="tpu_custom_call" | custom-call | flops 49999998976 | bytes 1000000 | tf_op jit(solution)/shard_map/attention_forward/pallas_call | solution.py:125
  94.5 3.2 %collective-permute-done.1.other_ref = bf16[384,1792]{1,0:T(8,128)(2,1)S(1)} collective-permute-done((bf16[384,1792]{1,0:T(8,128)(2,1)}, bf16[384,1792]{1,0:T(8,128)(2,1)S(1)}, u32[]{:S(2)}, u32[]{:S(2)}) %collective-permute-start.1) | collective-permute-done | bytes 1376288 | tf_op jit(solution)/shard_map/ppermute | solution.py:485
  97.7 1.1 copy-done.6
  98.8 45.3 %feed_forward.1 = (bf16[2560,384]{1,0:T(8,128)(2,1)}, f32[2560,384]{1,0:T(8,128)}, bf16[2560,384]{1,0:T(8,128)(2,1)}, bf16[384,1792]{1,0:T(8,128)(2,1)}, bf16[384,1792]{1,0:T(8,128)(2,1)}, /*index=5*/f32[16,384]{1,0:T(8,128)}) custom-call(s32[4]{0:T(128)} %copy-done.4, bf16[2560,384]{1,0:T(8,128)(2,1)} %bitcast.34, bf16[2560,384]{1,0:T(8,128)(2,1)} %bitcast.33, ...), custom_call_target="tpu_custom_call" | custom-call | flops 49999998976 | bytes 1000000 | tf_op jit(solution)/shard_map/feed_forward/pallas_call | solution.py:241
  144.4 3.2 %collective-permute-done.2 = bf16[384,1792]{1,0:T(8,128)(2,1)S(1)} collective-permute-done((bf16[384,1792]{1,0:T(8,128)(2,1)}, bf16[384,1792]{1,0:T(8,128)(2,1)S(1)}, u32[]{:S(2)}, u32[]{:S(2)}) %collective-permute-start.2) | collective-permute-done | bytes 1376288 | tf_op jit(solution)/shard_map/ppermute | solution.py:485
  147.6 2.8 %add_convert_fusion = bf16[384,1792]{1,0:T(8,128)(2,1)} fusion(bf16[384,1792]{1,0:T(8,128)(2,1)S(1)} %collective-permute-done.2, bf16[384,1792]{1,0:T(8,128)(2,1)} %get-tuple-element.66), kind=kLoop, calls=%fused_computation | loop fusion | flops 2752512 | bytes 4128768 | tf_op jit(solution)/shard_map/convert_element_type | solution.py:549
  150.4 40.2 %attention_backward.1 = (bf16[4,3,640,384]{3,2,1,0:T(8,128)(2,1)}, bf16[384,640]{1,0:T(8,128)(2,1)}, bf16[384,640]{1,0:T(8,128)(2,1)}) custom-call(bf16[4,384,640]{2,1,0:T(8,128)(2,1)} %get-tuple-element.57.n1t_ref, bf16[4,3,640,384]{3,2,1,0:T(8,128)(2,1)} %get-tuple-element.58.qkv_ref, bf16[4,6,640,640]{3,2,1,0:T(8,128)(2,1)} %get-tuple-element.59.p_ref, ...), custom_call_target="tpu_custom_call" | custom-call | flops 49999998976 | bytes 1000000 | tf_op jit(solution)/shard_map/attention_backward/pallas_call | solution.py:334
  190.9 1.9 collective-permute-done.3
  192.8 2.0 add_convert_fusion.1
  194.7 3.9 %all-to-all-start.1 = ((bf16[16,24,640]{2,1,0:T(8,128)(2,1)}), bf16[16,24,640]{2,1,0:T(8,128)(2,1)S(1)}, u32[]{:S(2)}, u32[]{:S(2)}) async-start(bf16[16,24,640]{2,1,0:T(8,128)(2,1)} %bitcast.12), calls=%async_computation.2 | async-start | bytes 983040 | tf_op jit(solution)/shard_map/all_to_all | solution.py:559
  198.6 10.5 %input_gradient.1 = (f32[4,640,384]{2,1,0:T(8,128)}, f32[8,384]{1,0:T(8,128)}) custom-call(bf16[4,640,384]{2,1,0:T(8,128)(2,1)} %tok_ref.3, bf16[4,3,640,384]{3,2,1,0:T(8,128)(2,1)} %get-tuple-element.61.gp_ref, f32[4,640,384]{2,1,0:T(8,128)} %bitcast.46, bf16[3,384,384]{2,1,0:T(8,128)(2,1)} %get-tuple-element.63.w_ref, f32[4,384]{1,0:T(4,128)} %reshape.74.norms_ref, ...), custom_call_target="tpu_custom_call" | custom-call | flops 12000000000 | bytes 1000000 | tf_op jit(solution)/shard_map/input_gradient/pallas_call | solution.py:378
  209.1 6.2 %reduce-scatter.7.cloned.1.call-done.rest_ref = bf16[24,1792]{1,0:T(8,128)(2,1)} async-done(((bf16[96,1792]{1,0:T(8,128)(2,1)}), bf16[24,1792]{1,0:T(8,128)(2,1)}) %reduce-scatter.7.cloned.1.call-update) | async-done | bytes 86032
  215.3 0.8 copy-done.1
  216.1 1.8 sum_parts.1
  217.9 1.4 collective-permute-done.4
  219.3 0.7 add.50
  220.0 1.4 collective-permute-start.5
  221.4 2.3 collective-permute-done.5
  223.7 1.4 collective-permute-start.6
  225.1 2.3 collective-permute-done.6
  227.4 1.5 collective-permute-start.7
  228.8 2.2 collective-permute-done.7
  231.1 2.4 collective-permute-start.8
  233.5 2.2 collective-permute-done.8
  235.7 0.7 constant_dynamic-slice_fusion.mine_ref
  236.4 2.4 update_weights.1
  (41 shorter events, 1.8 us)
Async XLA Ops:
  7.2 24.7 %copy-start.7 = (s32[8]{0:T(128)S(1)}, s32[8]{0:T(128)}, u32[]{:S(2)}) copy-start(s32[8]{0:T(128)} %param.16) | copy-start | bytes 100
  7.2 24.8 %copy-start.3 = (s32[8,640]{1,0:T(8,128)S(1)}, s32[8,640]{1,0:T(8,128)}, u32[]{:S(2)}) copy-start(s32[8,640]{1,0:T(8,128)} %param.17) | copy-start | bytes 61444
  9.1 22.8 %all-to-all-start = ((bf16[16,24,640]{2,1,0:T(8,128)(2,1)}), bf16[16,24,640]{2,1,0:T(8,128)(2,1)S(1)}, u32[]{:S(2)}, u32[]{:S(2)}) async-start(bf16[16,24,640]{2,1,0:T(8,128)(2,1)} %get-tuple-element.52), calls=%async_computation | async-start | bytes 983040 | tf_op jit(solution)/shard_map/all_to_all | solution.py:522
  17.4 76.9 %all-gather.2.cloned.1.call-start = ((), (), s32[]{:S(2)}) async-start(), calls=%async_computation.4 | async-start | bytes 1462272 | tf_op jit(solution)/shard_map/all_gather | solution.py:523
  18.1 172.5 %reduce-scatter.5.cloned.1.call-start = ((), (), s32[]{:S(2)}) async-start(), calls=%async_computation.5 | async-start | bytes 1720320 | tf_op jit(solution)/shard_map/reduce_scatter | solution.py:550
  31.9 2.7 %copy-start = (bf16[16,24,640]{2,1,0:T(8,128)(2,1)}, bf16[16,24,640]{2,1,0:T(8,128)(2,1)S(1)}, u32[]{:S(2)}) copy-start(bf16[16,24,640]{2,1,0:T(8,128)(2,1)S(1)} %all-to-all-done) | copy-start | bytes 1474564
  31.9 1.9 collective-permute-start
  32.0 62.3 %copy-start.4 = (s32[4]{0:T(128)}, s32[4]{0:T(128)S(1)}, u32[]{:S(2)}) copy-start(s32[4]{0:T(128)S(1)} %dynamic_slice.9.len_ref) | copy-start | bytes 52
  33.7 0.8 copy-start.5
  94.3 3.4 %collective-permute-start.1 = (bf16[384,1792]{1,0:T(8,128)(2,1)}, bf16[384,1792]{1,0:T(8,128)(2,1)S(1)}, u32[]{:S(2)}, u32[]{:S(2)}) collective-permute-start(bf16[384,1792]{1,0:T(8,128)(2,1)} %all-gather.2.cloned.1.call-done.own_ref), channel_id=1, source_target_pairs={{0,1},{1,0},{2,3},{3,2},{4,5},{5,4},{6,7},{7,6},{8,9},{9,8},{10,11... | collective-permute-start | bytes 4128776 | tf_op jit(solution)/shard_map/ppermute | solution.py:485
  97.7 1.1 copy-start.6
  144.2 3.4 %collective-permute-start.2 = (bf16[384,1792]{1,0:T(8,128)(2,1)}, bf16[384,1792]{1,0:T(8,128)(2,1)S(1)}, u32[]{:S(2)}, u32[]{:S(2)}) collective-permute-start(bf16[384,1792]{1,0:T(8,128)(2,1)} %get-tuple-element.67), channel_id=1, source_target_pairs={{0,1},{1,0},{2,3},{3,2},{4,5},{5,4},{6,7},{7,6},{8,9},{9,8},{10,11... | collective-permute-start | bytes 4128776 | tf_op jit(solution)/shard_map/ppermute | solution.py:485
  150.4 64.9 %reduce-scatter.7.cloned.1.call-start = ((), (), s32[]{:S(2)}) async-start(), calls=%async_computation.6 | async-start | bytes 430080
  190.6 2.1 collective-permute-start.3
  194.7 20.5 %all-to-all-start.1 = ((bf16[16,24,640]{2,1,0:T(8,128)(2,1)}), bf16[16,24,640]{2,1,0:T(8,128)(2,1)S(1)}, u32[]{:S(2)}, u32[]{:S(2)}) async-start(bf16[16,24,640]{2,1,0:T(8,128)(2,1)} %bitcast.12), calls=%async_computation.2 | async-start | bytes 983040 | tf_op jit(solution)/shard_map/all_to_all | solution.py:559
  215.3 0.8 copy-start.1
  217.9 1.4 collective-permute-start.4
  220.0 3.7 %collective-permute-start.5 = (f32[8,384]{1,0:T(8,128)S(1)}, f32[8,384]{1,0:T(8,128)S(1)}, u32[]{:S(2)}, u32[]{:S(2)}) collective-permute-start(f32[8,384]{1,0:T(8,128)S(1)} %add.50), channel_id=1, source_target_pairs={{0,2},{2,0},{4,6},{6,4},{8,10},{10,8},{12,14},{14,12},{16,18},{18,... | collective-permute-start | bytes 36872 | tf_op jit(solution)/shard_map/ppermute | solution.py:572
  223.7 3.7 %collective-permute-start.6 = (f32[8,384]{1,0:T(8,128)S(1)}, f32[8,384]{1,0:T(8,128)S(1)}, u32[]{:S(2)}, u32[]{:S(2)}) collective-permute-start(f32[8,384]{1,0:T(8,128)S(1)} %add.51), channel_id=1, source_target_pairs={{0,4},{2,6},{4,0},{6,2},{8,12},{10,14},{12,8},{14,10},{16,20},{18,... | collective-permute-start | bytes 36872 | tf_op jit(solution)/shard_map/ppermute | solution.py:572
  227.4 3.7 %collective-permute-start.7 = (f32[8,384]{1,0:T(8,128)S(1)}, f32[8,384]{1,0:T(8,128)S(1)}, u32[]{:S(2)}, u32[]{:S(2)}) collective-permute-start(f32[8,384]{1,0:T(8,128)S(1)} %add.52), channel_id=1, source_target_pairs={{0,8},{2,10},{4,12},{6,14},{8,0},{10,2},{12,4},{14,6},{16,24},{18,... | collective-permute-start | bytes 36872 | tf_op jit(solution)/shard_map/ppermute | solution.py:572
  231.1 4.6 %collective-permute-start.8 = (f32[8,384]{1,0:T(8,128)S(1)}, f32[8,384]{1,0:T(8,128)S(1)}, u32[]{:S(2)}, u32[]{:S(2)}) collective-permute-start(f32[8,384]{1,0:T(8,128)S(1)} %add.53), channel_id=1, source_target_pairs={{0,16},{2,18},{4,20},{6,22},{8,24},{10,26},{12,28},{14,30},{16,0},... | collective-permute-start | bytes 36872 | tf_op jit(solution)/shard_map/ppermute | solution.py:572
  235.7 0.7 copy-start.2
Sparse Core Ops, SparseCore 0:
  21.6 58.4 all-gather.1
  150.5 30.4 reduce-scatter.4
  191.0 24.2 reduce-scatter.6

commit v2 on v1

--- a/solution.py
+++ b/solution.py
@@ -407,19 +407,18 @@
         jnp.concatenate(columns + [extra, blank], axis=1).astype(BF16)[None], lead_ref.shape
     )
     blank = jnp.zeros((rows, HD), F32)
-    rest_ref[...] = jnp.concatenate([up_ref[...], down_ref[...], out_ref[...], blank], axis=1).astype(BF16)
-
-
-def sum_kernel(parts_ref, rest_ref, terms_ref, lead_ref, message_ref):
-    parts = parts_ref[...].astype(F32)
-    lead = jnp.sum(parts, axis=0)
-    lead_ref[...] = lead
-    rest = rest_ref[...].astype(F32)
-    lanes = message_ref.shape[1]
-    total = jnp.zeros((lead.shape[0], PAIR), F32)
-    for values in (lead, rest):
-        for start in range(0, values.shape[1], PAIR):
-            piece = values[:, start : start + PAIR]
+    rest_ref[...] = jnp.broadcast_to(
+        jnp.concatenate([up_ref[...], down_ref[...], out_ref[...], blank], axis=1).astype(BF16)[None], rest_ref.shape
+    )
+
+
+def sum_kernel(lead_parts_ref, rest_parts_ref, terms_ref, lead_ref, rest_ref, message_ref):
+    total = jnp.zeros((lead_ref.shape[0], PAIR), F32)
+    for parts_ref, ref in ((lead_parts_ref, lead_ref), (rest_parts_ref, rest_ref)):
+        for start in range(0, ref.shape[1], PAIR):
+            cols = slice(start, start + PAIR)
+            piece = jnp.sum(parts_ref[:, :, cols].astype(F32), axis=0)
+            ref[:, cols] = piece
             total = total + piece * piece
     message_ref[...] = terms_ref[...]
     message_ref[4:5, :PAIR] = jnp.sum(total, axis=0, keepdims=True)
@@ -468,7 +467,7 @@
     )
     for master, grad, moments, next_ref, state_ref, i in plain:
         next_ref[...], state_ref[0], state_ref[1] = adamw(
-            master[...], factor * grad.astype(F32), moments[...], RATE_LIST[i], DECAY_LIST[i]
+            master[...], factor * grad, moments[...], RATE_LIST[i], DECAY_LIST[i]
         )
     norm_n_ref[...], norm_s_ref[0:1, :], norm_s_ref[1:2, :] = adamw(
         norm_ref[...], norm_grads, (norm_m_ref[0:1, :], norm_m_ref[1:2, :]), RATE_LIST[4], DECAY_LIST[4]
@@ -486,7 +485,7 @@
 
 
 def per_device(
-    groups,
+    chips,
     tokens,
     cotangent,
     lengths,
@@ -503,7 +502,6 @@
     norm_moments,
 ):
     seqs, slot_rows, width = tokens.shape
-    chips = groups[2]
     shard_rows = qkv_master.shape[0]
     norm_part = norm_master.shape[0]
     units = up_master.shape[1]
@@ -516,11 +514,12 @@
     lead, rest = small_call(
         pack_kernel,
         "pack_weights",
-        [shape((chips, shard_rows, 10 * HD), BF16), shape((shard_rows, 2 * units + 4 * HD), BF16)],
+        [shape((chips, shard_rows, 10 * HD), BF16), shape((chips, shard_rows, 2 * units + 4 * HD), BF16)],
         *masters,
     )
     lead_own = lax.all_to_all(lead, "batch", 0, 0)
-    rest_own = lax.all_gather(rest, "batch", axis=0, tiled=True)
+    lead_own, rest = lax.optimization_barrier((lead_own, rest))
+    rest_own = lax.all_to_all(rest, "batch", 0, 0)
     lead_other = swap(lead_own)
 
     def norms_of(gathered):
@@ -543,27 +542,21 @@
     rest_own, attended = lax.optimization_barrier((rest_own, attended))
     rest_other = swap(rest_own)
     block_out, gmid, gatt, grest_own, grest_other, gnorm_two = middle(
-        own_lengths, tokens, cotangent, attended, rest_own, rest_other, norms
+        own_lengths, tokens, cotangent, attended, flat(rest_own), flat(rest_other), norms
     )
     per_seq = lambda a: a.reshape(seqs, slot_rows, width)
     rest_sum = (grest_own.astype(F32) + swap(grest_other).astype(F32)).astype(BF16)
-    rest_part = lax.psum_scatter(
-        rest_sum, "batch", scatter_dimension=0, tiled=True, axis_index_groups=groups[0]
-    )
+    rest_parts = lax.all_to_all(rest_sum.reshape(rest.shape), "batch", 0, 0)
     gp, glead_own, glead_other = backward(n1t, qkv, probs, per_seq(gatt), attended)
-    rest_part, glead_own, glead_other = lax.optimization_barrier((rest_part, glead_own, glead_other))
-    rest_shard = lax.psum_scatter(
-        rest_part, "batch", scatter_dimension=0, tiled=True, axis_index_groups=groups[1]
-    )
     lead_sum = (glead_own.astype(F32) + swap(glead_other).astype(F32)).astype(BF16)
     lead_parts = lax.all_to_all(lead_sum.reshape(chips, shard_rows, 10 * HD), "batch", 0, 0)
     input_grad, terms = input_gradient(tokens, gp, per_seq(gmid), wpairs, norms, gnorm_two)
-    lead_shard, message = small_call(
+    lead_shard, rest_shard, message = small_call(
         sum_kernel,
         "sum_parts",
-        [shape((shard_rows, 10 * HD), F32), shape(terms.shape, F32)],
+        [shape(lead.shape[1:], F32), shape(rest.shape[1:], F32), shape(terms.shape, F32)],
         lead_parts,
-        rest_shard,
+        rest_parts,
         terms,
     )
     message = message + swap(message)
@@ -614,11 +607,8 @@
 
 def solution(mesh):
     chips = mesh.shape["batch"]
-    near = 4
-    outer = [[c + near * z for z in range(chips // near)] for c in range(near)]
-    inner = [[near * z + c for c in range(near)] for z in range(chips // near)]
     return jax.shard_map(
-        functools.partial(per_device, (outer, inner, chips)),
+        functools.partial(per_device, chips),
         mesh=mesh,
         in_specs=(
             P(("batch", "head"), None, None),

time: 246 us -> 268 us (1.089)
  blocking collectives: 0 us -> 22.8 us
  between operations: 13.9 us -> 0.99 us
  waiting for transfers between devices: 40.4 us -> 48.9 us
  starting transfers between devices: 19.5 us -> 23.7 us
    all_to_all x0 -> x1, blocking collectives: none -> 22.8 us  [per_device(): lead_own = lax.all_to_all(lead, 'batch', 0, 0)]
    all_to_all x1, waiting for transfers between devices: 0.01 us -> 13.5 us  [per_device(): lax.all_to_all(lead_sum.reshape(chips, shard_rows, 10 * HD), 'batch', 0, 0)]
    unnamed x4 -> x0, waiting for transfers between devices: 6.92 us -> none
    all_to_all x1 -> x2, waiting for transfers between devices: 13.7 us -> 19.7 us  [the longest x1 19.7 us: per_device(): rest_parts = lax.all_to_all(rest_sum.reshape(rest.shape), 'batch', 0, 0)]
    ppermute x5, waiting for transfers between devices: 10.7 us -> 6.09 us  [swap(): return lax.ppermute(values, 'head', [(0, 1), (1, 0)])]
    all_to_all x1, starting transfers between devices: 3.85 us -> 6.7 us  [per_device(): lax.all_to_all(lead_sum.reshape(chips, shard_rows, 10 * HD), 'batch', 0, 0)]
    all_to_all x1 -> x2, starting transfers between devices: 8.31 us -> 7.8 us  [the longest x1 3.97 us: per_device(): rest_parts = lax.all_to_all(rest_sum.reshape(rest.shape), 'batch', 0, 0)]
  transfers between devices with their start and end apart: 14 -> 12, of which waited for: 11 -> 9; matrix products, arithmetic and copies ran while one was open for 1% -> 2% of each run, Pallas kernels for 45% -> 41%
where the time goes in v2:
time: 268 us
  Pallas kernels  163 us (61%)
  waiting for transfers between devices  48.9 us (18%)
  starting transfers between devices  23.7 us (9%)
  blocking collectives  22.8 us (9%)
  other arithmetic  4.34 us (2%)
  local copies, waits for them, and re-layouts  4.22 us (2%)
    pallas_call x1, Pallas kernels, forward(): pl.pallas_call(forward_kernel, grid=(seqs,), in_specs=[pl.BlockSpec((sq,...  59.7 us
    pallas_call x1, Pallas kernels, middle(): pl.pallas_call(functools.partial(middle_kernel, seq_rows, units), grid=(t...  45.3 us
    pallas_call x1, Pallas kernels, backward(): pl.pallas_call(backward_kernel, grid=(seqs, pairs), in_specs=[pl.BlockSpe...  40.2 us
    all_to_all x1, blocking collectives, per_device(): lead_own = lax.all_to_all(lead, 'batch', 0, 0)  22.8 us
    all_to_all x1, waiting for transfers between devices, per_device(): rest_parts = lax.all_to_all(rest_sum.reshape(rest.shape), 'batch', 0, 0)  19.7 us
    all_to_all x1, waiting for transfers between devices, per_device(): lax.all_to_all(lead_sum.reshape(chips, shard_rows, 10 * HD), 'batch', 0, 0)  13.5 us
    pallas_call x1, Pallas kernels, input_gradient(): pl.pallas_call(input_kernel, grid=(seqs,), in_specs=[full, pl.BlockSpec((...  10.4 us
    ppermute x4, waiting for transfers between devices, per_device(): lax.ppermute(message, 'batch', [(i, i ^ stride) for i in range(chips)])  9.63 us
  transfers between devices with their start and end apart: 12, of which 9 were waited for; matrix products, arithmetic and copies ran while one was open for 2% of the time, Pallas kernels for 41%

profile of v2, /device:TPU:0, one launch (start us, length us, event | category | flops | bytes accessed | tf_op | source)
XLA Modules:
  0.0 267.6 jit_solution(14251434400032038422)
XLA Ops:
  0.7 2.3 pack_weights.1
  3.0 22.8 %all_to_all.20 = bf16[16,24,640]{2,1,0:T(8,128)(2,1)S(1)} all-to-all(bf16[16,24,640]{2,1,0:T(8,128)(2,1)} %get-tuple-element.51), channel_id=1, replica_groups=mesh['batch'=16,'head'=2] {'batch'}, dimensions={0} | all-to-all | bytes 983040 | tf_op jit(solution)/shard_map/all_to_all | solution.py:520
  26.0 0.6 broadcast_in_dim.20.bias_ref
  26.6 3.8 %all-to-all-start.1 = ((bf16[16,24,1792]{2,1,0:T(8,128)(2,1)}), bf16[16,24,1792]{2,1,0:T(8,128)(2,1)S(1)}, u32[]{:S(2)}, u32[]{:S(2)}) async-start(bf16[16,24,1792]{2,1,0:T(8,128)(2,1)} %get-tuple-element.53), calls=%async_computation.1 | async-start | bytes 2752512 | tf_op jit(solution)/shard_map/all_to_all | solution.py:522
  30.7 0.7 reshape.83.norms_ref
  31.3 59.7 %attention_forward.1 = (bf16[4,384,640]{2,1,0:T(8,128)(2,1)}, bf16[4,3,640,384]{3,2,1,0:T(8,128)(2,1)}, bf16[4,640,384]{2,1,0:T(8,128)(2,1)}, bf16[4,6,640,640]{3,2,1,0:T(8,128)(2,1)}, bf16[3,384,384]{2,1,0:T(8,128)(2,1)}) custom-call(bf16[4,640,384]{2,1,0:T(8,128)(2,1)} %tok_ref.3, f32[4,1,640]{2,1,0:T(1,128)} %broadcast_in_dim.20.bias_ref, ...), custom_call_target="tpu_custom_call" | custom-call | flops 49999998976 | bytes 1000000 | tf_op jit(solution)/shard_map/attention_forward/pallas_call | solution.py:125
  91.5 2.8 %collective-permute-done.1 = bf16[16,24,1792]{2,1,0:T(8,128)(2,1)S(1)} collective-permute-done((bf16[16,24,1792]{2,1,0:T(8,128)(2,1)S(1)}, bf16[16,24,1792]{2,1,0:T(8,128)(2,1)S(1)}, u32[]{:S(2)}, u32[]{:S(2)}) %collective-permute-start.1) | collective-permute-done | bytes 1376288 | tf_op jit(solution)/shard_map/ppermute | solution.py:484
  94.2 1.1 copy-done.9
  95.3 45.3 %feed_forward.1 = (bf16[2560,384]{1,0:T(8,128)(2,1)}, f32[2560,384]{1,0:T(8,128)}, bf16[2560,384]{1,0:T(8,128)(2,1)}, bf16[384,1792]{1,0:T(8,128)(2,1)}, bf16[384,1792]{1,0:T(8,128)(2,1)}, /*index=5*/f32[16,384]{1,0:T(8,128)}) custom-call(s32[4]{0:T(128)} %copy-done.7, bf16[2560,384]{1,0:T(8,128)(2,1)} %bitcast.37, bf16[2560,384]{1,0:T(8,128)(2,1)} %bitcast.36, ...), custom_call_target="tpu_custom_call" | custom-call | flops 49999998976 | bytes 1000000 | tf_op jit(solution)/shard_map/feed_forward/pallas_call | solution.py:241
  141.1 40.2 %attention_backward.1 = (bf16[4,3,640,384]{3,2,1,0:T(8,128)(2,1)}, bf16[384,640]{1,0:T(8,128)(2,1)}, bf16[384,640]{1,0:T(8,128)(2,1)}) custom-call(bf16[4,384,640]{2,1,0:T(8,128)(2,1)} %get-tuple-element.59.n1t_ref, bf16[4,3,640,384]{3,2,1,0:T(8,128)(2,1)} %get-tuple-element.60.qkv_ref, bf16[4,6,640,640]{3,2,1,0:T(8,128)(2,1)} %get-tuple-element.61.p_ref, ...), custom_call_target="tpu_custom_call" | custom-call | flops 49999998976 | bytes 1000000 | tf_op jit(solution)/shard_map/attention_backward/pallas_call | solution.py:334
  181.5 1.9 collective-permute-done.2
  183.4 1.9 add_convert_fusion.1
  185.4 6.7 %all-to-all-start.2 = ((bf16[16,24,640]{2,1,0:T(8,128)(2,1)}), bf16[16,24,640]{2,1,0:T(8,128)(2,1)S(1)}, u32[]{:S(2)}, u32[]{:S(2)}) async-start(bf16[16,24,640]{2,1,0:T(8,128)(2,1)} %bitcast.14), calls=%async_computation.2 | async-start | bytes 983040 | tf_op jit(solution)/shard_map/all_to_all | solution.py:552
  192.1 1.4 add_convert_fusion
  193.5 13.5 %all-to-all-done.2.lead_parts_ref = bf16[16,24,640]{2,1,0:T(8,128)(2,1)S(1)} async-done(((bf16[16,24,640]{2,1,0:T(8,128)(2,1)}), bf16[16,24,640]{2,1,0:T(8,128)(2,1)S(1)}, u32[]{:S(2)}, u32[]{:S(2)}) %all-to-all-start.2) | async-done | bytes 491552 | tf_op jit(solution)/shard_map/all_to_all | solution.py:552
  207.0 4.0 %all-to-all-start.3 = ((bf16[16,24,1792]{2,1,0:T(8,128)(2,1)}), bf16[16,24,1792]{2,1,0:T(8,128)(2,1)S(1)}, u32[]{:S(2)}, u32[]{:S(2)}) async-start(bf16[16,24,1792]{2,1,0:T(8,128)(2,1)} %bitcast.15), calls=%async_computation.3 | async-start | bytes 2752512 | tf_op jit(solution)/shard_map/all_to_all | solution.py:549
  211.0 10.4 %input_gradient.1 = (f32[4,640,384]{2,1,0:T(8,128)}, f32[8,384]{1,0:T(8,128)}) custom-call(bf16[4,640,384]{2,1,0:T(8,128)(2,1)} %tok_ref.3, bf16[4,3,640,384]{3,2,1,0:T(8,128)(2,1)} %get-tuple-element.63.gp_ref, f32[4,640,384]{2,1,0:T(8,128)} %bitcast.50, bf16[3,384,384]{2,1,0:T(8,128)(2,1)} %get-tuple-element.65.w_ref, f32[4,384]{1,0:T(4,128)} %reshape.83.norms_ref, ...), custom_call_target="tpu_custom_call" | custom-call | flops 12000000000 | bytes 1000000 | tf_op jit(solution)/shard_map/input_gradient/pallas_call | solution.py:378
  221.3 19.7 %all-to-all-done.3.rest_parts_ref = bf16[16,24,1792]{2,1,0:T(8,128)(2,1)S(1)} async-done(((bf16[16,24,1792]{2,1,0:T(8,128)(2,1)}), bf16[16,24,1792]{2,1,0:T(8,128)(2,1)S(1)}, u32[]{:S(2)}, u32[]{:S(2)}) %all-to-all-start.3) | async-done | bytes 1376288 | tf_op jit(solution)/shard_map/all_to_all | solution.py:549
  241.1 1.1 copy-done.2
  242.2 2.3 sum_parts.1
  244.5 1.4 collective-permute-done.4
  245.9 0.7 add.46
  246.6 0.6 collective-permute-start.5
  247.2 3.1 %collective-permute-done.5 = f32[8,384]{1,0:T(8,128)S(1)} collective-permute-done((f32[8,384]{1,0:T(8,128)S(1)}, f32[8,384]{1,0:T(8,128)S(1)}, u32[]{:S(2)}, u32[]{:S(2)}) %collective-permute-start.5) | collective-permute-done | bytes 12320 | tf_op jit(solution)/shard_map/ppermute | solution.py:565
  250.3 2.4 collective-permute-start.6
  252.7 1.7 collective-permute-done.6
  254.4 3.7 %collective-permute-start.7 = (f32[8,384]{1,0:T(8,128)S(1)}, f32[8,384]{1,0:T(8,128)S(1)}, u32[]{:S(2)}, u32[]{:S(2)}) collective-permute-start(f32[8,384]{1,0:T(8,128)S(1)} %add.48), channel_id=1, source_target_pairs={{0,8},{2,10},{4,12},{6,14},{8,0},{10,2},{12,4},{14,6},{16,24},{18,... | collective-permute-start | bytes 36872 | tf_op jit(solution)/shard_map/ppermute | solution.py:565
  258.1 1.7 collective-permute-done.7
  259.8 1.4 collective-permute-start.8
  261.2 3.2 %collective-permute-done.8 = f32[8,384]{1,0:T(8,128)S(1)} collective-permute-done((f32[8,384]{1,0:T(8,128)S(1)}, f32[8,384]{1,0:T(8,128)S(1)}, u32[]{:S(2)}, u32[]{:S(2)}) %collective-permute-start.8) | collective-permute-done | bytes 12320 | tf_op jit(solution)/shard_map/ppermute | solution.py:565
  264.4 0.6 constant_dynamic-slice_fusion.mine_ref
  265.0 2.4 update_weights.1
  (41 shorter events, 1.5 us)
Async XLA Ops:
  0.6 25.2 %copy-start.10 = (s32[8]{0:T(128)S(1)}, s32[8]{0:T(128)}, u32[]{:S(2)}) copy-start(s32[8]{0:T(128)} %param.16) | copy-start | bytes 100
  0.7 25.2 %copy-start.6 = (s32[8,640]{1,0:T(8,128)S(1)}, s32[8,640]{1,0:T(8,128)}, u32[]{:S(2)}) copy-start(s32[8,640]{1,0:T(8,128)} %param.17) | copy-start | bytes 61444
  25.8 5.6 %copy-start.3 = (bf16[16,24,640]{2,1,0:T(8,128)(2,1)}, bf16[16,24,640]{2,1,0:T(8,128)(2,1)S(1)}, u32[]{:S(2)}) copy-start(bf16[16,24,640]{2,1,0:T(8,128)(2,1)S(1)} %all_to_all.20) | copy-start | bytes 1474564
  25.8 4.7 %collective-permute-start = (bf16[16,24,640]{2,1,0:T(8,128)(2,1)S(1)}, bf16[16,24,640]{2,1,0:T(8,128)(2,1)S(1)}, u32[]{:S(2)}, u32[]{:S(2)}) collective-permute-start(bf16[16,24,640]{2,1,0:T(8,128)(2,1)S(1)} %all_to_all.20), channel_id=1, source_target_pairs={{0,1},{1,0},{2,3},{3,2},{4,5},{5,4},{6,7},{7,6},{8,9},{9,8},{10,11... | collective-permute-start | bytes 1474568 | tf_op jit(solution)/shard_map/ppermute | solution.py:484
  25.9 65.1 %copy-start.7 = (s32[4]{0:T(128)}, s32[4]{0:T(128)S(1)}, u32[]{:S(2)}) copy-start(s32[4]{0:T(128)S(1)} %dynamic_slice.9.len_ref) | copy-start | bytes 52
  26.6 64.4 %all-to-all-start.1 = ((bf16[16,24,1792]{2,1,0:T(8,128)(2,1)}), bf16[16,24,1792]{2,1,0:T(8,128)(2,1)S(1)}, u32[]{:S(2)}, u32[]{:S(2)}) async-start(bf16[16,24,1792]{2,1,0:T(8,128)(2,1)} %get-tuple-element.53), calls=%async_computation.1 | async-start | bytes 2752512 | tf_op jit(solution)/shard_map/all_to_all | solution.py:522
  30.5 0.8 copy-start.8
  91.0 3.2 %copy-start = (bf16[16,24,1792]{2,1,0:T(8,128)(2,1)}, bf16[16,24,1792]{2,1,0:T(8,128)(2,1)S(1)}, u32[]{:S(2)}) copy-start(bf16[16,24,1792]{2,1,0:T(8,128)(2,1)S(1)} %all-to-all-done.1) | copy-start | bytes 4128772
  91.0 3.2 %collective-permute-start.1 = (bf16[16,24,1792]{2,1,0:T(8,128)(2,1)S(1)}, bf16[16,24,1792]{2,1,0:T(8,128)(2,1)S(1)}, u32[]{:S(2)}, u32[]{:S(2)}) collective-permute-start(bf16[16,24,1792]{2,1,0:T(8,128)(2,1)S(1)} %all-to-all-done.1), channel_id=1, source_target_pairs={{0,1},{1,0},{2,3},{3,2},{4,5},{5,4},{6,7},{7,6},{8,9},{9,8},{10,11... | collective-permute-start | bytes 4128776 | tf_op jit(solution)/shard_map/ppermute | solution.py:484
  94.2 1.1 copy-start.9
  140.7 51.4 %collective-permute-start.3 = (bf16[384,1792]{1,0:T(8,128)(2,1)}, bf16[384,1792]{1,0:T(8,128)(2,1)S(1)}, u32[]{:S(2)}, u32[]{:S(2)}) collective-permute-start(bf16[384,1792]{1,0:T(8,128)(2,1)} %get-tuple-element.71), channel_id=1, source_target_pairs={{0,1},{1,0},{2,3},{3,2},{4,5},{5,4},{6,7},{7,6},{8,9},{9,8},{10,11... | collective-permute-start | bytes 4128776 | tf_op jit(solution)/shard_map/ppermute | solution.py:484
  181.3 10.8 %copy-start.1 = (bf16[384,1792]{1,0:T(8,128)(2,1)S(1)}, bf16[384,1792]{1,0:T(8,128)(2,1)}, u32[]{:S(2)}) copy-start(bf16[384,1792]{1,0:T(8,128)(2,1)} %get-tuple-element.70) | copy-start | bytes 4128772
  181.3 2.1 collective-permute-start.2
  185.4 21.6 %all-to-all-start.2 = ((bf16[16,24,640]{2,1,0:T(8,128)(2,1)}), bf16[16,24,640]{2,1,0:T(8,128)(2,1)S(1)}, u32[]{:S(2)}, u32[]{:S(2)}) async-start(bf16[16,24,640]{2,1,0:T(8,128)(2,1)} %bitcast.14), calls=%async_computation.2 | async-start | bytes 983040 | tf_op jit(solution)/shard_map/all_to_all | solution.py:552
  207.0 14.4 %copy-start.4 = (bf16[16,24,640]{2,1,0:T(8,128)(2,1)}, bf16[16,24,640]{2,1,0:T(8,128)(2,1)S(1)}, u32[]{:S(2)}) copy-start(bf16[16,24,640]{2,1,0:T(8,128)(2,1)S(1)} %all-to-all-done.2.lead_parts_ref) | copy-start | bytes 1474564
  207.0 34.1 %all-to-all-start.3 = ((bf16[16,24,1792]{2,1,0:T(8,128)(2,1)}), bf16[16,24,1792]{2,1,0:T(8,128)(2,1)S(1)}, u32[]{:S(2)}, u32[]{:S(2)}) async-start(bf16[16,24,1792]{2,1,0:T(8,128)(2,1)} %bitcast.15), calls=%async_computation.3 | async-start | bytes 2752512 | tf_op jit(solution)/shard_map/all_to_all | solution.py:549
  241.1 1.1 copy-start.2
  244.5 1.4 collective-permute-start.4
  246.6 3.7 %collective-permute-start.5 = (f32[8,384]{1,0:T(8,128)S(1)}, f32[8,384]{1,0:T(8,128)S(1)}, u32[]{:S(2)}, u32[]{:S(2)}) collective-permute-start(f32[8,384]{1,0:T(8,128)S(1)} %add.46), channel_id=1, source_target_pairs={{0,2},{2,0},{4,6},{6,4},{8,10},{10,8},{12,14},{14,12},{16,18},{18,... | collective-permute-start | bytes 36872 | tf_op jit(solution)/shard_map/ppermute | solution.py:565
  250.3 4.1 %collective-permute-start.6 = (f32[8,384]{1,0:T(8,128)S(1)}, f32[8,384]{1,0:T(8,128)S(1)}, u32[]{:S(2)}, u32[]{:S(2)}) collective-permute-start(f32[8,384]{1,0:T(8,128)S(1)} %add.47), channel_id=1, source_target_pairs={{0,4},{2,6},{4,0},{6,2},{8,12},{10,14},{12,8},{14,10},{16,20},{18,... | collective-permute-start | bytes 36872 | tf_op jit(solution)/shard_map/ppermute | solution.py:565
  254.4 5.4 %collective-permute-start.7 = (f32[8,384]{1,0:T(8,128)S(1)}, f32[8,384]{1,0:T(8,128)S(1)}, u32[]{:S(2)}, u32[]{:S(2)}) collective-permute-start(f32[8,384]{1,0:T(8,128)S(1)} %add.48), channel_id=1, source_target_pairs={{0,8},{2,10},{4,12},{6,14},{8,0},{10,2},{12,4},{14,6},{16,24},{18,... | collective-permute-start | bytes 36872 | tf_op jit(solution)/shard_map/ppermute | solution.py:565
  259.8 4.6 %collective-permute-start.8 = (f32[8,384]{1,0:T(8,128)S(1)}, f32[8,384]{1,0:T(8,128)S(1)}, u32[]{:S(2)}, u32[]{:S(2)}) collective-permute-start(f32[8,384]{1,0:T(8,128)S(1)} %add.49), channel_id=1, source_target_pairs={{0,16},{2,18},{4,20},{6,22},{8,24},{10,26},{12,28},{14,30},{16,0},... | collective-permute-start | bytes 36872 | tf_op jit(solution)/shard_map/ppermute | solution.py:565
  264.4 0.6 copy-start.5

commit v3 on v2

--- a/solution.py
+++ b/solution.py
@@ -546,9 +546,11 @@
     )
     per_seq = lambda a: a.reshape(seqs, slot_rows, width)
     rest_sum = (grest_own.astype(F32) + swap(grest_other).astype(F32)).astype(BF16)
+    rest_sum, gatt = lax.optimization_barrier((rest_sum, gatt))
     rest_parts = lax.all_to_all(rest_sum.reshape(rest.shape), "batch", 0, 0)
     gp, glead_own, glead_other = backward(n1t, qkv, probs, per_seq(gatt), attended)
     lead_sum = (glead_own.astype(F32) + swap(glead_other).astype(F32)).astype(BF16)
+    lead_sum, rest_parts = lax.optimization_barrier((lead_sum, rest_parts))
     lead_parts = lax.all_to_all(lead_sum.reshape(chips, shard_rows, 10 * HD), "batch", 0, 0)
     input_grad, terms = input_gradient(tokens, gp, per_seq(gmid), wpairs, norms, gnorm_two)
     lead_shard, rest_shard, message = small_call(

time: 268 us -> 245 us (0.914)
  waiting for transfers between devices: 48.9 us -> 26 us
    all_to_all x1, waiting for transfers between devices: 19.7 us -> 0.01 us  [per_device(): rest_parts = lax.all_to_all(rest_sum.reshape(rest.shape), 'batch', 0, 0)]
    all_to_all x1, waiting for transfers between devices: 13.5 us -> 4.43 us  [per_device(): lax.all_to_all(lead_sum.reshape(chips, shard_rows, 10 * HD), 'batch', 0, 0)]
    ppermute x4, starting transfers between devices: 8.13 us -> 3.33 us  [per_device(): lax.ppermute(message, 'batch', [(i, i ^ stride) for i in range(chips)])]
    ppermute x5, waiting for transfers between devices: 6.09 us -> 9.22 us  [swap(): return lax.ppermute(values, 'head', [(0, 1), (1, 0)])]
    all_to_all x1, starting transfers between devices: 3.97 us -> 6.92 us  [per_device(): rest_parts = lax.all_to_all(rest_sum.reshape(rest.shape), 'batch', 0, 0)]
    ppermute x4, waiting for transfers between devices: 9.63 us -> 12.4 us  [per_device(): lax.ppermute(message, 'batch', [(i, i ^ stride) for i in range(chips)])]
  transfers between devices with their start and end apart: 12 -> 12, of which waited for: 9 -> 9; matrix products, arithmetic and copies ran while one was open for 2% -> 1% of each run, Pallas kernels for 41% -> 45%
where the time goes in v3:
time: 245 us; the launch traced here: 244 us
  Pallas kernels  163 us (67%)
  waiting for transfers between devices  26 us (11%)
  blocking collectives  22.8 us (9%)
  starting transfers between devices  21.8 us (9%)
  other arithmetic  5.75 us (2%)
  local copies, waits for them, and re-layouts  4.03 us (2%)
    pallas_call x1, Pallas kernels, forward(): pl.pallas_call(forward_kernel, grid=(seqs,), in_specs=[pl.BlockSpec((sq,...  59.7 us
    pallas_call x1, Pallas kernels, middle(): pl.pallas_call(functools.partial(middle_kernel, seq_rows, units), grid=(t...  45.3 us
    pallas_call x1, Pallas kernels, backward(): pl.pallas_call(backward_kernel, grid=(seqs, pairs), in_specs=[pl.BlockSpe...  40.2 us
    all_to_all x1, blocking collectives, per_device(): lead_own = lax.all_to_all(lead, 'batch', 0, 0)  22.8 us
    ppermute x4, waiting for transfers between devices, per_device(): lax.ppermute(message, 'batch', [(i, i ^ stride) for i in range(chips)])  12.4 us
    pallas_call x1, Pallas kernels, input_gradient(): pl.pallas_call(input_kernel, grid=(seqs,), in_specs=[full, pl.BlockSpec((...  10.4 us
    ppermute x5, waiting for transfers between devices, swap(): return lax.ppermute(values, 'head', [(0, 1), (1, 0)])  9.22 us
    pallas_call x3, Pallas kernels, small_call(): pl.pallas_call(kernel, out_shape=out_shape, compiler_params=VMEM, cost_es...  7.08 us
  transfers between devices with their start and end apart: 12, of which 9 were waited for; matrix products, arithmetic and copies ran while one was open for 1% of the time, Pallas kernels for 45%

profile of v3, /device:TPU:0, one launch (start us, length us, event | category | flops | bytes accessed | tf_op | source)
XLA Modules:
  0.0 244.0 jit_solution(14701743179117985043)
XLA Ops:
  0.7 2.3 pack_weights.1
  3.0 22.8 %all_to_all.20 = bf16[16,24,640]{2,1,0:T(8,128)(2,1)S(1)} all-to-all(bf16[16,24,640]{2,1,0:T(8,128)(2,1)} %get-tuple-element.55), channel_id=1, replica_groups=mesh['batch'=16,'head'=2] {'batch'}, dimensions={0} | all-to-all | bytes 983040 | tf_op jit(solution)/shard_map/all_to_all | solution.py:520
  26.0 0.6 broadcast_in_dim.20.bias_ref
  26.6 3.8 %all-to-all-start.1 = ((bf16[16,24,1792]{2,1,0:T(8,128)(2,1)}), bf16[16,24,1792]{2,1,0:T(8,128)(2,1)S(1)}, u32[]{:S(2)}, u32[]{:S(2)}) async-start(bf16[16,24,1792]{2,1,0:T(8,128)(2,1)} %get-tuple-element.57), calls=%async_computation.1 | async-start | bytes 2752512 | tf_op jit(solution)/shard_map/all_to_all | solution.py:522
  30.7 0.7 reshape.83.norms_ref
  31.4 59.7 %attention_forward.1 = (bf16[4,384,640]{2,1,0:T(8,128)(2,1)}, bf16[4,3,640,384]{3,2,1,0:T(8,128)(2,1)}, bf16[4,640,384]{2,1,0:T(8,128)(2,1)}, bf16[4,6,640,640]{3,2,1,0:T(8,128)(2,1)}, bf16[3,384,384]{2,1,0:T(8,128)(2,1)}) custom-call(bf16[4,640,384]{2,1,0:T(8,128)(2,1)} %tok_ref.3, f32[4,1,640]{2,1,0:T(1,128)} %broadcast_in_dim.20.bias_ref, ...), custom_call_target="tpu_custom_call" | custom-call | flops 49999998976 | bytes 1000000 | tf_op jit(solution)/shard_map/attention_forward/pallas_call | solution.py:125
  91.5 2.8 %collective-permute-done.1 = bf16[16,24,1792]{2,1,0:T(8,128)(2,1)S(1)} collective-permute-done((bf16[16,24,1792]{2,1,0:T(8,128)(2,1)S(1)}, bf16[16,24,1792]{2,1,0:T(8,128)(2,1)S(1)}, u32[]{:S(2)}, u32[]{:S(2)}) %collective-permute-start.1) | collective-permute-done | bytes 1376288 | tf_op jit(solution)/shard_map/ppermute | solution.py:484
  94.3 1.1 copy-done.8
  95.4 45.3 %feed_forward.1 = (bf16[2560,384]{1,0:T(8,128)(2,1)}, f32[2560,384]{1,0:T(8,128)}, bf16[2560,384]{1,0:T(8,128)(2,1)}, bf16[384,1792]{1,0:T(8,128)(2,1)}, bf16[384,1792]{1,0:T(8,128)(2,1)}, /*index=5*/f32[16,384]{1,0:T(8,128)}) custom-call(s32[4]{0:T(128)} %copy-done.6, bf16[2560,384]{1,0:T(8,128)(2,1)} %bitcast.37, bf16[2560,384]{1,0:T(8,128)(2,1)} %bitcast.36, ...), custom_call_target="tpu_custom_call" | custom-call | flops 49999998976 | bytes 1000000 | tf_op jit(solution)/shard_map/feed_forward/pallas_call | solution.py:241
  141.1 3.0 %collective-permute-done.2 = bf16[384,1792]{1,0:T(8,128)(2,1)S(1)} collective-permute-done((bf16[384,1792]{1,0:T(8,128)(2,1)}, bf16[384,1792]{1,0:T(8,128)(2,1)S(1)}, u32[]{:S(2)}, u32[]{:S(2)}) %collective-permute-start.2) | collective-permute-done | bytes 1376288 | tf_op jit(solution)/shard_map/ppermute | solution.py:484
  144.1 2.8 %add_convert_fusion = bf16[384,1792]{1,0:T(8,128)(2,1)} fusion(bf16[384,1792]{1,0:T(8,128)(2,1)S(1)} %collective-permute-done.2, bf16[384,1792]{1,0:T(8,128)(2,1)} %get-tuple-element.66), kind=kLoop, calls=%fused_computation | loop fusion | flops 2752512 | bytes 4128768 | tf_op jit(solution)/shard_map/convert_element_type | solution.py:548
  146.9 6.9 %all-to-all-start.2 = ((bf16[16,24,1792]{2,1,0:T(8,128)(2,1)}), bf16[16,24,1792]{2,1,0:T(8,128)(2,1)S(1)}, u32[]{:S(2)}, u32[]{:S(2)}) async-start(bf16[16,24,1792]{2,1,0:T(8,128)(2,1)} %bitcast.14), calls=%async_computation.2 | async-start | bytes 2752512 | tf_op jit(solution)/shard_map/all_to_all | solution.py:550
  153.8 40.2 %attention_backward.1 = (bf16[4,3,640,384]{3,2,1,0:T(8,128)(2,1)}, bf16[384,640]{1,0:T(8,128)(2,1)}, bf16[384,640]{1,0:T(8,128)(2,1)}) custom-call(bf16[4,384,640]{2,1,0:T(8,128)(2,1)} %get-tuple-element.63.n1t_ref, bf16[4,3,640,384]{3,2,1,0:T(8,128)(2,1)} %get-tuple-element.64.qkv_ref, bf16[4,6,640,640]{3,2,1,0:T(8,128)(2,1)} %get-tuple-element.65.p_ref, ...), custom_call_target="tpu_custom_call" | custom-call | flops 49999998976 | bytes 1000000 | tf_op jit(solution)/shard_map/attention_backward/pallas_call | solution.py:334
  194.0 2.1 collective-permute-done.3
  196.1 2.0 add_convert_fusion.1
  198.1 6.9 %all-to-all-start.3 = ((bf16[16,24,640]{2,1,0:T(8,128)(2,1)}), bf16[16,24,640]{2,1,0:T(8,128)(2,1)S(1)}, u32[]{:S(2)}, u32[]{:S(2)}) async-start(bf16[16,24,640]{2,1,0:T(8,128)(2,1)} %bitcast.15), calls=%async_computation.3 | async-start | bytes 983040 | tf_op jit(solution)/shard_map/all_to_all | solution.py:554
  205.0 10.4 %input_gradient.1 = (f32[4,640,384]{2,1,0:T(8,128)}, f32[8,384]{1,0:T(8,128)}) custom-call(bf16[4,640,384]{2,1,0:T(8,128)(2,1)} %tok_ref.3, bf16[4,3,640,384]{3,2,1,0:T(8,128)(2,1)} %get-tuple-element.70.gp_ref, f32[4,640,384]{2,1,0:T(8,128)} %bitcast.50, bf16[3,384,384]{2,1,0:T(8,128)(2,1)} %get-tuple-element.72.w_ref, f32[4,384]{1,0:T(4,128)} %reshape.83.norms_ref, ...), custom_call_target="tpu_custom_call" | custom-call | flops 12000000000 | bytes 1000000 | tf_op jit(solution)/shard_map/input_gradient/pallas_call | solution.py:378
  215.3 4.4 %all-to-all-done.3.lead_parts_ref = bf16[16,24,640]{2,1,0:T(8,128)(2,1)S(1)} async-done(((bf16[16,24,640]{2,1,0:T(8,128)(2,1)}), bf16[16,24,640]{2,1,0:T(8,128)(2,1)S(1)}, u32[]{:S(2)}, u32[]{:S(2)}) %all-to-all-start.3) | async-done | bytes 491552 | tf_op jit(solution)/shard_map/all_to_all | solution.py:554
  219.8 0.8 copy-done.3
  220.6 2.3 sum_parts.1
  222.9 1.4 collective-permute-done.4
  224.3 0.7 add.46
  225.0 0.6 collective-permute-start.5
  225.6 3.1 %collective-permute-done.5 = f32[8,384]{1,0:T(8,128)S(1)} collective-permute-done((f32[8,384]{1,0:T(8,128)S(1)}, f32[8,384]{1,0:T(8,128)S(1)}, u32[]{:S(2)}, u32[]{:S(2)}) %collective-permute-start.5) | collective-permute-done | bytes 12320 | tf_op jit(solution)/shard_map/ppermute | solution.py:567
  228.7 0.9 collective-permute-start.6
  229.6 2.8 %collective-permute-done.6 = f32[8,384]{1,0:T(8,128)S(1)} collective-permute-done((f32[8,384]{1,0:T(8,128)S(1)}, f32[8,384]{1,0:T(8,128)S(1)}, u32[]{:S(2)}, u32[]{:S(2)}) %collective-permute-start.6) | collective-permute-done | bytes 12320 | tf_op jit(solution)/shard_map/ppermute | solution.py:567
  232.4 1.2 collective-permute-start.7
  233.6 2.5 %collective-permute-done.7 = f32[8,384]{1,0:T(8,128)S(1)} collective-permute-done((f32[8,384]{1,0:T(8,128)S(1)}, f32[8,384]{1,0:T(8,128)S(1)}, u32[]{:S(2)}, u32[]{:S(2)}) %collective-permute-start.7) | collective-permute-done | bytes 12320 | tf_op jit(solution)/shard_map/ppermute | solution.py:567
  236.1 0.6 collective-permute-start.8
  236.7 3.9 %collective-permute-done.8 = f32[8,384]{1,0:T(8,128)S(1)} collective-permute-done((f32[8,384]{1,0:T(8,128)S(1)}, f32[8,384]{1,0:T(8,128)S(1)}, u32[]{:S(2)}, u32[]{:S(2)}) %collective-permute-start.8) | collective-permute-done | bytes 12320 | tf_op jit(solution)/shard_map/ppermute | solution.py:567
  240.7 0.7 constant_dynamic-slice_fusion.mine_ref
  241.4 2.4 %update_weights.1 = (f32[1,1]{1,0:T(1,128)}, f32[3,24,192]{2,1,0:T(8,128)}, f32[24,192]{1,0:T(8,128)}, f32[24,768]{1,0:T(8,128)}, f32[24,768]{1,0:T(8,128)}, /*i...) custom-call(f32[8,384]{1,0:T(8,128)} %copy-done.4, ...), custom_call_target="tpu_custom_call" | custom-call | flops 3000000000 | bytes 1000000 | tf_op jit(solution)/shard_map/update_weights/pallas_call | solution.py:478
  (39 shorter events, 1.3 us)
Async XLA Ops:
  0.6 25.2 %copy-start.9 = (s32[8]{0:T(128)S(1)}, s32[8]{0:T(128)}, u32[]{:S(2)}) copy-start(s32[8]{0:T(128)} %param.16) | copy-start | bytes 100
  0.7 25.2 %copy-start.5 = (s32[8,640]{1,0:T(8,128)S(1)}, s32[8,640]{1,0:T(8,128)}, u32[]{:S(2)}) copy-start(s32[8,640]{1,0:T(8,128)} %param.17) | copy-start | bytes 61444
  25.8 5.6 %copy-start.2 = (bf16[16,24,640]{2,1,0:T(8,128)(2,1)}, bf16[16,24,640]{2,1,0:T(8,128)(2,1)S(1)}, u32[]{:S(2)}) copy-start(bf16[16,24,640]{2,1,0:T(8,128)(2,1)S(1)} %all_to_all.20) | copy-start | bytes 1474564
  25.8 4.7 %collective-permute-start = (bf16[16,24,640]{2,1,0:T(8,128)(2,1)S(1)}, bf16[16,24,640]{2,1,0:T(8,128)(2,1)S(1)}, u32[]{:S(2)}, u32[]{:S(2)}) collective-permute-start(bf16[16,24,640]{2,1,0:T(8,128)(2,1)S(1)} %all_to_all.20), channel_id=1, source_target_pairs={{0,1},{1,0},{2,3},{3,2},{4,5},{5,4},{6,7},{7,6},{8,9},{9,8},{10,11... | collective-permute-start | bytes 1474568 | tf_op jit(solution)/shard_map/ppermute | solution.py:484
  25.9 65.1 %copy-start.6 = (s32[4]{0:T(128)}, s32[4]{0:T(128)S(1)}, u32[]{:S(2)}) copy-start(s32[4]{0:T(128)S(1)} %dynamic_slice.9.len_ref) | copy-start | bytes 52
  26.6 64.4 %all-to-all-start.1 = ((bf16[16,24,1792]{2,1,0:T(8,128)(2,1)}), bf16[16,24,1792]{2,1,0:T(8,128)(2,1)S(1)}, u32[]{:S(2)}, u32[]{:S(2)}) async-start(bf16[16,24,1792]{2,1,0:T(8,128)(2,1)} %get-tuple-element.57), calls=%async_computation.1 | async-start | bytes 2752512 | tf_op jit(solution)/shard_map/all_to_all | solution.py:522
  30.5 0.8 copy-start.7
  91.0 3.2 %copy-start.1 = (bf16[16,24,1792]{2,1,0:T(8,128)(2,1)}, bf16[16,24,1792]{2,1,0:T(8,128)(2,1)S(1)}, u32[]{:S(2)}) copy-start(bf16[16,24,1792]{2,1,0:T(8,128)(2,1)S(1)} %all-to-all-done.1) | copy-start | bytes 4128772
  91.1 3.2 %collective-permute-start.1 = (bf16[16,24,1792]{2,1,0:T(8,128)(2,1)S(1)}, bf16[16,24,1792]{2,1,0:T(8,128)(2,1)S(1)}, u32[]{:S(2)}, u32[]{:S(2)}) collective-permute-start(bf16[16,24,1792]{2,1,0:T(8,128)(2,1)S(1)} %all-to-all-done.1), channel_id=1, source_target_pairs={{0,1},{1,0},{2,3},{3,2},{4,5},{5,4},{6,7},{7,6},{8,9},{9,8},{10,11... | collective-permute-start | bytes 4128776 | tf_op jit(solution)/shard_map/ppermute | solution.py:484
  94.3 1.1 copy-start.8
  140.7 3.4 %collective-permute-start.2 = (bf16[384,1792]{1,0:T(8,128)(2,1)}, bf16[384,1792]{1,0:T(8,128)(2,1)S(1)}, u32[]{:S(2)}, u32[]{:S(2)}) collective-permute-start(bf16[384,1792]{1,0:T(8,128)(2,1)} %get-tuple-element.67), channel_id=1, source_target_pairs={{0,1},{1,0},{2,3},{3,2},{4,5},{5,4},{6,7},{7,6},{8,9},{9,8},{10,11... | collective-permute-start | bytes 4128776 | tf_op jit(solution)/shard_map/ppermute | solution.py:484
  146.9 51.1 %all-to-all-start.2 = ((bf16[16,24,1792]{2,1,0:T(8,128)(2,1)}), bf16[16,24,1792]{2,1,0:T(8,128)(2,1)S(1)}, u32[]{:S(2)}, u32[]{:S(2)}) async-start(bf16[16,24,1792]{2,1,0:T(8,128)(2,1)} %bitcast.14), calls=%async_computation.2 | async-start | bytes 2752512 | tf_op jit(solution)/shard_map/all_to_all | solution.py:550
  194.0 2.1 collective-permute-start.3
  198.1 17.3 %copy-start = (bf16[16,24,1792]{2,1,0:T(8,128)(2,1)}, bf16[16,24,1792]{2,1,0:T(8,128)(2,1)S(1)}, u32[]{:S(2)}) copy-start(bf16[16,24,1792]{2,1,0:T(8,128)(2,1)S(1)} %all-to-all-done.2.rest_parts_ref) | copy-start | bytes 4128772
  198.1 21.7 %all-to-all-start.3 = ((bf16[16,24,640]{2,1,0:T(8,128)(2,1)}), bf16[16,24,640]{2,1,0:T(8,128)(2,1)S(1)}, u32[]{:S(2)}, u32[]{:S(2)}) async-start(bf16[16,24,640]{2,1,0:T(8,128)(2,1)} %bitcast.15), calls=%async_computation.3 | async-start | bytes 983040 | tf_op jit(solution)/shard_map/all_to_all | solution.py:554
  219.8 0.8 copy-start.3
  222.9 1.4 collective-permute-start.4
  225.0 3.7 %collective-permute-start.5 = (f32[8,384]{1,0:T(8,128)S(1)}, f32[8,384]{1,0:T(8,128)S(1)}, u32[]{:S(2)}, u32[]{:S(2)}) collective-permute-start(f32[8,384]{1,0:T(8,128)S(1)} %add.46), channel_id=1, source_target_pairs={{0,2},{2,0},{4,6},{6,4},{8,10},{10,8},{12,14},{14,12},{16,18},{18,... | collective-permute-start | bytes 36872 | tf_op jit(solution)/shard_map/ppermute | solution.py:567
  228.7 3.7 %collective-permute-start.6 = (f32[8,384]{1,0:T(8,128)S(1)}, f32[8,384]{1,0:T(8,128)S(1)}, u32[]{:S(2)}, u32[]{:S(2)}) collective-permute-start(f32[8,384]{1,0:T(8,128)S(1)} %add.47), channel_id=1, source_target_pairs={{0,4},{2,6},{4,0},{6,2},{8,12},{10,14},{12,8},{14,10},{16,20},{18,... | collective-permute-start | bytes 36872 | tf_op jit(solution)/shard_map/ppermute | solution.py:567
  232.4 3.7 %collective-permute-start.7 = (f32[8,384]{1,0:T(8,128)S(1)}, f32[8,384]{1,0:T(8,128)S(1)}, u32[]{:S(2)}, u32[]{:S(2)}) collective-permute-start(f32[8,384]{1,0:T(8,128)S(1)} %add.48), channel_id=1, source_target_pairs={{0,8},{2,10},{4,12},{6,14},{8,0},{10,2},{12,4},{14,6},{16,24},{18,... | collective-permute-start | bytes 36872 | tf_op jit(solution)/shard_map/ppermute | solution.py:567
  236.1 4.6 %collective-permute-start.8 = (f32[8,384]{1,0:T(8,128)S(1)}, f32[8,384]{1,0:T(8,128)S(1)}, u32[]{:S(2)}, u32[]{:S(2)}) collective-permute-start(f32[8,384]{1,0:T(8,128)S(1)} %add.49), channel_id=1, source_target_pairs={{0,16},{2,18},{4,20},{6,22},{8,24},{10,26},{12,28},{14,30},{16,0},... | collective-permute-start | bytes 36872 | tf_op jit(solution)/shard_map/ppermute | solution.py:567
  240.7 0.7 copy-start.4

commit v4 on v3

--- a/solution.py
+++ b/solution.py
@@ -22,11 +22,11 @@
 NN = (((1,), (0,)), ((), ()))
 NT = (((1,), (1,)), ((), ()))
 TN = (((0,), (0,)), ((), ()))
-QB = 128
+QB = 320
 FB = 512
 FC = 256
 PAIR = 2 * HD
-VMEM = pltpu.CompilerParams(vmem_limit_bytes=56 * 2**20)
+VMEM = pltpu.CompilerParams(vmem_limit_bytes=60 * 2**20)
 
 
 def cost(microseconds):
@@ -49,15 +49,10 @@
     return rs * (gained - jnp.mean(gained, axis=-1, keepdims=True) - normal * inner)
 
 
-def gelu_parts(h):
-    gauss = jnp.exp(h * h * -0.5)
-    t = 1.0 / (1.0 + (0.3275911 * 0.7071067811865476) * jnp.abs(h))
-    poly = t * (
-        0.127414796
-        + t * (-0.142248368 + t * (0.7107068705 + t * (-0.7265760135 + t * 0.5307027145)))
-    )
-    tail = poly * gauss
-    return jnp.where(h < 0.0, tail, 1.0 - tail), gauss
+def gelu_both(h, gradient):
+    cdf = 0.5 + 0.5 * lax.erf(h * 0.7071067811865476)
+    density = jnp.exp(h * h * -0.5) * 0.3989422804014327
+    return (h * cdf).astype(BF16), (gradient * (cdf + h * density)).astype(BF16)
 
 
 def split_pairs(own, other, per_pair):
@@ -77,83 +72,134 @@
     return [first] + parts[0], [third] + parts[1]
 
 
+def gathered_norms(first, second, chips, part, width):
+    shard_rows = first.shape[0] // chips
+    cols = slice(9 * HD, 9 * HD + part)
+    pieces = []
+    for chip in range(chips):
+        row = chip * shard_rows
+        for values in (first, second):
+            pieces.append(values[row : row + 1, cols] + values[row + 1 : row + 2, cols])
+    per_row = width // part
+    return [jnp.concatenate(pieces[i * per_row : (i + 1) * per_row], axis=1) for i in range(4)]
+
+
 def forward_kernel(
-    tok_ref, bias_ref, own_ref, other_ref, norms_ref, n1t_ref, qkv_ref, att_ref, p_ref, w_ref
+    chips, part, side_ref, len_ref, tok_ref, mask_ref, own_ref, other_ref,
+    n1t_ref, qkv_ref, att_ref, linv_ref, p_ref, w_ref, norms_ref,
 ):
     rows, width = tok_ref.shape
-
-    @pl.when(pl.program_id(0) == 0)
+    pairs = width // PAIR
+    side, seq = side_ref[0], pl.program_id(0)
+
+    @pl.when(seq == 0)
     def _():
-        cols = 9 * HD
-        for i, part in enumerate(split_pairs(own_ref[:, :cols], other_ref[:, :cols], 3 * HD)):
-            w_ref[i] = part
-
-    x = tok_ref[...].astype(F32)
-    normal, _ = normalize(x)
+        own, other = own_ref[...], other_ref[...]
+        for i, weights in enumerate(split_pairs(own[:, : 9 * HD], other[:, : 9 * HD], 3 * HD)):
+            w_ref[i] = weights
+        tail = slice(8 * HD, 10 * HD)
+        mine, theirs = own[:, tail].astype(F32), other[:, tail].astype(F32)
+        pad = jnp.zeros((own.shape[0], 8 * HD), F32)
+        first = jnp.concatenate([pad, jnp.where(side == 0, mine, theirs)], axis=1)
+        second = jnp.concatenate([pad, jnp.where(side == 0, theirs, mine)], axis=1)
+        for i, row in enumerate(gathered_norms(first, second, chips, part, width)):
+            norms_ref[i : i + 1, :] = row
+
+    member = side * pl.num_programs(0) + seq
+    position = lax.broadcasted_iota(jnp.int32, (1, rows), 1)
+    mask = mask_ref[pl.ds(member, 1), :]
+    visible = (position < len_ref[member]) & ((mask == 1) | (position == 0))
+    hidden = jnp.where(visible, 0.0, -1e30)
+    hidden = jnp.broadcast_to(hidden, (PAIR, rows)).T.astype(BF16)
+
+    normal, _ = normalize(tok_ref[...].astype(F32))
     n1 = (normal * norms_ref[0:1, :] + norms_ref[1:2, :]).astype(BF16)
     n1t_ref[...] = n1.T
-    bias = bias_ref[...]
     lane = lax.broadcasted_iota(jnp.int32, (QB, PAIR), 1)
-    for pair in range(width // PAIR):
-        part = mm(n1, w_ref[pair])
-        qkv_ref[pair, :, :PAIR] = (part[:, :PAIR].astype(BF16).astype(F32) * (HD**-0.5)).astype(BF16)
-        qkv_ref[pair, :, PAIR:] = part[:, PAIR:].astype(BF16)
-        kp = qkv_ref[pair, :, PAIR : 2 * PAIR]
-        vp = qkv_ref[pair, :, 2 * PAIR :]
-        for qb in range(rows // QB):
-            sl = slice(qb * QB, (qb + 1) * QB)
-            qp = qkv_ref[pair, sl, :PAIR]
-            outs = []
+    key_lane = lax.broadcasted_iota(jnp.int32, (rows, PAIR), 1)
+    ones = jnp.ones((rows, PAIR), BF16)
+    ready = {}
+
+    def project(pair):
+        out = mm(n1, w_ref[pair])
+        queries = (out[:, :PAIR].astype(BF16).astype(F32) * (HD**-0.5)).astype(BF16)
+        others = out[:, PAIR:].astype(BF16)
+        qkv_ref[pair, :, :PAIR] = queries
+        qkv_ref[pair, :, PAIR:] = others
+        keys = [jnp.where(key_lane == HD * (1 - half), hidden, others[:, :PAIR]) for half in range(2)]
+        return queries, keys, jnp.concatenate([others[:, PAIR:], ones], axis=1)
+
+    def scores(pair, block, half):
+        if pair not in ready:
+            ready[pair] = project(pair)
+        queries, keys, _ = ready[pair]
+        spot = jnp.where(lane == HD * (1 - half), 1.0, 0.0).astype(BF16)
+        part_queries = jnp.where((lane < HD) == (half == 0), queries[block * QB : (block + 1) * QB], spot)
+        return mm(part_queries, keys[half], NT)
+
+    outs = {}
+
+    def finish(pair, block, half, s):
+        sl = slice(block * QB, (block + 1) * QB)
+        p = jnp.exp(s - jnp.max(s, axis=-1, keepdims=True)).astype(BF16)
+        p_ref[pair * 2 + half, sl, :] = p
+        out = mm(p, ready[pair][2])
+        inverse = 1.0 / out[:, PAIR:]
+        outs[half] = (out[:, :PAIR] * inverse, inverse)
+        if half == 1:
+            cols = slice(pair * PAIR, (pair + 1) * PAIR)
+            att_ref[sl, cols] = jnp.where(lane < HD, outs[0][0], outs[1][0]).astype(BF16)
+            linv_ref[sl, cols] = jnp.where(lane < HD, outs[0][1], outs[1][1])
+
+    pending = None
+    for pair in range(pairs):
+        for block in range(rows // QB):
             for half in range(2):
-                qm = jnp.where((lane < HD) == (half == 0), qp, jnp.zeros_like(qp))
-                s = mm(qm, kp, NT) + bias
-                e = jnp.exp(s - jnp.max(s, axis=-1, keepdims=True))
-                p = (e * (1.0 / jnp.sum(e, axis=-1, keepdims=True))).astype(BF16)
-                p_ref[pair * 2 + half, sl, :] = p
-                outs.append(mm(p, vp))
-            att_ref[sl, pair * PAIR : (pair + 1) * PAIR] = jnp.where(
-                lane < HD, outs[0], outs[1]
-            ).astype(BF16)
-
-
-def forward(tokens, bias, own, other, norms):
+                fresh = (pair, block, half, scores(pair, block, half))
+                if pending is not None:
+                    finish(*pending)
+                pending = fresh
+    finish(*pending)
+
+
+def forward(chips, part, side, lengths, tokens, key_masks, own, other):
     seqs, rows, width = tokens.shape
     heads, pairs = width // HD, width // PAIR
     sq = pl.squeezed
     shape = jax.ShapeDtypeStruct
     whole = lambda *dims: pl.BlockSpec(dims, lambda s: (0,) * len(dims))
+    row_spec = pl.BlockSpec((sq, rows, width), lambda s: (s, 0, 0))
+    scalars = pl.BlockSpec(memory_space=pltpu.SMEM)
     return pl.pallas_call(
-        forward_kernel,
+        functools.partial(forward_kernel, chips, part),
         grid=(seqs,),
-        in_specs=[
-            pl.BlockSpec((sq, rows, width), lambda s: (s, 0, 0)),
-            pl.BlockSpec((sq, 1, rows), lambda s: (s, 0, 0)),
-            whole(*own.shape),
-            whole(*other.shape),
-            whole(4, width),
-        ],
+        in_specs=[scalars, scalars, row_spec, whole(*key_masks.shape), whole(*own.shape), whole(*other.shape)],
         out_specs=[
             pl.BlockSpec((sq, width, rows), lambda s: (s, 0, 0)),
             pl.BlockSpec((sq, pairs, rows, 3 * PAIR), lambda s: (s, 0, 0, 0)),
-            pl.BlockSpec((sq, rows, width), lambda s: (s, 0, 0)),
+            row_spec,
+            row_spec,
             pl.BlockSpec((sq, heads, rows, rows), lambda s: (s, 0, 0, 0)),
             whole(pairs, width, 3 * PAIR),
+            whole(4, width),
         ],
         out_shape=[
             shape((seqs, width, rows), BF16),
             shape((seqs, pairs, rows, 3 * PAIR), BF16),
             shape((seqs, rows, width), BF16),
+            shape((seqs, rows, width), F32),
             shape((seqs, heads, rows, rows), BF16),
             shape((pairs, width, 3 * PAIR), BF16),
+            shape((4, width), F32),
         ],
         compiler_params=VMEM,
-        cost_estimate=cost(50),
+        cost_estimate=cost(24),
         name="attention_forward",
-    )(tokens, bias, own, other, norms)
+    )(side, lengths, tokens, key_masks, own, other)
 
 
 def middle_kernel(
-    seq_rows, units, len_ref, tok_ref, cot_ref, att_ref, own_ref, other_ref, norms_ref,
+    seq_rows, units, side_ref, len_ref, tok_ref, cot_ref, att_ref, linv_ref, own_ref, other_ref, norms_ref,
     out_ref, gmid_ref, gatt_ref, gown_ref, gother_ref, gnorm_ref,
     wo_ref, gout_ref, gup_ref, gdown_ref,
 ):
@@ -175,10 +221,10 @@
     first = step * rows
     row = first + lax.broadcasted_iota(jnp.int32, (rows, 1), 0)
     live = row < 0
-    last = len_ref.shape[0] - 1
+    seqs = rows * pl.num_programs(0) // seq_rows
     for near in range(-(-rows // seq_rows) + 1):
         s = first // seq_rows + near
-        bound = jnp.where(s <= last, len_ref[jnp.minimum(s, last)], 0)
+        bound = jnp.where(s < seqs, len_ref[side_ref[0] * seqs + jnp.minimum(s, seqs - 1)], 0)
         live = live | ((row >= s * seq_rows) & (row < s * seq_rows + bound))
 
     x = tok_ref[...].astype(F32)
@@ -191,22 +237,30 @@
     up = jnp.where(live, cot_ref[...].astype(F32), 0.0)
     gb = up.astype(BF16)
     gbt = gb.T
-    bo = mid
-    gtwo = jnp.zeros_like(mid)
+    sums = [mid, jnp.zeros_like(mid)]
+
+    def begin(half, c):
+        wu = halves[half][:, c * FC : (c + 1) * FC]
+        wd = halves[half][:, units + c * FC : units + (c + 1) * FC]
+        return half, c, wu, wd, mm(n2, wu), mm(gb, wd)
+
+    def finish(half, c, wu, wd, h, ga):
+        cols = slice(c * FC, (c + 1) * FC)
+        act, gh = gelu_both(h, ga)
+        sums[0] = sums[0] + mm(act, wd, NT)
+        sums[1] = sums[1] + mm(gh, wu, NT)
+        gup_ref[half, :, cols] += mm(n2t, gh)
+        gdown_ref[half, :, cols] += mm(gbt, act)
+
+    pending = None
     for half in range(2):
         for c in range(units // FC):
-            cols = slice(c * FC, (c + 1) * FC)
-            wu = halves[half][:, c * FC : (c + 1) * FC]
-            wd = halves[half][:, units + c * FC : units + (c + 1) * FC]
-            h = mm(n2, wu)
-            ga = mm(gb, wd)
-            cdf, gauss = gelu_parts(h)
-            act = (h * cdf).astype(BF16)
-            gh = (ga * (cdf + h * (gauss * 0.3989422804014327))).astype(BF16)
-            bo = bo + mm(act, wd, NT)
-            gtwo = gtwo + mm(gh, wu, NT)
-            gup_ref[half, :, cols] += mm(n2t, gh)
-            gdown_ref[half, :, cols] += mm(gbt, act)
+            fresh = begin(half, c)
+            if pending is not None:
+                finish(*pending)
+            pending = fresh
+    finish(*pending)
+    bo, gtwo = sums
     out_ref[...] = bo.astype(BF16)
     gnorm_ref[0:8, :] += jnp.sum((gtwo * normal).reshape(rows // 8, 8, width), axis=0)
     gnorm_ref[8:16, :] += jnp.sum(gtwo.reshape(rows // 8, 8, width), axis=0)
@@ -214,7 +268,7 @@
     gmid_ref[...] = gmid
     gm = gmid.astype(BF16)
     gout_ref[...] += mm(gm, att, TN)
-    gatt_ref[...] = mm(gm, wo_ref[...]).astype(BF16)
+    gatt_ref[...] = (mm(gm, wo_ref[...]) * linv_ref[...]).astype(BF16)
 
     @pl.when(step == pl.num_programs(0) - 1)
     def _():
@@ -229,7 +283,7 @@
             ref[:, 2 * units :] = jnp.concatenate(sides[half] + [blank], axis=1).astype(BF16)
 
 
-def middle(lengths, tokens, cotangent, attended, own, other, norms):
+def middle(side, lengths, tokens, cotangent, attended, linv, own, other, norms):
     seqs, seq_rows, width = tokens.shape
     total = seqs * seq_rows
     packed = own.shape[1]
@@ -243,6 +297,8 @@
         grid=(total // FB,),
         in_specs=[
             pl.BlockSpec(memory_space=pltpu.SMEM),
+            pl.BlockSpec(memory_space=pltpu.SMEM),
+            rowspec,
             rowspec,
             rowspec,
             rowspec,
@@ -266,55 +322,65 @@
             pltpu.VMEM((2, width, units), F32),
         ],
         compiler_params=VMEM,
-        cost_estimate=cost(50),
+        cost_estimate=cost(36),
         name="feed_forward",
-    )(lengths, flat(tokens), flat(cotangent), flat(attended), own, other, norms)
-
-
-def backward_kernel(
-    n1t_ref, qkv_ref, p_ref, gatt_ref, att_ref, gp_ref, gown_ref, gother_ref, gqkv_ref
-):
-    seq, pair = pl.program_id(0), pl.program_id(1)
-    rows = qkv_ref.shape[0]
-    qp, kp, vp = qkv_ref[:, :PAIR], qkv_ref[:, PAIR : 2 * PAIR], qkv_ref[:, 2 * PAIR :]
-    ga = gatt_ref[...]
-    prod = ga.astype(F32) * att_ref[...].astype(F32)
-    lane = lax.broadcasted_iota(jnp.int32, (QB, PAIR), 1)
-    gat, qt = ga.T, qp.T
-    zero = jnp.zeros((QB, PAIR), BF16)
-    gq = [[], []]
-    gkt, gvt = [], []
-    for half in range(2):
-        ds_all = []
-        mask = (lane < HD) == (half == 0)
-        for qb in range(rows // QB):
-            sl = slice(qb * QB, (qb + 1) * QB)
-            dp = mm(jnp.where(mask, ga[sl], zero), vp, NT)
-            inner = jnp.sum(jnp.where(mask, prod[sl], 0.0), axis=-1, keepdims=True)
-            ds = (p_ref[half, sl, :].astype(F32) * (dp - inner)).astype(BF16)
-            ds_all.append(ds)
-            gq[half].append(mm(ds, kp))
-        ds = jnp.concatenate(ds_all, axis=0)
-        hs = slice(half * HD, half * HD + HD)
-        gkt.append(mm(qt[hs], ds))
-        gvt.append(mm(gat[hs], p_ref[half]))
-    for qb in range(rows // QB):
-        sl = slice(qb * QB, (qb + 1) * QB)
-        joined = jnp.where(lane < HD, gq[0][qb], gq[1][qb])
-        gp_ref[sl, :PAIR] = (joined * (HD**-0.5)).astype(BF16)
-    gp_ref[:, PAIR : 2 * PAIR] = jnp.concatenate(gkt, axis=0).astype(BF16).T
-    gp_ref[:, 2 * PAIR :] = jnp.concatenate(gvt, axis=0).astype(BF16).T
-    new = mm(n1t_ref[...], gp_ref[...])
+    )(side, lengths, flat(tokens), flat(cotangent), flat(attended), flat(linv), own, other, norms)
+
+
+def backward_kernel(n1t_ref, qkv_ref, p_ref, gatt_ref, att_ref, gp_ref, gown_ref, gother_ref, gqkv_ref):
+    seq = pl.program_id(0)
+    pairs, rows = qkv_ref.shape[:2]
 
     @pl.when(seq == 0)
     def _():
-        gqkv_ref[pair] = new
-
-    @pl.when(seq > 0)
-    def _():
-        gqkv_ref[pair] += new
-
-    @pl.when((seq == pl.num_programs(0) - 1) & (pair == pl.num_programs(1) - 1))
+        gqkv_ref[...] = jnp.zeros_like(gqkv_ref)
+
+    lane = lax.broadcasted_iota(jnp.int32, (rows, PAIR), 1)
+    zero = jnp.zeros((rows, PAIR), BF16)
+    state = {}
+
+    def begin(pair, half):
+        if half == 0:
+            cols = slice(pair * PAIR, (pair + 1) * PAIR)
+            ga = gatt_ref[:, cols]
+            state[pair] = dict(
+                ga=ga,
+                inner=ga.astype(F32) * att_ref[:, cols].astype(F32),
+                gat=ga.T,
+                qt=qkv_ref[pair, :, :PAIR].T,
+                gq=[],
+                gkt=[],
+                gvt=[],
+            )
+        mask = (lane < HD) == (half == 0)
+        return pair, half, mask, mm(jnp.where(mask, state[pair]["ga"], zero), qkv_ref[pair, :, 2 * PAIR :], NT)
+
+    def finish(pair, half, mask, dp):
+        mine = state[pair]
+        hs = slice(half * HD, half * HD + HD)
+        p = p_ref[pair * 2 + half]
+        mine["gvt"].append(mm(mine["gat"][hs], p))
+        inner = jnp.sum(jnp.where(mask, mine["inner"], 0.0), axis=-1, keepdims=True)
+        ds = (p.astype(F32) * (dp - inner)).astype(BF16)
+        mine["gq"].append(mm(ds, qkv_ref[pair, :, PAIR : 2 * PAIR]))
+        mine["gkt"].append(mm(mine["qt"][hs], ds))
+        if half == 1:
+            joined = jnp.where(lane < HD, mine["gq"][0], mine["gq"][1])
+            gp_ref[pair, :, :PAIR] = (joined * (HD**-0.5)).astype(BF16)
+            gp_ref[pair, :, PAIR : 2 * PAIR] = jnp.concatenate(mine["gkt"], axis=0).astype(BF16).T
+            gp_ref[pair, :, 2 * PAIR :] = jnp.concatenate(mine["gvt"], axis=0).astype(BF16).T
+            gqkv_ref[pair] += mm(n1t_ref[...], gp_ref[pair])
+
+    pending = None
+    for pair in range(pairs):
+        for half in range(2):
+            fresh = begin(pair, half)
+            if pending is not None:
+                finish(*pending)
+            pending = fresh
+    finish(*pending)
+
+    @pl.when(seq == pl.num_programs(0) - 1)
     def _():
         sides = join_pairs(gqkv_ref[0], gqkv_ref[1], gqkv_ref[2], 3 * HD)
         blank = jnp.zeros((gqkv_ref.shape[1], HD), F32)
@@ -326,26 +392,26 @@
     seqs, rows, width = attended.shape
     pairs = width // PAIR
     sq = pl.squeezed
-    pairspec = pl.BlockSpec((sq, rows, PAIR), lambda s, p: (s, 0, p))
-    groupspec = pl.BlockSpec((sq, sq, rows, 3 * PAIR), lambda s, p: (s, p, 0, 0))
-    whole = lambda *dims: pl.BlockSpec(dims, lambda s, p: (0,) * len(dims))
+    rowspec = pl.BlockSpec((sq, rows, width), lambda s: (s, 0, 0))
+    groupspec = pl.BlockSpec((sq, pairs, rows, 3 * PAIR), lambda s: (s, 0, 0, 0))
+    whole = lambda *dims: pl.BlockSpec(dims, lambda s: (0,) * len(dims))
     shape = jax.ShapeDtypeStruct
     packed = (width, 10 * HD)
     return pl.pallas_call(
         backward_kernel,
-        grid=(seqs, pairs),
+        grid=(seqs,),
         in_specs=[
-            pl.BlockSpec((sq, width, rows), lambda s, p: (s, 0, 0)),
+            pl.BlockSpec((sq, width, rows), lambda s: (s, 0, 0)),
             groupspec,
-            pl.BlockSpec((sq, 2, rows, rows), lambda s, p: (s, p, 0, 0)),
-            pairspec,
-            pairspec,
+            pl.BlockSpec((sq, 2 * pairs, rows, rows), lambda s: (s, 0, 0, 0)),
+            rowspec,
+            rowspec,
         ],
         out_specs=[groupspec, whole(*packed), whole(*packed)],
         out_shape=[shape(qkv.shape, BF16), shape(packed, BF16), shape(packed, BF16)],
         scratch_shapes=[pltpu.VMEM((pairs, width, 3 * PAIR), F32)],
         compiler_params=VMEM,
-        cost_estimate=cost(50),
+        cost_estimate=cost(27),
         name="attention_backward",
     )(n1t, qkv, probs, gatt, attended)
 
@@ -506,7 +572,6 @@
     norm_part = norm_master.shape[0]
     units = up_master.shape[1]
     side = lax.axis_index("head")
-    own_first = side == 0
 
     qkv_rows = qkv_master.transpose(1, 0, 2)
     masters = (qkv_rows, out_master.T, up_master, down_master.T, norm_master[None])
@@ -518,31 +583,17 @@
         *masters,
     )
     lead_own = lax.all_to_all(lead, "batch", 0, 0)
-    lead_own, rest = lax.optimization_barrier((lead_own, rest))
     rest_own = lax.all_to_all(rest, "batch", 0, 0)
     lead_other = swap(lead_own)
-
-    def norms_of(gathered):
-        parts = gathered[:, :2, 9 * HD : 9 * HD + norm_part].astype(F32)
-        return parts[:, 0] + parts[:, 1]
-
-    norms_own, norms_other = norms_of(lead_own), norms_of(lead_other)
-    norms = jnp.stack(
-        [jnp.where(own_first, norms_own, norms_other), jnp.where(own_first, norms_other, norms_own)], axis=1
-    ).reshape(4, width)
-
-    positions = jnp.arange(slot_rows, dtype=jnp.int32)
-    own_lengths = lax.dynamic_slice_in_dim(lengths, side * seqs, seqs)
-    own_masks = lax.dynamic_slice_in_dim(key_masks, side * seqs, seqs)
-    visible = (positions[None, :] < own_lengths[:, None]) & ((own_masks == 1) | (positions[None, :] == 0))
-    bias = jnp.where(visible, 0.0, -1e30).astype(F32)[:, None, :]
-
     flat = lambda a: a.reshape(chips * shard_rows, a.shape[-1])
-    n1t, qkv, attended, probs, wpairs = forward(tokens, bias, flat(lead_own), flat(lead_other), norms)
+    place = side.astype(jnp.int32).reshape(1)
+    n1t, qkv, attended, linv, probs, wpairs, norms = forward(
+        chips, norm_part, place, lengths, tokens, key_masks, flat(lead_own), flat(lead_other)
+    )
     rest_own, attended = lax.optimization_barrier((rest_own, attended))
     rest_other = swap(rest_own)
     block_out, gmid, gatt, grest_own, grest_other, gnorm_two = middle(
-        own_lengths, tokens, cotangent, attended, flat(rest_own), flat(rest_other), norms
+        place, lengths, tokens, cotangent, attended, linv, flat(rest_own), flat(rest_other), norms
     )
     per_seq = lambda a: a.reshape(seqs, slot_rows, width)
     rest_sum = (grest_own.astype(F32) + swap(grest_other).astype(F32)).astype(BF16)
@@ -566,8 +617,8 @@
     while stride < chips:
         message = message + lax.ppermute(message, "batch", [(i, i ^ stride) for i in range(chips)])
         stride *= 2
-    place = (lax.axis_index("batch") * 2 + side) * norm_part
-    mine = lax.dynamic_slice_in_dim(message[:4].reshape(1, 4 * width), place, norm_part, axis=1)
+    start = (lax.axis_index("batch") * 2 + side) * norm_part
+    mine = lax.dynamic_slice_in_dim(message[:4].reshape(1, 4 * width), start, norm_part, axis=1)
     like = lambda a: shape(a.shape, F32)
     moments = (
         qkv_moments.transpose(0, 2, 1, 3),

time: 245 us -> 193 us (0.79)
  Pallas kernels: 163 us -> 105 us
  waiting for transfers between devices: 26 us -> 32.2 us
    pallas_call x2, Pallas kernels: 99.8 us -> 51.8 us  [the longest x1 27.4 us: backward(): pl.pallas_call(backward_kernel, grid=(seqs,), in_specs=[pl.BlockSpec((sq,...]
    pallas_call x1, Pallas kernels: 45.3 us -> 35.9 us  [middle(): pl.pallas_call(functools.partial(middle_kernel, seq_rows, units), grid=(t...]
    all_to_all x1, waiting for transfers between devices: 0.01 us -> 5.66 us  [per_device(): rest_own = lax.all_to_all(rest, 'batch', 0, 0)]
  transfers between devices with their start and end apart: 12 -> 12, of which waited for: 9 -> 10; matrix products, arithmetic and copies ran while one was open for 1% -> 1% of each run, Pallas kernels for 45% -> 32%
where the time goes in v4:
time: 193 us; the launch traced here: 192 us
  Pallas kernels  105 us (54%)
  waiting for transfers between devices  32.2 us (17%)
  blocking collectives  22.8 us (12%)
  starting transfers between devices  22.1 us (11%)
  other arithmetic  5.45 us (3%)
  local copies, waits for them, and re-layouts  3.29 us (2%)
    pallas_call x1, Pallas kernels, middle(): pl.pallas_call(functools.partial(middle_kernel, seq_rows, units), grid=(t...  35.9 us
    pallas_call x1, Pallas kernels, backward(): pl.pallas_call(backward_kernel, grid=(seqs,), in_specs=[pl.BlockSpec((sq,...  27.4 us
    pallas_call x1, Pallas kernels, forward(): pl.pallas_call(functools.partial(forward_kernel, chips, part), grid=(seqs...  24.4 us
    all_to_all x1, blocking collectives, per_device(): lead_own = lax.all_to_all(lead, 'batch', 0, 0)  22.8 us
    ppermute x4, waiting for transfers between devices, per_device(): lax.ppermute(message, 'batch', [(i, i ^ stride) for i in range(chips)])  12.4 us
    pallas_call x1, Pallas kernels, input_gradient(): pl.pallas_call(input_kernel, grid=(seqs,), in_specs=[full, pl.BlockSpec((...  10.4 us
    ppermute x5, waiting for transfers between devices, swap(): return lax.ppermute(values, 'head', [(0, 1), (1, 0)])  9.78 us
    all_to_all x1, starting transfers between devices, per_device(): rest_parts = lax.all_to_all(rest_sum.reshape(rest.shape), 'batch', 0, 0)  7.78 us
  transfers between devices with their start and end apart: 12, of which 10 were waited for; matrix products, arithmetic and copies ran while one was open for 1% of the time, Pallas kernels for 32%

profile of v4, /device:TPU:0, one launch (start us, length us, event | category | flops | bytes accessed | tf_op | source)
XLA Modules:
  0.0 191.9 jit_solution(11835756219075639356)
XLA Ops:
  0.6 2.3 %pack_weights.1 = (bf16[16,24,640]{2,1,0:T(8,128)(2,1)}, bf16[16,24,1792]{2,1,0:T(8,128)(2,1)}) custom-call(f32[3,24,192]{2,1,0:T(8,128)} %bitcast.43, f32[24,192]{1,0:T(8,128)} %bitcast.48, f32[24,768]{1,0:T(8,128)} %up_ref.3, f32[24,768]{1,0:T(8,128)} %bitcast.45, f32[1,48]{1,0:T(1,128)} %bitcast.50), custom_call_target="tpu_custom_call" | custom-call | flops 3000000000 | bytes 1000000 | tf_op jit(solution)/shard_map/pack_weights/pallas_call | solution.py:544
  2.9 22.8 %all_to_all.20 = bf16[16,24,640]{2,1,0:T(8,128)(2,1)S(1)} all-to-all(bf16[16,24,640]{2,1,0:T(8,128)(2,1)} %get-tuple-element.56), channel_id=1, replica_groups=mesh['batch'=16,'head'=2] {'batch'}, dimensions={0} | all-to-all | bytes 983040 | tf_op jit(solution)/shard_map/all_to_all | solution.py:585
  25.8 3.8 %all-to-all-start = ((bf16[16,24,1792]{2,1,0:T(8,128)(2,1)}), bf16[16,24,1792]{2,1,0:T(8,128)(2,1)S(1)}, u32[]{:S(2)}, u32[]{:S(2)}) async-start(bf16[16,24,1792]{2,1,0:T(8,128)(2,1)} %get-tuple-element.55), calls=%async_computation | async-start | bytes 2752512 | tf_op jit(solution)/shard_map/all_to_all | solution.py:586
  29.6 0.8 copy-done.6
  30.4 24.4 %attention_forward.1 = (bf16[4,384,640]{2,1,0:T(8,128)(2,1)}, bf16[4,3,640,384]{3,2,1,0:T(8,128)(2,1)}, bf16[4,640,384]{2,1,0:T(8,128)(2,1)}, f32[4,640,384]{2,1...) custom-call(s32[1]{0:T(128)} %bitcast.side_ref, s32[8]{0:T(128)} %len_ref.3, ...), custom_call_target="tpu_custom_call" | custom-call | flops 24000000000 | bytes 1000000 | tf_op jit(solution)/shard_map/attention_forward/pallas_call | solution.py:173
  54.8 5.7 %all-to-all-done = bf16[16,24,1792]{2,1,0:T(8,128)(2,1)S(1)} async-done(((bf16[16,24,1792]{2,1,0:T(8,128)(2,1)}), bf16[16,24,1792]{2,1,0:T(8,128)(2,1)S(1)}, u32[]{:S(2)}, u32[]{:S(2)}) %all-to-all-start) | async-done | bytes 1376288 | tf_op jit(solution)/shard_map/all_to_all | solution.py:586
  60.5 3.1 %collective-permute-done.1 = bf16[16,24,1792]{2,1,0:T(8,128)(2,1)S(1)} collective-permute-done((bf16[16,24,1792]{2,1,0:T(8,128)(2,1)S(1)}, bf16[16,24,1792]{2,1,0:T(8,128)(2,1)S(1)}, u32[]{:S(2)}, u32[]{:S(2)}) %collective-permute-start.1) | collective-permute-done | bytes 1376288 | tf_op jit(solution)/shard_map/ppermute | solution.py:550
  63.6 1.1 copy-done.5
  64.7 35.9 %feed_forward.1 = (bf16[2560,384]{1,0:T(8,128)(2,1)}, f32[2560,384]{1,0:T(8,128)}, bf16[2560,384]{1,0:T(8,128)(2,1)}, bf16[384,1792]{1,0:T(8,128)(2,1)}, bf16[384,1792]{1,0:T(8,128)(2,1)}, /*index=5*/f32[16,384]{1,0:T(8,128)}) custom-call(s32[1]{0:T(128)} %bitcast.side_ref, s32[8]{0:T(128)} %len_ref.3, bf16[2560,384]{1,0:T(8,128)(2,1)} %bitcast.38, ...), custom_call_target="tpu_custom_call" | custom-call | flops 35999997952 | bytes 1000000 | tf_op jit(solution)/shard_map/feed_forward/pallas_call | solution.py:295
  100.8 3.2 %collective-permute-done.2 = bf16[384,1792]{1,0:T(8,128)(2,1)S(1)} collective-permute-done((bf16[384,1792]{1,0:T(8,128)(2,1)}, bf16[384,1792]{1,0:T(8,128)(2,1)S(1)}, u32[]{:S(2)}, u32[]{:S(2)}) %collective-permute-start.2) | collective-permute-done | bytes 1376288 | tf_op jit(solution)/shard_map/ppermute | solution.py:550
  104.0 2.8 %add_convert_fusion = bf16[384,1792]{1,0:T(8,128)(2,1)} fusion(bf16[384,1792]{1,0:T(8,128)(2,1)S(1)} %collective-permute-done.2, bf16[384,1792]{1,0:T(8,128)(2,1)} %get-tuple-element.66), kind=kLoop, calls=%fused_computation | loop fusion | flops 2752512 | bytes 4128768 | tf_op jit(solution)/shard_map/convert_element_type | solution.py:599
  106.8 7.8 %all-to-all-start.2 = ((bf16[16,24,1792]{2,1,0:T(8,128)(2,1)}), bf16[16,24,1792]{2,1,0:T(8,128)(2,1)S(1)}, u32[]{:S(2)}, u32[]{:S(2)}) async-start(bf16[16,24,1792]{2,1,0:T(8,128)(2,1)} %bitcast.16), calls=%async_computation.2 | async-start | bytes 2752512 | tf_op jit(solution)/shard_map/all_to_all | solution.py:601
  114.6 27.4 %attention_backward.1 = (bf16[4,3,640,384]{3,2,1,0:T(8,128)(2,1)}, bf16[384,640]{1,0:T(8,128)(2,1)}, bf16[384,640]{1,0:T(8,128)(2,1)}) custom-call(bf16[4,384,640]{2,1,0:T(8,128)(2,1)} %get-tuple-element.63.n1t_ref, bf16[4,3,640,384]{3,2,1,0:T(8,128)(2,1)} %get-tuple-element.64.qkv_ref, bf16[4,6,640,640]{3,2,1,0:T(8,128)(2,1)} %get-tuple-element.65.p_ref, ...), custom_call_target="tpu_custom_call" | custom-call | flops 27000000512 | bytes 1000000 | tf_op jit(solution)/shard_map/attention_backward/pallas_call | solution.py:400
  142.0 2.1 %collective-permute-done.3 = bf16[384,640]{1,0:T(8,128)(2,1)S(1)} collective-permute-done((bf16[384,640]{1,0:T(8,128)(2,1)}, bf16[384,640]{1,0:T(8,128)(2,1)S(1)}, u32[]{:S(2)}, u32[]{:S(2)}) %collective-permute-start.3) | collective-permute-done | bytes 491552 | tf_op jit(solution)/shard_map/ppermute | solution.py:550
  144.1 1.9 %add_convert_fusion.1 = bf16[384,640]{1,0:T(8,128)(2,1)} fusion(bf16[384,640]{1,0:T(8,128)(2,1)S(1)} %collective-permute-done.3, bf16[384,640]{1,0:T(8,128)(2,1)} %get-tuple-element.75), kind=kLoop, calls=%fused_computation.1 | loop fusion | flops 983040 | bytes 1474560 | tf_op jit(solution)/shard_map/convert_element_type | solution.py:603
  146.0 6.9 %all-to-all-start.3 = ((bf16[16,24,640]{2,1,0:T(8,128)(2,1)}), bf16[16,24,640]{2,1,0:T(8,128)(2,1)S(1)}, u32[]{:S(2)}, u32[]{:S(2)}) async-start(bf16[16,24,640]{2,1,0:T(8,128)(2,1)} %bitcast.17), calls=%async_computation.3 | async-start | bytes 983040 | tf_op jit(solution)/shard_map/all_to_all | solution.py:605
  152.9 10.4 %input_gradient.1 = (f32[4,640,384]{2,1,0:T(8,128)}, f32[8,384]{1,0:T(8,128)}) custom-call(bf16[4,640,384]{2,1,0:T(8,128)(2,1)} %tok_ref.3, bf16[4,3,640,384]{3,2,1,0:T(8,128)(2,1)} %get-tuple-element.70.gp_ref, f32[4,640,384]{2,1,0:T(8,128)} %bitcast.52, bf16[3,384,384]{2,1,0:T(8,128)(2,1)} %get-tuple-element.72.w_ref, ...), custom_call_target="tpu_custom_call" | custom-call | flops 12000000000 | bytes 1000000 | tf_op jit(solution)/shard_map/input_gradient/pallas_call | solution.py:444
  163.3 4.4 %all-to-all-done.3.lead_parts_ref = bf16[16,24,640]{2,1,0:T(8,128)(2,1)S(1)} async-done(((bf16[16,24,640]{2,1,0:T(8,128)(2,1)}), bf16[16,24,640]{2,1,0:T(8,128)(2,1)S(1)}, u32[]{:S(2)}, u32[]{:S(2)}) %all-to-all-start.3) | async-done | bytes 491552 | tf_op jit(solution)/shard_map/all_to_all | solution.py:605
  167.7 0.8 copy-done.3
  168.5 2.3 %sum_parts.1 = (f32[24,640]{1,0:T(8,128)}, f32[24,1792]{1,0:T(8,128)}, f32[8,384]{1,0:T(8,128)}) custom-call(bf16[16,24,640]{2,1,0:T(8,128)(2,1)} %copy-done.3, bf16[16,24,1792]{2,1,0:T(8,128)(2,1)} %copy-done, f32[8,384]{1,0:T(8,128)} %get-tuple-element.80.terms_ref), custom_call_target="tpu_custom_call" | custom-call | flops 3000000000 | bytes 1000000 | tf_op jit(solution)/shard_map/sum_parts/pallas_call | solution.py:544
  170.8 1.4 collective-permute-done.4
  172.2 0.7 add.29
  172.9 0.6 collective-permute-start.5
  173.5 3.1 %collective-permute-done.5 = f32[8,384]{1,0:T(8,128)S(1)} collective-permute-done((f32[8,384]{1,0:T(8,128)S(1)}, f32[8,384]{1,0:T(8,128)S(1)}, u32[]{:S(2)}, u32[]{:S(2)}) %collective-permute-start.5) | collective-permute-done | bytes 12320 | tf_op jit(solution)/shard_map/ppermute | solution.py:618
  176.6 0.9 collective-permute-start.6
  177.5 2.8 %collective-permute-done.6 = f32[8,384]{1,0:T(8,128)S(1)} collective-permute-done((f32[8,384]{1,0:T(8,128)S(1)}, f32[8,384]{1,0:T(8,128)S(1)}, u32[]{:S(2)}, u32[]{:S(2)}) %collective-permute-start.6) | collective-permute-done | bytes 12320 | tf_op jit(solution)/shard_map/ppermute | solution.py:618
  180.3 1.2 collective-permute-start.7
  181.6 2.5 %collective-permute-done.7 = f32[8,384]{1,0:T(8,128)S(1)} collective-permute-done((f32[8,384]{1,0:T(8,128)S(1)}, f32[8,384]{1,0:T(8,128)S(1)}, u32[]{:S(2)}, u32[]{:S(2)}) %collective-permute-start.7) | collective-permute-done | bytes 12320 | tf_op jit(solution)/shard_map/ppermute | solution.py:618
  184.0 0.6 collective-permute-start.8
  184.7 3.9 %collective-permute-done.8 = f32[8,384]{1,0:T(8,128)S(1)} collective-permute-done((f32[8,384]{1,0:T(8,128)S(1)}, f32[8,384]{1,0:T(8,128)S(1)}, u32[]{:S(2)}, u32[]{:S(2)}) %collective-permute-start.8) | collective-permute-done | bytes 12320 | tf_op jit(solution)/shard_map/ppermute | solution.py:618
  188.7 0.6 constant_dynamic-slice_fusion.mine_ref
  189.3 2.4 %update_weights.1 = (f32[1,1]{1,0:T(1,128)}, f32[3,24,192]{2,1,0:T(8,128)}, f32[24,192]{1,0:T(8,128)}, f32[24,768]{1,0:T(8,128)}, f32[24,768]{1,0:T(8,128)}, /*i...) custom-call(f32[8,384]{1,0:T(8,128)} %copy-done.4, ...), custom_call_target="tpu_custom_call" | custom-call | flops 3000000000 | bytes 1000000 | tf_op jit(solution)/shard_map/update_weights/pallas_call | solution.py:544
  (24 shorter events, 0.3 us)
Async XLA Ops:
  25.8 3.9 %copy-start.2 = (bf16[16,24,640]{2,1,0:T(8,128)(2,1)}, bf16[16,24,640]{2,1,0:T(8,128)(2,1)S(1)}, u32[]{:S(2)}) copy-start(bf16[16,24,640]{2,1,0:T(8,128)(2,1)S(1)} %all_to_all.20) | copy-start | bytes 1474564
  25.8 3.8 %collective-permute-start = (bf16[16,24,640]{2,1,0:T(8,128)(2,1)S(1)}, bf16[16,24,640]{2,1,0:T(8,128)(2,1)S(1)}, u32[]{:S(2)}, u32[]{:S(2)}) collective-permute-start(bf16[16,24,640]{2,1,0:T(8,128)(2,1)S(1)} %all_to_all.20), channel_id=1, source_target_pairs={{0,1},{1,0},{2,3},{3,2},{4,5},{5,4},{6,7},{7,6},{8,9},{9,8},{10,11... | collective-permute-start | bytes 1474568 | tf_op jit(solution)/shard_map/ppermute | solution.py:550
  25.8 34.7 %all-to-all-start = ((bf16[16,24,1792]{2,1,0:T(8,128)(2,1)}), bf16[16,24,1792]{2,1,0:T(8,128)(2,1)S(1)}, u32[]{:S(2)}, u32[]{:S(2)}) async-start(bf16[16,24,1792]{2,1,0:T(8,128)(2,1)} %get-tuple-element.55), calls=%async_computation | async-start | bytes 2752512 | tf_op jit(solution)/shard_map/all_to_all | solution.py:586
  29.6 0.8 copy-start.6
  60.5 3.1 %copy-start.1 = (bf16[16,24,1792]{2,1,0:T(8,128)(2,1)}, bf16[16,24,1792]{2,1,0:T(8,128)(2,1)S(1)}, u32[]{:S(2)}) copy-start(bf16[16,24,1792]{2,1,0:T(8,128)(2,1)S(1)} %all-to-all-done) | copy-start | bytes 4128772
  60.5 3.1 %collective-permute-start.1 = (bf16[16,24,1792]{2,1,0:T(8,128)(2,1)S(1)}, bf16[16,24,1792]{2,1,0:T(8,128)(2,1)S(1)}, u32[]{:S(2)}, u32[]{:S(2)}) collective-permute-start(bf16[16,24,1792]{2,1,0:T(8,128)(2,1)S(1)} %all-to-all-done), channel_id=1, source_target_pairs={{0,1},{1,0},{2,3},{3,2},{4,5},{5,4},{6,7},{7,6},{8,9},{9,8},{10,11... | collective-permute-start | bytes 4128776 | tf_op jit(solution)/shard_map/ppermute | solution.py:550
  63.6 1.1 copy-start.5
  100.6 3.4 %collective-permute-start.2 = (bf16[384,1792]{1,0:T(8,128)(2,1)}, bf16[384,1792]{1,0:T(8,128)(2,1)S(1)}, u32[]{:S(2)}, u32[]{:S(2)}) collective-permute-start(bf16[384,1792]{1,0:T(8,128)(2,1)} %get-tuple-element.67), channel_id=1, source_target_pairs={{0,1},{1,0},{2,3},{3,2},{4,5},{5,4},{6,7},{7,6},{8,9},{9,8},{10,11... | collective-permute-start | bytes 4128776 | tf_op jit(solution)/shard_map/ppermute | solution.py:550
  106.8 39.2 %all-to-all-start.2 = ((bf16[16,24,1792]{2,1,0:T(8,128)(2,1)}), bf16[16,24,1792]{2,1,0:T(8,128)(2,1)S(1)}, u32[]{:S(2)}, u32[]{:S(2)}) async-start(bf16[16,24,1792]{2,1,0:T(8,128)(2,1)} %bitcast.16), calls=%async_computation.2 | async-start | bytes 2752512 | tf_op jit(solution)/shard_map/all_to_all | solution.py:601
  142.0 2.1 %collective-permute-start.3 = (bf16[384,640]{1,0:T(8,128)(2,1)}, bf16[384,640]{1,0:T(8,128)(2,1)S(1)}, u32[]{:S(2)}, u32[]{:S(2)}) collective-permute-start(bf16[384,640]{1,0:T(8,128)(2,1)} %get-tuple-element.76), channel_id=1, source_target_pairs={{0,1},{1,0},{2,3},{3,2},{4,5},{5,4},{6,7},{7,6},{8,9},{9,8},{10,11... | collective-permute-start | bytes 1474568 | tf_op jit(solution)/shard_map/ppermute | solution.py:550
  146.0 17.3 %copy-start = (bf16[16,24,1792]{2,1,0:T(8,128)(2,1)}, bf16[16,24,1792]{2,1,0:T(8,128)(2,1)S(1)}, u32[]{:S(2)}) copy-start(bf16[16,24,1792]{2,1,0:T(8,128)(2,1)S(1)} %all-to-all-done.2.rest_parts_ref) | copy-start | bytes 4128772
  146.0 21.7 %all-to-all-start.3 = ((bf16[16,24,640]{2,1,0:T(8,128)(2,1)}), bf16[16,24,640]{2,1,0:T(8,128)(2,1)S(1)}, u32[]{:S(2)}, u32[]{:S(2)}) async-start(bf16[16,24,640]{2,1,0:T(8,128)(2,1)} %bitcast.17), calls=%async_computation.3 | async-start | bytes 983040 | tf_op jit(solution)/shard_map/all_to_all | solution.py:605
  167.7 0.8 copy-start.3
  170.8 1.4 collective-permute-start.4
  172.9 3.7 %collective-permute-start.5 = (f32[8,384]{1,0:T(8,128)S(1)}, f32[8,384]{1,0:T(8,128)S(1)}, u32[]{:S(2)}, u32[]{:S(2)}) collective-permute-start(f32[8,384]{1,0:T(8,128)S(1)} %add.29), channel_id=1, source_target_pairs={{0,2},{2,0},{4,6},{6,4},{8,10},{10,8},{12,14},{14,12},{16,18},{18,... | collective-permute-start | bytes 36872 | tf_op jit(solution)/shard_map/ppermute | solution.py:618
  176.6 3.7 %collective-permute-start.6 = (f32[8,384]{1,0:T(8,128)S(1)}, f32[8,384]{1,0:T(8,128)S(1)}, u32[]{:S(2)}, u32[]{:S(2)}) collective-permute-start(f32[8,384]{1,0:T(8,128)S(1)} %add.30), channel_id=1, source_target_pairs={{0,4},{2,6},{4,0},{6,2},{8,12},{10,14},{12,8},{14,10},{16,20},{18,... | collective-permute-start | bytes 36872 | tf_op jit(solution)/shard_map/ppermute | solution.py:618
  180.3 3.7 %collective-permute-start.7 = (f32[8,384]{1,0:T(8,128)S(1)}, f32[8,384]{1,0:T(8,128)S(1)}, u32[]{:S(2)}, u32[]{:S(2)}) collective-permute-start(f32[8,384]{1,0:T(8,128)S(1)} %add.31), channel_id=1, source_target_pairs={{0,8},{2,10},{4,12},{6,14},{8,0},{10,2},{12,4},{14,6},{16,24},{18,... | collective-permute-start | bytes 36872 | tf_op jit(solution)/shard_map/ppermute | solution.py:618
  184.0 4.6 %collective-permute-start.8 = (f32[8,384]{1,0:T(8,128)S(1)}, f32[8,384]{1,0:T(8,128)S(1)}, u32[]{:S(2)}, u32[]{:S(2)}) collective-permute-start(f32[8,384]{1,0:T(8,128)S(1)} %add.32), channel_id=1, source_target_pairs={{0,16},{2,18},{4,20},{6,22},{8,24},{10,26},{12,28},{14,30},{16,0},... | collective-permute-start | bytes 36872 | tf_op jit(solution)/shard_map/ppermute | solution.py:618
  188.6 0.6 copy-start.4

commit v5 on v4

--- a/solution.py
+++ b/solution.py
@@ -26,7 +26,11 @@
 FB = 512
 FC = 256
 PAIR = 2 * HD
-VMEM = pltpu.CompilerParams(vmem_limit_bytes=60 * 2**20)
+LIMIT_A, LIMIT_B, LIMIT_C, LIMIT_D, LIMIT_S = (
+    pltpu.CompilerParams(vmem_limit_bytes=m * 2**20) for m in (56, 46, 52, 52, 16)
+)
+IN_VMEM = pl.BlockSpec(memory_space=pltpu.VMEM)
+IN_SMEM = pl.BlockSpec(memory_space=pltpu.SMEM)
 
 
 def cost(microseconds):
@@ -169,11 +173,10 @@
     shape = jax.ShapeDtypeStruct
     whole = lambda *dims: pl.BlockSpec(dims, lambda s: (0,) * len(dims))
     row_spec = pl.BlockSpec((sq, rows, width), lambda s: (s, 0, 0))
-    scalars = pl.BlockSpec(memory_space=pltpu.SMEM)
     return pl.pallas_call(
         functools.partial(forward_kernel, chips, part),
         grid=(seqs,),
-        in_specs=[scalars, scalars, row_spec, whole(*key_masks.shape), whole(*own.shape), whole(*other.shape)],
+        in_specs=[IN_SMEM, IN_SMEM, row_spec, IN_VMEM, IN_VMEM, IN_VMEM],
         out_specs=[
             pl.BlockSpec((sq, width, rows), lambda s: (s, 0, 0)),
             pl.BlockSpec((sq, pairs, rows, 3 * PAIR), lambda s: (s, 0, 0, 0)),
@@ -192,7 +195,7 @@
             shape((pairs, width, 3 * PAIR), BF16),
             shape((4, width), F32),
         ],
-        compiler_params=VMEM,
+        compiler_params=LIMIT_A,
         cost_estimate=cost(24),
         name="attention_forward",
     )(side, lengths, tokens, key_masks, own, other)
@@ -201,11 +204,10 @@
 def middle_kernel(
     seq_rows, units, side_ref, len_ref, tok_ref, cot_ref, att_ref, linv_ref, own_ref, other_ref, norms_ref,
     out_ref, gmid_ref, gatt_ref, gown_ref, gother_ref, gnorm_ref,
-    wo_ref, gout_ref, gup_ref, gdown_ref,
+    halves, wo_ref, gout_ref, gup_ref, gdown_ref,
 ):
     step = pl.program_id(0)
     rows, width = tok_ref.shape
-    halves = (own_ref, other_ref)
 
     @pl.when(step == 0)
     def _():
@@ -213,8 +215,10 @@
         gup_ref[...] = jnp.zeros_like(gup_ref)
         gdown_ref[...] = jnp.zeros_like(gdown_ref)
         gnorm_ref[...] = jnp.zeros_like(gnorm_ref)
+        for half, ref in enumerate((own_ref, other_ref)):
+            halves[half] = ref[...]
         cols = slice(2 * units, 2 * units + 3 * HD)
-        parts = split_pairs(own_ref[:, cols], other_ref[:, cols], HD)
+        parts = split_pairs(halves[0, :, cols], halves[1, :, cols], HD)
         for i, part in enumerate(parts):
             wo_ref[:, i * PAIR : (i + 1) * PAIR] = part
 
@@ -240,8 +244,8 @@
     sums = [mid, jnp.zeros_like(mid)]
 
     def begin(half, c):
-        wu = halves[half][:, c * FC : (c + 1) * FC]
-        wd = halves[half][:, units + c * FC : units + (c + 1) * FC]
+        wu = halves[half, :, c * FC : (c + 1) * FC]
+        wd = halves[half, :, units + c * FC : units + (c + 1) * FC]
         return half, c, wu, wd, mm(n2, wu), mm(gb, wd)
 
     def finish(half, c, wu, wd, h, ga):
@@ -286,7 +290,7 @@
 def middle(side, lengths, tokens, cotangent, attended, linv, own, other, norms):
     seqs, seq_rows, width = tokens.shape
     total = seqs * seq_rows
-    packed = own.shape[1]
+    packed = own.shape[-1]
     units = (packed - 4 * HD) // 2
     flat = lambda a: a.reshape(total, width)
     rowspec = pl.BlockSpec((FB, width), lambda s: (s, 0))
@@ -296,32 +300,33 @@
         functools.partial(middle_kernel, seq_rows, units),
         grid=(total // FB,),
         in_specs=[
-            pl.BlockSpec(memory_space=pltpu.SMEM),
-            pl.BlockSpec(memory_space=pltpu.SMEM),
+            IN_SMEM,
+            IN_SMEM,
             rowspec,
             rowspec,
             rowspec,
             rowspec,
-            whole(*own.shape),
-            whole(*other.shape),
+            IN_VMEM,
+            IN_VMEM,
             whole(4, width),
         ],
-        out_specs=[rowspec] * 3 + [whole(*own.shape), whole(*own.shape), whole(16, width)],
+        out_specs=[rowspec] * 3 + [IN_VMEM, IN_VMEM, whole(16, width)],
         out_shape=[
             shape((total, width), BF16),
             shape((total, width), F32),
             shape((total, width), BF16),
-            shape(own.shape, BF16),
-            shape(own.shape, BF16),
+            shape((width, packed), BF16),
+            shape((width, packed), BF16),
             shape((16, width), F32),
         ],
         scratch_shapes=[
+            pltpu.VMEM((2, width, packed), BF16),
             pltpu.VMEM((width, width), BF16),
             pltpu.VMEM((width, width), F32),
             pltpu.VMEM((2, width, units), F32),
             pltpu.VMEM((2, width, units), F32),
         ],
-        compiler_params=VMEM,
+        compiler_params=LIMIT_B,
         cost_estimate=cost(36),
         name="feed_forward",
     )(side, lengths, flat(tokens), flat(cotangent), flat(attended), flat(linv), own, other, norms)
@@ -394,7 +399,6 @@
     sq = pl.squeezed
     rowspec = pl.BlockSpec((sq, rows, width), lambda s: (s, 0, 0))
     groupspec = pl.BlockSpec((sq, pairs, rows, 3 * PAIR), lambda s: (s, 0, 0, 0))
-    whole = lambda *dims: pl.BlockSpec(dims, lambda s: (0,) * len(dims))
     shape = jax.ShapeDtypeStruct
     packed = (width, 10 * HD)
     return pl.pallas_call(
@@ -407,10 +411,10 @@
             rowspec,
             rowspec,
         ],
-        out_specs=[groupspec, whole(*packed), whole(*packed)],
+        out_specs=[groupspec, IN_VMEM, IN_VMEM],
         out_shape=[shape(qkv.shape, BF16), shape(packed, BF16), shape(packed, BF16)],
         scratch_shapes=[pltpu.VMEM((pairs, width, 3 * PAIR), F32)],
-        compiler_params=VMEM,
+        compiler_params=LIMIT_C,
         cost_estimate=cost(27),
         name="attention_backward",
     )(n1t, qkv, probs, gatt, attended)
@@ -454,13 +458,13 @@
         ],
         out_specs=[full, whole(8, width)],
         out_shape=[shape((seqs, rows, width), F32), shape((8, width), F32)],
-        compiler_params=VMEM,
+        compiler_params=LIMIT_D,
         cost_estimate=cost(12),
         name="input_gradient",
     )(tokens, gp, gmid, wpairs, norms, gnorm_two)
 
 
-def pack_kernel(qkv_ref, out_ref, up_ref, down_ref, norm_ref, lead_ref, rest_ref):
+def pack_lead_kernel(qkv_ref, norm_ref, lead_ref):
     chips, rows, _ = lead_ref.shape
     part = norm_ref.shape[1]
     norm = norm_ref[...]
@@ -469,25 +473,37 @@
     extra = jnp.where(row == 0, high, jnp.where(row == 1, norm - high, 0.0))
     columns = [qkv_ref[c, :, :PAIR] for c in range(3)] + [qkv_ref[c, :, PAIR:] for c in range(3)]
     blank = jnp.zeros((rows, HD - part), F32)
-    lead_ref[...] = jnp.broadcast_to(
-        jnp.concatenate(columns + [extra, blank], axis=1).astype(BF16)[None], lead_ref.shape
-    )
-    blank = jnp.zeros((rows, HD), F32)
-    rest_ref[...] = jnp.broadcast_to(
-        jnp.concatenate([up_ref[...], down_ref[...], out_ref[...], blank], axis=1).astype(BF16)[None], rest_ref.shape
-    )
-
-
-def sum_kernel(lead_parts_ref, rest_parts_ref, terms_ref, lead_ref, rest_ref, message_ref):
-    total = jnp.zeros((lead_ref.shape[0], PAIR), F32)
-    for parts_ref, ref in ((lead_parts_ref, lead_ref), (rest_parts_ref, rest_ref)):
-        for start in range(0, ref.shape[1], PAIR):
-            cols = slice(start, start + PAIR)
-            piece = jnp.sum(parts_ref[:, :, cols].astype(F32), axis=0)
-            ref[:, cols] = piece
-            total = total + piece * piece
+    packed = jnp.concatenate(columns + [extra, blank], axis=1).astype(BF16)
+    lead_ref[...] = jnp.broadcast_to(packed[None], lead_ref.shape)
+
+
+def pack_rest_kernel(out_ref, up_ref, down_ref, rest_ref):
+    blank = jnp.zeros((out_ref.shape[0], HD), F32)
+    packed = jnp.concatenate([up_ref[...], down_ref[...], out_ref[...], blank], axis=1).astype(BF16)
+    rest_ref[...] = jnp.broadcast_to(packed[None], rest_ref.shape)
+
+
+def add_kernel(left_ref, right_ref, out_ref):
+    out_ref[...] = (left_ref[...].astype(F32) + right_ref[...].astype(F32)).astype(BF16)
+
+
+def sum_parts(parts_ref, out_ref):
+    total = jnp.zeros((out_ref.shape[0], PAIR), F32)
+    for start in range(0, out_ref.shape[1], PAIR):
+        cols = slice(start, start + PAIR)
+        piece = jnp.sum(parts_ref[:, :, cols].astype(F32), axis=0)
+        out_ref[:, cols] = piece
+        total = total + piece * piece
+    return jnp.sum(total, axis=0, keepdims=True)
+
+
+def sum_rest_kernel(parts_ref, out_ref, squares_ref):
+    squares_ref[...] = sum_parts(parts_ref, out_ref)
+
+
+def sum_lead_kernel(parts_ref, squares_ref, terms_ref, out_ref, message_ref):
     message_ref[...] = terms_ref[...]
-    message_ref[4:5, :PAIR] = jnp.sum(total, axis=0, keepdims=True)
+    message_ref[4:5, :PAIR] = sum_parts(parts_ref, out_ref) + squares_ref[...]
 
 
 def adamw(master, gradient, moments, rate, decay):
@@ -500,7 +516,7 @@
 
 
 def update_kernel(
-    message_ref, mine_ref, lead_ref, rest_ref,
+    index_ref, message_ref, lead_ref, rest_ref,
     qkv_ref, out_ref, up_ref, down_ref, norm_ref,
     qkv_m_ref, out_m_ref, up_m_ref, down_m_ref, norm_m_ref,
     gn_ref, qkv_n_ref, out_n_ref, up_n_ref, down_n_ref, norm_n_ref,
@@ -524,7 +540,11 @@
             qkv_n_ref[c, :, cols] = new
             qkv_s_ref[0, c, :, cols] = moment
             qkv_s_ref[1, c, :, cols] = second
-    norm_grads = factor * mine_ref[...]
+    part = norm_ref.shape[1]
+    per_row = terms.shape[1] // part
+    row = message_ref[pl.ds(index_ref[0] // per_row, 1), :]
+    mine = pltpu.roll(row, lax.rem(per_row - lax.rem(index_ref[0], per_row), per_row) * part, 1)[:, :part]
+    norm_grads = factor * mine
     grads_ref[...] = norm_grads
     plain = (
         (out_ref, rest_ref[:, 2 * units : 2 * units + 3 * HD], out_m_ref, out_n_ref, out_s_ref, 1),
@@ -540,10 +560,16 @@
     )
 
 
-def small_call(kernel, name, out_shape, *operands):
-    return pl.pallas_call(kernel, out_shape=out_shape, compiler_params=VMEM, cost_estimate=cost(3), name=name)(
-        *operands
-    )
+def small_call(kernel, name, out_shape, *operands, in_spec=IN_VMEM):
+    return pl.pallas_call(
+        kernel,
+        in_specs=[IN_SMEM if a.dtype == jnp.int32 else in_spec for a in operands],
+        out_specs=jax.tree.map(lambda a: IN_VMEM, out_shape),
+        out_shape=out_shape,
+        compiler_params=LIMIT_S,
+        cost_estimate=cost(2),
+        name=name,
+    )(*operands)
 
 
 def swap(values):
@@ -576,13 +602,19 @@
     qkv_rows = qkv_master.transpose(1, 0, 2)
     masters = (qkv_rows, out_master.T, up_master, down_master.T, norm_master[None])
     shape = jax.ShapeDtypeStruct
-    lead, rest = small_call(
-        pack_kernel,
-        "pack_weights",
-        [shape((chips, shard_rows, 10 * HD), BF16), shape((chips, shard_rows, 2 * units + 4 * HD), BF16)],
-        *masters,
+    lead = small_call(
+        pack_lead_kernel,
+        "pack_lead",
+        shape((chips, shard_rows, 10 * HD), BF16),
+        qkv_rows,
+        norm_master[None],
+        in_spec=pl.BlockSpec(),
+    )
+    rest = small_call(
+        pack_rest_kernel, "pack_rest", shape((chips, shard_rows, 2 * units + 4 * HD), BF16), masters[1], *masters[2:4]
     )
     lead_own = lax.all_to_all(lead, "batch", 0, 0)
+    lead_own, rest = lax.optimization_barrier((lead_own, rest))
     rest_own = lax.all_to_all(rest, "batch", 0, 0)
     lead_other = swap(lead_own)
     flat = lambda a: a.reshape(chips * shard_rows, a.shape[-1])
@@ -596,20 +628,24 @@
         place, lengths, tokens, cotangent, attended, linv, flat(rest_own), flat(rest_other), norms
     )
     per_seq = lambda a: a.reshape(seqs, slot_rows, width)
-    rest_sum = (grest_own.astype(F32) + swap(grest_other).astype(F32)).astype(BF16)
+    plus = lambda name, a, b: small_call(add_kernel, name, shape(a.shape, BF16), a, b)
+    rest_sum = plus("add_rest", grest_own, swap(grest_other))
     rest_sum, gatt = lax.optimization_barrier((rest_sum, gatt))
     rest_parts = lax.all_to_all(rest_sum.reshape(rest.shape), "batch", 0, 0)
     gp, glead_own, glead_other = backward(n1t, qkv, probs, per_seq(gatt), attended)
-    lead_sum = (glead_own.astype(F32) + swap(glead_other).astype(F32)).astype(BF16)
+    lead_sum = plus("add_lead", glead_own, swap(glead_other))
     lead_sum, rest_parts = lax.optimization_barrier((lead_sum, rest_parts))
     lead_parts = lax.all_to_all(lead_sum.reshape(chips, shard_rows, 10 * HD), "batch", 0, 0)
     input_grad, terms = input_gradient(tokens, gp, per_seq(gmid), wpairs, norms, gnorm_two)
-    lead_shard, rest_shard, message = small_call(
-        sum_kernel,
-        "sum_parts",
-        [shape(lead.shape[1:], F32), shape(rest.shape[1:], F32), shape(terms.shape, F32)],
+    rest_shard, squares = small_call(
+        sum_rest_kernel, "sum_rest", [shape(rest.shape[1:], F32), shape((1, PAIR), F32)], rest_parts
+    )
+    lead_shard, message = small_call(
+        sum_lead_kernel,
+        "sum_lead",
+        [shape(lead.shape[1:], F32), shape(terms.shape, F32)],
         lead_parts,
-        rest_parts,
+        squares,
         terms,
     )
     message = message + swap(message)
@@ -617,8 +653,6 @@
     while stride < chips:
         message = message + lax.ppermute(message, "batch", [(i, i ^ stride) for i in range(chips)])
         stride *= 2
-    start = (lax.axis_index("batch") * 2 + side) * norm_part
-    mine = lax.dynamic_slice_in_dim(message[:4].reshape(1, 4 * width), start, norm_part, axis=1)
     like = lambda a: shape(a.shape, F32)
     moments = (
         qkv_moments.transpose(0, 2, 1, 3),
@@ -630,9 +664,9 @@
     results = small_call(
         update_kernel,
         "update_weights",
-        [shape((1, 1), F32)] + [like(a) for a in masters + moments] + [like(mine)],
+        [shape((1, 1), F32)] + [like(a) for a in masters + moments] + [shape((1, norm_part), F32)],
+        (lax.axis_index("batch") * 2 + side).astype(jnp.int32).reshape(1),
         message,
-        mine,
         lead_shard,
         rest_shard,
         *masters,

time: 193 us -> 181 us (0.938)
  blocking collectives: 22.8 us -> 0 us
  waiting for transfers between devices: 32.2 us -> 45 us
  starting transfers between devices: 22.1 us -> 30.8 us
  other arithmetic: 5.45 us -> 0.02 us
  Pallas kernels: 105 us -> 101 us
    all_to_all x1 -> x0, blocking collectives: 22.8 us -> none  [per_device(): lead_own = lax.all_to_all(lead, 'batch', 0, 0)]
    all_to_all x0 -> x1, waiting for transfers between devices: none -> 13.3 us  [per_device(): lead_own = lax.all_to_all(lead, 'batch', 0, 0)]
    all_to_all x0 -> x1, starting transfers between devices: none -> 8.31 us  [per_device(): lead_own = lax.all_to_all(lead, 'batch', 0, 0)]
    convert_element_type x2 -> x0, other arithmetic: 4.72 us -> none  [the longest x1 2.78 us: per_device(): (grest_own.astype(F32) + swap(grest_other).astype(F32)).astype(BF16)]
    pallas_call x1, Pallas kernels: 35.9 us -> 33.9 us  [middle(): pl.pallas_call(functools.partial(middle_kernel, seq_rows, units), grid=(t...]
    pallas_call x3 -> x7, Pallas kernels: 7.07 us -> 5.79 us  [small_call(): pl.pallas_call(kernel, in_specs=[IN_SMEM if a.dtype == jnp.int32 else in_...]
  transfers between devices with their start and end apart: 12 -> 13, of which waited for: 10 -> 12; matrix products, arithmetic and copies ran while one was open for 1% -> 0% of each run, Pallas kernels for 32% -> 35%
where the time goes in v5:
time: 181 us
  Pallas kernels  101 us (56%)
  waiting for transfers between devices  45 us (25%)
  starting transfers between devices  30.8 us (17%)
  local copies, waits for them, and re-layouts  3.06 us (2%)
    pallas_call x1, Pallas kernels, middle(): pl.pallas_call(functools.partial(middle_kernel, seq_rows, units), grid=(t...  33.9 us
    pallas_call x1, Pallas kernels, backward(): pl.pallas_call(backward_kernel, grid=(seqs,), in_specs=[pl.BlockSpec((sq,...  27 us
    pallas_call x1, Pallas kernels, forward(): pl.pallas_call(functools.partial(forward_kernel, chips, part), grid=(seqs...  24.4 us
    all_to_all x1, waiting for transfers between devices, per_device(): lead_own = lax.all_to_all(lead, 'batch', 0, 0)  13.3 us
    ppermute x4, waiting for transfers between devices, per_device(): lax.ppermute(message, 'batch', [(i, i ^ stride) for i in range(chips)])  12.4 us
    pallas_call x1, Pallas kernels, input_gradient(): pl.pallas_call(input_kernel, grid=(seqs,), in_specs=[full, pl.BlockSpec((...  9.65 us
    ppermute x5, waiting for transfers between devices, swap(): return lax.ppermute(values, 'head', [(0, 1), (1, 0)])  9.15 us
    all_to_all x1, starting transfers between devices, per_device(): lead_own = lax.all_to_all(lead, 'batch', 0, 0)  8.31 us
  transfers between devices with their start and end apart: 13, of which 12 were waited for; matrix products, arithmetic and copies ran while one was open for 0% of the time, Pallas kernels for 35%

profile of v5, /device:TPU:0, one launch (start us, length us, event | category | flops | bytes accessed | tf_op | source)
XLA Modules:
  0.0 180.7 jit_solution(1883911668666234414)
XLA Ops:
  0.7 0.9 copy-done.3
  1.5 0.7 copy-done.11
  2.2 0.9 pack_lead.1
  3.1 8.3 %all-to-all-start = ((bf16[16,24,640]{2,1,0:T(8,128)(2,1)}), bf16[16,24,640]{2,1,0:T(8,128)(2,1)S(1)}, u32[]{:S(2)}, u32[]{:S(2)}) async-start(bf16[16,24,640]{2,1,0:T(8,128)(2,1)} %pack_lead.1), calls=%async_computation | async-start | bytes 983040 | tf_op jit(solution)/shard_map/all_to_all | solution.py:616
  11.4 1.2 pack_rest.1
  12.6 13.3 %all-to-all-done = bf16[16,24,640]{2,1,0:T(8,128)(2,1)S(1)} async-done(((bf16[16,24,640]{2,1,0:T(8,128)(2,1)}), bf16[16,24,640]{2,1,0:T(8,128)(2,1)S(1)}, u32[]{:S(2)}, u32[]{:S(2)}) %all-to-all-start) | async-done | bytes 491552 | tf_op jit(solution)/shard_map/all_to_all | solution.py:616
  25.9 3.8 %all-to-all-start.1 = ((bf16[16,24,1792]{2,1,0:T(8,128)(2,1)}), bf16[16,24,1792]{2,1,0:T(8,128)(2,1)S(1)}, u32[]{:S(2)}, u32[]{:S(2)}) async-start(bf16[16,24,1792]{2,1,0:T(8,128)(2,1)} %pack_rest.1), calls=%async_computation.1 | async-start | bytes 2752512 | tf_op jit(solution)/shard_map/all_to_all | solution.py:618
  29.8 0.8 copy-done.18
  30.5 24.4 %attention_forward.1 = (bf16[4,384,640]{2,1,0:T(8,128)(2,1)}, bf16[4,3,640,384]{3,2,1,0:T(8,128)(2,1)}, bf16[4,640,384]{2,1,0:T(8,128)(2,1)}, f32[4,640,384]{2,1...) custom-call(s32[1]{0:T(128)} %bitcast.side_ref, s32[8]{0:T(128)} %len_ref.3, ...), custom_call_target="tpu_custom_call" | custom-call | flops 24000000000 | bytes 1000000 | tf_op jit(solution)/shard_map/attention_forward/pallas_call | solution.py:176
  55.0 5.7 %all-to-all-done.1 = bf16[16,24,1792]{2,1,0:T(8,128)(2,1)S(1)} async-done(((bf16[16,24,1792]{2,1,0:T(8,128)(2,1)}), bf16[16,24,1792]{2,1,0:T(8,128)(2,1)S(1)}, u32[]{:S(2)}, u32[]{:S(2)}) %all-to-all-start.1) | async-done | bytes 1376288 | tf_op jit(solution)/shard_map/all_to_all | solution.py:618
  60.6 3.1 %collective-permute-done.1 = bf16[16,24,1792]{2,1,0:T(8,128)(2,1)S(1)} collective-permute-done((bf16[16,24,1792]{2,1,0:T(8,128)(2,1)S(1)}, bf16[16,24,1792]{2,1,0:T(8,128)(2,1)S(1)}, u32[]{:S(2)}, u32[]{:S(2)}) %collective-permute-start.1) | collective-permute-done | bytes 1376288 | tf_op jit(solution)/shard_map/ppermute | solution.py:576
  63.8 0.7 copy-done.15
  64.4 33.9 %feed_forward.1 = (bf16[2560,384]{1,0:T(8,128)(2,1)}, f32[2560,384]{1,0:T(8,128)}, bf16[2560,384]{1,0:T(8,128)(2,1)S(1)}, bf16[384,1792]{1,0:T(8,128)(2,1)S(1)},...) custom-call(s32[1]{0:T(128)} %bitcast.side_ref, s32[8]{0:T(128)S(1)} %copy-done.10, bf16[2560,384]{1,0:T(8,128)(2,1)} %bitcast.47, ...), custom_call_target="tpu_custom_call" | custom-call | flops 35999997952 | bytes 1000000 | tf_op jit(solution)/shard_map/feed_forward/pallas_call | solution.py:299
  98.5 3.0 %collective-permute-done.2.right_ref = bf16[384,1792]{1,0:T(8,128)(2,1)S(1)} collective-permute-done((bf16[384,1792]{1,0:T(8,128)(2,1)S(1)}, bf16[384,1792]{1,0:T(8,128)(2,1)S(1)}, u32[]{:S(2)}, u32[]{:S(2)}) %collective-permute-start.2) | collective-permute-done | bytes 1376288 | tf_op jit(solution)/shard_map/ppermute | solution.py:576
  101.5 1.4 add_rest.1
  102.9 7.8 %all-to-all-start.2 = ((bf16[16,24,1792]{2,1,0:T(8,128)(2,1)}), bf16[16,24,1792]{2,1,0:T(8,128)(2,1)S(1)}, u32[]{:S(2)}, u32[]{:S(2)}) async-start(bf16[16,24,1792]{2,1,0:T(8,128)(2,1)} %bitcast.17), calls=%async_computation.2 | async-start | bytes 2752512 | tf_op jit(solution)/shard_map/all_to_all | solution.py:634
  110.7 27.0 %attention_backward.1 = (bf16[4,3,640,384]{3,2,1,0:T(8,128)(2,1)}, bf16[384,640]{1,0:T(8,128)(2,1)S(1)}, bf16[384,640]{1,0:T(8,128)(2,1)S(1)}) custom-call(bf16[4,384,640]{2,1,0:T(8,128)(2,1)} %get-tuple-element.64.n1t_ref, bf16[4,3,640,384]{3,2,1,0:T(8,128)(2,1)} %get-tuple-element.65.qkv_ref, bf16[4,6,640,640]{3,2,1,0:T(8,128)(2,1)} %get-tuple-element.66.p_ref, ...), custom_call_target="tpu_custom_call" | custom-call | flops 27000000512 | bytes 1000000 | tf_op jit(solution)/shard_map/attention_backward/pallas_call | solution.py:404
  137.7 1.9 %collective-permute-done.3.right_ref = bf16[384,640]{1,0:T(8,128)(2,1)S(1)} collective-permute-done((bf16[384,640]{1,0:T(8,128)(2,1)S(1)}, bf16[384,640]{1,0:T(8,128)(2,1)S(1)}, u32[]{:S(2)}, u32[]{:S(2)}) %collective-permute-start.3) | collective-permute-done | bytes 491552 | tf_op jit(solution)/shard_map/ppermute | solution.py:576
  139.6 0.9 add_lead.1
  140.5 1.0 all-to-all-done.2.parts_ref
  141.5 7.3 %all-to-all-start.3 = ((bf16[16,24,640]{2,1,0:T(8,128)(2,1)}), bf16[16,24,640]{2,1,0:T(8,128)(2,1)S(1)}, u32[]{:S(2)}, u32[]{:S(2)}) async-start(bf16[16,24,640]{2,1,0:T(8,128)(2,1)} %bitcast.18), calls=%async_computation.3 | async-start | bytes 983040 | tf_op jit(solution)/shard_map/all_to_all | solution.py:638
  148.8 9.6 %input_gradient.1 = (f32[4,640,384]{2,1,0:T(8,128)}, f32[8,384]{1,0:T(8,128)S(1)}) custom-call(bf16[4,640,384]{2,1,0:T(8,128)(2,1)} %tok_ref.3, bf16[4,3,640,384]{3,2,1,0:T(8,128)(2,1)} %get-tuple-element.71.gp_ref, f32[4,640,384]{2,1,0:T(8,128)} %bitcast.49, bf16[3,384,384]{2,1,0:T(8,128)(2,1)S(1)} %copy-done.14, f32[4,384]{1,0:T(4,128)S(1)} %copy-done.16, ...), custom_call_target="tpu_custom_call" | custom-call | flops 12000000000 | bytes 1000000 | tf_op jit(solution)/shard_map/input_gradient/pallas_call | solution.py:448
  158.6 3.6 %all-to-all-done.3.parts_ref = bf16[16,24,640]{2,1,0:T(8,128)(2,1)S(1)} async-done(((bf16[16,24,640]{2,1,0:T(8,128)(2,1)}), bf16[16,24,640]{2,1,0:T(8,128)(2,1)S(1)}, u32[]{:S(2)}, u32[]{:S(2)}) %all-to-all-start.3) | async-done | bytes 491552 | tf_op jit(solution)/shard_map/all_to_all | solution.py:638
  162.5 1.2 collective-permute-done.4
  164.2 3.1 %collective-permute-done.5 = f32[8,384]{1,0:T(8,128)S(1)} collective-permute-done((f32[8,384]{1,0:T(8,128)S(1)}, f32[8,384]{1,0:T(8,128)S(1)}, u32[]{:S(2)}, u32[]{:S(2)}) %collective-permute-start.5) | collective-permute-done | bytes 12320 | tf_op jit(solution)/shard_map/ppermute | solution.py:654
  167.3 0.9 collective-permute-start.6
  168.2 2.8 %collective-permute-done.6 = f32[8,384]{1,0:T(8,128)S(1)} collective-permute-done((f32[8,384]{1,0:T(8,128)S(1)}, f32[8,384]{1,0:T(8,128)S(1)}, u32[]{:S(2)}, u32[]{:S(2)}) %collective-permute-start.6) | collective-permute-done | bytes 12320 | tf_op jit(solution)/shard_map/ppermute | solution.py:654
  171.0 1.2 collective-permute-start.7
  172.3 2.5 %collective-permute-done.7 = f32[8,384]{1,0:T(8,128)S(1)} collective-permute-done((f32[8,384]{1,0:T(8,128)S(1)}, f32[8,384]{1,0:T(8,128)S(1)}, u32[]{:S(2)}, u32[]{:S(2)}) %collective-permute-start.7) | collective-permute-done | bytes 12320 | tf_op jit(solution)/shard_map/ppermute | solution.py:654
  174.7 0.6 collective-permute-start.8
  175.4 3.9 %collective-permute-done.8 = f32[8,384]{1,0:T(8,128)S(1)} collective-permute-done((f32[8,384]{1,0:T(8,128)S(1)}, f32[8,384]{1,0:T(8,128)S(1)}, u32[]{:S(2)}, u32[]{:S(2)}) %collective-permute-start.8) | collective-permute-done | bytes 12320 | tf_op jit(solution)/shard_map/ppermute | solution.py:654
  179.4 1.2 update_weights.1
  (48 shorter events, 1.2 us)
Async XLA Ops:
  0.6 0.9 copy-start.3
  1.5 0.7 copy-start.11
  2.2 9.2 %copy-start.5 = (f32[24,768]{1,0:T(8,128)S(1)}, f32[24,768]{1,0:T(8,128)}, u32[]{:S(2)}) copy-start(f32[24,768]{1,0:T(8,128)} %up_ref.3) | copy-start | bytes 221188
  2.2 9.2 %copy-start.6 = (f32[768,24]{0,1:T(8,128)S(1)}, f32[768,24]{0,1:T(8,128)}, u32[]{:S(2)}) copy-start(f32[768,24]{0,1:T(8,128)} %param.21) | copy-start | bytes 221188
  2.2 9.2 %copy-start.8 = (f32[192,24]{0,1:T(8,128)S(1)}, f32[192,24]{0,1:T(8,128)}, u32[]{:S(2)}) copy-start(f32[192,24]{0,1:T(8,128)} %param.19) | copy-start | bytes 55300
  3.1 22.8 %all-to-all-start = ((bf16[16,24,640]{2,1,0:T(8,128)(2,1)}), bf16[16,24,640]{2,1,0:T(8,128)(2,1)S(1)}, u32[]{:S(2)}, u32[]{:S(2)}) async-start(bf16[16,24,640]{2,1,0:T(8,128)(2,1)} %pack_lead.1), calls=%async_computation | async-start | bytes 983040 | tf_op jit(solution)/shard_map/all_to_all | solution.py:616
  25.9 3.9 %copy-start.17 = (bf16[16,24,640]{2,1,0:T(8,128)(2,1)}, bf16[16,24,640]{2,1,0:T(8,128)(2,1)S(1)}, u32[]{:S(2)}) copy-start(bf16[16,24,640]{2,1,0:T(8,128)(2,1)S(1)} %all-to-all-done) | copy-start | bytes 1474564
  25.9 3.8 %collective-permute-start = (bf16[16,24,640]{2,1,0:T(8,128)(2,1)S(1)}, bf16[16,24,640]{2,1,0:T(8,128)(2,1)S(1)}, u32[]{:S(2)}, u32[]{:S(2)}) collective-permute-start(bf16[16,24,640]{2,1,0:T(8,128)(2,1)S(1)} %all-to-all-done), channel_id=1, source_target_pairs={{0,1},{1,0},{2,3},{3,2},{4,5},{5,4},{6,7},{7,6},{8,9},{9,8},{10,11... | collective-permute-start | bytes 1474568 | tf_op jit(solution)/shard_map/ppermute | solution.py:576
  25.9 34.7 %all-to-all-start.1 = ((bf16[16,24,1792]{2,1,0:T(8,128)(2,1)}), bf16[16,24,1792]{2,1,0:T(8,128)(2,1)S(1)}, u32[]{:S(2)}, u32[]{:S(2)}) async-start(bf16[16,24,1792]{2,1,0:T(8,128)(2,1)} %pack_rest.1), calls=%async_computation.1 | async-start | bytes 2752512 | tf_op jit(solution)/shard_map/all_to_all | solution.py:618
  29.7 0.8 copy-start.18
  30.5 33.2 %copy-start.10 = (s32[8]{0:T(128)S(1)}, s32[8]{0:T(128)}, u32[]{:S(2)}) copy-start(s32[8]{0:T(128)} %len_ref.3) | copy-start | bytes 100
  60.6 3.1 %collective-permute-start.1 = (bf16[16,24,1792]{2,1,0:T(8,128)(2,1)S(1)}, bf16[16,24,1792]{2,1,0:T(8,128)(2,1)S(1)}, u32[]{:S(2)}, u32[]{:S(2)}) collective-permute-start(bf16[16,24,1792]{2,1,0:T(8,128)(2,1)S(1)} %all-to-all-done.1), channel_id=1, source_target_pairs={{0,1},{1,0},{2,3},{3,2},{4,5},{5,4},{6,7},{7,6},{8,9},{9,8},{10,11... | collective-permute-start | bytes 4128776 | tf_op jit(solution)/shard_map/ppermute | solution.py:576
  63.8 0.7 copy-start.15
  98.3 4.6 %copy-start.13 = (bf16[2560,384]{1,0:T(8,128)(2,1)}, bf16[2560,384]{1,0:T(8,128)(2,1)S(1)}, u32[]{:S(2)}) copy-start(bf16[2560,384]{1,0:T(8,128)(2,1)S(1)} %get-tuple-element.70) | copy-start | bytes 5898244
  98.3 3.2 %collective-permute-start.2 = (bf16[384,1792]{1,0:T(8,128)(2,1)S(1)}, bf16[384,1792]{1,0:T(8,128)(2,1)S(1)}, u32[]{:S(2)}, u32[]{:S(2)}) collective-permute-start(bf16[384,1792]{1,0:T(8,128)(2,1)S(1)} %get-tuple-element.68), channel_id=1, source_target_pairs={{0,1},{1,0},{2,3},{3,2},{4,5},{5,4},{6,7},{7,6},{8,9},{9,8},{10,11... | collective-permute-start | bytes 4128776 | tf_op jit(solution)/shard_map/ppermute | solution.py:576
  102.9 38.6 %all-to-all-start.2 = ((bf16[16,24,1792]{2,1,0:T(8,128)(2,1)}), bf16[16,24,1792]{2,1,0:T(8,128)(2,1)S(1)}, u32[]{:S(2)}, u32[]{:S(2)}) async-start(bf16[16,24,1792]{2,1,0:T(8,128)(2,1)} %bitcast.17), calls=%async_computation.2 | async-start | bytes 2752512 | tf_op jit(solution)/shard_map/all_to_all | solution.py:634
  137.7 1.9 %collective-permute-start.3 = (bf16[384,640]{1,0:T(8,128)(2,1)S(1)}, bf16[384,640]{1,0:T(8,128)(2,1)S(1)}, u32[]{:S(2)}, u32[]{:S(2)}) collective-permute-start(bf16[384,640]{1,0:T(8,128)(2,1)S(1)} %get-tuple-element.77), channel_id=1, source_target_pairs={{0,1},{1,0},{2,3},{3,2},{4,5},{5,4},{6,7},{7,6},{8,9},{9,8},{10,11... | collective-permute-start | bytes 1474568 | tf_op jit(solution)/shard_map/ppermute | solution.py:576
  139.6 9.2 %copy-start.14 = (bf16[3,384,384]{2,1,0:T(8,128)(2,1)S(1)}, bf16[3,384,384]{2,1,0:T(8,128)(2,1)}, u32[]{:S(2)}) copy-start(bf16[3,384,384]{2,1,0:T(8,128)(2,1)} %get-tuple-element.73.w_ref) | copy-start | bytes 2654212
  139.6 9.2 %copy-start.16 = (f32[4,384]{1,0:T(4,128)S(1)}, f32[4,384]{1,0:T(4,128)}, u32[]{:S(2)}) copy-start(f32[4,384]{1,0:T(4,128)} %get-tuple-element.62.norms_ref) | copy-start | bytes 18436
  141.5 20.8 %all-to-all-start.3 = ((bf16[16,24,640]{2,1,0:T(8,128)(2,1)}), bf16[16,24,640]{2,1,0:T(8,128)(2,1)S(1)}, u32[]{:S(2)}, u32[]{:S(2)}) async-start(bf16[16,24,640]{2,1,0:T(8,128)(2,1)} %bitcast.18), calls=%async_computation.3 | async-start | bytes 983040 | tf_op jit(solution)/shard_map/all_to_all | solution.py:638
  162.3 17.1 %copy-start = (f32[2,24,3,192]{3,1,2,0:T(8,128)S(1)}, f32[2,24,3,192]{3,1,2,0:T(8,128)}, u32[]{:S(2)}) copy-start(f32[2,24,3,192]{3,1,2,0:T(8,128)} %param.23) | copy-start | bytes 331780
  162.3 17.1 %copy-start.1 = (f32[2,24,768]{2,1,0:T(8,128)S(1)}, f32[2,24,768]{2,1,0:T(8,128)}, u32[]{:S(2)}) copy-start(f32[2,24,768]{2,1,0:T(8,128)} %up_m_ref.1) | copy-start | bytes 442372
  162.3 17.1 %copy-start.2 = (f32[2,768,24]{1,2,0:T(8,128)S(1)}, f32[2,768,24]{1,2,0:T(8,128)}, u32[]{:S(2)}) copy-start(f32[2,768,24]{1,2,0:T(8,128)} %param.26) | copy-start | bytes 442372
  162.3 17.1 %copy-start.4 = (f32[24,3,192]{2,0,1:T(8,128)S(1)}, f32[24,3,192]{2,0,1:T(8,128)}, u32[]{:S(2)}) copy-start(f32[24,3,192]{2,0,1:T(8,128)} %param.18) | copy-start | bytes 165892
  162.3 17.1 %copy-start.7 = (f32[2,192,24]{1,2,0:T(8,128)S(1)}, f32[2,192,24]{1,2,0:T(8,128)}, u32[]{:S(2)}) copy-start(f32[2,192,24]{1,2,0:T(8,128)} %param.24) | copy-start | bytes 110596
  162.3 17.1 %copy-start.9 = (f32[2,48]{1,0:T(2,128)S(1)}, f32[2,48]{1,0:T(2,128)}, u32[]{:S(2)}) copy-start(f32[2,48]{1,0:T(2,128)} %norm_m_ref.1) | copy-start | bytes 1156
  162.3 17.1 %copy-start.12 = (f32[48]{0:T(128)S(1)}, f32[48]{0:T(128)}, u32[]{:S(2)}) copy-start(f32[48]{0:T(128)} %param.22) | copy-start | bytes 580
  162.4 1.2 collective-permute-start.4
  163.6 3.7 %collective-permute-start.5 = (f32[8,384]{1,0:T(8,128)S(1)}, f32[8,384]{1,0:T(8,128)S(1)}, u32[]{:S(2)}, u32[]{:S(2)}) collective-permute-start(f32[8,384]{1,0:T(8,128)S(1)} %add.19), channel_id=1, source_target_pairs={{0,2},{2,0},{4,6},{6,4},{8,10},{10,8},{12,14},{14,12},{16,18},{18,... | collective-permute-start | bytes 36872 | tf_op jit(solution)/shard_map/ppermute | solution.py:654
  167.3 3.7 %collective-permute-start.6 = (f32[8,384]{1,0:T(8,128)S(1)}, f32[8,384]{1,0:T(8,128)S(1)}, u32[]{:S(2)}, u32[]{:S(2)}) collective-permute-start(f32[8,384]{1,0:T(8,128)S(1)} %add.20), channel_id=1, source_target_pairs={{0,4},{2,6},{4,0},{6,2},{8,12},{10,14},{12,8},{14,10},{16,20},{18,... | collective-permute-start | bytes 36872 | tf_op jit(solution)/shard_map/ppermute | solution.py:654
  171.0 3.7 %collective-permute-start.7 = (f32[8,384]{1,0:T(8,128)S(1)}, f32[8,384]{1,0:T(8,128)S(1)}, u32[]{:S(2)}, u32[]{:S(2)}) collective-permute-start(f32[8,384]{1,0:T(8,128)S(1)} %add.21), channel_id=1, source_target_pairs={{0,8},{2,10},{4,12},{6,14},{8,0},{10,2},{12,4},{14,6},{16,24},{18,... | collective-permute-start | bytes 36872 | tf_op jit(solution)/shard_map/ppermute | solution.py:654
  174.7 4.6 %collective-permute-start.8 = (f32[8,384]{1,0:T(8,128)S(1)}, f32[8,384]{1,0:T(8,128)S(1)}, u32[]{:S(2)}, u32[]{:S(2)}) collective-permute-start(f32[8,384]{1,0:T(8,128)S(1)} %add.22), channel_id=1, source_target_pairs={{0,16},{2,18},{4,20},{6,22},{8,24},{10,26},{12,28},{14,30},{16,0},... | collective-permute-start | bytes 36872 | tf_op jit(solution)/shard_map/ppermute | solution.py:654

commit v6 on v5

--- a/solution.py
+++ b/solution.py
@@ -26,8 +26,8 @@
 FB = 512
 FC = 256
 PAIR = 2 * HD
-LIMIT_A, LIMIT_B, LIMIT_C, LIMIT_D, LIMIT_S = (
-    pltpu.CompilerParams(vmem_limit_bytes=m * 2**20) for m in (56, 46, 52, 52, 16)
+LIMIT_A, LIMIT_B, LIMIT_C, LIMIT_D, LIMIT_S, LIMIT_P = (
+    pltpu.CompilerParams(vmem_limit_bytes=m * 2**20) for m in (52, 46, 52, 52, 16, 62)
 )
 IN_VMEM = pl.BlockSpec(memory_space=pltpu.VMEM)
 IN_SMEM = pl.BlockSpec(memory_space=pltpu.SMEM)
@@ -88,11 +88,51 @@
     return [jnp.concatenate(pieces[i * per_row : (i + 1) * per_row], axis=1) for i in range(4)]
 
 
+def prepare_kernel(seq_rows, side_ref, len_ref, tok_ref, cot_ref, normal_ref, masked_ref, masked_t_ref):
+    step = pl.program_id(0)
+    rows = tok_ref.shape[0]
+    first = step * rows
+    row = first + lax.broadcasted_iota(jnp.int32, (rows, 1), 0)
+    live = row < 0
+    seqs = rows * pl.num_programs(0) // seq_rows
+    for near in range(-(-rows // seq_rows) + 1):
+        s = first // seq_rows + near
+        bound = jnp.where(s < seqs, len_ref[side_ref[0] * seqs + jnp.minimum(s, seqs - 1)], 0)
+        live = live | ((row >= s * seq_rows) & (row < s * seq_rows + bound))
+
+    normal_ref[...], _ = normalize(tok_ref[...].astype(F32))
+    masked = jnp.where(live, cot_ref[...].astype(F32), 0.0).astype(BF16)
+    masked_ref[...] = masked
+    masked_t_ref[...] = masked.T
+
+
+def prepare(side, lengths, tokens, cotangent):
+    seqs, seq_rows, width = tokens.shape
+    total = seqs * seq_rows
+    flat = lambda a: a.reshape(total, width)
+    rowspec = pl.BlockSpec((FB, width), lambda s: (s, 0))
+    shape = jax.ShapeDtypeStruct
+    return pl.pallas_call(
+        functools.partial(prepare_kernel, seq_rows),
+        grid=(total // FB,),
+        in_specs=[IN_SMEM, IN_SMEM, rowspec, rowspec],
+        out_specs=[rowspec, rowspec, pl.BlockSpec((width, FB), lambda s: (0, s))],
+        out_shape=[shape((total, width), F32), shape((total, width), BF16), shape((width, total), BF16)],
+        compiler_params=LIMIT_P,
+        cost_estimate=cost(5),
+        name="prepare",
+    )(side, lengths, flat(tokens), flat(cotangent))
+
+
+def key_limits(rows):
+    return [*range(256, rows, 256), rows]
+
+
 def forward_kernel(
-    chips, part, side_ref, len_ref, tok_ref, mask_ref, own_ref, other_ref,
+    chips, part, side_ref, len_ref, normal_ref, mask_ref, own_ref, other_ref,
     n1t_ref, qkv_ref, att_ref, linv_ref, p_ref, w_ref, norms_ref,
 ):
-    rows, width = tok_ref.shape
+    rows, width = normal_ref.shape
     pairs = width // PAIR
     side, seq = side_ref[0], pl.program_id(0)
 
@@ -116,12 +156,25 @@
     hidden = jnp.where(visible, 0.0, -1e30)
     hidden = jnp.broadcast_to(hidden, (PAIR, rows)).T.astype(BF16)
 
-    normal, _ = normalize(tok_ref[...].astype(F32))
-    n1 = (normal * norms_ref[0:1, :] + norms_ref[1:2, :]).astype(BF16)
+    low = 0
+    for keys in key_limits(rows):
+        pl.when((len_ref[member] > low) & (len_ref[member] <= keys))(
+            functools.partial(
+                attend, keys, hidden, normal_ref, norms_ref, w_ref, n1t_ref, qkv_ref, att_ref, linv_ref, p_ref
+            )
+        )
+        low = keys
+
+
+def attend(count, hidden, normal_ref, norms_ref, w_ref, n1t_ref, qkv_ref, att_ref, linv_ref, p_ref):
+    rows, width = normal_ref.shape
+    pairs = width // PAIR
+    n1 = (normal_ref[...] * norms_ref[0:1, :] + norms_ref[1:2, :]).astype(BF16)
     n1t_ref[...] = n1.T
     lane = lax.broadcasted_iota(jnp.int32, (QB, PAIR), 1)
-    key_lane = lax.broadcasted_iota(jnp.int32, (rows, PAIR), 1)
-    ones = jnp.ones((rows, PAIR), BF16)
+    key_lane = lax.broadcasted_iota(jnp.int32, (count, PAIR), 1)
+    ones = jnp.ones((count, PAIR), BF16)
+    hidden = hidden[:count]
     ready = {}
 
     def project(pair):
@@ -130,8 +183,8 @@
         others = out[:, PAIR:].astype(BF16)
         qkv_ref[pair, :, :PAIR] = queries
         qkv_ref[pair, :, PAIR:] = others
-        keys = [jnp.where(key_lane == HD * (1 - half), hidden, others[:, :PAIR]) for half in range(2)]
-        return queries, keys, jnp.concatenate([others[:, PAIR:], ones], axis=1)
+        keys = [jnp.where(key_lane == HD * (1 - half), hidden, others[:count, :PAIR]) for half in range(2)]
+        return queries, keys, jnp.concatenate([others[:count, PAIR:], ones], axis=1)
 
     def scores(pair, block, half):
         if pair not in ready:
@@ -146,7 +199,7 @@
     def finish(pair, block, half, s):
         sl = slice(block * QB, (block + 1) * QB)
         p = jnp.exp(s - jnp.max(s, axis=-1, keepdims=True)).astype(BF16)
-        p_ref[pair * 2 + half, sl, :] = p
+        p_ref[pair * 2 + half, sl, :count] = p
         out = mm(p, ready[pair][2])
         inverse = 1.0 / out[:, PAIR:]
         outs[half] = (out[:, :PAIR] * inverse, inverse)
@@ -166,8 +219,8 @@
     finish(*pending)
 
 
-def forward(chips, part, side, lengths, tokens, key_masks, own, other):
-    seqs, rows, width = tokens.shape
+def forward(chips, part, side, lengths, normal, key_masks, own, other):
+    seqs, rows, width = normal.shape
     heads, pairs = width // HD, width // PAIR
     sq = pl.squeezed
     shape = jax.ShapeDtypeStruct
@@ -184,7 +237,7 @@
             row_spec,
             pl.BlockSpec((sq, heads, rows, rows), lambda s: (s, 0, 0, 0)),
             whole(pairs, width, 3 * PAIR),
-            whole(4, width),
+            IN_VMEM,
         ],
         out_shape=[
             shape((seqs, width, rows), BF16),
@@ -198,11 +251,11 @@
         compiler_params=LIMIT_A,
         cost_estimate=cost(24),
         name="attention_forward",
-    )(side, lengths, tokens, key_masks, own, other)
+    )(side, lengths, normal, key_masks, own, other)
 
 
 def middle_kernel(
-    seq_rows, units, side_ref, len_ref, tok_ref, cot_ref, att_ref, linv_ref, own_ref, other_ref, norms_ref,
+    units, tok_ref, gb_ref, gbt_ref, att_ref, linv_ref, own_ref, other_ref, norms_ref,
     out_ref, gmid_ref, gatt_ref, gown_ref, gother_ref, gnorm_ref,
     halves, wo_ref, gout_ref, gup_ref, gdown_ref,
 ):
@@ -215,21 +268,14 @@
         gup_ref[...] = jnp.zeros_like(gup_ref)
         gdown_ref[...] = jnp.zeros_like(gdown_ref)
         gnorm_ref[...] = jnp.zeros_like(gnorm_ref)
+        members, sides, part, _ = own_ref.shape
         for half, ref in enumerate((own_ref, other_ref)):
-            halves[half] = ref[...]
+            for place in range(members * sides):
+                halves[half, place * part : (place + 1) * part, :] = ref[place % members, place // members]
         cols = slice(2 * units, 2 * units + 3 * HD)
         parts = split_pairs(halves[0, :, cols], halves[1, :, cols], HD)
         for i, part in enumerate(parts):
             wo_ref[:, i * PAIR : (i + 1) * PAIR] = part
-
-    first = step * rows
-    row = first + lax.broadcasted_iota(jnp.int32, (rows, 1), 0)
-    live = row < 0
-    seqs = rows * pl.num_programs(0) // seq_rows
-    for near in range(-(-rows // seq_rows) + 1):
-        s = first // seq_rows + near
-        bound = jnp.where(s < seqs, len_ref[side_ref[0] * seqs + jnp.minimum(s, seqs - 1)], 0)
-        live = live | ((row >= s * seq_rows) & (row < s * seq_rows + bound))
 
     x = tok_ref[...].astype(F32)
     att = att_ref[...]
@@ -238,9 +284,7 @@
     gain, shift = norms_ref[2:3, :], norms_ref[3:4, :]
     n2 = (normal * gain + shift).astype(BF16)
     n2t = n2.T
-    up = jnp.where(live, cot_ref[...].astype(F32), 0.0)
-    gb = up.astype(BF16)
-    gbt = gb.T
+    gb, gbt = gb_ref[...], gbt_ref[...]
     sums = [mid, jnp.zeros_like(mid)]
 
     def begin(half, c):
@@ -268,7 +312,7 @@
     out_ref[...] = bo.astype(BF16)
     gnorm_ref[0:8, :] += jnp.sum((gtwo * normal).reshape(rows // 8, 8, width), axis=0)
     gnorm_ref[8:16, :] += jnp.sum(gtwo.reshape(rows // 8, 8, width), axis=0)
-    gmid = up + norm_backward(normal, rs, gtwo * gain)
+    gmid = gb.astype(F32) + norm_backward(normal, rs, gtwo * gain)
     gmid_ref[...] = gmid
     gm = gmid.astype(BF16)
     gout_ref[...] += mm(gm, att, TN)
@@ -287,7 +331,7 @@
             ref[:, 2 * units :] = jnp.concatenate(sides[half] + [blank], axis=1).astype(BF16)
 
 
-def middle(side, lengths, tokens, cotangent, attended, linv, own, other, norms):
+def middle(tokens, masked, masked_t, attended, linv, own, other, norms):
     seqs, seq_rows, width = tokens.shape
     total = seqs * seq_rows
     packed = own.shape[-1]
@@ -297,18 +341,17 @@
     whole = lambda *dims: pl.BlockSpec(dims, lambda s: (0,) * len(dims))
     shape = jax.ShapeDtypeStruct
     return pl.pallas_call(
-        functools.partial(middle_kernel, seq_rows, units),
+        functools.partial(middle_kernel, units),
         grid=(total // FB,),
         in_specs=[
-            IN_SMEM,
-            IN_SMEM,
             rowspec,
             rowspec,
+            pl.BlockSpec((width, FB), lambda s: (0, s)),
             rowspec,
             rowspec,
             IN_VMEM,
             IN_VMEM,
-            whole(4, width),
+            IN_VMEM,
         ],
         out_specs=[rowspec] * 3 + [IN_VMEM, IN_VMEM, whole(16, width)],
         out_shape=[
@@ -329,52 +372,75 @@
         compiler_params=LIMIT_B,
         cost_estimate=cost(36),
         name="feed_forward",
-    )(side, lengths, flat(tokens), flat(cotangent), flat(attended), flat(linv), own, other, norms)
-
-
-def backward_kernel(n1t_ref, qkv_ref, p_ref, gatt_ref, att_ref, gp_ref, gown_ref, gother_ref, gqkv_ref):
+    )(flat(tokens), masked, masked_t, flat(attended), flat(linv), own, other, norms)
+
+
+def backward_kernel(
+    side_ref, len_ref, n1t_ref, qkv_ref, p_ref, gatt_ref, att_ref, gp_ref, gown_ref, gother_ref, gqkv_ref
+):
     seq = pl.program_id(0)
-    pairs, rows = qkv_ref.shape[:2]
+    rows = qkv_ref.shape[1]
 
     @pl.when(seq == 0)
     def _():
         gqkv_ref[...] = jnp.zeros_like(gqkv_ref)
 
-    lane = lax.broadcasted_iota(jnp.int32, (rows, PAIR), 1)
-    zero = jnp.zeros((rows, PAIR), BF16)
+    length = len_ref[side_ref[0] * pl.num_programs(0) + seq]
+    low = 0
+    for count in key_limits(rows):
+        pl.when((length > low) & (length <= count))(
+            functools.partial(attend_backward, count, n1t_ref, qkv_ref, p_ref, gatt_ref, att_ref, gp_ref, gqkv_ref)
+        )
+        low = count
+
+    @pl.when(seq == pl.num_programs(0) - 1)
+    def _():
+        sides = join_pairs(gqkv_ref[0], gqkv_ref[1], gqkv_ref[2], 3 * HD)
+        blank = jnp.zeros((gqkv_ref.shape[1], HD), F32)
+        for columns, ref in zip(sides, (gown_ref, gother_ref)):
+            ref[...] = jnp.concatenate(columns + [blank], axis=1).astype(BF16)
+
+
+def attend_backward(count, n1t_ref, qkv_ref, p_ref, gatt_ref, att_ref, gp_ref, gqkv_ref):
+    pairs, rows = qkv_ref.shape[:2]
+    lane = lax.broadcasted_iota(jnp.int32, (count, PAIR), 1)
+    zero = jnp.zeros((count, PAIR), BF16)
     state = {}
 
     def begin(pair, half):
         if half == 0:
             cols = slice(pair * PAIR, (pair + 1) * PAIR)
-            ga = gatt_ref[:, cols]
+            ga = gatt_ref[:count, cols]
             state[pair] = dict(
                 ga=ga,
-                inner=ga.astype(F32) * att_ref[:, cols].astype(F32),
+                inner=ga.astype(F32) * att_ref[:count, cols].astype(F32),
                 gat=ga.T,
-                qt=qkv_ref[pair, :, :PAIR].T,
+                qt=qkv_ref[pair, :count, :PAIR].T,
                 gq=[],
                 gkt=[],
                 gvt=[],
             )
         mask = (lane < HD) == (half == 0)
-        return pair, half, mask, mm(jnp.where(mask, state[pair]["ga"], zero), qkv_ref[pair, :, 2 * PAIR :], NT)
+        values = qkv_ref[pair, :count, 2 * PAIR :]
+        return pair, half, mask, mm(jnp.where(mask, state[pair]["ga"], zero), values, NT)
 
     def finish(pair, half, mask, dp):
         mine = state[pair]
         hs = slice(half * HD, half * HD + HD)
-        p = p_ref[pair * 2 + half]
+        p = p_ref[pair * 2 + half, :count, :count]
         mine["gvt"].append(mm(mine["gat"][hs], p))
         inner = jnp.sum(jnp.where(mask, mine["inner"], 0.0), axis=-1, keepdims=True)
         ds = (p.astype(F32) * (dp - inner)).astype(BF16)
-        mine["gq"].append(mm(ds, qkv_ref[pair, :, PAIR : 2 * PAIR]))
+        mine["gq"].append(mm(ds, qkv_ref[pair, :count, PAIR : 2 * PAIR]))
         mine["gkt"].append(mm(mine["qt"][hs], ds))
         if half == 1:
             joined = jnp.where(lane < HD, mine["gq"][0], mine["gq"][1])
-            gp_ref[pair, :, :PAIR] = (joined * (HD**-0.5)).astype(BF16)
-            gp_ref[pair, :, PAIR : 2 * PAIR] = jnp.concatenate(mine["gkt"], axis=0).astype(BF16).T
-            gp_ref[pair, :, 2 * PAIR :] = jnp.concatenate(mine["gvt"], axis=0).astype(BF16).T
-            gqkv_ref[pair] += mm(n1t_ref[...], gp_ref[pair])
+            gp_ref[pair, :count, :PAIR] = (joined * (HD**-0.5)).astype(BF16)
+            gp_ref[pair, :count, PAIR : 2 * PAIR] = jnp.concatenate(mine["gkt"], axis=0).astype(BF16).T
+            gp_ref[pair, :count, 2 * PAIR :] = jnp.concatenate(mine["gvt"], axis=0).astype(BF16).T
+            if count < rows:
+                gp_ref[pair, count:, :] = jnp.zeros((rows - count, 3 * PAIR), BF16)
+            gqkv_ref[pair] += mm(n1t_ref[:, :count], gp_ref[pair, :count, :])
 
     pending = None
     for pair in range(pairs):
@@ -385,15 +451,8 @@
             pending = fresh
     finish(*pending)
 
-    @pl.when(seq == pl.num_programs(0) - 1)
-    def _():
-        sides = join_pairs(gqkv_ref[0], gqkv_ref[1], gqkv_ref[2], 3 * HD)
-        blank = jnp.zeros((gqkv_ref.shape[1], HD), F32)
-        for columns, ref in zip(sides, (gown_ref, gother_ref)):
-            ref[...] = jnp.concatenate(columns + [blank], axis=1).astype(BF16)
-
-
-def backward(n1t, qkv, probs, gatt, attended):
+
+def backward(side, lengths, n1t, qkv, probs, gatt, attended):
     seqs, rows, width = attended.shape
     pairs = width // PAIR
     sq = pl.squeezed
@@ -405,6 +464,8 @@
         backward_kernel,
         grid=(seqs,),
         in_specs=[
+            IN_SMEM,
+            IN_SMEM,
             pl.BlockSpec((sq, width, rows), lambda s: (s, 0, 0)),
             groupspec,
             pl.BlockSpec((sq, 2 * pairs, rows, rows), lambda s: (s, 0, 0, 0)),
@@ -417,7 +478,7 @@
         compiler_params=LIMIT_C,
         cost_estimate=cost(27),
         name="attention_backward",
-    )(n1t, qkv, probs, gatt, attended)
+    )(side, lengths, n1t, qkv, probs, gatt, attended)
 
 
 def input_kernel(tok_ref, gp_ref, gmid_ref, w_ref, norms_ref, two_ref, gin_ref, terms_ref):
@@ -453,10 +514,10 @@
             pl.BlockSpec((sq, pairs, rows, 3 * PAIR), lambda s: (s, 0, 0, 0)),
             full,
             whole(pairs, width, 3 * PAIR),
-            whole(4, width),
+            IN_VMEM,
             whole(16, width),
         ],
-        out_specs=[full, whole(8, width)],
+        out_specs=[full, IN_VMEM],
         out_shape=[shape((seqs, rows, width), F32), shape((8, width), F32)],
         compiler_params=LIMIT_D,
         cost_estimate=cost(12),
@@ -479,12 +540,28 @@
 
 def pack_rest_kernel(out_ref, up_ref, down_ref, rest_ref):
     blank = jnp.zeros((out_ref.shape[0], HD), F32)
-    packed = jnp.concatenate([up_ref[...], down_ref[...], out_ref[...], blank], axis=1).astype(BF16)
-    rest_ref[...] = jnp.broadcast_to(packed[None], rest_ref.shape)
+    rest_ref[...] = jnp.concatenate([up_ref[...], down_ref[...], out_ref[...], blank], axis=1).astype(BF16)
+
+
+def pair_kernel(half_ref, own_ref, far_ref, out_ref):
+    own, far = own_ref[...], far_ref[...]
+    first = half_ref[0] == 0
+    for slot, value in enumerate((jnp.where(first, own, far), jnp.where(first, far, own))):
+        for member in range(out_ref.shape[0]):
+            out_ref[member, slot] = value
 
 
 def add_kernel(left_ref, right_ref, out_ref):
     out_ref[...] = (left_ref[...].astype(F32) + right_ref[...].astype(F32)).astype(BF16)
+
+
+def add_split_kernel(left_ref, right_ref, out_ref):
+    total = (left_ref[...].astype(F32) + right_ref[...].astype(F32)).astype(BF16)
+    members, halves, rows, _ = out_ref.shape
+    for half in range(halves):
+        for member in range(members):
+            start = (half * members + member) * rows
+            out_ref[member, half] = total[start : start + rows]
 
 
 def sum_parts(parts_ref, out_ref):
@@ -497,13 +574,26 @@
     return jnp.sum(total, axis=0, keepdims=True)
 
 
-def sum_rest_kernel(parts_ref, out_ref, squares_ref):
-    squares_ref[...] = sum_parts(parts_ref, out_ref)
-
-
-def sum_lead_kernel(parts_ref, squares_ref, terms_ref, out_ref, message_ref):
+def sum_rest_kernel(half_ref, parts_ref, mine_ref, theirs_ref):
+    first = half_ref[0] == 0
+    for start in range(0, mine_ref.shape[1], PAIR):
+        cols = slice(start, start + PAIR)
+        low = jnp.sum(parts_ref[:, 0, :, cols].astype(F32), axis=0)
+        high = jnp.sum(parts_ref[:, 1, :, cols].astype(F32), axis=0)
+        mine_ref[:, cols] = jnp.where(first, low, high)
+        theirs_ref[:, cols] = jnp.where(first, high, low).astype(BF16)
+
+
+def sum_lead_kernel(parts_ref, mine_ref, far_ref, terms_ref, out_ref, rest_ref, message_ref):
+    squares = sum_parts(parts_ref, out_ref)
+    rest = mine_ref[...] + far_ref[...].astype(F32)
+    rest_ref[...] = rest
+    total = jnp.zeros((rest.shape[0], PAIR), F32)
+    for start in range(0, rest.shape[1], PAIR):
+        piece = rest[:, start : start + PAIR]
+        total = total + piece * piece
     message_ref[...] = terms_ref[...]
-    message_ref[4:5, :PAIR] = sum_parts(parts_ref, out_ref) + squares_ref[...]
+    message_ref[4:5, :PAIR] = squares + jnp.sum(total, axis=0, keepdims=True)
 
 
 def adamw(master, gradient, moments, rate, decay):
@@ -560,13 +650,13 @@
     )
 
 
-def small_call(kernel, name, out_shape, *operands, in_spec=IN_VMEM):
+def small_call(kernel, name, out_shape, *operands, in_spec=IN_VMEM, limit=LIMIT_S):
     return pl.pallas_call(
         kernel,
         in_specs=[IN_SMEM if a.dtype == jnp.int32 else in_spec for a in operands],
         out_specs=jax.tree.map(lambda a: IN_VMEM, out_shape),
         out_shape=out_shape,
-        compiler_params=LIMIT_S,
+        compiler_params=limit,
         cost_estimate=cost(2),
         name=name,
     )(*operands)
@@ -609,43 +699,54 @@
         qkv_rows,
         norm_master[None],
         in_spec=pl.BlockSpec(),
+        limit=LIMIT_P,
     )
     rest = small_call(
-        pack_rest_kernel, "pack_rest", shape((chips, shard_rows, 2 * units + 4 * HD), BF16), masters[1], *masters[2:4]
+        pack_rest_kernel, "pack_rest", shape((shard_rows, 2 * units + 4 * HD), BF16), masters[1], *masters[2:4]
     )
     lead_own = lax.all_to_all(lead, "batch", 0, 0)
-    lead_own, rest = lax.optimization_barrier((lead_own, rest))
-    rest_own = lax.all_to_all(rest, "batch", 0, 0)
+    place = side.astype(jnp.int32).reshape(1)
+    normal, masked, masked_t = prepare(place, lengths, tokens, cotangent)
+    members = chips // 2
+    far_pairs = [(i, i ^ members) for i in range(chips)]
+    teams = [list(range(members)), list(range(members, chips))]
+    half = (lax.axis_index("batch") // members).astype(jnp.int32).reshape(1)
+    team_shape = shape((members, 2) + rest.shape, BF16)
+    rest_pair = small_call(pair_kernel, "pair_rest", team_shape, half, rest, lax.ppermute(rest, "batch", far_pairs))
+    lead_own, rest_pair, normal, masked, masked_t = lax.optimization_barrier(
+        (lead_own, rest_pair, normal, masked, masked_t)
+    )
+    rest_own = lax.all_to_all(rest_pair, "batch", 0, 0, axis_index_groups=teams)
     lead_other = swap(lead_own)
     flat = lambda a: a.reshape(chips * shard_rows, a.shape[-1])
-    place = side.astype(jnp.int32).reshape(1)
+    per_seq = lambda a: a.reshape(seqs, slot_rows, width)
     n1t, qkv, attended, linv, probs, wpairs, norms = forward(
-        chips, norm_part, place, lengths, tokens, key_masks, flat(lead_own), flat(lead_other)
+        chips, norm_part, place, lengths, per_seq(normal), key_masks, flat(lead_own), flat(lead_other)
     )
     rest_own, attended = lax.optimization_barrier((rest_own, attended))
     rest_other = swap(rest_own)
     block_out, gmid, gatt, grest_own, grest_other, gnorm_two = middle(
-        place, lengths, tokens, cotangent, attended, linv, flat(rest_own), flat(rest_other), norms
-    )
-    per_seq = lambda a: a.reshape(seqs, slot_rows, width)
-    plus = lambda name, a, b: small_call(add_kernel, name, shape(a.shape, BF16), a, b)
-    rest_sum = plus("add_rest", grest_own, swap(grest_other))
+        tokens, masked, masked_t, attended, linv, rest_own, rest_other, norms
+    )
+    rest_sum = small_call(add_split_kernel, "add_rest", team_shape, grest_own, swap(grest_other))
     rest_sum, gatt = lax.optimization_barrier((rest_sum, gatt))
-    rest_parts = lax.all_to_all(rest_sum.reshape(rest.shape), "batch", 0, 0)
-    gp, glead_own, glead_other = backward(n1t, qkv, probs, per_seq(gatt), attended)
-    lead_sum = plus("add_lead", glead_own, swap(glead_other))
+    rest_parts = lax.all_to_all(rest_sum, "batch", 0, 0, axis_index_groups=teams)
+    gp, glead_own, glead_other = backward(place, lengths, n1t, qkv, probs, per_seq(gatt), attended)
+    lead_sum = small_call(add_kernel, "add_lead", shape(glead_own.shape, BF16), glead_own, swap(glead_other))
     lead_sum, rest_parts = lax.optimization_barrier((lead_sum, rest_parts))
     lead_parts = lax.all_to_all(lead_sum.reshape(chips, shard_rows, 10 * HD), "batch", 0, 0)
     input_grad, terms = input_gradient(tokens, gp, per_seq(gmid), wpairs, norms, gnorm_two)
-    rest_shard, squares = small_call(
-        sum_rest_kernel, "sum_rest", [shape(rest.shape[1:], F32), shape((1, PAIR), F32)], rest_parts
-    )
-    lead_shard, message = small_call(
+    rest_mine, rest_theirs = small_call(
+        sum_rest_kernel, "sum_rest", [shape(rest.shape, F32), shape(rest.shape, BF16)], half, rest_parts
+    )
+    rest_far = lax.ppermute(rest_theirs, "batch", far_pairs)
+    lead_shard, rest_shard, message = small_call(
         sum_lead_kernel,
         "sum_lead",
-        [shape(lead.shape[1:], F32), shape(terms.shape, F32)],
+        [shape(lead.shape[1:], F32), shape(rest.shape, F32), shape(terms.shape, F32)],
         lead_parts,
-        squares,
+        rest_mine,
+        rest_far,
         terms,
     )
     message = message + swap(message)

time: 181 us -> 173 us (0.956)
  waiting for transfers between devices: 45 us -> 33.4 us
  starting transfers between devices: 30.8 us -> 38.1 us
  local copies, waits for them, and re-layouts: 3.06 us -> 0.99 us
    all_to_all x1, waiting for transfers between devices: 13.3 us -> 0.01 us  [per_device(): lead_own = lax.all_to_all(lead, 'batch', 0, 0)]
    ppermute x0 -> x2, waiting for transfers between devices: none -> 12.4 us  [the longest x1 7.39 us: per_device(): lax.ppermute(rest, 'batch', far_pairs)]
    all_to_all x2, waiting for transfers between devices: 6.62 us -> 0.01 us  [the longest x1 0.01 us: per_device(): lax.all_to_all(rest_sum, 'batch', 0, 0, axis_index_groups=teams)]
    ppermute x0 -> x2, starting transfers between devices: none -> 5.77 us  [the longest x1 2.89 us: per_device(): lax.ppermute(rest, 'batch', far_pairs)]
    all_to_all x1, starting transfers between devices: 7.31 us -> 12.3 us  [per_device(): lax.all_to_all(lead_sum.reshape(chips, shard_rows, 10 * HD), 'batch', 0, 0)]
    all_to_all x2, starting transfers between devices: 11.6 us -> 7.68 us  [the longest x1 3.89 us: per_device(): lax.all_to_all(rest_sum, 'batch', 0, 0, axis_index_groups=teams)]
    all_to_all x1, waiting for transfers between devices: 3.62 us -> 0.01 us  [per_device(): lax.all_to_all(lead_sum.reshape(chips, shard_rows, 10 * HD), 'batch', 0, 0)]
    pallas_call x1, Pallas kernels: 24.4 us -> 21 us  [forward(): pl.pallas_call(functools.partial(forward_kernel, chips, part), grid=(seqs...]
  transfers between devices with their start and end apart: 13 -> 15, of which waited for: 12 -> 10; matrix products, arithmetic and copies ran while one was open for 0% -> 0% of each run, Pallas kernels for 35% -> 36%
where the time goes in v6:
time: 173 us
  Pallas kernels  99.8 us (58%)
  starting transfers between devices  38.1 us (22%)
  waiting for transfers between devices  33.4 us (19%)
    pallas_call x1, Pallas kernels, middle(): pl.pallas_call(functools.partial(middle_kernel, units), grid=(total // FB...  33.4 us
    pallas_call x1, Pallas kernels, backward(): pl.pallas_call(backward_kernel, grid=(seqs,), in_specs=[IN_SMEM, IN_SMEM,...  22.1 us
    pallas_call x1, Pallas kernels, forward(): pl.pallas_call(functools.partial(forward_kernel, chips, part), grid=(seqs...  21 us
    all_to_all x1, starting transfers between devices, per_device(): lax.all_to_all(lead_sum.reshape(chips, shard_rows, 10 * HD), 'batch', 0, 0)  12.3 us
    ppermute x4, waiting for transfers between devices, per_device(): lax.ppermute(message, 'batch', [(i, i ^ stride) for i in range(chips)])  11.9 us
    pallas_call x1, Pallas kernels, input_gradient(): pl.pallas_call(input_kernel, grid=(seqs,), in_specs=[full, pl.BlockSpec((...  9.6 us
    ppermute x5, waiting for transfers between devices, swap(): return lax.ppermute(values, 'head', [(0, 1), (1, 0)])  9.14 us
    all_to_all x1, starting transfers between devices, per_device(): lead_own = lax.all_to_all(lead, 'batch', 0, 0)  8.31 us
  transfers between devices with their start and end apart: 15, of which 10 were waited for; matrix products, arithmetic and copies ran while one was open for 0% of the time, Pallas kernels for 36%

profile of v6, /device:TPU:0, one launch (start us, length us, event | category | flops | bytes accessed | tf_op | source)
XLA Modules:
  0.0 173.4 jit_solution(7547828589848845707)
XLA Ops:
  0.7 1.8 %pack_lead.1 = bf16[16,24,640]{2,1,0:T(8,128)(2,1)} custom-call(f32[3,24,192]{2,1,0:T(8,128)} %bitcast.34, f32[1,48]{1,0:T(1,128)} %bitcast.41), custom_call_target="tpu_custom_call" | custom-call | flops 2000000000 | bytes 1000000 | tf_op jit(solution)/shard_map/pack_lead/pallas_call | solution.py:654
  2.5 8.3 %all-to-all-start = ((bf16[16,24,640]{2,1,0:T(8,128)(2,1)}), bf16[16,24,640]{2,1,0:T(8,128)(2,1)S(1)}, u32[]{:S(2)}, u32[]{:S(2)}) async-start(bf16[16,24,640]{2,1,0:T(8,128)(2,1)} %pack_lead.1), calls=%async_computation | async-start | bytes 983040 | tf_op jit(solution)/shard_map/all_to_all | solution.py:707
  10.9 2.9 %collective-permute-start = (bf16[24,1792]{1,0:T(8,128)(2,1)S(1)}, bf16[24,1792]{1,0:T(8,128)(2,1)S(1)}, u32[]{:S(2)}, u32[]{:S(2)}) collective-permute-start(bf16[24,1792]{1,0:T(8,128)(2,1)S(1)} %pack_rest.1.own_ref), channel_id=1, source_target_pairs={{0,16},{2,18},{4,20},{6,22},{8,24},{10,26},{12,28},{14,30},{16,0},... | collective-permute-start | bytes 258056 | tf_op jit(solution)/shard_map/ppermute | solution.py:715
  13.7 7.0 %prepare.1 = (f32[2560,384]{1,0:T(8,128)}, bf16[2560,384]{1,0:T(8,128)(2,1)}, bf16[384,2560]{1,0:T(8,128)(2,1)}) custom-call(s32[1]{0:T(128)} %bitcast.6.side_ref, s32[8]{0:T(128)} %len_ref.5, bf16[2560,384]{1,0:T(8,128)(2,1)} %bitcast.45, bf16[2560,384]{1,0:T(8,128)(2,1)} %bitcast.44), custom_call_target="tpu_custom_call" | custom-call | flops 5000000000 | bytes 1000000 | tf_op jit(solution)/shard_map/prepare/pallas_call | solution.py:115
  20.8 7.4 %collective-permute-done.far_ref = bf16[24,1792]{1,0:T(8,128)(2,1)S(1)} collective-permute-done((bf16[24,1792]{1,0:T(8,128)(2,1)S(1)}, bf16[24,1792]{1,0:T(8,128)(2,1)S(1)}, u32[]{:S(2)}, u32[]{:S(2)}) %collective-permute-start) | collective-permute-done | bytes 86048 | tf_op jit(solution)/shard_map/ppermute | solution.py:715
  28.2 1.2 pair_rest.1
  29.4 3.8 %all-to-all-start.1 = ((bf16[8,2,24,1792]{3,2,1,0:T(8,128)(2,1)}), bf16[8,2,24,1792]{3,2,1,0:T(8,128)(2,1)S(1)}, u32[]{:S(2)}, u32[]{:S(2)}) async-start(bf16[8,2,24,1792]{3,2,1,0:T(8,128)(2,1)} %pair_rest.1), calls=%async_computation.1 | async-start | bytes 2752512 | tf_op jit(solution)/shard_map/all_to_all | solution.py:719
  33.2 21.0 %attention_forward.1 = (bf16[4,384,640]{2,1,0:T(8,128)(2,1)}, bf16[4,3,640,384]{3,2,1,0:T(8,128)(2,1)}, bf16[4,640,384]{2,1,0:T(8,128)(2,1)}, f32[4,640,384]{2,1...) custom-call(s32[1]{0:T(128)} %bitcast.6.side_ref, ...), custom_call_target="tpu_custom_call" | custom-call | flops 24000000000 | bytes 1000000 | tf_op jit(solution)/shard_map/attention_forward/pallas_call | solution.py:229
  54.2 0.9 copy-done.13
  55.1 3.1 %collective-permute-done.2.other_ref = bf16[8,2,24,1792]{3,2,1,0:T(8,128)(2,1)S(1)} collective-permute-done((bf16[8,2,24,1792]{3,2,1,0:T(8,128)(2,1)S(1)}, bf16[8,2,24,1792]{3,2,1,0:T(8,128)(2,1)S(1)}, u32[]{:S(2)}, u32[]{:S(2)}) %collective-permute-start.2) | collective-permute-done | bytes 1376288 | tf_op jit(solution)/shard_map/ppermute | solution.py:666
  58.3 33.4 %feed_forward.1 = (bf16[2560,384]{1,0:T(8,128)(2,1)}, f32[2560,384]{1,0:T(8,128)}, bf16[2560,384]{1,0:T(8,128)(2,1)S(1)}, bf16[384,1792]{1,0:T(8,128)(2,1)S(1)},...) custom-call(bf16[2560,384]{1,0:T(8,128)(2,1)} %bitcast.46, bf16[2560,384]{1,0:T(8,128)(2,1)} %get-tuple-element.66.gb_ref, ...), custom_call_target="tpu_custom_call" | custom-call | flops 35999997952 | bytes 1000000 | tf_op jit(solution)/shard_map/feed_forward/pallas_call | solution.py:343
  91.6 0.1 collective-permute-start.3
  91.7 3.0 %collective-permute-done.3.right_ref = bf16[384,1792]{1,0:T(8,128)(2,1)S(1)} collective-permute-done((bf16[384,1792]{1,0:T(8,128)(2,1)S(1)}, bf16[384,1792]{1,0:T(8,128)(2,1)S(1)}, u32[]{:S(2)}, u32[]{:S(2)}) %collective-permute-start.3) | collective-permute-done | bytes 1376288 | tf_op jit(solution)/shard_map/ppermute | solution.py:666
  94.7 1.4 add_rest.1
  96.1 3.9 %all-to-all-start.2 = ((bf16[8,2,24,1792]{3,2,1,0:T(8,128)(2,1)}), bf16[8,2,24,1792]{3,2,1,0:T(8,128)(2,1)S(1)}, u32[]{:S(2)}, u32[]{:S(2)}) async-start(bf16[8,2,24,1792]{3,2,1,0:T(8,128)(2,1)} %add_rest.1), calls=%async_computation.2 | async-start | bytes 2752512 | tf_op jit(solution)/shard_map/all_to_all | solution.py:733
  100.0 22.1 %attention_backward.1 = (bf16[4,3,640,384]{3,2,1,0:T(8,128)(2,1)}, bf16[384,640]{1,0:T(8,128)(2,1)S(1)}, bf16[384,640]{1,0:T(8,128)(2,1)S(1)}) custom-call(s32[1]{0:T(128)} %bitcast.6.side_ref, s32[8]{0:T(128)S(1)} %copy-done.10, bf16[4,384,640]{2,1,0:T(8,128)(2,1)} %get-tuple-element.77.n1t_ref, bf16[4,3,640,384]{3,2,1,0:T(8,128)(2,1)} %get-tuple-element.78.qkv_ref, ...), custom_call_target="tpu_custom_call" | custom-call | flops 27000000512 | bytes 1000000 | tf_op jit(solution)/shard_map/attention_backward/pallas_call | solution.py:463
  122.1 1.9 %collective-permute-done.4.right_ref = bf16[384,640]{1,0:T(8,128)(2,1)S(1)} collective-permute-done((bf16[384,640]{1,0:T(8,128)(2,1)S(1)}, bf16[384,640]{1,0:T(8,128)(2,1)S(1)}, u32[]{:S(2)}, u32[]{:S(2)}) %collective-permute-start.4) | collective-permute-done | bytes 491552 | tf_op jit(solution)/shard_map/ppermute | solution.py:666
  124.0 0.9 add_lead.1
  124.9 12.3 %all-to-all-start.3 = ((bf16[16,24,640]{2,1,0:T(8,128)(2,1)}), bf16[16,24,640]{2,1,0:T(8,128)(2,1)S(1)}, u32[]{:S(2)}, u32[]{:S(2)}) async-start(bf16[16,24,640]{2,1,0:T(8,128)(2,1)} %bitcast.17), calls=%async_computation.3 | async-start | bytes 983040 | tf_op jit(solution)/shard_map/all_to_all | solution.py:737
  137.2 0.2 sum_rest.1
  137.4 2.9 %collective-permute-start.5 = (bf16[24,1792]{1,0:T(8,128)(2,1)S(1)}, bf16[24,1792]{1,0:T(8,128)(2,1)S(1)}, u32[]{:S(2)}, u32[]{:S(2)}) collective-permute-start(bf16[24,1792]{1,0:T(8,128)(2,1)S(1)} %get-tuple-element.95), channel_id=1, source_target_pairs={{0,16},{2,18},{4,20},{6,22},{8,24},{10,26},{12,28},{14,30},{16,0},... | collective-permute-start | bytes 258056 | tf_op jit(solution)/shard_map/ppermute | solution.py:742
  140.3 9.6 %input_gradient.1 = (f32[4,640,384]{2,1,0:T(8,128)}, f32[8,384]{1,0:T(8,128)S(1)}) custom-call(bf16[4,640,384]{2,1,0:T(8,128)(2,1)} %tok_ref.1, bf16[4,3,640,384]{3,2,1,0:T(8,128)(2,1)} %get-tuple-element.84.gp_ref, f32[4,640,384]{2,1,0:T(8,128)} %bitcast.48, bf16[3,384,384]{2,1,0:T(8,128)(2,1)S(1)} %copy-done.14, f32[4,384]{1,0:T(4,128)S(1)} %get-tuple-element.75.norms_ref, ...), custom_call_target="tpu_custom_call" | custom-call | flops 12000000000 | bytes 1000000 | tf_op jit(solution)/shard_map/input_gradient/pallas_call | solution.py:509
  149.9 5.0 %collective-permute-done.5.far_ref = bf16[24,1792]{1,0:T(8,128)(2,1)S(1)} collective-permute-done((bf16[24,1792]{1,0:T(8,128)(2,1)S(1)}, bf16[24,1792]{1,0:T(8,128)(2,1)S(1)}, u32[]{:S(2)}, u32[]{:S(2)}) %collective-permute-start.5) | collective-permute-done | bytes 86048 | tf_op jit(solution)/shard_map/ppermute | solution.py:742
  155.1 1.2 collective-permute-done.6
  156.3 1.5 collective-permute-start.7
  157.8 2.2 %collective-permute-done.7 = f32[8,384]{1,0:T(8,128)S(1)} collective-permute-done((f32[8,384]{1,0:T(8,128)S(1)}, f32[8,384]{1,0:T(8,128)S(1)}, u32[]{:S(2)}, u32[]{:S(2)}) %collective-permute-start.7) | collective-permute-done | bytes 12320 | tf_op jit(solution)/shard_map/ppermute | solution.py:755
  160.0 1.5 collective-permute-start.8
  161.5 2.2 %collective-permute-done.8 = f32[8,384]{1,0:T(8,128)S(1)} collective-permute-done((f32[8,384]{1,0:T(8,128)S(1)}, f32[8,384]{1,0:T(8,128)S(1)}, u32[]{:S(2)}, u32[]{:S(2)}) %collective-permute-start.8) | collective-permute-done | bytes 12320 | tf_op jit(solution)/shard_map/ppermute | solution.py:755
  163.7 0.9 collective-permute-start.9
  164.6 2.8 %collective-permute-done.9 = f32[8,384]{1,0:T(8,128)S(1)} collective-permute-done((f32[8,384]{1,0:T(8,128)S(1)}, f32[8,384]{1,0:T(8,128)S(1)}, u32[]{:S(2)}, u32[]{:S(2)}) %collective-permute-start.9) | collective-permute-done | bytes 12320 | tf_op jit(solution)/shard_map/ppermute | solution.py:755
  167.4 4.6 %collective-permute-done.10 = f32[8,384]{1,0:T(8,128)S(1)} collective-permute-done((f32[8,384]{1,0:T(8,128)S(1)}, f32[8,384]{1,0:T(8,128)S(1)}, u32[]{:S(2)}, u32[]{:S(2)}) %collective-permute-start.10) | collective-permute-done | bytes 12320 | tf_op jit(solution)/shard_map/ppermute | solution.py:755
  172.1 1.2 update_weights.1
  (46 shorter events, 0.3 us)
Async XLA Ops:
  0.6 10.2 %copy-start.4 = (f32[24,768]{1,0:T(8,128)S(1)}, f32[24,768]{1,0:T(8,128)}, u32[]{:S(2)}) copy-start(f32[24,768]{1,0:T(8,128)} %up_ref.3) | copy-start | bytes 221188
  0.7 10.2 %copy-start.5 = (f32[768,24]{0,1:T(8,128)S(1)}, f32[768,24]{0,1:T(8,128)}, u32[]{:S(2)}) copy-start(f32[768,24]{0,1:T(8,128)} %param.21) | copy-start | bytes 221188
  0.7 10.2 %copy-start.7 = (f32[192,24]{0,1:T(8,128)S(1)}, f32[192,24]{0,1:T(8,128)}, u32[]{:S(2)}) copy-start(f32[192,24]{0,1:T(8,128)} %param.19) | copy-start | bytes 55300
  2.5 26.9 %all-to-all-start = ((bf16[16,24,640]{2,1,0:T(8,128)(2,1)}), bf16[16,24,640]{2,1,0:T(8,128)(2,1)S(1)}, u32[]{:S(2)}, u32[]{:S(2)}) async-start(bf16[16,24,640]{2,1,0:T(8,128)(2,1)} %pack_lead.1), calls=%async_computation | async-start | bytes 983040 | tf_op jit(solution)/shard_map/all_to_all | solution.py:707
  10.9 17.3 %collective-permute-start = (bf16[24,1792]{1,0:T(8,128)(2,1)S(1)}, bf16[24,1792]{1,0:T(8,128)(2,1)S(1)}, u32[]{:S(2)}, u32[]{:S(2)}) collective-permute-start(bf16[24,1792]{1,0:T(8,128)(2,1)S(1)} %pack_rest.1.own_ref), channel_id=1, source_target_pairs={{0,16},{2,18},{4,20},{6,22},{8,24},{10,26},{12,28},{14,30},{16,0},... | collective-permute-start | bytes 258056 | tf_op jit(solution)/shard_map/ppermute | solution.py:715
  29.4 3.8 %copy-start.8 = (s32[8,640]{1,0:T(8,128)S(1)}, s32[8,640]{1,0:T(8,128)}, u32[]{:S(2)}) copy-start(s32[8,640]{1,0:T(8,128)} %mask_ref.1) | copy-start | bytes 61444
  29.4 3.8 %copy-start.10 = (s32[8]{0:T(128)S(1)}, s32[8]{0:T(128)}, u32[]{:S(2)}) copy-start(s32[8]{0:T(128)} %len_ref.5) | copy-start | bytes 100
  29.4 3.8 %collective-permute-start.1 = (bf16[16,24,640]{2,1,0:T(8,128)(2,1)S(1)}, bf16[16,24,640]{2,1,0:T(8,128)(2,1)S(1)}, u32[]{:S(2)}, u32[]{:S(2)}) collective-permute-start(bf16[16,24,640]{2,1,0:T(8,128)(2,1)S(1)} %all-to-all-done), channel_id=1, source_target_pairs={{0,1},{1,0},{2,3},{3,2},{4,5},{5,4},{6,7},{7,6},{8,9},{9,8},{10,11... | collective-permute-start | bytes 1474568 | tf_op jit(solution)/shard_map/ppermute | solution.py:666
  29.4 25.8 %all-to-all-start.1 = ((bf16[8,2,24,1792]{3,2,1,0:T(8,128)(2,1)}), bf16[8,2,24,1792]{3,2,1,0:T(8,128)(2,1)S(1)}, u32[]{:S(2)}, u32[]{:S(2)}) async-start(bf16[8,2,24,1792]{3,2,1,0:T(8,128)(2,1)} %pair_rest.1), calls=%async_computation.1 | async-start | bytes 2752512 | tf_op jit(solution)/shard_map/all_to_all | solution.py:719
  54.2 0.9 copy-start.13
  55.1 3.1 %collective-permute-start.2 = (bf16[8,2,24,1792]{3,2,1,0:T(8,128)(2,1)S(1)}, bf16[8,2,24,1792]{3,2,1,0:T(8,128)(2,1)S(1)}, u32[]{:S(2)}, u32[]{:S(2)}) collective-permute-start(bf16[8,2,24,1792]{3,2,1,0:T(8,128)(2,1)S(1)} %all-to-all-done.1.own_ref), channel_id=1, source_target_pairs={{0,1},{1,0},{2,3},{3,2},{4,5},{5,4},{6,7},{7,6},{8,9},{9,8},{10,11... | collective-permute-start | bytes 4128776 | tf_op jit(solution)/shard_map/ppermute | solution.py:666
  91.6 4.5 %copy-start.12 = (bf16[2560,384]{1,0:T(8,128)(2,1)}, bf16[2560,384]{1,0:T(8,128)(2,1)S(1)}, u32[]{:S(2)}) copy-start(bf16[2560,384]{1,0:T(8,128)(2,1)S(1)} %get-tuple-element.83) | copy-start | bytes 5898244
  91.6 3.1 %collective-permute-start.3 = (bf16[384,1792]{1,0:T(8,128)(2,1)S(1)}, bf16[384,1792]{1,0:T(8,128)(2,1)S(1)}, u32[]{:S(2)}, u32[]{:S(2)}) collective-permute-start(bf16[384,1792]{1,0:T(8,128)(2,1)S(1)} %get-tuple-element.81), channel_id=1, source_target_pairs={{0,1},{1,0},{2,3},{3,2},{4,5},{5,4},{6,7},{7,6},{8,9},{9,8},{10,11... | collective-permute-start | bytes 4128776 | tf_op jit(solution)/shard_map/ppermute | solution.py:666
  96.1 28.8 %all-to-all-start.2 = ((bf16[8,2,24,1792]{3,2,1,0:T(8,128)(2,1)}), bf16[8,2,24,1792]{3,2,1,0:T(8,128)(2,1)S(1)}, u32[]{:S(2)}, u32[]{:S(2)}) async-start(bf16[8,2,24,1792]{3,2,1,0:T(8,128)(2,1)} %add_rest.1), calls=%async_computation.2 | async-start | bytes 2752512 | tf_op jit(solution)/shard_map/all_to_all | solution.py:733
  122.1 1.9 %collective-permute-start.4 = (bf16[384,640]{1,0:T(8,128)(2,1)S(1)}, bf16[384,640]{1,0:T(8,128)(2,1)S(1)}, u32[]{:S(2)}, u32[]{:S(2)}) collective-permute-start(bf16[384,640]{1,0:T(8,128)(2,1)S(1)} %get-tuple-element.90), channel_id=1, source_target_pairs={{0,1},{1,0},{2,3},{3,2},{4,5},{5,4},{6,7},{7,6},{8,9},{9,8},{10,11... | collective-permute-start | bytes 1474568 | tf_op jit(solution)/shard_map/ppermute | solution.py:666
  124.9 30.0 %all-to-all-start.3 = ((bf16[16,24,640]{2,1,0:T(8,128)(2,1)}), bf16[16,24,640]{2,1,0:T(8,128)(2,1)S(1)}, u32[]{:S(2)}, u32[]{:S(2)}) async-start(bf16[16,24,640]{2,1,0:T(8,128)(2,1)} %bitcast.17), calls=%async_computation.3 | async-start | bytes 983040 | tf_op jit(solution)/shard_map/all_to_all | solution.py:737
  137.2 3.1 %copy-start.14 = (bf16[3,384,384]{2,1,0:T(8,128)(2,1)S(1)}, bf16[3,384,384]{2,1,0:T(8,128)(2,1)}, u32[]{:S(2)}) copy-start(bf16[3,384,384]{2,1,0:T(8,128)(2,1)} %copy-done.13) | copy-start | bytes 2654212
  137.4 17.5 %collective-permute-start.5 = (bf16[24,1792]{1,0:T(8,128)(2,1)S(1)}, bf16[24,1792]{1,0:T(8,128)(2,1)S(1)}, u32[]{:S(2)}, u32[]{:S(2)}) collective-permute-start(bf16[24,1792]{1,0:T(8,128)(2,1)S(1)} %get-tuple-element.95), channel_id=1, source_target_pairs={{0,16},{2,18},{4,20},{6,22},{8,24},{10,26},{12,28},{14,30},{16,0},... | collective-permute-start | bytes 258056 | tf_op jit(solution)/shard_map/ppermute | solution.py:742
  154.9 17.1 %copy-start = (f32[2,24,3,192]{3,1,2,0:T(8,128)S(1)}, f32[2,24,3,192]{3,1,2,0:T(8,128)}, u32[]{:S(2)}) copy-start(f32[2,24,3,192]{3,1,2,0:T(8,128)} %param.23) | copy-start | bytes 331780
  154.9 17.1 %copy-start.1 = (f32[2,24,768]{2,1,0:T(8,128)S(1)}, f32[2,24,768]{2,1,0:T(8,128)}, u32[]{:S(2)}) copy-start(f32[2,24,768]{2,1,0:T(8,128)} %up_m_ref.1) | copy-start | bytes 442372
  154.9 17.1 %copy-start.2 = (f32[2,768,24]{1,2,0:T(8,128)S(1)}, f32[2,768,24]{1,2,0:T(8,128)}, u32[]{:S(2)}) copy-start(f32[2,768,24]{1,2,0:T(8,128)} %param.26) | copy-start | bytes 442372
  154.9 17.1 %copy-start.3 = (f32[24,3,192]{2,0,1:T(8,128)S(1)}, f32[24,3,192]{2,0,1:T(8,128)}, u32[]{:S(2)}) copy-start(f32[24,3,192]{2,0,1:T(8,128)} %param.18) | copy-start | bytes 165892
  154.9 17.1 %copy-start.6 = (f32[2,192,24]{1,2,0:T(8,128)S(1)}, f32[2,192,24]{1,2,0:T(8,128)}, u32[]{:S(2)}) copy-start(f32[2,192,24]{1,2,0:T(8,128)} %param.24) | copy-start | bytes 110596
  154.9 17.1 %copy-start.9 = (f32[2,48]{1,0:T(2,128)S(1)}, f32[2,48]{1,0:T(2,128)}, u32[]{:S(2)}) copy-start(f32[2,48]{1,0:T(2,128)} %norm_m_ref.1) | copy-start | bytes 1156
  154.9 17.1 %copy-start.11 = (f32[48]{0:T(128)S(1)}, f32[48]{0:T(128)}, u32[]{:S(2)}) copy-start(f32[48]{0:T(128)} %param.22) | copy-start | bytes 580
  155.1 1.2 collective-permute-start.6
  156.3 3.7 %collective-permute-start.7 = (f32[8,384]{1,0:T(8,128)S(1)}, f32[8,384]{1,0:T(8,128)S(1)}, u32[]{:S(2)}, u32[]{:S(2)}) collective-permute-start(f32[8,384]{1,0:T(8,128)S(1)} %add.20), channel_id=1, source_target_pairs={{0,2},{2,0},{4,6},{6,4},{8,10},{10,8},{12,14},{14,12},{16,18},{18,... | collective-permute-start | bytes 36872 | tf_op jit(solution)/shard_map/ppermute | solution.py:755
  160.0 3.7 %collective-permute-start.8 = (f32[8,384]{1,0:T(8,128)S(1)}, f32[8,384]{1,0:T(8,128)S(1)}, u32[]{:S(2)}, u32[]{:S(2)}) collective-permute-start(f32[8,384]{1,0:T(8,128)S(1)} %add.21), channel_id=1, source_target_pairs={{0,4},{2,6},{4,0},{6,2},{8,12},{10,14},{12,8},{14,10},{16,20},{18,... | collective-permute-start | bytes 36872 | tf_op jit(solution)/shard_map/ppermute | solution.py:755
  163.7 3.7 %collective-permute-start.9 = (f32[8,384]{1,0:T(8,128)S(1)}, f32[8,384]{1,0:T(8,128)S(1)}, u32[]{:S(2)}, u32[]{:S(2)}) collective-permute-start(f32[8,384]{1,0:T(8,128)S(1)} %add.22), channel_id=1, source_target_pairs={{0,8},{2,10},{4,12},{6,14},{8,0},{10,2},{12,4},{14,6},{16,24},{18,... | collective-permute-start | bytes 36872 | tf_op jit(solution)/shard_map/ppermute | solution.py:755
  167.4 4.6 %collective-permute-start.10 = (f32[8,384]{1,0:T(8,128)S(1)}, f32[8,384]{1,0:T(8,128)S(1)}, u32[]{:S(2)}, u32[]{:S(2)}) collective-permute-start(f32[8,384]{1,0:T(8,128)S(1)} %add.23), channel_id=1, source_target_pairs={{0,16},{2,18},{4,20},{6,22},{8,24},{10,26},{12,28},{14,30},{16,0},... | collective-permute-start | bytes 36872 | tf_op jit(solution)/shard_map/ppermute | solution.py:755

commit v7 on v6

--- a/solution.py
+++ b/solution.py
@@ -23,6 +23,7 @@
 NT = (((1,), (1,)), ((), ()))
 TN = (((0,), (0,)), ((), ()))
 QB = 320
+DB = 640
 FB = 512
 FC = 256
 PAIR = 2 * HD
@@ -74,6 +75,13 @@
         for side in range(2)
     ]
     return [first] + parts[0], [third] + parts[1]
+
+
+def in_order(out_ref, own_ref, other_ref):
+    members, sides, part, _ = own_ref.shape
+    for head, ref in enumerate((own_ref, other_ref)):
+        for place in range(members * sides):
+            out_ref[head, place * part : (place + 1) * part, :] = ref[place % members, place // members]
 
 
 def gathered_norms(first, second, chips, part, width):
@@ -130,7 +138,7 @@
 
 def forward_kernel(
     chips, part, side_ref, len_ref, normal_ref, mask_ref, own_ref, other_ref,
-    n1t_ref, qkv_ref, att_ref, linv_ref, p_ref, w_ref, norms_ref,
+    n1t_ref, qkv_ref, att_ref, linv_ref, p_ref, w_ref, norms_ref, lead_ref,
 ):
     rows, width = normal_ref.shape
     pairs = width // PAIR
@@ -138,9 +146,10 @@
 
     @pl.when(seq == 0)
     def _():
-        own, other = own_ref[...], other_ref[...]
+        in_order(lead_ref, own_ref, other_ref)
+        own, other = lead_ref[0], lead_ref[1]
         for i, weights in enumerate(split_pairs(own[:, : 9 * HD], other[:, : 9 * HD], 3 * HD)):
-            w_ref[i] = weights
+            w_ref[:, i * 3 * PAIR : (i + 1) * 3 * PAIR] = weights
         tail = slice(8 * HD, 10 * HD)
         mine, theirs = own[:, tail].astype(F32), other[:, tail].astype(F32)
         pad = jnp.zeros((own.shape[0], 8 * HD), F32)
@@ -176,9 +185,10 @@
     ones = jnp.ones((count, PAIR), BF16)
     hidden = hidden[:count]
     ready = {}
+    projected = mm(n1, w_ref[...])
 
     def project(pair):
-        out = mm(n1, w_ref[pair])
+        out = projected[:, pair * 3 * PAIR : (pair + 1) * 3 * PAIR]
         queries = (out[:, :PAIR].astype(BF16).astype(F32) * (HD**-0.5)).astype(BF16)
         others = out[:, PAIR:].astype(BF16)
         qkv_ref[pair, :, :PAIR] = queries
@@ -236,7 +246,7 @@
             row_spec,
             row_spec,
             pl.BlockSpec((sq, heads, rows, rows), lambda s: (s, 0, 0, 0)),
-            whole(pairs, width, 3 * PAIR),
+            IN_VMEM,
             IN_VMEM,
         ],
         out_shape=[
@@ -245,9 +255,10 @@
             shape((seqs, rows, width), BF16),
             shape((seqs, rows, width), F32),
             shape((seqs, heads, rows, rows), BF16),
-            shape((pairs, width, 3 * PAIR), BF16),
+            shape((width, 3 * width), BF16),
             shape((4, width), F32),
         ],
+        scratch_shapes=[pltpu.VMEM((2, width, own.shape[-1]), BF16)],
         compiler_params=LIMIT_A,
         cost_estimate=cost(24),
         name="attention_forward",
@@ -256,8 +267,8 @@
 
 def middle_kernel(
     units, tok_ref, gb_ref, gbt_ref, att_ref, linv_ref, own_ref, other_ref, norms_ref,
-    out_ref, gmid_ref, gatt_ref, gown_ref, gother_ref, gnorm_ref,
-    halves, wo_ref, gout_ref, gup_ref, gdown_ref,
+    mid_ref, act_ref, gmid_ref, gatt_ref, gown_ref, gother_ref, gnorm_ref, halves,
+    wo_ref, gout_ref, gup_ref, gdown_ref,
 ):
     step = pl.program_id(0)
     rows, width = tok_ref.shape
@@ -268,10 +279,7 @@
         gup_ref[...] = jnp.zeros_like(gup_ref)
         gdown_ref[...] = jnp.zeros_like(gdown_ref)
         gnorm_ref[...] = jnp.zeros_like(gnorm_ref)
-        members, sides, part, _ = own_ref.shape
-        for half, ref in enumerate((own_ref, other_ref)):
-            for place in range(members * sides):
-                halves[half, place * part : (place + 1) * part, :] = ref[place % members, place // members]
+        in_order(halves, own_ref, other_ref)
         cols = slice(2 * units, 2 * units + 3 * HD)
         parts = split_pairs(halves[0, :, cols], halves[1, :, cols], HD)
         for i, part in enumerate(parts):
@@ -285,7 +293,8 @@
     n2 = (normal * gain + shift).astype(BF16)
     n2t = n2.T
     gb, gbt = gb_ref[...], gbt_ref[...]
-    sums = [mid, jnp.zeros_like(mid)]
+    mid_ref[...] = mid
+    sums = [jnp.zeros_like(mid)]
 
     def begin(half, c):
         wu = halves[half, :, c * FC : (c + 1) * FC]
@@ -295,8 +304,8 @@
     def finish(half, c, wu, wd, h, ga):
         cols = slice(c * FC, (c + 1) * FC)
         act, gh = gelu_both(h, ga)
-        sums[0] = sums[0] + mm(act, wd, NT)
-        sums[1] = sums[1] + mm(gh, wu, NT)
+        act_ref[half, :, cols] = act
+        sums[0] = sums[0] + mm(gh, wu, NT)
         gup_ref[half, :, cols] += mm(n2t, gh)
         gdown_ref[half, :, cols] += mm(gbt, act)
 
@@ -308,8 +317,7 @@
                 finish(*pending)
             pending = fresh
     finish(*pending)
-    bo, gtwo = sums
-    out_ref[...] = bo.astype(BF16)
+    gtwo = sums[0]
     gnorm_ref[0:8, :] += jnp.sum((gtwo * normal).reshape(rows // 8, 8, width), axis=0)
     gnorm_ref[8:16, :] += jnp.sum(gtwo.reshape(rows // 8, 8, width), axis=0)
     gmid = gb.astype(F32) + norm_backward(normal, rs, gtwo * gain)
@@ -353,17 +361,27 @@
             IN_VMEM,
             IN_VMEM,
         ],
-        out_specs=[rowspec] * 3 + [IN_VMEM, IN_VMEM, whole(16, width)],
+        out_specs=[
+            rowspec,
+            pl.BlockSpec((2, FB, units), lambda s: (0, s, 0)),
+            rowspec,
+            rowspec,
+            IN_VMEM,
+            IN_VMEM,
+            whole(16, width),
+            IN_VMEM,
+        ],
         out_shape=[
-            shape((total, width), BF16),
+            shape((total, width), F32),
+            shape((2, total, units), BF16),
             shape((total, width), F32),
             shape((total, width), BF16),
             shape((width, packed), BF16),
             shape((width, packed), BF16),
             shape((16, width), F32),
+            shape((2, width, packed), BF16),
         ],
         scratch_shapes=[
-            pltpu.VMEM((2, width, packed), BF16),
             pltpu.VMEM((width, width), BF16),
             pltpu.VMEM((width, width), F32),
             pltpu.VMEM((2, width, units), F32),
@@ -395,8 +413,10 @@
 
     @pl.when(seq == pl.num_programs(0) - 1)
     def _():
-        sides = join_pairs(gqkv_ref[0], gqkv_ref[1], gqkv_ref[2], 3 * HD)
-        blank = jnp.zeros((gqkv_ref.shape[1], HD), F32)
+        group = 3 * PAIR
+        thirds = [gqkv_ref[:, i * group : (i + 1) * group] for i in range(3)]
+        sides = join_pairs(*thirds, 3 * HD)
+        blank = jnp.zeros((gqkv_ref.shape[0], HD), F32)
         for columns, ref in zip(sides, (gown_ref, gother_ref)):
             ref[...] = jnp.concatenate(columns + [blank], axis=1).astype(BF16)
 
@@ -435,12 +455,14 @@
         mine["gkt"].append(mm(mine["qt"][hs], ds))
         if half == 1:
             joined = jnp.where(lane < HD, mine["gq"][0], mine["gq"][1])
-            gp_ref[pair, :count, :PAIR] = (joined * (HD**-0.5)).astype(BF16)
-            gp_ref[pair, :count, PAIR : 2 * PAIR] = jnp.concatenate(mine["gkt"], axis=0).astype(BF16).T
-            gp_ref[pair, :count, 2 * PAIR :] = jnp.concatenate(mine["gvt"], axis=0).astype(BF16).T
-            if count < rows:
-                gp_ref[pair, count:, :] = jnp.zeros((rows - count, 3 * PAIR), BF16)
-            gqkv_ref[pair] += mm(n1t_ref[:, :count], gp_ref[pair, :count, :])
+            columns = (
+                (joined * (HD**-0.5)).astype(BF16),
+                jnp.concatenate(mine["gkt"], axis=0).astype(BF16).T,
+                jnp.concatenate(mine["gvt"], axis=0).astype(BF16).T,
+            )
+            for i, values in enumerate(columns):
+                start = (3 * pair + i) * PAIR
+                gp_ref[:count, start : start + PAIR] = values
 
     pending = None
     for pair in range(pairs):
@@ -450,6 +472,9 @@
                 finish(*pending)
             pending = fresh
     finish(*pending)
+    gqkv_ref[...] += mm(n1t_ref[:, :count], gp_ref[:count, :])
+    if count < rows:
+        gp_ref[count:, :] = jnp.zeros((rows - count, gp_ref.shape[1]), BF16)
 
 
 def backward(side, lengths, n1t, qkv, probs, gatt, attended):
@@ -472,23 +497,25 @@
             rowspec,
             rowspec,
         ],
-        out_specs=[groupspec, IN_VMEM, IN_VMEM],
-        out_shape=[shape(qkv.shape, BF16), shape(packed, BF16), shape(packed, BF16)],
-        scratch_shapes=[pltpu.VMEM((pairs, width, 3 * PAIR), F32)],
+        out_specs=[pl.BlockSpec((sq, rows, 3 * width), lambda s: (s, 0, 0)), IN_VMEM, IN_VMEM],
+        out_shape=[shape((seqs, rows, 3 * width), BF16), shape(packed, BF16), shape(packed, BF16)],
+        scratch_shapes=[pltpu.VMEM((width, 3 * width), F32)],
         compiler_params=LIMIT_C,
         cost_estimate=cost(27),
         name="attention_backward",
     )(side, lengths, n1t, qkv, probs, gatt, attended)
 
 
-def input_kernel(tok_ref, gp_ref, gmid_ref, w_ref, norms_ref, two_ref, gin_ref, terms_ref):
+def input_kernel(
+    tok_ref, gp_ref, gmid_ref, w_ref, norms_ref, two_ref, mid_ref, act_ref, weights_ref,
+    gin_ref, terms_ref, out_ref,
+):
     rows, width = tok_ref.shape
-    gone = mm(gp_ref[0], w_ref[0], NT)
-    for pair in range(1, w_ref.shape[0]):
-        gone = gone + mm(gp_ref[pair], w_ref[pair], NT)
+    units = act_ref.shape[2]
+    gone = mm(gp_ref[...], w_ref[...], NT)
     normal, rs = normalize(tok_ref[...].astype(F32))
 
-    @pl.when(pl.program_id(0) == 0)
+    @pl.when((pl.program_id(0) == 0) & (pl.program_id(1) == 0))
     def _():
         terms_ref[...] = jnp.zeros_like(terms_ref)
         terms_ref[2:3, :] = jnp.sum(two_ref[0:8, :], axis=0, keepdims=True)
@@ -497,36 +524,46 @@
     terms_ref[0:1, :] += jnp.sum(gone * normal, axis=0, keepdims=True)
     terms_ref[1:2, :] += jnp.sum(gone, axis=0, keepdims=True)
     gin_ref[...] = gmid_ref[...] + norm_backward(normal, rs, gone * norms_ref[0:1, :])
-
-
-def input_gradient(tokens, gp, gmid, wpairs, norms, gnorm_two):
+    out = mid_ref[...]
+    for half in range(2):
+        out = out + mm(act_ref[half], weights_ref[half, :, units : 2 * units], NT)
+    out_ref[...] = out.astype(BF16)
+
+
+def input_gradient(tokens, gp, gmid, wpairs, norms, gnorm_two, mid, act, weights):
     seqs, rows, width = tokens.shape
-    pairs = width // PAIR
+    units = act.shape[2]
     sq = pl.squeezed
-    full = pl.BlockSpec((sq, rows, width), lambda s: (s, 0, 0))
-    whole = lambda *dims: pl.BlockSpec(dims, lambda s: (0,) * len(dims))
+    full = pl.BlockSpec((sq, DB, width), lambda s, r: (s, r, 0))
     shape = jax.ShapeDtypeStruct
     return pl.pallas_call(
         input_kernel,
-        grid=(seqs,),
+        grid=(seqs, rows // DB),
         in_specs=[
             full,
-            pl.BlockSpec((sq, pairs, rows, 3 * PAIR), lambda s: (s, 0, 0, 0)),
+            pl.BlockSpec((sq, DB, 3 * width), lambda s, r: (s, r, 0)),
             full,
-            whole(pairs, width, 3 * PAIR),
-            IN_VMEM,
-            whole(16, width),
+            IN_VMEM,
+            IN_VMEM,
+            IN_VMEM,
+            full,
+            pl.BlockSpec((2, DB, units), lambda s, r: (0, s * (rows // DB) + r, 0)),
+            IN_VMEM,
         ],
-        out_specs=[full, IN_VMEM],
-        out_shape=[shape((seqs, rows, width), F32), shape((8, width), F32)],
+        out_specs=[full, IN_VMEM, full],
+        out_shape=[
+            shape((seqs, rows, width), F32),
+            shape((8, width), F32),
+            shape((seqs, rows, width), BF16),
+        ],
         compiler_params=LIMIT_D,
-        cost_estimate=cost(12),
+        cost_estimate=cost(13),
         name="input_gradient",
-    )(tokens, gp, gmid, wpairs, norms, gnorm_two)
-
-
-def pack_lead_kernel(qkv_ref, norm_ref, lead_ref):
-    chips, rows, _ = lead_ref.shape
+    )(tokens, gp, gmid, wpairs, norms, gnorm_two, mid, act, weights)
+
+
+def pack_kernel(qkv_ref, out_ref, up_ref, down_ref, norm_ref, lead_ref, rest_ref):
+    rows = lead_ref.shape[0]
     part = norm_ref.shape[1]
     norm = norm_ref[...]
     high = norm.astype(BF16).astype(F32)
@@ -534,12 +571,8 @@
     extra = jnp.where(row == 0, high, jnp.where(row == 1, norm - high, 0.0))
     columns = [qkv_ref[c, :, :PAIR] for c in range(3)] + [qkv_ref[c, :, PAIR:] for c in range(3)]
     blank = jnp.zeros((rows, HD - part), F32)
-    packed = jnp.concatenate(columns + [extra, blank], axis=1).astype(BF16)
-    lead_ref[...] = jnp.broadcast_to(packed[None], lead_ref.shape)
-
-
-def pack_rest_kernel(out_ref, up_ref, down_ref, rest_ref):
-    blank = jnp.zeros((out_ref.shape[0], HD), F32)
+    lead_ref[...] = jnp.concatenate(columns + [extra, blank], axis=1).astype(BF16)
+    blank = jnp.zeros((rows, HD), F32)
     rest_ref[...] = jnp.concatenate([up_ref[...], down_ref[...], out_ref[...], blank], axis=1).astype(BF16)
 
 
@@ -692,50 +725,50 @@
     qkv_rows = qkv_master.transpose(1, 0, 2)
     masters = (qkv_rows, out_master.T, up_master, down_master.T, norm_master[None])
     shape = jax.ShapeDtypeStruct
-    lead = small_call(
-        pack_lead_kernel,
-        "pack_lead",
-        shape((chips, shard_rows, 10 * HD), BF16),
-        qkv_rows,
-        norm_master[None],
+    lead, rest = small_call(
+        pack_kernel,
+        "pack_weights",
+        [shape((shard_rows, 10 * HD), BF16), shape((shard_rows, 2 * units + 4 * HD), BF16)],
+        *masters,
         in_spec=pl.BlockSpec(),
         limit=LIMIT_P,
     )
-    rest = small_call(
-        pack_rest_kernel, "pack_rest", shape((shard_rows, 2 * units + 4 * HD), BF16), masters[1], *masters[2:4]
-    )
-    lead_own = lax.all_to_all(lead, "batch", 0, 0)
-    place = side.astype(jnp.int32).reshape(1)
-    normal, masked, masked_t = prepare(place, lengths, tokens, cotangent)
     members = chips // 2
     far_pairs = [(i, i ^ members) for i in range(chips)]
     teams = [list(range(members)), list(range(members, chips))]
     half = (lax.axis_index("batch") // members).astype(jnp.int32).reshape(1)
-    team_shape = shape((members, 2) + rest.shape, BF16)
-    rest_pair = small_call(pair_kernel, "pair_rest", team_shape, half, rest, lax.ppermute(rest, "batch", far_pairs))
+    lead_far = lax.ppermute(lead, "batch", far_pairs)
+    rest_far = lax.ppermute(rest, "batch", far_pairs)
+    team_of = lambda a: shape((members, 2) + a.shape, BF16)
+    lead_pair = small_call(pair_kernel, "pair_lead", team_of(lead), half, lead, lead_far)
+    lead_own = lax.all_to_all(lead_pair, "batch", 0, 0, axis_index_groups=teams)
+    place = side.astype(jnp.int32).reshape(1)
+    normal, masked, masked_t = prepare(place, lengths, tokens, cotangent)
+    rest_pair = small_call(pair_kernel, "pair_rest", team_of(rest), half, rest, rest_far)
     lead_own, rest_pair, normal, masked, masked_t = lax.optimization_barrier(
         (lead_own, rest_pair, normal, masked, masked_t)
     )
     rest_own = lax.all_to_all(rest_pair, "batch", 0, 0, axis_index_groups=teams)
     lead_other = swap(lead_own)
-    flat = lambda a: a.reshape(chips * shard_rows, a.shape[-1])
     per_seq = lambda a: a.reshape(seqs, slot_rows, width)
     n1t, qkv, attended, linv, probs, wpairs, norms = forward(
-        chips, norm_part, place, lengths, per_seq(normal), key_masks, flat(lead_own), flat(lead_other)
+        chips, norm_part, place, lengths, per_seq(normal), key_masks, lead_own, lead_other
     )
     rest_own, attended = lax.optimization_barrier((rest_own, attended))
     rest_other = swap(rest_own)
-    block_out, gmid, gatt, grest_own, grest_other, gnorm_two = middle(
+    mid, act, gmid, gatt, grest_own, grest_other, gnorm_two, weights = middle(
         tokens, masked, masked_t, attended, linv, rest_own, rest_other, norms
     )
-    rest_sum = small_call(add_split_kernel, "add_rest", team_shape, grest_own, swap(grest_other))
+    rest_sum = small_call(add_split_kernel, "add_rest", team_of(rest), grest_own, swap(grest_other))
     rest_sum, gatt = lax.optimization_barrier((rest_sum, gatt))
     rest_parts = lax.all_to_all(rest_sum, "batch", 0, 0, axis_index_groups=teams)
     gp, glead_own, glead_other = backward(place, lengths, n1t, qkv, probs, per_seq(gatt), attended)
     lead_sum = small_call(add_kernel, "add_lead", shape(glead_own.shape, BF16), glead_own, swap(glead_other))
     lead_sum, rest_parts = lax.optimization_barrier((lead_sum, rest_parts))
     lead_parts = lax.all_to_all(lead_sum.reshape(chips, shard_rows, 10 * HD), "batch", 0, 0)
-    input_grad, terms = input_gradient(tokens, gp, per_seq(gmid), wpairs, norms, gnorm_two)
+    input_grad, terms, block_out = input_gradient(
+        tokens, gp, per_seq(gmid), wpairs, norms, gnorm_two, per_seq(mid), act, weights
+    )
     rest_mine, rest_theirs = small_call(
         sum_rest_kernel, "sum_rest", [shape(rest.shape, F32), shape(rest.shape, BF16)], half, rest_parts
     )
@@ -743,7 +776,7 @@
     lead_shard, rest_shard, message = small_call(
         sum_lead_kernel,
         "sum_lead",
-        [shape(lead.shape[1:], F32), shape(rest.shape, F32), shape(terms.shape, F32)],
+        [shape(lead.shape, F32), shape(rest.shape, F32), shape(terms.shape, F32)],
         lead_parts,
         rest_mine,
         rest_far,
@@ -776,7 +809,7 @@
     grad_norm, qkv_next, out_next, up_next, down_next, norm_next = results[:6]
     qkv_states, out_states, up_states, down_states, norm_states, norm_grads = results[6:]
     return (
-        per_seq(block_out),
+        block_out,
         input_grad,
         grad_norm.reshape(()),
         qkv_next.transpose(1, 0, 2),

time: 173 us -> 166 us (0.960)
  waiting for transfers between devices: 33.4 us -> 21.8 us
  starting transfers between devices: 38.1 us -> 41 us
    all_to_all x1, starting transfers between devices: 12.3 us -> 6.75 us  [per_device(): lax.all_to_all(lead_sum.reshape(chips, shard_rows, 10 * HD), 'batch', 0, 0)]
    pallas_call x1, Pallas kernels: 9.6 us -> 15.1 us  [input_gradient(): pl.pallas_call(input_kernel, grid=(seqs, rows // DB), in_specs=[full, pl....]
    ppermute x1 -> x2, waiting for transfers between devices: 7.39 us -> 2.41 us  [the longest x1 2.41 us: per_device(): lead_far = lax.ppermute(lead, 'batch', far_pairs)]
    ppermute x1, waiting for transfers between devices: 4.97 us -> 0.01 us  [per_device(): rest_far = lax.ppermute(rest_theirs, 'batch', far_pairs)]
    ppermute x1 -> x2, starting transfers between devices: 2.89 us -> 6.91 us  [the longest x1 4.04 us: per_device(): lead_far = lax.ppermute(lead, 'batch', far_pairs)]
    all_to_all x1, starting transfers between devices: 8.31 us -> 4.74 us  [per_device(): lead_own = lax.all_to_all(lead_pair, 'batch', 0, 0, axis_index_groups=teams)]
    ppermute x5, starting transfers between devices: 0.22 us -> 3.22 us  [swap(): return lax.ppermute(values, 'head', [(0, 1), (1, 0)])]
    all_to_all x1, starting transfers between devices: 3.89 us -> 6.75 us  [per_device(): lax.all_to_all(rest_sum, 'batch', 0, 0, axis_index_groups=teams)]
  transfers between devices with their start and end apart: 15 -> 16, of which waited for: 10 -> 9; matrix products, arithmetic and copies ran while one was open for 0% -> 0% of each run, Pallas kernels for 36% -> 39%
where the time goes in v7:
time: 166 us
  Pallas kernels  101 us (61%)
  starting transfers between devices  41 us (25%)
  waiting for transfers between devices  21.8 us (13%)
    pallas_call x1, Pallas kernels, middle(): pl.pallas_call(functools.partial(middle_kernel, units), grid=(total // FB...  31.2 us
    pallas_call x1, Pallas kernels, backward(): pl.pallas_call(backward_kernel, grid=(seqs,), in_specs=[IN_SMEM, IN_SMEM,...  20.8 us
    pallas_call x1, Pallas kernels, forward(): pl.pallas_call(functools.partial(forward_kernel, chips, part), grid=(seqs...  19.8 us
    pallas_call x1, Pallas kernels, input_gradient(): pl.pallas_call(input_kernel, grid=(seqs, rows // DB), in_specs=[full, pl....  15.1 us
    ppermute x4, waiting for transfers between devices, per_device(): lax.ppermute(message, 'batch', [(i, i ^ stride) for i in range(chips)])  11.2 us
    ppermute x5, waiting for transfers between devices, swap(): return lax.ppermute(values, 'head', [(0, 1), (1, 0)])  8.17 us
    pallas_call x8, Pallas kernels, small_call(): pl.pallas_call(kernel, in_specs=[IN_SMEM if a.dtype == jnp.int32 else in_...  7.46 us
    pallas_call x1, Pallas kernels, prepare(): pl.pallas_call(functools.partial(prepare_kernel, seq_rows), grid=(total /...  7.01 us
  transfers between devices with their start and end apart: 16, of which 9 were waited for; matrix products, arithmetic and copies ran while one was open for 0% of the time, Pallas kernels for 39%

profile of v7, /device:TPU:0, one launch (start us, length us, event | category | flops | bytes accessed | tf_op | source)
XLA Modules:
  0.0 166.0 jit_solution(10363275510277182908)
XLA Ops:
  0.6 1.7 %pack_weights.1 = (bf16[24,640]{1,0:T(8,128)(2,1)}, bf16[24,1792]{1,0:T(8,128)(2,1)}) custom-call(f32[3,24,192]{2,1,0:T(8,128)} %bitcast.30, f32[24,192]{1,0:T(8,128)} %bitcast.35, f32[24,768]{1,0:T(8,128)} %up_ref.3, f32[24,768]{1,0:T(8,128)} %bitcast.32, f32[1,48]{1,0:T(1,128)} %bitcast.37), custom_call_target="tpu_custom_call" | custom-call | flops 2000000000 | bytes 1000000 | tf_op jit(solution)/shard_map/pack_weights/pallas_call | solution.py:687
  2.3 4.0 %collective-permute-start = (bf16[24,640]{1,0:T(8,128)(2,1)}, bf16[24,640]{1,0:T(8,128)(2,1)S(1)}, u32[]{:S(2)}, u32[]{:S(2)}) collective-permute-start(bf16[24,640]{1,0:T(8,128)(2,1)} %get-tuple-element.68.own_ref), channel_id=1, source_target_pairs={{0,16},{2,18},{4,20},{6,22},{8,24},{10,26},{12,28},{14,30},{16,0},... | collective-permute-start | bytes 92168 | tf_op jit(solution)/shard_map/ppermute | solution.py:740
  6.4 2.4 %collective-permute-done.far_ref = bf16[24,640]{1,0:T(8,128)(2,1)S(1)} collective-permute-done((bf16[24,640]{1,0:T(8,128)(2,1)}, bf16[24,640]{1,0:T(8,128)(2,1)S(1)}, u32[]{:S(2)}, u32[]{:S(2)}) %collective-permute-start) | collective-permute-done | bytes 30752 | tf_op jit(solution)/shard_map/ppermute | solution.py:740
  9.5 0.8 pair_lead.1
  10.3 4.7 %all-to-all-start = ((bf16[8,2,24,640]{3,2,1,0:T(8,128)(2,1)}), bf16[8,2,24,640]{3,2,1,0:T(8,128)(2,1)S(1)}, u32[]{:S(2)}, u32[]{:S(2)}) async-start(bf16[8,2,24,640]{3,2,1,0:T(8,128)(2,1)} %pair_lead.1), calls=%async_computation | async-start | bytes 983040 | tf_op jit(solution)/shard_map/all_to_all | solution.py:744
  15.1 2.9 %collective-permute-start.1 = (bf16[24,1792]{1,0:T(8,128)(2,1)S(1)}, bf16[24,1792]{1,0:T(8,128)(2,1)S(1)}, u32[]{:S(2)}, u32[]{:S(2)}) collective-permute-start(bf16[24,1792]{1,0:T(8,128)(2,1)S(1)} %copy-done.3), channel_id=1, source_target_pairs={{0,16},{2,18},{4,20},{6,22},{8,24},{10,26},{12,28},{14,30},{16,0},... | collective-permute-start | bytes 258056 | tf_op jit(solution)/shard_map/ppermute | solution.py:741
  18.0 7.0 %prepare.1 = (f32[2560,384]{1,0:T(8,128)}, bf16[2560,384]{1,0:T(8,128)(2,1)}, bf16[384,2560]{1,0:T(8,128)(2,1)}) custom-call(s32[1]{0:T(128)} %bitcast.side_ref, s32[8]{0:T(128)} %len_ref.5, bf16[2560,384]{1,0:T(8,128)(2,1)} %bitcast.41, bf16[2560,384]{1,0:T(8,128)(2,1)} %bitcast.40), custom_call_target="tpu_custom_call" | custom-call | flops 5000000000 | bytes 1000000 | tf_op jit(solution)/shard_map/prepare/pallas_call | solution.py:123
  25.0 1.2 pair_rest.1
  26.2 5.2 %all-to-all-start.1 = ((bf16[8,2,24,1792]{3,2,1,0:T(8,128)(2,1)}), bf16[8,2,24,1792]{3,2,1,0:T(8,128)(2,1)S(1)}, u32[]{:S(2)}, u32[]{:S(2)}) async-start(bf16[8,2,24,1792]{3,2,1,0:T(8,128)(2,1)} %pair_rest.1), calls=%async_computation.1 | async-start | bytes 2752512 | tf_op jit(solution)/shard_map/all_to_all | solution.py:751
  31.4 19.8 %attention_forward.1 = (bf16[4,384,640]{2,1,0:T(8,128)(2,1)}, bf16[4,3,640,384]{3,2,1,0:T(8,128)(2,1)}, bf16[4,640,384]{2,1,0:T(8,128)(2,1)}, f32[4,640,384]{2,1...) custom-call(s32[1]{0:T(128)} %bitcast.side_ref, ...), custom_call_target="tpu_custom_call" | custom-call | flops 24000000000 | bytes 1000000 | tf_op jit(solution)/shard_map/attention_forward/pallas_call | solution.py:239
  51.2 0.9 collective-permute-start.3
  52.1 2.8 %collective-permute-done.3.other_ref = bf16[8,2,24,1792]{3,2,1,0:T(8,128)(2,1)S(1)} collective-permute-done((bf16[8,2,24,1792]{3,2,1,0:T(8,128)(2,1)S(1)}, bf16[8,2,24,1792]{3,2,1,0:T(8,128)(2,1)S(1)}, u32[]{:S(2)}, u32[]{:S(2)}) %collective-permute-start.3) | collective-permute-done | bytes 1376288 | tf_op jit(solution)/shard_map/ppermute | solution.py:699
  54.8 31.2 %feed_forward.1 = (f32[2560,384]{1,0:T(8,128)}, bf16[2,2560,768]{2,1,0:T(8,128)(2,1)}, f32[2560,384]{1,0:T(8,128)}, bf16[2560,384]{1,0:T(8,128)(2,1)S(1)}, bf16[...) custom-call(bf16[2560,384]{1,0:T(8,128)(2,1)} %bitcast.42, ...), custom_call_target="tpu_custom_call" | custom-call | flops 35999997952 | bytes 1000000 | tf_op jit(solution)/shard_map/feed_forward/pallas_call | solution.py:351
  86.5 2.8 %collective-permute-done.4.right_ref = bf16[384,1792]{1,0:T(8,128)(2,1)S(1)} collective-permute-done((bf16[384,1792]{1,0:T(8,128)(2,1)S(1)}, bf16[384,1792]{1,0:T(8,128)(2,1)S(1)}, u32[]{:S(2)}, u32[]{:S(2)}) %collective-permute-start.4) | collective-permute-done | bytes 1376288 | tf_op jit(solution)/shard_map/ppermute | solution.py:699
  89.2 1.4 add_rest.1
  90.6 6.8 %all-to-all-start.2 = ((bf16[8,2,24,1792]{3,2,1,0:T(8,128)(2,1)}), bf16[8,2,24,1792]{3,2,1,0:T(8,128)(2,1)S(1)}, u32[]{:S(2)}, u32[]{:S(2)}) async-start(bf16[8,2,24,1792]{3,2,1,0:T(8,128)(2,1)} %add_rest.1), calls=%async_computation.2 | async-start | bytes 2752512 | tf_op jit(solution)/shard_map/all_to_all | solution.py:764
  97.4 20.8 %attention_backward.1 = (bf16[4,640,1152]{2,1,0:T(8,128)(2,1)}, bf16[384,640]{1,0:T(8,128)(2,1)S(1)}, bf16[384,640]{1,0:T(8,128)(2,1)S(1)}) custom-call(s32[1]{0:T(128)} %bitcast.side_ref, s32[8]{0:T(128)S(1)} %copy-done.12, bf16[4,384,640]{2,1,0:T(8,128)(2,1)} %get-tuple-element.75.n1t_ref, bf16[4,3,640,384]{3,2,1,0:T(8,128)(2,1)} %get-tuple-element.76.qkv_ref, ...), custom_call_target="tpu_custom_call" | custom-call | flops 27000000512 | bytes 1000000 | tf_op jit(solution)/shard_map/attention_backward/pallas_call | solution.py:488
  118.2 1.8 %collective-permute-start.5 = (bf16[384,640]{1,0:T(8,128)(2,1)S(1)}, bf16[384,640]{1,0:T(8,128)(2,1)S(1)}, u32[]{:S(2)}, u32[]{:S(2)}) collective-permute-start(bf16[384,640]{1,0:T(8,128)(2,1)S(1)} %get-tuple-element.100), channel_id=1, source_target_pairs={{0,1},{1,0},{2,3},{3,2},{4,5},{5,4},{6,7},{7,6},{8,9},{9,8},{10,11... | collective-permute-start | bytes 1474568 | tf_op jit(solution)/shard_map/ppermute | solution.py:699
  120.0 1.5 collective-permute-done.5.right_ref
  121.5 0.9 add_lead.1
  122.4 6.8 %all-to-all-start.3 = ((bf16[16,24,640]{2,1,0:T(8,128)(2,1)}), bf16[16,24,640]{2,1,0:T(8,128)(2,1)S(1)}, u32[]{:S(2)}, u32[]{:S(2)}) async-start(bf16[16,24,640]{2,1,0:T(8,128)(2,1)} %bitcast.15), calls=%async_computation.3 | async-start | bytes 983040 | tf_op jit(solution)/shard_map/all_to_all | solution.py:768
  129.4 2.9 %collective-permute-start.6 = (bf16[24,1792]{1,0:T(8,128)(2,1)S(1)}, bf16[24,1792]{1,0:T(8,128)(2,1)S(1)}, u32[]{:S(2)}, u32[]{:S(2)}) collective-permute-start(bf16[24,1792]{1,0:T(8,128)(2,1)S(1)} %get-tuple-element.105), channel_id=1, source_target_pairs={{0,16},{2,18},{4,20},{6,22},{8,24},{10,26},{12,28},{14,30},{16,0},... | collective-permute-start | bytes 258056 | tf_op jit(solution)/shard_map/ppermute | solution.py:775
  132.3 15.1 %input_gradient.1 = (f32[4,640,384]{2,1,0:T(8,128)}, f32[8,384]{1,0:T(8,128)S(1)}, bf16[4,640,384]{2,1,0:T(8,128)(2,1)}) custom-call(bf16[4,640,384]{2,1,0:T(8,128)(2,1)} %tok_ref.1, bf16[4,640,1152]{2,1,0:T(8,128)(2,1)} %get-tuple-element.90.gp_ref, f32[4,640,384]{2,1,0:T(8,128)} %bitcast.44, bf16[384,1152]{1,0:T(8,128)(2,1)S(1)} %get-tuple-element.92.w_ref, ...), custom_call_target="tpu_custom_call" | custom-call | flops 12999999488 | bytes 1000000 | tf_op jit(solution)/shard_map/input_gradient/pallas_call | solution.py:539
  147.7 1.2 collective-permute-done.7
  148.9 1.5 collective-permute-start.8
  150.3 2.2 %collective-permute-done.8 = f32[8,384]{1,0:T(8,128)S(1)} collective-permute-done((f32[8,384]{1,0:T(8,128)S(1)}, f32[8,384]{1,0:T(8,128)S(1)}, u32[]{:S(2)}, u32[]{:S(2)}) %collective-permute-start.8) | collective-permute-done | bytes 12320 | tf_op jit(solution)/shard_map/ppermute | solution.py:788
  152.6 1.5 collective-permute-start.9
  154.0 2.2 %collective-permute-done.9 = f32[8,384]{1,0:T(8,128)S(1)} collective-permute-done((f32[8,384]{1,0:T(8,128)S(1)}, f32[8,384]{1,0:T(8,128)S(1)}, u32[]{:S(2)}, u32[]{:S(2)}) %collective-permute-start.9) | collective-permute-done | bytes 12320 | tf_op jit(solution)/shard_map/ppermute | solution.py:788
  156.3 1.5 collective-permute-start.10
  157.7 2.2 %collective-permute-done.10 = f32[8,384]{1,0:T(8,128)S(1)} collective-permute-done((f32[8,384]{1,0:T(8,128)S(1)}, f32[8,384]{1,0:T(8,128)S(1)}, u32[]{:S(2)}, u32[]{:S(2)}) %collective-permute-start.10) | collective-permute-done | bytes 12320 | tf_op jit(solution)/shard_map/ppermute | solution.py:788
  160.1 4.5 %collective-permute-done.11 = f32[8,384]{1,0:T(8,128)S(1)} collective-permute-done((f32[8,384]{1,0:T(8,128)S(1)}, f32[8,384]{1,0:T(8,128)S(1)}, u32[]{:S(2)}, u32[]{:S(2)}) %collective-permute-start.11) | collective-permute-done | bytes 12320 | tf_op jit(solution)/shard_map/ppermute | solution.py:788
  164.7 1.2 update_weights.1
  (48 shorter events, 1.8 us)
Async XLA Ops:
  2.3 6.4 %collective-permute-start = (bf16[24,640]{1,0:T(8,128)(2,1)}, bf16[24,640]{1,0:T(8,128)(2,1)S(1)}, u32[]{:S(2)}, u32[]{:S(2)}) collective-permute-start(bf16[24,640]{1,0:T(8,128)(2,1)} %get-tuple-element.68.own_ref), channel_id=1, source_target_pairs={{0,16},{2,18},{4,20},{6,22},{8,24},{10,26},{12,28},{14,30},{16,0},... | collective-permute-start | bytes 92168 | tf_op jit(solution)/shard_map/ppermute | solution.py:740
  8.8 0.8 copy-start.8
  9.5 5.6 %copy-start.3 = (bf16[24,1792]{1,0:T(8,128)(2,1)S(1)}, bf16[24,1792]{1,0:T(8,128)(2,1)}, u32[]{:S(2)}) copy-start(bf16[24,1792]{1,0:T(8,128)(2,1)} %get-tuple-element.69.own_ref) | copy-start | bytes 258052
  10.3 15.8 %all-to-all-start = ((bf16[8,2,24,640]{3,2,1,0:T(8,128)(2,1)}), bf16[8,2,24,640]{3,2,1,0:T(8,128)(2,1)S(1)}, u32[]{:S(2)}, u32[]{:S(2)}) async-start(bf16[8,2,24,640]{3,2,1,0:T(8,128)(2,1)} %pair_lead.1), calls=%async_computation | async-start | bytes 983040 | tf_op jit(solution)/shard_map/all_to_all | solution.py:744
  15.1 9.9 %collective-permute-start.1 = (bf16[24,1792]{1,0:T(8,128)(2,1)S(1)}, bf16[24,1792]{1,0:T(8,128)(2,1)S(1)}, u32[]{:S(2)}, u32[]{:S(2)}) collective-permute-start(bf16[24,1792]{1,0:T(8,128)(2,1)S(1)} %copy-done.3), channel_id=1, source_target_pairs={{0,16},{2,18},{4,20},{6,22},{8,24},{10,26},{12,28},{14,30},{16,0},... | collective-permute-start | bytes 258056 | tf_op jit(solution)/shard_map/ppermute | solution.py:741
  26.2 5.2 %copy-start.10 = (s32[8,640]{1,0:T(8,128)S(1)}, s32[8,640]{1,0:T(8,128)}, u32[]{:S(2)}) copy-start(s32[8,640]{1,0:T(8,128)} %mask_ref.1) | copy-start | bytes 61444
  26.2 5.2 %copy-start.12 = (s32[8]{0:T(128)S(1)}, s32[8]{0:T(128)}, u32[]{:S(2)}) copy-start(s32[8]{0:T(128)} %len_ref.5) | copy-start | bytes 100
  26.2 5.2 %collective-permute-start.2 = (bf16[8,2,24,640]{3,2,1,0:T(8,128)(2,1)S(1)}, bf16[8,2,24,640]{3,2,1,0:T(8,128)(2,1)S(1)}, u32[]{:S(2)}, u32[]{:S(2)}) collective-permute-start(bf16[8,2,24,640]{3,2,1,0:T(8,128)(2,1)S(1)} %all-to-all-done.own_ref), channel_id=1, source_target_pairs={{0,1},{1,0},{2,3},{3,2},{4,5},{5,4},{6,7},{7,6},{8,9},{9,8},{10,11... | collective-permute-start | bytes 1474568 | tf_op jit(solution)/shard_map/ppermute | solution.py:699
  26.2 25.1 %all-to-all-start.1 = ((bf16[8,2,24,1792]{3,2,1,0:T(8,128)(2,1)}), bf16[8,2,24,1792]{3,2,1,0:T(8,128)(2,1)S(1)}, u32[]{:S(2)}, u32[]{:S(2)}) async-start(bf16[8,2,24,1792]{3,2,1,0:T(8,128)(2,1)} %pair_rest.1), calls=%async_computation.1 | async-start | bytes 2752512 | tf_op jit(solution)/shard_map/all_to_all | solution.py:751
  51.2 3.6 %collective-permute-start.3 = (bf16[8,2,24,1792]{3,2,1,0:T(8,128)(2,1)S(1)}, bf16[8,2,24,1792]{3,2,1,0:T(8,128)(2,1)S(1)}, u32[]{:S(2)}, u32[]{:S(2)}) collective-permute-start(bf16[8,2,24,1792]{3,2,1,0:T(8,128)(2,1)S(1)} %all-to-all-done.1.own_ref), channel_id=1, source_target_pairs={{0,1},{1,0},{2,3},{3,2},{4,5},{5,4},{6,7},{7,6},{8,9},{9,8},{10,11... | collective-permute-start | bytes 4128776 | tf_op jit(solution)/shard_map/ppermute | solution.py:699
  86.0 4.6 %copy-start.14 = (bf16[2560,384]{1,0:T(8,128)(2,1)}, bf16[2560,384]{1,0:T(8,128)(2,1)S(1)}, u32[]{:S(2)}) copy-start(bf16[2560,384]{1,0:T(8,128)(2,1)S(1)} %get-tuple-element.89) | copy-start | bytes 5898244
  86.0 3.2 %collective-permute-start.4 = (bf16[384,1792]{1,0:T(8,128)(2,1)S(1)}, bf16[384,1792]{1,0:T(8,128)(2,1)S(1)}, u32[]{:S(2)}, u32[]{:S(2)}) collective-permute-start(bf16[384,1792]{1,0:T(8,128)(2,1)S(1)} %get-tuple-element.87), channel_id=1, source_target_pairs={{0,1},{1,0},{2,3},{3,2},{4,5},{5,4},{6,7},{7,6},{8,9},{9,8},{10,11... | collective-permute-start | bytes 4128776 | tf_op jit(solution)/shard_map/ppermute | solution.py:699
  90.6 31.8 %all-to-all-start.2 = ((bf16[8,2,24,1792]{3,2,1,0:T(8,128)(2,1)}), bf16[8,2,24,1792]{3,2,1,0:T(8,128)(2,1)S(1)}, u32[]{:S(2)}, u32[]{:S(2)}) async-start(bf16[8,2,24,1792]{3,2,1,0:T(8,128)(2,1)} %add_rest.1), calls=%async_computation.2 | async-start | bytes 2752512 | tf_op jit(solution)/shard_map/all_to_all | solution.py:764
  118.2 3.3 %collective-permute-start.5 = (bf16[384,640]{1,0:T(8,128)(2,1)S(1)}, bf16[384,640]{1,0:T(8,128)(2,1)S(1)}, u32[]{:S(2)}, u32[]{:S(2)}) collective-permute-start(bf16[384,640]{1,0:T(8,128)(2,1)S(1)} %get-tuple-element.100), channel_id=1, source_target_pairs={{0,1},{1,0},{2,3},{3,2},{4,5},{5,4},{6,7},{7,6},{8,9},{9,8},{10,11... | collective-permute-start | bytes 1474568 | tf_op jit(solution)/shard_map/ppermute | solution.py:699
  122.4 24.9 %all-to-all-start.3 = ((bf16[16,24,640]{2,1,0:T(8,128)(2,1)}), bf16[16,24,640]{2,1,0:T(8,128)(2,1)S(1)}, u32[]{:S(2)}, u32[]{:S(2)}) async-start(bf16[16,24,640]{2,1,0:T(8,128)(2,1)} %bitcast.15), calls=%async_computation.3 | async-start | bytes 983040 | tf_op jit(solution)/shard_map/all_to_all | solution.py:768
  129.4 18.0 %collective-permute-start.6 = (bf16[24,1792]{1,0:T(8,128)(2,1)S(1)}, bf16[24,1792]{1,0:T(8,128)(2,1)S(1)}, u32[]{:S(2)}, u32[]{:S(2)}) collective-permute-start(bf16[24,1792]{1,0:T(8,128)(2,1)S(1)} %get-tuple-element.105), channel_id=1, source_target_pairs={{0,16},{2,18},{4,20},{6,22},{8,24},{10,26},{12,28},{14,30},{16,0},... | collective-permute-start | bytes 258056 | tf_op jit(solution)/shard_map/ppermute | solution.py:775
  147.4 17.2 %copy-start = (f32[2,24,3,192]{3,1,2,0:T(8,128)S(1)}, f32[2,24,3,192]{3,1,2,0:T(8,128)}, u32[]{:S(2)}) copy-start(f32[2,24,3,192]{3,1,2,0:T(8,128)} %param.23) | copy-start | bytes 331780
  147.4 17.2 %copy-start.1 = (f32[2,24,768]{2,1,0:T(8,128)S(1)}, f32[2,24,768]{2,1,0:T(8,128)}, u32[]{:S(2)}) copy-start(f32[2,24,768]{2,1,0:T(8,128)} %up_m_ref.1) | copy-start | bytes 442372
  147.4 17.2 %copy-start.2 = (f32[2,768,24]{1,2,0:T(8,128)S(1)}, f32[2,768,24]{1,2,0:T(8,128)}, u32[]{:S(2)}) copy-start(f32[2,768,24]{1,2,0:T(8,128)} %param.26) | copy-start | bytes 442372
  147.4 17.2 %copy-start.4 = (f32[24,3,192]{2,0,1:T(8,128)S(1)}, f32[24,3,192]{2,0,1:T(8,128)}, u32[]{:S(2)}) copy-start(f32[24,3,192]{2,0,1:T(8,128)} %param.18) | copy-start | bytes 165892
  147.4 17.2 %copy-start.5 = (f32[24,768]{1,0:T(8,128)S(1)}, f32[24,768]{1,0:T(8,128)}, u32[]{:S(2)}) copy-start(f32[24,768]{1,0:T(8,128)} %up_ref.3) | copy-start | bytes 221188
  147.4 17.2 %copy-start.6 = (f32[768,24]{0,1:T(8,128)S(1)}, f32[768,24]{0,1:T(8,128)}, u32[]{:S(2)}) copy-start(f32[768,24]{0,1:T(8,128)} %param.21) | copy-start | bytes 221188
  147.5 17.2 %copy-start.7 = (f32[2,192,24]{1,2,0:T(8,128)S(1)}, f32[2,192,24]{1,2,0:T(8,128)}, u32[]{:S(2)}) copy-start(f32[2,192,24]{1,2,0:T(8,128)} %param.24) | copy-start | bytes 110596
  147.5 17.2 %copy-start.9 = (f32[192,24]{0,1:T(8,128)S(1)}, f32[192,24]{0,1:T(8,128)}, u32[]{:S(2)}) copy-start(f32[192,24]{0,1:T(8,128)} %param.19) | copy-start | bytes 55300
  147.5 17.2 %copy-start.11 = (f32[2,48]{1,0:T(2,128)S(1)}, f32[2,48]{1,0:T(2,128)}, u32[]{:S(2)}) copy-start(f32[2,48]{1,0:T(2,128)} %norm_m_ref.1) | copy-start | bytes 1156
  147.5 17.2 %copy-start.13 = (f32[48]{0:T(128)S(1)}, f32[48]{0:T(128)}, u32[]{:S(2)}) copy-start(f32[48]{0:T(128)} %param.22) | copy-start | bytes 580
  147.6 1.2 collective-permute-start.7
  148.9 3.7 %collective-permute-start.8 = (f32[8,384]{1,0:T(8,128)S(1)}, f32[8,384]{1,0:T(8,128)S(1)}, u32[]{:S(2)}, u32[]{:S(2)}) collective-permute-start(f32[8,384]{1,0:T(8,128)S(1)} %add.20), channel_id=1, source_target_pairs={{0,2},{2,0},{4,6},{6,4},{8,10},{10,8},{12,14},{14,12},{16,18},{18,... | collective-permute-start | bytes 36872 | tf_op jit(solution)/shard_map/ppermute | solution.py:788
  152.6 3.7 %collective-permute-start.9 = (f32[8,384]{1,0:T(8,128)S(1)}, f32[8,384]{1,0:T(8,128)S(1)}, u32[]{:S(2)}, u32[]{:S(2)}) collective-permute-start(f32[8,384]{1,0:T(8,128)S(1)} %add.21), channel_id=1, source_target_pairs={{0,4},{2,6},{4,0},{6,2},{8,12},{10,14},{12,8},{14,10},{16,20},{18,... | collective-permute-start | bytes 36872 | tf_op jit(solution)/shard_map/ppermute | solution.py:788
  156.3 3.7 %collective-permute-start.10 = (f32[8,384]{1,0:T(8,128)S(1)}, f32[8,384]{1,0:T(8,128)S(1)}, u32[]{:S(2)}, u32[]{:S(2)}) collective-permute-start(f32[8,384]{1,0:T(8,128)S(1)} %add.22), channel_id=1, source_target_pairs={{0,8},{2,10},{4,12},{6,14},{8,0},{10,2},{12,4},{14,6},{16,24},{18,... | collective-permute-start | bytes 36872 | tf_op jit(solution)/shard_map/ppermute | solution.py:788
  160.0 4.6 %collective-permute-start.11 = (f32[8,384]{1,0:T(8,128)S(1)}, f32[8,384]{1,0:T(8,128)S(1)}, u32[]{:S(2)}, u32[]{:S(2)}) collective-permute-start(f32[8,384]{1,0:T(8,128)S(1)} %add.23), channel_id=1, source_target_pairs={{0,16},{2,18},{4,20},{6,22},{8,24},{10,26},{12,28},{14,30},{16,0},... | collective-permute-start | bytes 36872 | tf_op jit(solution)/shard_map/ppermute | solution.py:788

commit v8 on v7

--- a/solution.py
+++ b/solution.py
@@ -118,13 +118,13 @@
     seqs, seq_rows, width = tokens.shape
     total = seqs * seq_rows
     flat = lambda a: a.reshape(total, width)
-    rowspec = pl.BlockSpec((FB, width), lambda s: (s, 0))
+    rowspec = pl.BlockSpec((DB, width), lambda s: (s, 0))
     shape = jax.ShapeDtypeStruct
     return pl.pallas_call(
         functools.partial(prepare_kernel, seq_rows),
-        grid=(total // FB,),
+        grid=(total // DB,),
         in_specs=[IN_SMEM, IN_SMEM, rowspec, rowspec],
-        out_specs=[rowspec, rowspec, pl.BlockSpec((width, FB), lambda s: (0, s))],
+        out_specs=[rowspec, rowspec, pl.BlockSpec((width, DB), lambda s: (0, s))],
         out_shape=[shape((total, width), F32), shape((total, width), BF16), shape((width, total), BF16)],
         compiler_params=LIMIT_P,
         cost_estimate=cost(5),
@@ -268,7 +268,7 @@
 def middle_kernel(
     units, tok_ref, gb_ref, gbt_ref, att_ref, linv_ref, own_ref, other_ref, norms_ref,
     mid_ref, act_ref, gmid_ref, gatt_ref, gown_ref, gother_ref, gnorm_ref, halves,
-    wo_ref, gout_ref, gup_ref, gdown_ref,
+    wo_ref, gout_ref, gup_ref, gdown_ref, gh_ref,
 ):
     step = pl.program_id(0)
     rows, width = tok_ref.shape
@@ -288,26 +288,31 @@
     x = tok_ref[...].astype(F32)
     att = att_ref[...]
     mid = x + mm(att, wo_ref[...], NT)
+    gb, gbt = gb_ref[...], gbt_ref[...]
+    early = [mm(gb, halves[0, :, units + c * FC : units + (c + 1) * FC]) for c in range(2)]
     normal, rs = normalize(mid)
     gain, shift = norms_ref[2:3, :], norms_ref[3:4, :]
     n2 = (normal * gain + shift).astype(BF16)
     n2t = n2.T
-    gb, gbt = gb_ref[...], gbt_ref[...]
     mid_ref[...] = mid
     sums = [jnp.zeros_like(mid)]
 
     def begin(half, c):
         wu = halves[half, :, c * FC : (c + 1) * FC]
         wd = halves[half, :, units + c * FC : units + (c + 1) * FC]
-        return half, c, wu, wd, mm(n2, wu), mm(gb, wd)
+        ga = early[c] if half == 0 and c < len(early) else mm(gb, wd)
+        return half, c, wu, wd, mm(n2, wu), ga
 
     def finish(half, c, wu, wd, h, ga):
         cols = slice(c * FC, (c + 1) * FC)
         act, gh = gelu_both(h, ga)
         act_ref[half, :, cols] = act
         sums[0] = sums[0] + mm(gh, wu, NT)
-        gup_ref[half, :, cols] += mm(n2t, gh)
-        gdown_ref[half, :, cols] += mm(gbt, act)
+        gh_ref[half, :, cols] = gh
+
+    def weigh(half):
+        gup_ref[half] += mm(n2t, gh_ref[half])
+        gdown_ref[half] += mm(gbt, act_ref[half])
 
     pending = None
     for half in range(2):
@@ -316,12 +321,15 @@
             if pending is not None:
                 finish(*pending)
             pending = fresh
+        if half == 1:
+            weigh(0)
     finish(*pending)
     gtwo = sums[0]
     gnorm_ref[0:8, :] += jnp.sum((gtwo * normal).reshape(rows // 8, 8, width), axis=0)
     gnorm_ref[8:16, :] += jnp.sum(gtwo.reshape(rows // 8, 8, width), axis=0)
     gmid = gb.astype(F32) + norm_backward(normal, rs, gtwo * gain)
     gmid_ref[...] = gmid
+    weigh(1)
     gm = gmid.astype(BF16)
     gout_ref[...] += mm(gm, att, TN)
     gatt_ref[...] = (mm(gm, wo_ref[...]) * linv_ref[...]).astype(BF16)
@@ -386,6 +394,7 @@
             pltpu.VMEM((width, width), F32),
             pltpu.VMEM((2, width, units), F32),
             pltpu.VMEM((2, width, units), F32),
+            pltpu.VMEM((2, FB, units), BF16),
         ],
         compiler_params=LIMIT_B,
         cost_estimate=cost(36),

time: 166 us -> 164 us (0.988); the launches traced: 166 us -> 162 us
  starting transfers between devices: 41 us -> 38.1 us
  Pallas kernels: 101 us -> 99.2 us
    ppermute x5, starting transfers between devices: 3.22 us -> 0.28 us  [swap(): return lax.ppermute(values, 'head', [(0, 1), (1, 0)])]
  transfers between devices with their start and end apart: 16 -> 16, of which waited for: 9 -> 9; matrix products, arithmetic and copies ran while one was open for 0% -> 0% of each run, Pallas kernels for 39% -> 40%
where the time goes in v8:
time: 164 us; the launch traced here: 162 us
  Pallas kernels  99.2 us (60%)
  starting transfers between devices  38.1 us (23%)
  waiting for transfers between devices  22.7 us (14%)
    pallas_call x1, Pallas kernels, middle(): pl.pallas_call(functools.partial(middle_kernel, units), grid=(total // FB...  29.7 us
    pallas_call x1, Pallas kernels, backward(): pl.pallas_call(backward_kernel, grid=(seqs,), in_specs=[IN_SMEM, IN_SMEM,...  21.1 us
    pallas_call x1, Pallas kernels, forward(): pl.pallas_call(functools.partial(forward_kernel, chips, part), grid=(seqs...  19.7 us
    pallas_call x1, Pallas kernels, input_gradient(): pl.pallas_call(input_kernel, grid=(seqs, rows // DB), in_specs=[full, pl....  15.1 us
    ppermute x4, waiting for transfers between devices, per_device(): lax.ppermute(message, 'batch', [(i, i ^ stride) for i in range(chips)])  11.2 us
    ppermute x5, waiting for transfers between devices, swap(): return lax.ppermute(values, 'head', [(0, 1), (1, 0)])  9.14 us
    pallas_call x8, Pallas kernels, small_call(): pl.pallas_call(kernel, in_specs=[IN_SMEM if a.dtype == jnp.int32 else in_...  7.46 us
    all_to_all x1, starting transfers between devices, per_device(): lax.all_to_all(lead_sum.reshape(chips, shard_rows, 10 * HD), 'batch', 0, 0)  6.99 us
  transfers between devices with their start and end apart: 16, of which 9 were waited for; matrix products, arithmetic and copies ran while one was open for 0% of the time, Pallas kernels for 40%

profile of v8, /device:TPU:0, one launch (start us, length us, event | category | flops | bytes accessed | tf_op | source)
XLA Modules:
  0.0 162.0 jit_solution(4209720692757456484)
XLA Ops:
  0.6 1.7 %pack_weights.1 = (bf16[24,640]{1,0:T(8,128)(2,1)}, bf16[24,1792]{1,0:T(8,128)(2,1)}) custom-call(f32[3,24,192]{2,1,0:T(8,128)} %bitcast.30, f32[24,192]{1,0:T(8,128)} %bitcast.35, f32[24,768]{1,0:T(8,128)} %up_ref.3, f32[24,768]{1,0:T(8,128)} %bitcast.32, f32[1,48]{1,0:T(1,128)} %bitcast.37), custom_call_target="tpu_custom_call" | custom-call | flops 2000000000 | bytes 1000000 | tf_op jit(solution)/shard_map/pack_weights/pallas_call | solution.py:696
  2.3 4.0 %collective-permute-start = (bf16[24,640]{1,0:T(8,128)(2,1)}, bf16[24,640]{1,0:T(8,128)(2,1)S(1)}, u32[]{:S(2)}, u32[]{:S(2)}) collective-permute-start(bf16[24,640]{1,0:T(8,128)(2,1)} %get-tuple-element.68.own_ref), channel_id=1, source_target_pairs={{0,16},{2,18},{4,20},{6,22},{8,24},{10,26},{12,28},{14,30},{16,0},... | collective-permute-start | bytes 92168 | tf_op jit(solution)/shard_map/ppermute | solution.py:749
  6.4 2.4 %collective-permute-done.far_ref = bf16[24,640]{1,0:T(8,128)(2,1)S(1)} collective-permute-done((bf16[24,640]{1,0:T(8,128)(2,1)}, bf16[24,640]{1,0:T(8,128)(2,1)S(1)}, u32[]{:S(2)}, u32[]{:S(2)}) %collective-permute-start) | collective-permute-done | bytes 30752 | tf_op jit(solution)/shard_map/ppermute | solution.py:749
  8.8 0.8 copy-done.8
  9.5 0.8 pair_lead.1
  10.3 4.7 %all-to-all-start = ((bf16[8,2,24,640]{3,2,1,0:T(8,128)(2,1)}), bf16[8,2,24,640]{3,2,1,0:T(8,128)(2,1)S(1)}, u32[]{:S(2)}, u32[]{:S(2)}) async-start(bf16[8,2,24,640]{3,2,1,0:T(8,128)(2,1)} %pair_lead.1), calls=%async_computation | async-start | bytes 983040 | tf_op jit(solution)/shard_map/all_to_all | solution.py:753
  15.1 2.9 %collective-permute-start.1 = (bf16[24,1792]{1,0:T(8,128)(2,1)S(1)}, bf16[24,1792]{1,0:T(8,128)(2,1)S(1)}, u32[]{:S(2)}, u32[]{:S(2)}) collective-permute-start(bf16[24,1792]{1,0:T(8,128)(2,1)S(1)} %copy-done.3), channel_id=1, source_target_pairs={{0,16},{2,18},{4,20},{6,22},{8,24},{10,26},{12,28},{14,30},{16,0},... | collective-permute-start | bytes 258056 | tf_op jit(solution)/shard_map/ppermute | solution.py:750
  18.0 6.2 %prepare.1 = (f32[2560,384]{1,0:T(8,128)}, bf16[2560,384]{1,0:T(8,128)(2,1)}, bf16[384,2560]{1,0:T(8,128)(2,1)}) custom-call(s32[1]{0:T(128)} %bitcast.side_ref, s32[8]{0:T(128)} %len_ref.5, bf16[2560,384]{1,0:T(8,128)(2,1)} %bitcast.41, bf16[2560,384]{1,0:T(8,128)(2,1)} %bitcast.40), custom_call_target="tpu_custom_call" | custom-call | flops 5000000000 | bytes 1000000 | tf_op jit(solution)/shard_map/prepare/pallas_call | solution.py:123
  24.1 1.2 pair_rest.1
  25.3 5.3 %all-to-all-start.1 = ((bf16[8,2,24,1792]{3,2,1,0:T(8,128)(2,1)}), bf16[8,2,24,1792]{3,2,1,0:T(8,128)(2,1)S(1)}, u32[]{:S(2)}, u32[]{:S(2)}) async-start(bf16[8,2,24,1792]{3,2,1,0:T(8,128)(2,1)} %pair_rest.1), calls=%async_computation.1 | async-start | bytes 2752512 | tf_op jit(solution)/shard_map/all_to_all | solution.py:760
  30.7 19.7 %attention_forward.1 = (bf16[4,384,640]{2,1,0:T(8,128)(2,1)}, bf16[4,3,640,384]{3,2,1,0:T(8,128)(2,1)}, bf16[4,640,384]{2,1,0:T(8,128)(2,1)}, f32[4,640,384]{2,1...) custom-call(s32[1]{0:T(128)} %bitcast.side_ref, ...), custom_call_target="tpu_custom_call" | custom-call | flops 24000000000 | bytes 1000000 | tf_op jit(solution)/shard_map/attention_forward/pallas_call | solution.py:239
  50.3 3.1 %collective-permute-done.3.other_ref = bf16[8,2,24,1792]{3,2,1,0:T(8,128)(2,1)S(1)} collective-permute-done((bf16[8,2,24,1792]{3,2,1,0:T(8,128)(2,1)S(1)}, bf16[8,2,24,1792]{3,2,1,0:T(8,128)(2,1)S(1)}, u32[]{:S(2)}, u32[]{:S(2)}) %collective-permute-start.3) | collective-permute-done | bytes 1376288 | tf_op jit(solution)/shard_map/ppermute | solution.py:708
  53.5 29.7 %feed_forward.1 = (f32[2560,384]{1,0:T(8,128)}, bf16[2,2560,768]{2,1,0:T(8,128)(2,1)}, f32[2560,384]{1,0:T(8,128)}, bf16[2560,384]{1,0:T(8,128)(2,1)S(1)}, bf16[...) custom-call(bf16[2560,384]{1,0:T(8,128)(2,1)} %bitcast.42, ...), custom_call_target="tpu_custom_call" | custom-call | flops 35999997952 | bytes 1000000 | tf_op jit(solution)/shard_map/feed_forward/pallas_call | solution.py:359
  83.2 0.2 collective-permute-start.4
  83.4 3.0 %collective-permute-done.4.right_ref = bf16[384,1792]{1,0:T(8,128)(2,1)S(1)} collective-permute-done((bf16[384,1792]{1,0:T(8,128)(2,1)S(1)}, bf16[384,1792]{1,0:T(8,128)(2,1)S(1)}, u32[]{:S(2)}, u32[]{:S(2)}) %collective-permute-start.4) | collective-permute-done | bytes 1376288 | tf_op jit(solution)/shard_map/ppermute | solution.py:708
  86.4 1.4 add_rest.1
  87.8 6.5 %all-to-all-start.2 = ((bf16[8,2,24,1792]{3,2,1,0:T(8,128)(2,1)}), bf16[8,2,24,1792]{3,2,1,0:T(8,128)(2,1)S(1)}, u32[]{:S(2)}, u32[]{:S(2)}) async-start(bf16[8,2,24,1792]{3,2,1,0:T(8,128)(2,1)} %add_rest.1), calls=%async_computation.2 | async-start | bytes 2752512 | tf_op jit(solution)/shard_map/all_to_all | solution.py:773
  94.3 21.1 %attention_backward.1 = (bf16[4,640,1152]{2,1,0:T(8,128)(2,1)}, bf16[384,640]{1,0:T(8,128)(2,1)S(1)}, bf16[384,640]{1,0:T(8,128)(2,1)S(1)}) custom-call(s32[1]{0:T(128)} %bitcast.side_ref, s32[8]{0:T(128)S(1)} %copy-done.12, bf16[4,384,640]{2,1,0:T(8,128)(2,1)} %get-tuple-element.75.n1t_ref, bf16[4,3,640,384]{3,2,1,0:T(8,128)(2,1)} %get-tuple-element.76.qkv_ref, ...), custom_call_target="tpu_custom_call" | custom-call | flops 27000000512 | bytes 1000000 | tf_op jit(solution)/shard_map/attention_backward/pallas_call | solution.py:497
  115.4 1.9 %collective-permute-done.5.right_ref = bf16[384,640]{1,0:T(8,128)(2,1)S(1)} collective-permute-done((bf16[384,640]{1,0:T(8,128)(2,1)S(1)}, bf16[384,640]{1,0:T(8,128)(2,1)S(1)}, u32[]{:S(2)}, u32[]{:S(2)}) %collective-permute-start.5) | collective-permute-done | bytes 491552 | tf_op jit(solution)/shard_map/ppermute | solution.py:708
  117.3 0.9 add_lead.1
  118.2 7.0 %all-to-all-start.3 = ((bf16[16,24,640]{2,1,0:T(8,128)(2,1)}), bf16[16,24,640]{2,1,0:T(8,128)(2,1)S(1)}, u32[]{:S(2)}, u32[]{:S(2)}) async-start(bf16[16,24,640]{2,1,0:T(8,128)(2,1)} %bitcast.15), calls=%async_computation.3 | async-start | bytes 983040 | tf_op jit(solution)/shard_map/all_to_all | solution.py:777
  125.4 2.9 %collective-permute-start.6 = (bf16[24,1792]{1,0:T(8,128)(2,1)S(1)}, bf16[24,1792]{1,0:T(8,128)(2,1)S(1)}, u32[]{:S(2)}, u32[]{:S(2)}) collective-permute-start(bf16[24,1792]{1,0:T(8,128)(2,1)S(1)} %get-tuple-element.105), channel_id=1, source_target_pairs={{0,16},{2,18},{4,20},{6,22},{8,24},{10,26},{12,28},{14,30},{16,0},... | collective-permute-start | bytes 258056 | tf_op jit(solution)/shard_map/ppermute | solution.py:784
  128.3 15.1 %input_gradient.1 = (f32[4,640,384]{2,1,0:T(8,128)}, f32[8,384]{1,0:T(8,128)S(1)}, bf16[4,640,384]{2,1,0:T(8,128)(2,1)}) custom-call(bf16[4,640,384]{2,1,0:T(8,128)(2,1)} %tok_ref.1, bf16[4,640,1152]{2,1,0:T(8,128)(2,1)} %get-tuple-element.90.gp_ref, f32[4,640,384]{2,1,0:T(8,128)} %bitcast.44, bf16[384,1152]{1,0:T(8,128)(2,1)S(1)} %get-tuple-element.92.w_ref, ...), custom_call_target="tpu_custom_call" | custom-call | flops 12999999488 | bytes 1000000 | tf_op jit(solution)/shard_map/input_gradient/pallas_call | solution.py:548
  143.7 1.2 collective-permute-done.7
  144.9 1.5 collective-permute-start.8
  146.3 2.2 %collective-permute-done.8 = f32[8,384]{1,0:T(8,128)S(1)} collective-permute-done((f32[8,384]{1,0:T(8,128)S(1)}, f32[8,384]{1,0:T(8,128)S(1)}, u32[]{:S(2)}, u32[]{:S(2)}) %collective-permute-start.8) | collective-permute-done | bytes 12320 | tf_op jit(solution)/shard_map/ppermute | solution.py:797
  148.6 1.5 collective-permute-start.9
  150.0 2.2 %collective-permute-done.9 = f32[8,384]{1,0:T(8,128)S(1)} collective-permute-done((f32[8,384]{1,0:T(8,128)S(1)}, f32[8,384]{1,0:T(8,128)S(1)}, u32[]{:S(2)}, u32[]{:S(2)}) %collective-permute-start.9) | collective-permute-done | bytes 12320 | tf_op jit(solution)/shard_map/ppermute | solution.py:797
  152.3 1.5 collective-permute-start.10
  153.7 2.2 %collective-permute-done.10 = f32[8,384]{1,0:T(8,128)S(1)} collective-permute-done((f32[8,384]{1,0:T(8,128)S(1)}, f32[8,384]{1,0:T(8,128)S(1)}, u32[]{:S(2)}, u32[]{:S(2)}) %collective-permute-start.10) | collective-permute-done | bytes 12320 | tf_op jit(solution)/shard_map/ppermute | solution.py:797
  156.1 4.5 %collective-permute-done.11 = f32[8,384]{1,0:T(8,128)S(1)} collective-permute-done((f32[8,384]{1,0:T(8,128)S(1)}, f32[8,384]{1,0:T(8,128)S(1)}, u32[]{:S(2)}, u32[]{:S(2)}) %collective-permute-start.11) | collective-permute-done | bytes 12320 | tf_op jit(solution)/shard_map/ppermute | solution.py:797
  160.7 1.2 update_weights.1
  (48 shorter events, 0.6 us)
Async XLA Ops:
  2.3 6.4 %collective-permute-start = (bf16[24,640]{1,0:T(8,128)(2,1)}, bf16[24,640]{1,0:T(8,128)(2,1)S(1)}, u32[]{:S(2)}, u32[]{:S(2)}) collective-permute-start(bf16[24,640]{1,0:T(8,128)(2,1)} %get-tuple-element.68.own_ref), channel_id=1, source_target_pairs={{0,16},{2,18},{4,20},{6,22},{8,24},{10,26},{12,28},{14,30},{16,0},... | collective-permute-start | bytes 92168 | tf_op jit(solution)/shard_map/ppermute | solution.py:749
  8.8 0.8 copy-start.8
  9.5 5.6 %copy-start.3 = (bf16[24,1792]{1,0:T(8,128)(2,1)S(1)}, bf16[24,1792]{1,0:T(8,128)(2,1)}, u32[]{:S(2)}) copy-start(bf16[24,1792]{1,0:T(8,128)(2,1)} %get-tuple-element.69.own_ref) | copy-start | bytes 258052
  10.3 15.0 %all-to-all-start = ((bf16[8,2,24,640]{3,2,1,0:T(8,128)(2,1)}), bf16[8,2,24,640]{3,2,1,0:T(8,128)(2,1)S(1)}, u32[]{:S(2)}, u32[]{:S(2)}) async-start(bf16[8,2,24,640]{3,2,1,0:T(8,128)(2,1)} %pair_lead.1), calls=%async_computation | async-start | bytes 983040 | tf_op jit(solution)/shard_map/all_to_all | solution.py:753
  15.1 9.0 %collective-permute-start.1 = (bf16[24,1792]{1,0:T(8,128)(2,1)S(1)}, bf16[24,1792]{1,0:T(8,128)(2,1)S(1)}, u32[]{:S(2)}, u32[]{:S(2)}) collective-permute-start(bf16[24,1792]{1,0:T(8,128)(2,1)S(1)} %copy-done.3), channel_id=1, source_target_pairs={{0,16},{2,18},{4,20},{6,22},{8,24},{10,26},{12,28},{14,30},{16,0},... | collective-permute-start | bytes 258056 | tf_op jit(solution)/shard_map/ppermute | solution.py:750
  25.3 5.3 %copy-start.10 = (s32[8,640]{1,0:T(8,128)S(1)}, s32[8,640]{1,0:T(8,128)}, u32[]{:S(2)}) copy-start(s32[8,640]{1,0:T(8,128)} %mask_ref.1) | copy-start | bytes 61444
  25.3 5.3 %copy-start.12 = (s32[8]{0:T(128)S(1)}, s32[8]{0:T(128)}, u32[]{:S(2)}) copy-start(s32[8]{0:T(128)} %len_ref.5) | copy-start | bytes 100
  25.3 5.3 %collective-permute-start.2 = (bf16[8,2,24,640]{3,2,1,0:T(8,128)(2,1)S(1)}, bf16[8,2,24,640]{3,2,1,0:T(8,128)(2,1)S(1)}, u32[]{:S(2)}, u32[]{:S(2)}) collective-permute-start(bf16[8,2,24,640]{3,2,1,0:T(8,128)(2,1)S(1)} %all-to-all-done.own_ref), channel_id=1, source_target_pairs={{0,1},{1,0},{2,3},{3,2},{4,5},{5,4},{6,7},{7,6},{8,9},{9,8},{10,11... | collective-permute-start | bytes 1474568 | tf_op jit(solution)/shard_map/ppermute | solution.py:708
  25.3 25.0 %all-to-all-start.1 = ((bf16[8,2,24,1792]{3,2,1,0:T(8,128)(2,1)}), bf16[8,2,24,1792]{3,2,1,0:T(8,128)(2,1)S(1)}, u32[]{:S(2)}, u32[]{:S(2)}) async-start(bf16[8,2,24,1792]{3,2,1,0:T(8,128)(2,1)} %pair_rest.1), calls=%async_computation.1 | async-start | bytes 2752512 | tf_op jit(solution)/shard_map/all_to_all | solution.py:760
  50.3 3.1 %collective-permute-start.3 = (bf16[8,2,24,1792]{3,2,1,0:T(8,128)(2,1)S(1)}, bf16[8,2,24,1792]{3,2,1,0:T(8,128)(2,1)S(1)}, u32[]{:S(2)}, u32[]{:S(2)}) collective-permute-start(bf16[8,2,24,1792]{3,2,1,0:T(8,128)(2,1)S(1)} %all-to-all-done.1.own_ref), channel_id=1, source_target_pairs={{0,1},{1,0},{2,3},{3,2},{4,5},{5,4},{6,7},{7,6},{8,9},{9,8},{10,11... | collective-permute-start | bytes 4128776 | tf_op jit(solution)/shard_map/ppermute | solution.py:708
  83.2 4.6 %copy-start.14 = (bf16[2560,384]{1,0:T(8,128)(2,1)}, bf16[2560,384]{1,0:T(8,128)(2,1)S(1)}, u32[]{:S(2)}) copy-start(bf16[2560,384]{1,0:T(8,128)(2,1)S(1)} %get-tuple-element.89) | copy-start | bytes 5898244
  83.2 3.2 %collective-permute-start.4 = (bf16[384,1792]{1,0:T(8,128)(2,1)S(1)}, bf16[384,1792]{1,0:T(8,128)(2,1)S(1)}, u32[]{:S(2)}, u32[]{:S(2)}) collective-permute-start(bf16[384,1792]{1,0:T(8,128)(2,1)S(1)} %get-tuple-element.87), channel_id=1, source_target_pairs={{0,1},{1,0},{2,3},{3,2},{4,5},{5,4},{6,7},{7,6},{8,9},{9,8},{10,11... | collective-permute-start | bytes 4128776 | tf_op jit(solution)/shard_map/ppermute | solution.py:708
  87.8 30.4 %all-to-all-start.2 = ((bf16[8,2,24,1792]{3,2,1,0:T(8,128)(2,1)}), bf16[8,2,24,1792]{3,2,1,0:T(8,128)(2,1)S(1)}, u32[]{:S(2)}, u32[]{:S(2)}) async-start(bf16[8,2,24,1792]{3,2,1,0:T(8,128)(2,1)} %add_rest.1), calls=%async_computation.2 | async-start | bytes 2752512 | tf_op jit(solution)/shard_map/all_to_all | solution.py:773
  115.4 1.9 %collective-permute-start.5 = (bf16[384,640]{1,0:T(8,128)(2,1)S(1)}, bf16[384,640]{1,0:T(8,128)(2,1)S(1)}, u32[]{:S(2)}, u32[]{:S(2)}) collective-permute-start(bf16[384,640]{1,0:T(8,128)(2,1)S(1)} %get-tuple-element.100), channel_id=1, source_target_pairs={{0,1},{1,0},{2,3},{3,2},{4,5},{5,4},{6,7},{7,6},{8,9},{9,8},{10,11... | collective-permute-start | bytes 1474568 | tf_op jit(solution)/shard_map/ppermute | solution.py:708
  118.2 25.2 %all-to-all-start.3 = ((bf16[16,24,640]{2,1,0:T(8,128)(2,1)}), bf16[16,24,640]{2,1,0:T(8,128)(2,1)S(1)}, u32[]{:S(2)}, u32[]{:S(2)}) async-start(bf16[16,24,640]{2,1,0:T(8,128)(2,1)} %bitcast.15), calls=%async_computation.3 | async-start | bytes 983040 | tf_op jit(solution)/shard_map/all_to_all | solution.py:777
  125.4 18.0 %collective-permute-start.6 = (bf16[24,1792]{1,0:T(8,128)(2,1)S(1)}, bf16[24,1792]{1,0:T(8,128)(2,1)S(1)}, u32[]{:S(2)}, u32[]{:S(2)}) collective-permute-start(bf16[24,1792]{1,0:T(8,128)(2,1)S(1)} %get-tuple-element.105), channel_id=1, source_target_pairs={{0,16},{2,18},{4,20},{6,22},{8,24},{10,26},{12,28},{14,30},{16,0},... | collective-permute-start | bytes 258056 | tf_op jit(solution)/shard_map/ppermute | solution.py:784
  143.4 17.2 %copy-start = (f32[2,24,3,192]{3,1,2,0:T(8,128)S(1)}, f32[2,24,3,192]{3,1,2,0:T(8,128)}, u32[]{:S(2)}) copy-start(f32[2,24,3,192]{3,1,2,0:T(8,128)} %param.23) | copy-start | bytes 331780
  143.4 17.2 %copy-start.1 = (f32[2,24,768]{2,1,0:T(8,128)S(1)}, f32[2,24,768]{2,1,0:T(8,128)}, u32[]{:S(2)}) copy-start(f32[2,24,768]{2,1,0:T(8,128)} %up_m_ref.1) | copy-start | bytes 442372
  143.4 17.2 %copy-start.2 = (f32[2,768,24]{1,2,0:T(8,128)S(1)}, f32[2,768,24]{1,2,0:T(8,128)}, u32[]{:S(2)}) copy-start(f32[2,768,24]{1,2,0:T(8,128)} %param.26) | copy-start | bytes 442372
  143.4 17.2 %copy-start.4 = (f32[24,3,192]{2,0,1:T(8,128)S(1)}, f32[24,3,192]{2,0,1:T(8,128)}, u32[]{:S(2)}) copy-start(f32[24,3,192]{2,0,1:T(8,128)} %param.18) | copy-start | bytes 165892
  143.4 17.2 %copy-start.5 = (f32[24,768]{1,0:T(8,128)S(1)}, f32[24,768]{1,0:T(8,128)}, u32[]{:S(2)}) copy-start(f32[24,768]{1,0:T(8,128)} %up_ref.3) | copy-start | bytes 221188
  143.5 17.2 %copy-start.6 = (f32[768,24]{0,1:T(8,128)S(1)}, f32[768,24]{0,1:T(8,128)}, u32[]{:S(2)}) copy-start(f32[768,24]{0,1:T(8,128)} %param.21) | copy-start | bytes 221188
  143.5 17.2 %copy-start.7 = (f32[2,192,24]{1,2,0:T(8,128)S(1)}, f32[2,192,24]{1,2,0:T(8,128)}, u32[]{:S(2)}) copy-start(f32[2,192,24]{1,2,0:T(8,128)} %param.24) | copy-start | bytes 110596
  143.5 17.2 %copy-start.9 = (f32[192,24]{0,1:T(8,128)S(1)}, f32[192,24]{0,1:T(8,128)}, u32[]{:S(2)}) copy-start(f32[192,24]{0,1:T(8,128)} %param.19) | copy-start | bytes 55300
  143.5 17.2 %copy-start.11 = (f32[2,48]{1,0:T(2,128)S(1)}, f32[2,48]{1,0:T(2,128)}, u32[]{:S(2)}) copy-start(f32[2,48]{1,0:T(2,128)} %norm_m_ref.1) | copy-start | bytes 1156
  143.5 17.2 %copy-start.13 = (f32[48]{0:T(128)S(1)}, f32[48]{0:T(128)}, u32[]{:S(2)}) copy-start(f32[48]{0:T(128)} %param.22) | copy-start | bytes 580
  143.6 1.2 collective-permute-start.7
  144.9 3.7 %collective-permute-start.8 = (f32[8,384]{1,0:T(8,128)S(1)}, f32[8,384]{1,0:T(8,128)S(1)}, u32[]{:S(2)}, u32[]{:S(2)}) collective-permute-start(f32[8,384]{1,0:T(8,128)S(1)} %add.20), channel_id=1, source_target_pairs={{0,2},{2,0},{4,6},{6,4},{8,10},{10,8},{12,14},{14,12},{16,18},{18,... | collective-permute-start | bytes 36872 | tf_op jit(solution)/shard_map/ppermute | solution.py:797
  148.6 3.7 %collective-permute-start.9 = (f32[8,384]{1,0:T(8,128)S(1)}, f32[8,384]{1,0:T(8,128)S(1)}, u32[]{:S(2)}, u32[]{:S(2)}) collective-permute-start(f32[8,384]{1,0:T(8,128)S(1)} %add.21), channel_id=1, source_target_pairs={{0,4},{2,6},{4,0},{6,2},{8,12},{10,14},{12,8},{14,10},{16,20},{18,... | collective-permute-start | bytes 36872 | tf_op jit(solution)/shard_map/ppermute | solution.py:797
  152.3 3.7 %collective-permute-start.10 = (f32[8,384]{1,0:T(8,128)S(1)}, f32[8,384]{1,0:T(8,128)S(1)}, u32[]{:S(2)}, u32[]{:S(2)}) collective-permute-start(f32[8,384]{1,0:T(8,128)S(1)} %add.22), channel_id=1, source_target_pairs={{0,8},{2,10},{4,12},{6,14},{8,0},{10,2},{12,4},{14,6},{16,24},{18,... | collective-permute-start | bytes 36872 | tf_op jit(solution)/shard_map/ppermute | solution.py:797
  156.0 4.6 %collective-permute-start.11 = (f32[8,384]{1,0:T(8,128)S(1)}, f32[8,384]{1,0:T(8,128)S(1)}, u32[]{:S(2)}, u32[]{:S(2)}) collective-permute-start(f32[8,384]{1,0:T(8,128)S(1)} %add.23), channel_id=1, source_target_pairs={{0,16},{2,18},{4,20},{6,22},{8,24},{10,26},{12,28},{14,30},{16,0},... | collective-permute-start | bytes 36872 | tf_op jit(solution)/shard_map/ppermute | solution.py:797

commit v9 on v8

--- a/solution.py
+++ b/solution.py
@@ -794,7 +794,8 @@
     message = message + swap(message)
     stride = 1
     while stride < chips:
-        message = message + lax.ppermute(message, "batch", [(i, i ^ stride) for i in range(chips)])
+        across = [(2 * i + core, 2 * (i ^ stride) + 1 - core) for i in range(chips) for core in range(2)]
+        message = message + lax.ppermute(message, ("batch", "head"), across)
         stride *= 2
     like = lambda a: shape(a.shape, F32)
     moments = (

time: 164 us -> 161 us (0.982)
  waiting for transfers between devices: 22.7 us -> 20.3 us
    ppermute x5, starting transfers between devices: 0.28 us -> 2.3 us  [swap(): return lax.ppermute(values, 'head', [(0, 1), (1, 0)])]
where the time goes in v9:
time: 161 us; the launch traced here: 159 us
  Pallas kernels  99.1 us (62%)
  starting transfers between devices  37.9 us (24%)
  waiting for transfers between devices  20.3 us (13%)
    pallas_call x1, Pallas kernels, middle(): pl.pallas_call(functools.partial(middle_kernel, units), grid=(total // FB...  29.7 us
    pallas_call x1, Pallas kernels, backward(): pl.pallas_call(backward_kernel, grid=(seqs,), in_specs=[IN_SMEM, IN_SMEM,...  20.8 us
    pallas_call x1, Pallas kernels, forward(): pl.pallas_call(functools.partial(forward_kernel, chips, part), grid=(seqs...  19.8 us
    pallas_call x1, Pallas kernels, input_gradient(): pl.pallas_call(input_kernel, grid=(seqs, rows // DB), in_specs=[full, pl....  15.1 us
    ppermute x4, waiting for transfers between devices, per_device(): message = message + lax.ppermute(message, ('batch', 'head'), across)  9.66 us
    ppermute x5, waiting for transfers between devices, swap(): return lax.ppermute(values, 'head', [(0, 1), (1, 0)])  8.17 us
    pallas_call x8, Pallas kernels, small_call(): pl.pallas_call(kernel, in_specs=[IN_SMEM if a.dtype == jnp.int32 else in_...  7.46 us
    all_to_all x1, starting transfers between devices, per_device(): lax.all_to_all(lead_sum.reshape(chips, shard_rows, 10 * HD), 'batch', 0, 0)  6.89 us
  transfers between devices with their start and end apart: 16, of which 9 were waited for; matrix products, arithmetic and copies ran while one was open for 0% of the time, Pallas kernels for 40%

profile of v9, /device:TPU:0, one launch (start us, length us, event | category | flops | bytes accessed | tf_op | source)
XLA Modules:
  0.0 159.1 jit_solution(11375204235267842942)
XLA Ops:
  0.6 1.7 %pack_weights.1 = (bf16[24,640]{1,0:T(8,128)(2,1)}, bf16[24,1792]{1,0:T(8,128)(2,1)}) custom-call(f32[3,24,192]{2,1,0:T(8,128)} %bitcast.30, f32[24,192]{1,0:T(8,128)} %bitcast.35, f32[24,768]{1,0:T(8,128)} %up_ref.3, f32[24,768]{1,0:T(8,128)} %bitcast.32, f32[1,48]{1,0:T(1,128)} %bitcast.37), custom_call_target="tpu_custom_call" | custom-call | flops 2000000000 | bytes 1000000 | tf_op jit(solution)/shard_map/pack_weights/pallas_call | solution.py:696
  2.3 4.0 %collective-permute-start = (bf16[24,640]{1,0:T(8,128)(2,1)}, bf16[24,640]{1,0:T(8,128)(2,1)S(1)}, u32[]{:S(2)}, u32[]{:S(2)}) collective-permute-start(bf16[24,640]{1,0:T(8,128)(2,1)} %get-tuple-element.68.own_ref), channel_id=1, source_target_pairs={{0,16},{2,18},{4,20},{6,22},{8,24},{10,26},{12,28},{14,30},{16,0},... | collective-permute-start | bytes 92168 | tf_op jit(solution)/shard_map/ppermute | solution.py:749
  6.4 2.4 %collective-permute-done.far_ref = bf16[24,640]{1,0:T(8,128)(2,1)S(1)} collective-permute-done((bf16[24,640]{1,0:T(8,128)(2,1)}, bf16[24,640]{1,0:T(8,128)(2,1)S(1)}, u32[]{:S(2)}, u32[]{:S(2)}) %collective-permute-start) | collective-permute-done | bytes 30752 | tf_op jit(solution)/shard_map/ppermute | solution.py:749
  8.8 0.8 copy-done.8
  9.5 0.8 pair_lead.1
  10.3 4.7 %all-to-all-start = ((bf16[8,2,24,640]{3,2,1,0:T(8,128)(2,1)}), bf16[8,2,24,640]{3,2,1,0:T(8,128)(2,1)S(1)}, u32[]{:S(2)}, u32[]{:S(2)}) async-start(bf16[8,2,24,640]{3,2,1,0:T(8,128)(2,1)} %pair_lead.1), calls=%async_computation | async-start | bytes 983040 | tf_op jit(solution)/shard_map/all_to_all | solution.py:753
  15.1 2.9 %collective-permute-start.1 = (bf16[24,1792]{1,0:T(8,128)(2,1)S(1)}, bf16[24,1792]{1,0:T(8,128)(2,1)S(1)}, u32[]{:S(2)}, u32[]{:S(2)}) collective-permute-start(bf16[24,1792]{1,0:T(8,128)(2,1)S(1)} %copy-done.3), channel_id=1, source_target_pairs={{0,16},{2,18},{4,20},{6,22},{8,24},{10,26},{12,28},{14,30},{16,0},... | collective-permute-start | bytes 258056 | tf_op jit(solution)/shard_map/ppermute | solution.py:750
  18.0 6.2 %prepare.1 = (f32[2560,384]{1,0:T(8,128)}, bf16[2560,384]{1,0:T(8,128)(2,1)}, bf16[384,2560]{1,0:T(8,128)(2,1)}) custom-call(s32[1]{0:T(128)} %bitcast.side_ref, s32[8]{0:T(128)} %len_ref.5, bf16[2560,384]{1,0:T(8,128)(2,1)} %bitcast.41, bf16[2560,384]{1,0:T(8,128)(2,1)} %bitcast.40), custom_call_target="tpu_custom_call" | custom-call | flops 5000000000 | bytes 1000000 | tf_op jit(solution)/shard_map/prepare/pallas_call | solution.py:123
  24.1 1.2 pair_rest.1
  25.3 5.3 %all-to-all-start.1 = ((bf16[8,2,24,1792]{3,2,1,0:T(8,128)(2,1)}), bf16[8,2,24,1792]{3,2,1,0:T(8,128)(2,1)S(1)}, u32[]{:S(2)}, u32[]{:S(2)}) async-start(bf16[8,2,24,1792]{3,2,1,0:T(8,128)(2,1)} %pair_rest.1), calls=%async_computation.1 | async-start | bytes 2752512 | tf_op jit(solution)/shard_map/all_to_all | solution.py:760
  30.7 19.8 %attention_forward.1 = (bf16[4,384,640]{2,1,0:T(8,128)(2,1)}, bf16[4,3,640,384]{3,2,1,0:T(8,128)(2,1)}, bf16[4,640,384]{2,1,0:T(8,128)(2,1)}, f32[4,640,384]{2,1...) custom-call(s32[1]{0:T(128)} %bitcast.side_ref, ...), custom_call_target="tpu_custom_call" | custom-call | flops 24000000000 | bytes 1000000 | tf_op jit(solution)/shard_map/attention_forward/pallas_call | solution.py:239
  50.5 1.1 collective-permute-start.3
  51.6 2.8 %collective-permute-done.3.other_ref = bf16[8,2,24,1792]{3,2,1,0:T(8,128)(2,1)S(1)} collective-permute-done((bf16[8,2,24,1792]{3,2,1,0:T(8,128)(2,1)S(1)}, bf16[8,2,24,1792]{3,2,1,0:T(8,128)(2,1)S(1)}, u32[]{:S(2)}, u32[]{:S(2)}) %collective-permute-start.3) | collective-permute-done | bytes 1376288 | tf_op jit(solution)/shard_map/ppermute | solution.py:708
  54.4 29.7 %feed_forward.1 = (f32[2560,384]{1,0:T(8,128)}, bf16[2,2560,768]{2,1,0:T(8,128)(2,1)}, f32[2560,384]{1,0:T(8,128)}, bf16[2560,384]{1,0:T(8,128)(2,1)S(1)}, bf16[...) custom-call(bf16[2560,384]{1,0:T(8,128)(2,1)} %bitcast.42, ...), custom_call_target="tpu_custom_call" | custom-call | flops 35999997952 | bytes 1000000 | tf_op jit(solution)/shard_map/feed_forward/pallas_call | solution.py:359
  84.5 2.8 %collective-permute-done.4.right_ref = bf16[384,1792]{1,0:T(8,128)(2,1)S(1)} collective-permute-done((bf16[384,1792]{1,0:T(8,128)(2,1)S(1)}, bf16[384,1792]{1,0:T(8,128)(2,1)S(1)}, u32[]{:S(2)}, u32[]{:S(2)}) %collective-permute-start.4) | collective-permute-done | bytes 1376288 | tf_op jit(solution)/shard_map/ppermute | solution.py:708
  87.3 1.4 add_rest.1
  88.7 5.1 %all-to-all-start.2 = ((bf16[8,2,24,1792]{3,2,1,0:T(8,128)(2,1)}), bf16[8,2,24,1792]{3,2,1,0:T(8,128)(2,1)S(1)}, u32[]{:S(2)}, u32[]{:S(2)}) async-start(bf16[8,2,24,1792]{3,2,1,0:T(8,128)(2,1)} %add_rest.1), calls=%async_computation.2 | async-start | bytes 2752512 | tf_op jit(solution)/shard_map/all_to_all | solution.py:773
  93.8 20.8 %attention_backward.1 = (bf16[4,640,1152]{2,1,0:T(8,128)(2,1)}, bf16[384,640]{1,0:T(8,128)(2,1)S(1)}, bf16[384,640]{1,0:T(8,128)(2,1)S(1)}) custom-call(s32[1]{0:T(128)} %bitcast.side_ref, s32[8]{0:T(128)S(1)} %copy-done.12, bf16[4,384,640]{2,1,0:T(8,128)(2,1)} %get-tuple-element.75.n1t_ref, bf16[4,3,640,384]{3,2,1,0:T(8,128)(2,1)} %get-tuple-element.76.qkv_ref, ...), custom_call_target="tpu_custom_call" | custom-call | flops 27000000512 | bytes 1000000 | tf_op jit(solution)/shard_map/attention_backward/pallas_call | solution.py:497
  115.3 1.5 collective-permute-done.5.right_ref
  116.8 0.9 add_lead.1
  117.7 6.9 %all-to-all-start.3 = ((bf16[16,24,640]{2,1,0:T(8,128)(2,1)}), bf16[16,24,640]{2,1,0:T(8,128)(2,1)S(1)}, u32[]{:S(2)}, u32[]{:S(2)}) async-start(bf16[16,24,640]{2,1,0:T(8,128)(2,1)} %bitcast.15), calls=%async_computation.3 | async-start | bytes 983040 | tf_op jit(solution)/shard_map/all_to_all | solution.py:777
  124.8 2.9 %collective-permute-start.6 = (bf16[24,1792]{1,0:T(8,128)(2,1)S(1)}, bf16[24,1792]{1,0:T(8,128)(2,1)S(1)}, u32[]{:S(2)}, u32[]{:S(2)}) collective-permute-start(bf16[24,1792]{1,0:T(8,128)(2,1)S(1)} %get-tuple-element.105), channel_id=1, source_target_pairs={{0,16},{2,18},{4,20},{6,22},{8,24},{10,26},{12,28},{14,30},{16,0},... | collective-permute-start | bytes 258056 | tf_op jit(solution)/shard_map/ppermute | solution.py:784
  127.7 15.1 %input_gradient.1 = (f32[4,640,384]{2,1,0:T(8,128)}, f32[8,384]{1,0:T(8,128)S(1)}, bf16[4,640,384]{2,1,0:T(8,128)(2,1)}) custom-call(bf16[4,640,384]{2,1,0:T(8,128)(2,1)} %tok_ref.1, bf16[4,640,1152]{2,1,0:T(8,128)(2,1)} %get-tuple-element.90.gp_ref, f32[4,640,384]{2,1,0:T(8,128)} %bitcast.44, bf16[384,1152]{1,0:T(8,128)(2,1)S(1)} %get-tuple-element.92.w_ref, ...), custom_call_target="tpu_custom_call" | custom-call | flops 12999999488 | bytes 1000000 | tf_op jit(solution)/shard_map/input_gradient/pallas_call | solution.py:548
  143.1 1.2 collective-permute-done.7
  144.3 1.2 collective-permute-start.8
  145.5 1.9 %collective-permute-done.8 = f32[8,384]{1,0:T(8,128)S(1)} collective-permute-done((f32[8,384]{1,0:T(8,128)S(1)}, f32[8,384]{1,0:T(8,128)S(1)}, u32[]{:S(2)}, u32[]{:S(2)}) %collective-permute-start.8) | collective-permute-done | bytes 12320 | tf_op jit(solution)/shard_map/ppermute | solution.py:798
  147.4 1.2 collective-permute-start.9
  148.7 1.9 %collective-permute-done.9 = f32[8,384]{1,0:T(8,128)S(1)} collective-permute-done((f32[8,384]{1,0:T(8,128)S(1)}, f32[8,384]{1,0:T(8,128)S(1)}, u32[]{:S(2)}, u32[]{:S(2)}) %collective-permute-start.9) | collective-permute-done | bytes 12320 | tf_op jit(solution)/shard_map/ppermute | solution.py:798
  150.6 1.2 collective-permute-start.10
  151.8 1.9 %collective-permute-done.10 = f32[8,384]{1,0:T(8,128)S(1)} collective-permute-done((f32[8,384]{1,0:T(8,128)S(1)}, f32[8,384]{1,0:T(8,128)S(1)}, u32[]{:S(2)}, u32[]{:S(2)}) %collective-permute-start.10) | collective-permute-done | bytes 12320 | tf_op jit(solution)/shard_map/ppermute | solution.py:798
  153.7 4.0 %collective-permute-done.11 = f32[8,384]{1,0:T(8,128)S(1)} collective-permute-done((f32[8,384]{1,0:T(8,128)S(1)}, f32[8,384]{1,0:T(8,128)S(1)}, u32[]{:S(2)}, u32[]{:S(2)}) %collective-permute-start.11) | collective-permute-done | bytes 12320 | tf_op jit(solution)/shard_map/ppermute | solution.py:798
  157.8 1.2 update_weights.1
  (48 shorter events, 1.6 us)
Async XLA Ops:
  2.3 6.4 %collective-permute-start = (bf16[24,640]{1,0:T(8,128)(2,1)}, bf16[24,640]{1,0:T(8,128)(2,1)S(1)}, u32[]{:S(2)}, u32[]{:S(2)}) collective-permute-start(bf16[24,640]{1,0:T(8,128)(2,1)} %get-tuple-element.68.own_ref), channel_id=1, source_target_pairs={{0,16},{2,18},{4,20},{6,22},{8,24},{10,26},{12,28},{14,30},{16,0},... | collective-permute-start | bytes 92168 | tf_op jit(solution)/shard_map/ppermute | solution.py:749
  8.8 0.8 copy-start.8
  9.5 5.6 %copy-start.3 = (bf16[24,1792]{1,0:T(8,128)(2,1)S(1)}, bf16[24,1792]{1,0:T(8,128)(2,1)}, u32[]{:S(2)}) copy-start(bf16[24,1792]{1,0:T(8,128)(2,1)} %get-tuple-element.69.own_ref) | copy-start | bytes 258052
  10.3 15.0 %all-to-all-start = ((bf16[8,2,24,640]{3,2,1,0:T(8,128)(2,1)}), bf16[8,2,24,640]{3,2,1,0:T(8,128)(2,1)S(1)}, u32[]{:S(2)}, u32[]{:S(2)}) async-start(bf16[8,2,24,640]{3,2,1,0:T(8,128)(2,1)} %pair_lead.1), calls=%async_computation | async-start | bytes 983040 | tf_op jit(solution)/shard_map/all_to_all | solution.py:753
  15.1 9.0 %collective-permute-start.1 = (bf16[24,1792]{1,0:T(8,128)(2,1)S(1)}, bf16[24,1792]{1,0:T(8,128)(2,1)S(1)}, u32[]{:S(2)}, u32[]{:S(2)}) collective-permute-start(bf16[24,1792]{1,0:T(8,128)(2,1)S(1)} %copy-done.3), channel_id=1, source_target_pairs={{0,16},{2,18},{4,20},{6,22},{8,24},{10,26},{12,28},{14,30},{16,0},... | collective-permute-start | bytes 258056 | tf_op jit(solution)/shard_map/ppermute | solution.py:750
  25.3 5.3 %copy-start.10 = (s32[8,640]{1,0:T(8,128)S(1)}, s32[8,640]{1,0:T(8,128)}, u32[]{:S(2)}) copy-start(s32[8,640]{1,0:T(8,128)} %mask_ref.1) | copy-start | bytes 61444
  25.3 5.3 %copy-start.12 = (s32[8]{0:T(128)S(1)}, s32[8]{0:T(128)}, u32[]{:S(2)}) copy-start(s32[8]{0:T(128)} %len_ref.5) | copy-start | bytes 100
  25.3 5.3 %collective-permute-start.2 = (bf16[8,2,24,640]{3,2,1,0:T(8,128)(2,1)S(1)}, bf16[8,2,24,640]{3,2,1,0:T(8,128)(2,1)S(1)}, u32[]{:S(2)}, u32[]{:S(2)}) collective-permute-start(bf16[8,2,24,640]{3,2,1,0:T(8,128)(2,1)S(1)} %all-to-all-done.own_ref), channel_id=1, source_target_pairs={{0,1},{1,0},{2,3},{3,2},{4,5},{5,4},{6,7},{7,6},{8,9},{9,8},{10,11... | collective-permute-start | bytes 1474568 | tf_op jit(solution)/shard_map/ppermute | solution.py:708
  25.3 25.2 %all-to-all-start.1 = ((bf16[8,2,24,1792]{3,2,1,0:T(8,128)(2,1)}), bf16[8,2,24,1792]{3,2,1,0:T(8,128)(2,1)S(1)}, u32[]{:S(2)}, u32[]{:S(2)}) async-start(bf16[8,2,24,1792]{3,2,1,0:T(8,128)(2,1)} %pair_rest.1), calls=%async_computation.1 | async-start | bytes 2752512 | tf_op jit(solution)/shard_map/all_to_all | solution.py:760
  50.5 3.8 %collective-permute-start.3 = (bf16[8,2,24,1792]{3,2,1,0:T(8,128)(2,1)S(1)}, bf16[8,2,24,1792]{3,2,1,0:T(8,128)(2,1)S(1)}, u32[]{:S(2)}, u32[]{:S(2)}) collective-permute-start(bf16[8,2,24,1792]{3,2,1,0:T(8,128)(2,1)S(1)} %all-to-all-done.1.own_ref), channel_id=1, source_target_pairs={{0,1},{1,0},{2,3},{3,2},{4,5},{5,4},{6,7},{7,6},{8,9},{9,8},{10,11... | collective-permute-start | bytes 4128776 | tf_op jit(solution)/shard_map/ppermute | solution.py:708
  84.1 4.6 %copy-start.14 = (bf16[2560,384]{1,0:T(8,128)(2,1)}, bf16[2560,384]{1,0:T(8,128)(2,1)S(1)}, u32[]{:S(2)}) copy-start(bf16[2560,384]{1,0:T(8,128)(2,1)S(1)} %get-tuple-element.89) | copy-start | bytes 5898244
  84.1 3.2 %collective-permute-start.4 = (bf16[384,1792]{1,0:T(8,128)(2,1)S(1)}, bf16[384,1792]{1,0:T(8,128)(2,1)S(1)}, u32[]{:S(2)}, u32[]{:S(2)}) collective-permute-start(bf16[384,1792]{1,0:T(8,128)(2,1)S(1)} %get-tuple-element.87), channel_id=1, source_target_pairs={{0,1},{1,0},{2,3},{3,2},{4,5},{5,4},{6,7},{7,6},{8,9},{9,8},{10,11... | collective-permute-start | bytes 4128776 | tf_op jit(solution)/shard_map/ppermute | solution.py:708
  88.7 29.1 %all-to-all-start.2 = ((bf16[8,2,24,1792]{3,2,1,0:T(8,128)(2,1)}), bf16[8,2,24,1792]{3,2,1,0:T(8,128)(2,1)S(1)}, u32[]{:S(2)}, u32[]{:S(2)}) async-start(bf16[8,2,24,1792]{3,2,1,0:T(8,128)(2,1)} %add_rest.1), calls=%async_computation.2 | async-start | bytes 2752512 | tf_op jit(solution)/shard_map/all_to_all | solution.py:773
  114.6 2.2 %collective-permute-start.5 = (bf16[384,640]{1,0:T(8,128)(2,1)S(1)}, bf16[384,640]{1,0:T(8,128)(2,1)S(1)}, u32[]{:S(2)}, u32[]{:S(2)}) collective-permute-start(bf16[384,640]{1,0:T(8,128)(2,1)S(1)} %get-tuple-element.100), channel_id=1, source_target_pairs={{0,1},{1,0},{2,3},{3,2},{4,5},{5,4},{6,7},{7,6},{8,9},{9,8},{10,11... | collective-permute-start | bytes 1474568 | tf_op jit(solution)/shard_map/ppermute | solution.py:708
  117.7 25.1 %all-to-all-start.3 = ((bf16[16,24,640]{2,1,0:T(8,128)(2,1)}), bf16[16,24,640]{2,1,0:T(8,128)(2,1)S(1)}, u32[]{:S(2)}, u32[]{:S(2)}) async-start(bf16[16,24,640]{2,1,0:T(8,128)(2,1)} %bitcast.15), calls=%async_computation.3 | async-start | bytes 983040 | tf_op jit(solution)/shard_map/all_to_all | solution.py:777
  124.8 18.0 %collective-permute-start.6 = (bf16[24,1792]{1,0:T(8,128)(2,1)S(1)}, bf16[24,1792]{1,0:T(8,128)(2,1)S(1)}, u32[]{:S(2)}, u32[]{:S(2)}) collective-permute-start(bf16[24,1792]{1,0:T(8,128)(2,1)S(1)} %get-tuple-element.105), channel_id=1, source_target_pairs={{0,16},{2,18},{4,20},{6,22},{8,24},{10,26},{12,28},{14,30},{16,0},... | collective-permute-start | bytes 258056 | tf_op jit(solution)/shard_map/ppermute | solution.py:784
  142.8 14.9 %copy-start = (f32[2,24,3,192]{3,1,2,0:T(8,128)S(1)}, f32[2,24,3,192]{3,1,2,0:T(8,128)}, u32[]{:S(2)}) copy-start(f32[2,24,3,192]{3,1,2,0:T(8,128)} %param.23) | copy-start | bytes 331780
  142.8 14.9 %copy-start.1 = (f32[2,24,768]{2,1,0:T(8,128)S(1)}, f32[2,24,768]{2,1,0:T(8,128)}, u32[]{:S(2)}) copy-start(f32[2,24,768]{2,1,0:T(8,128)} %up_m_ref.1) | copy-start | bytes 442372
  142.8 14.9 %copy-start.2 = (f32[2,768,24]{1,2,0:T(8,128)S(1)}, f32[2,768,24]{1,2,0:T(8,128)}, u32[]{:S(2)}) copy-start(f32[2,768,24]{1,2,0:T(8,128)} %param.26) | copy-start | bytes 442372
  142.9 14.9 %copy-start.4 = (f32[24,3,192]{2,0,1:T(8,128)S(1)}, f32[24,3,192]{2,0,1:T(8,128)}, u32[]{:S(2)}) copy-start(f32[24,3,192]{2,0,1:T(8,128)} %param.18) | copy-start | bytes 165892
  142.9 14.9 %copy-start.5 = (f32[24,768]{1,0:T(8,128)S(1)}, f32[24,768]{1,0:T(8,128)}, u32[]{:S(2)}) copy-start(f32[24,768]{1,0:T(8,128)} %up_ref.3) | copy-start | bytes 221188
  142.9 14.9 %copy-start.6 = (f32[768,24]{0,1:T(8,128)S(1)}, f32[768,24]{0,1:T(8,128)}, u32[]{:S(2)}) copy-start(f32[768,24]{0,1:T(8,128)} %param.21) | copy-start | bytes 221188
  142.9 14.9 %copy-start.7 = (f32[2,192,24]{1,2,0:T(8,128)S(1)}, f32[2,192,24]{1,2,0:T(8,128)}, u32[]{:S(2)}) copy-start(f32[2,192,24]{1,2,0:T(8,128)} %param.24) | copy-start | bytes 110596
  142.9 14.9 %copy-start.9 = (f32[192,24]{0,1:T(8,128)S(1)}, f32[192,24]{0,1:T(8,128)}, u32[]{:S(2)}) copy-start(f32[192,24]{0,1:T(8,128)} %param.19) | copy-start | bytes 55300
  142.9 14.9 %copy-start.11 = (f32[2,48]{1,0:T(2,128)S(1)}, f32[2,48]{1,0:T(2,128)}, u32[]{:S(2)}) copy-start(f32[2,48]{1,0:T(2,128)} %norm_m_ref.1) | copy-start | bytes 1156
  142.9 14.9 %copy-start.13 = (f32[48]{0:T(128)S(1)}, f32[48]{0:T(128)}, u32[]{:S(2)}) copy-start(f32[48]{0:T(128)} %param.22) | copy-start | bytes 580
  143.1 1.2 collective-permute-start.7
  144.3 3.1 %collective-permute-start.8 = (f32[8,384]{1,0:T(8,128)S(1)}, f32[8,384]{1,0:T(8,128)S(1)}, u32[]{:S(2)}, u32[]{:S(2)}) collective-permute-start(f32[8,384]{1,0:T(8,128)S(1)} %add.20), channel_id=1, source_target_pairs={{0,3},{1,2},{2,1},{3,0},{4,7},{5,6},{6,5},{7,4},{8,11},{9,10},{10,... | collective-permute-start | bytes 36872 | tf_op jit(solution)/shard_map/ppermute | solution.py:798
  147.4 3.1 %collective-permute-start.9 = (f32[8,384]{1,0:T(8,128)S(1)}, f32[8,384]{1,0:T(8,128)S(1)}, u32[]{:S(2)}, u32[]{:S(2)}) collective-permute-start(f32[8,384]{1,0:T(8,128)S(1)} %add.21), channel_id=1, source_target_pairs={{0,5},{1,4},{2,7},{3,6},{4,1},{5,0},{6,3},{7,2},{8,13},{9,12},{10,... | collective-permute-start | bytes 36872 | tf_op jit(solution)/shard_map/ppermute | solution.py:798
  150.6 3.1 %collective-permute-start.10 = (f32[8,384]{1,0:T(8,128)S(1)}, f32[8,384]{1,0:T(8,128)S(1)}, u32[]{:S(2)}, u32[]{:S(2)}) collective-permute-start(f32[8,384]{1,0:T(8,128)S(1)} %add.22), channel_id=1, source_target_pairs={{0,9},{1,8},{2,11},{3,10},{4,13},{5,12},{6,15},{7,14},{8,1},{9,0},... | collective-permute-start | bytes 36872 | tf_op jit(solution)/shard_map/ppermute | solution.py:798
  153.7 4.0 %collective-permute-start.11 = (f32[8,384]{1,0:T(8,128)S(1)}, f32[8,384]{1,0:T(8,128)S(1)}, u32[]{:S(2)}, u32[]{:S(2)}) collective-permute-start(f32[8,384]{1,0:T(8,128)S(1)} %add.23), channel_id=1, source_target_pairs={{0,17},{1,16},{2,19},{3,18},{4,21},{5,20},{6,23},{7,22},{8,25},{9,... | collective-permute-start | bytes 36872 | tf_op jit(solution)/shard_map/ppermute | solution.py:798

commit v10 on v9

--- a/solution.py
+++ b/solution.py
@@ -28,7 +28,7 @@
 FC = 256
 PAIR = 2 * HD
 LIMIT_A, LIMIT_B, LIMIT_C, LIMIT_D, LIMIT_S, LIMIT_P = (
-    pltpu.CompilerParams(vmem_limit_bytes=m * 2**20) for m in (52, 46, 52, 52, 16, 62)
+    pltpu.CompilerParams(vmem_limit_bytes=m * 2**20) for m in (52, 46, 52, 54, 16, 62)
 )
 IN_VMEM = pl.BlockSpec(memory_space=pltpu.VMEM)
 IN_SMEM = pl.BlockSpec(memory_space=pltpu.SMEM)
@@ -772,14 +772,15 @@
     rest_sum, gatt = lax.optimization_barrier((rest_sum, gatt))
     rest_parts = lax.all_to_all(rest_sum, "batch", 0, 0, axis_index_groups=teams)
     gp, glead_own, glead_other = backward(place, lengths, n1t, qkv, probs, per_seq(gatt), attended)
+    rest_mine, rest_theirs = small_call(
+        sum_rest_kernel, "sum_rest", [shape(rest.shape, F32), shape(rest.shape, BF16)], half, rest_parts
+    )
+    rest_theirs, glead_own = lax.optimization_barrier((rest_theirs, glead_own))
     lead_sum = small_call(add_kernel, "add_lead", shape(glead_own.shape, BF16), glead_own, swap(glead_other))
     lead_sum, rest_parts = lax.optimization_barrier((lead_sum, rest_parts))
     lead_parts = lax.all_to_all(lead_sum.reshape(chips, shard_rows, 10 * HD), "batch", 0, 0)
     input_grad, terms, block_out = input_gradient(
         tokens, gp, per_seq(gmid), wpairs, norms, gnorm_two, per_seq(mid), act, weights
-    )
-    rest_mine, rest_theirs = small_call(
-        sum_rest_kernel, "sum_rest", [shape(rest.shape, F32), shape(rest.shape, BF16)], half, rest_parts
     )
     rest_far = lax.ppermute(rest_theirs, "batch", far_pairs)
     lead_shard, rest_shard, message = small_call(

time: 161 us -> 160 us (level)
  starting transfers between devices: 37.9 us -> 44 us
  waiting for transfers between devices: 20.3 us -> 14.9 us
  Pallas kernels: 99.1 us -> 97 us
    ppermute x4, starting transfers between devices: 3.72 us -> 7.63 us  [per_device(): message = message + lax.ppermute(message, ('batch', 'head'), across)]
    ppermute x4, waiting for transfers between devices: 9.66 us -> 5.75 us  [per_device(): message = message + lax.ppermute(message, ('batch', 'head'), across)]
    ppermute x5, starting transfers between devices: 2.3 us -> 5.53 us  [swap(): return lax.ppermute(values, 'head', [(0, 1), (1, 0)])]
  transfers between devices with their start and end apart: 16 -> 16, of which waited for: 9 -> 8; matrix products, arithmetic and copies ran while one was open for 0% -> 0% of each run, Pallas kernels for 40% -> 39%
where the time goes in v10:
time: 160 us; the launch traced here: 159 us
  Pallas kernels  97 us (61%)
  starting transfers between devices  44 us (28%)
  waiting for transfers between devices  14.9 us (9%)
  local copies, waits for them, and re-layouts  2.44 us (2%)
    pallas_call x1, Pallas kernels, middle(): pl.pallas_call(functools.partial(middle_kernel, units), grid=(total // FB...  29.7 us
    pallas_call x1, Pallas kernels, backward(): pl.pallas_call(backward_kernel, grid=(seqs,), in_specs=[IN_SMEM, IN_SMEM,...  19.5 us
    pallas_call x1, Pallas kernels, forward(): pl.pallas_call(functools.partial(forward_kernel, chips, part), grid=(seqs...  18.8 us
    pallas_call x1, Pallas kernels, input_gradient(): pl.pallas_call(input_kernel, grid=(seqs, rows // DB), in_specs=[full, pl....  15.3 us
    ppermute x4, starting transfers between devices, per_device(): message = message + lax.ppermute(message, ('batch', 'head'), across)  7.63 us
    pallas_call x8, Pallas kernels, small_call(): pl.pallas_call(kernel, in_specs=[IN_SMEM if a.dtype == jnp.int32 else in_...  7.45 us
    all_to_all x1, starting transfers between devices, per_device(): lax.all_to_all(lead_sum.reshape(chips, shard_rows, 10 * HD), 'batch', 0, 0)  6.85 us
    ppermute x5, waiting for transfers between devices, swap(): return lax.ppermute(values, 'head', [(0, 1), (1, 0)])  6.68 us
  transfers between devices with their start and end apart: 16, of which 8 were waited for; matrix products, arithmetic and copies ran while one was open for 0% of the time, Pallas kernels for 39%

profile of v10, /device:TPU:0, one launch (start us, length us, event | category | flops | bytes accessed | tf_op | source)
XLA Modules:
  0.0 159.3 jit_solution(6555947051917924030)
XLA Ops:
  0.6 1.7 %pack_weights.1 = (bf16[24,640]{1,0:T(8,128)(2,1)}, bf16[24,1792]{1,0:T(8,128)(2,1)}) custom-call(f32[3,24,192]{2,1,0:T(8,128)} %bitcast.30, f32[24,192]{1,0:T(8,128)} %bitcast.35, f32[24,768]{1,0:T(8,128)} %up_ref.3, f32[24,768]{1,0:T(8,128)} %bitcast.32, f32[1,48]{1,0:T(1,128)} %bitcast.37), custom_call_target="tpu_custom_call" | custom-call | flops 2000000000 | bytes 1000000 | tf_op jit(solution)/shard_map/pack_weights/pallas_call | solution.py:696
  2.3 4.0 %collective-permute-start = (bf16[24,640]{1,0:T(8,128)(2,1)}, bf16[24,640]{1,0:T(8,128)(2,1)S(1)}, u32[]{:S(2)}, u32[]{:S(2)}) collective-permute-start(bf16[24,640]{1,0:T(8,128)(2,1)} %get-tuple-element.69.own_ref), channel_id=1, source_target_pairs={{0,16},{2,18},{4,20},{6,22},{8,24},{10,26},{12,28},{14,30},{16,0},... | collective-permute-start | bytes 92168 | tf_op jit(solution)/shard_map/ppermute | solution.py:749
  6.4 2.4 %collective-permute-done.far_ref = bf16[24,640]{1,0:T(8,128)(2,1)S(1)} collective-permute-done((bf16[24,640]{1,0:T(8,128)(2,1)}, bf16[24,640]{1,0:T(8,128)(2,1)S(1)}, u32[]{:S(2)}, u32[]{:S(2)}) %collective-permute-start) | collective-permute-done | bytes 30752 | tf_op jit(solution)/shard_map/ppermute | solution.py:749
  10.4 4.7 %all-to-all-start = ((bf16[8,2,24,640]{3,2,1,0:T(8,128)(2,1)}), bf16[8,2,24,640]{3,2,1,0:T(8,128)(2,1)S(1)}, u32[]{:S(2)}, u32[]{:S(2)}) async-start(bf16[8,2,24,640]{3,2,1,0:T(8,128)(2,1)} %pair_lead.1), calls=%async_computation | async-start | bytes 983040 | tf_op jit(solution)/shard_map/all_to_all | solution.py:753
  15.1 2.9 %collective-permute-start.1 = (bf16[24,1792]{1,0:T(8,128)(2,1)S(1)}, bf16[24,1792]{1,0:T(8,128)(2,1)S(1)}, u32[]{:S(2)}, u32[]{:S(2)}) collective-permute-start(bf16[24,1792]{1,0:T(8,128)(2,1)S(1)} %copy-done.3), channel_id=1, source_target_pairs={{0,16},{2,18},{4,20},{6,22},{8,24},{10,26},{12,28},{14,30},{16,0},... | collective-permute-start | bytes 258056 | tf_op jit(solution)/shard_map/ppermute | solution.py:750
  18.0 6.2 %prepare.1 = (f32[2560,384]{1,0:T(8,128)}, bf16[2560,384]{1,0:T(8,128)(2,1)}, bf16[384,2560]{1,0:T(8,128)(2,1)}) custom-call(s32[1]{0:T(128)} %bitcast.side_ref, s32[8]{0:T(128)} %len_ref.5, bf16[2560,384]{1,0:T(8,128)(2,1)} %bitcast.41, bf16[2560,384]{1,0:T(8,128)(2,1)} %bitcast.40), custom_call_target="tpu_custom_call" | custom-call | flops 5000000000 | bytes 1000000 | tf_op jit(solution)/shard_map/prepare/pallas_call | solution.py:123
  24.2 1.2 pair_rest.1
  25.4 5.3 %all-to-all-start.1 = ((bf16[8,2,24,1792]{3,2,1,0:T(8,128)(2,1)}), bf16[8,2,24,1792]{3,2,1,0:T(8,128)(2,1)S(1)}, u32[]{:S(2)}, u32[]{:S(2)}) async-start(bf16[8,2,24,1792]{3,2,1,0:T(8,128)(2,1)} %pair_rest.1), calls=%async_computation.1 | async-start | bytes 2752512 | tf_op jit(solution)/shard_map/all_to_all | solution.py:760
  30.7 18.8 %attention_forward.1 = (bf16[4,384,640]{2,1,0:T(8,128)(2,1)}, bf16[4,3,640,384]{3,2,1,0:T(8,128)(2,1)}, bf16[4,640,384]{2,1,0:T(8,128)(2,1)}, f32[4,640,384]{2,1...) custom-call(s32[1]{0:T(128)} %bitcast.side_ref, ...), custom_call_target="tpu_custom_call" | custom-call | flops 24000000000 | bytes 1000000 | tf_op jit(solution)/shard_map/attention_forward/pallas_call | solution.py:239
  49.4 0.9 copy-done.15
  50.3 2.4 %collective-permute-start.3 = (bf16[8,2,24,1792]{3,2,1,0:T(8,128)(2,1)S(1)}, bf16[8,2,24,1792]{3,2,1,0:T(8,128)(2,1)S(1)}, u32[]{:S(2)}, u32[]{:S(2)}) collective-permute-start(bf16[8,2,24,1792]{3,2,1,0:T(8,128)(2,1)S(1)} %all-to-all-done.1.own_ref), channel_id=1, source_target_pairs={{0,1},{1,0},{2,3},{3,2},{4,5},{5,4},{6,7},{7,6},{8,9},{9,8},{10,11... | collective-permute-start | bytes 4128776 | tf_op jit(solution)/shard_map/ppermute | solution.py:708
  52.7 2.8 %collective-permute-done.3.other_ref = bf16[8,2,24,1792]{3,2,1,0:T(8,128)(2,1)S(1)} collective-permute-done((bf16[8,2,24,1792]{3,2,1,0:T(8,128)(2,1)S(1)}, bf16[8,2,24,1792]{3,2,1,0:T(8,128)(2,1)S(1)}, u32[]{:S(2)}, u32[]{:S(2)}) %collective-permute-start.3) | collective-permute-done | bytes 1376288 | tf_op jit(solution)/shard_map/ppermute | solution.py:708
  55.5 29.7 %feed_forward.1 = (f32[2560,384]{1,0:T(8,128)}, bf16[2,2560,768]{2,1,0:T(8,128)(2,1)}, f32[2560,384]{1,0:T(8,128)}, bf16[2560,384]{1,0:T(8,128)(2,1)S(1)}, bf16[...) custom-call(bf16[2560,384]{1,0:T(8,128)(2,1)} %bitcast.42, ...), custom_call_target="tpu_custom_call" | custom-call | flops 35999997952 | bytes 1000000 | tf_op jit(solution)/shard_map/feed_forward/pallas_call | solution.py:359
  85.7 2.8 %collective-permute-done.4.right_ref = bf16[384,1792]{1,0:T(8,128)(2,1)S(1)} collective-permute-done((bf16[384,1792]{1,0:T(8,128)(2,1)S(1)}, bf16[384,1792]{1,0:T(8,128)(2,1)S(1)}, u32[]{:S(2)}, u32[]{:S(2)}) %collective-permute-start.4) | collective-permute-done | bytes 1376288 | tf_op jit(solution)/shard_map/ppermute | solution.py:708
  88.4 1.4 add_rest.1
  89.8 5.5 %all-to-all-start.2 = ((bf16[8,2,24,1792]{3,2,1,0:T(8,128)(2,1)}), bf16[8,2,24,1792]{3,2,1,0:T(8,128)(2,1)S(1)}, u32[]{:S(2)}, u32[]{:S(2)}) async-start(bf16[8,2,24,1792]{3,2,1,0:T(8,128)(2,1)} %add_rest.1), calls=%async_computation.2 | async-start | bytes 2752512 | tf_op jit(solution)/shard_map/all_to_all | solution.py:773
  95.3 19.5 %attention_backward.1 = (bf16[4,640,1152]{2,1,0:T(8,128)(2,1)}, bf16[384,640]{1,0:T(8,128)(2,1)S(1)}, bf16[384,640]{1,0:T(8,128)(2,1)S(1)}) custom-call(s32[1]{0:T(128)} %bitcast.side_ref, s32[8]{0:T(128)S(1)} %copy-done.12, bf16[4,384,640]{2,1,0:T(8,128)(2,1)} %get-tuple-element.76.n1t_ref, bf16[4,3,640,384]{3,2,1,0:T(8,128)(2,1)} %get-tuple-element.77.qkv_ref, ...), custom_call_target="tpu_custom_call" | custom-call | flops 27000000512 | bytes 1000000 | tf_op jit(solution)/shard_map/attention_backward/pallas_call | solution.py:497
  114.8 2.6 %collective-permute-start.5 = (bf16[384,640]{1,0:T(8,128)(2,1)S(1)}, bf16[384,640]{1,0:T(8,128)(2,1)S(1)}, u32[]{:S(2)}, u32[]{:S(2)}) collective-permute-start(bf16[384,640]{1,0:T(8,128)(2,1)S(1)} %get-tuple-element.104), channel_id=1, source_target_pairs={{0,1},{1,0},{2,3},{3,2},{4,5},{5,4},{6,7},{7,6},{8,9},{9,8},{10,11... | collective-permute-start | bytes 1474568 | tf_op jit(solution)/shard_map/ppermute | solution.py:708
  117.6 1.6 %collective-permute-start.6 = (bf16[24,1792]{1,0:T(8,128)(2,1)S(1)}, bf16[24,1792]{1,0:T(8,128)(2,1)S(1)}, u32[]{:S(2)}, u32[]{:S(2)}) collective-permute-start(bf16[24,1792]{1,0:T(8,128)(2,1)S(1)} %get-tuple-element.107), channel_id=1, source_target_pairs={{0,16},{2,18},{4,20},{6,22},{8,24},{10,26},{12,28},{14,30},{16,0},... | collective-permute-start | bytes 258056 | tf_op jit(solution)/shard_map/ppermute | solution.py:785
  119.2 0.9 add_lead.1
  120.1 6.9 %all-to-all-start.3 = ((bf16[16,24,640]{2,1,0:T(8,128)(2,1)}), bf16[16,24,640]{2,1,0:T(8,128)(2,1)S(1)}, u32[]{:S(2)}, u32[]{:S(2)}) async-start(bf16[16,24,640]{2,1,0:T(8,128)(2,1)} %bitcast.15), calls=%async_computation.3 | async-start | bytes 983040 | tf_op jit(solution)/shard_map/all_to_all | solution.py:781
  127.0 15.3 %input_gradient.1 = (f32[4,640,384]{2,1,0:T(8,128)}, f32[8,384]{1,0:T(8,128)}, bf16[4,640,384]{2,1,0:T(8,128)(2,1)}) custom-call(bf16[4,640,384]{2,1,0:T(8,128)(2,1)} %tok_ref.1, bf16[4,640,1152]{2,1,0:T(8,128)(2,1)} %get-tuple-element.91.gp_ref, f32[4,640,384]{2,1,0:T(8,128)} %bitcast.44, bf16[384,1152]{1,0:T(8,128)(2,1)} %copy-done.15, ...), custom_call_target="tpu_custom_call" | custom-call | flops 12999999488 | bytes 1000000 | tf_op jit(solution)/shard_map/input_gradient/pallas_call | solution.py:548
  143.3 1.2 collective-permute-done.7
  144.5 1.7 %collective-permute-start.8 = (f32[8,384]{1,0:T(8,128)S(1)}, f32[8,384]{1,0:T(8,128)S(1)}, u32[]{:S(2)}, u32[]{:S(2)}) collective-permute-start(f32[8,384]{1,0:T(8,128)S(1)} %add.20), channel_id=1, source_target_pairs={{0,3},{1,2},{2,1},{3,0},{4,7},{5,6},{6,5},{7,4},{8,11},{9,10},{10,... | collective-permute-start | bytes 36872 | tf_op jit(solution)/shard_map/ppermute | solution.py:799
  146.2 1.4 collective-permute-done.8
  147.6 1.7 %collective-permute-start.9 = (f32[8,384]{1,0:T(8,128)S(1)}, f32[8,384]{1,0:T(8,128)S(1)}, u32[]{:S(2)}, u32[]{:S(2)}) collective-permute-start(f32[8,384]{1,0:T(8,128)S(1)} %add.21), channel_id=1, source_target_pairs={{0,5},{1,4},{2,7},{3,6},{4,1},{5,0},{6,3},{7,2},{8,13},{9,12},{10,... | collective-permute-start | bytes 36872 | tf_op jit(solution)/shard_map/ppermute | solution.py:799
  149.3 1.4 collective-permute-done.9
  150.7 1.7 %collective-permute-start.10 = (f32[8,384]{1,0:T(8,128)S(1)}, f32[8,384]{1,0:T(8,128)S(1)}, u32[]{:S(2)}, u32[]{:S(2)}) collective-permute-start(f32[8,384]{1,0:T(8,128)S(1)} %add.22), channel_id=1, source_target_pairs={{0,9},{1,8},{2,11},{3,10},{4,13},{5,12},{6,15},{7,14},{8,1},{9,0},... | collective-permute-start | bytes 36872 | tf_op jit(solution)/shard_map/ppermute | solution.py:799
  152.4 1.4 collective-permute-done.10
  153.9 2.6 %collective-permute-start.11 = (f32[8,384]{1,0:T(8,128)S(1)}, f32[8,384]{1,0:T(8,128)S(1)}, u32[]{:S(2)}, u32[]{:S(2)}) collective-permute-start(f32[8,384]{1,0:T(8,128)S(1)} %add.23), channel_id=1, source_target_pairs={{0,17},{1,16},{2,19},{3,18},{4,21},{5,20},{6,23},{7,22},{8,25},{9,... | collective-permute-start | bytes 36872 | tf_op jit(solution)/shard_map/ppermute | solution.py:799
  156.4 1.4 collective-permute-done.11
  158.0 1.2 update_weights.1
  (56 shorter events, 3.2 us)
Async XLA Ops:
  2.3 6.4 %collective-permute-start = (bf16[24,640]{1,0:T(8,128)(2,1)}, bf16[24,640]{1,0:T(8,128)(2,1)S(1)}, u32[]{:S(2)}, u32[]{:S(2)}) collective-permute-start(bf16[24,640]{1,0:T(8,128)(2,1)} %get-tuple-element.69.own_ref), channel_id=1, source_target_pairs={{0,16},{2,18},{4,20},{6,22},{8,24},{10,26},{12,28},{14,30},{16,0},... | collective-permute-start | bytes 92168 | tf_op jit(solution)/shard_map/ppermute | solution.py:749
  9.5 5.6 %copy-start.3 = (bf16[24,1792]{1,0:T(8,128)(2,1)S(1)}, bf16[24,1792]{1,0:T(8,128)(2,1)}, u32[]{:S(2)}) copy-start(bf16[24,1792]{1,0:T(8,128)(2,1)} %get-tuple-element.70.own_ref) | copy-start | bytes 258052
  10.4 15.0 %all-to-all-start = ((bf16[8,2,24,640]{3,2,1,0:T(8,128)(2,1)}), bf16[8,2,24,640]{3,2,1,0:T(8,128)(2,1)S(1)}, u32[]{:S(2)}, u32[]{:S(2)}) async-start(bf16[8,2,24,640]{3,2,1,0:T(8,128)(2,1)} %pair_lead.1), calls=%async_computation | async-start | bytes 983040 | tf_op jit(solution)/shard_map/all_to_all | solution.py:753
  15.1 9.1 %collective-permute-start.1 = (bf16[24,1792]{1,0:T(8,128)(2,1)S(1)}, bf16[24,1792]{1,0:T(8,128)(2,1)S(1)}, u32[]{:S(2)}, u32[]{:S(2)}) collective-permute-start(bf16[24,1792]{1,0:T(8,128)(2,1)S(1)} %copy-done.3), channel_id=1, source_target_pairs={{0,16},{2,18},{4,20},{6,22},{8,24},{10,26},{12,28},{14,30},{16,0},... | collective-permute-start | bytes 258056 | tf_op jit(solution)/shard_map/ppermute | solution.py:750
  25.4 5.3 %copy-start.10 = (s32[8,640]{1,0:T(8,128)S(1)}, s32[8,640]{1,0:T(8,128)}, u32[]{:S(2)}) copy-start(s32[8,640]{1,0:T(8,128)} %mask_ref.1) | copy-start | bytes 61444
  25.4 5.3 %copy-start.12 = (s32[8]{0:T(128)S(1)}, s32[8]{0:T(128)}, u32[]{:S(2)}) copy-start(s32[8]{0:T(128)} %len_ref.5) | copy-start | bytes 100
  25.4 5.3 %collective-permute-start.2 = (bf16[8,2,24,640]{3,2,1,0:T(8,128)(2,1)S(1)}, bf16[8,2,24,640]{3,2,1,0:T(8,128)(2,1)S(1)}, u32[]{:S(2)}, u32[]{:S(2)}) collective-permute-start(bf16[8,2,24,640]{3,2,1,0:T(8,128)(2,1)S(1)} %all-to-all-done.own_ref), channel_id=1, source_target_pairs={{0,1},{1,0},{2,3},{3,2},{4,5},{5,4},{6,7},{7,6},{8,9},{9,8},{10,11... | collective-permute-start | bytes 1474568 | tf_op jit(solution)/shard_map/ppermute | solution.py:708
  25.4 25.0 %all-to-all-start.1 = ((bf16[8,2,24,1792]{3,2,1,0:T(8,128)(2,1)}), bf16[8,2,24,1792]{3,2,1,0:T(8,128)(2,1)S(1)}, u32[]{:S(2)}, u32[]{:S(2)}) async-start(bf16[8,2,24,1792]{3,2,1,0:T(8,128)(2,1)} %pair_rest.1), calls=%async_computation.1 | async-start | bytes 2752512 | tf_op jit(solution)/shard_map/all_to_all | solution.py:760
  50.3 34.9 %copy-start.18 = (f32[4,384]{1,0:T(4,128)}, f32[4,384]{1,0:T(4,128)S(1)}, u32[]{:S(2)}) copy-start(f32[4,384]{1,0:T(4,128)S(1)} %get-tuple-element.86.norms_ref) | copy-start | bytes 18436
  50.3 5.1 %collective-permute-start.3 = (bf16[8,2,24,1792]{3,2,1,0:T(8,128)(2,1)S(1)}, bf16[8,2,24,1792]{3,2,1,0:T(8,128)(2,1)S(1)}, u32[]{:S(2)}, u32[]{:S(2)}) collective-permute-start(bf16[8,2,24,1792]{3,2,1,0:T(8,128)(2,1)S(1)} %all-to-all-done.1.own_ref), channel_id=1, source_target_pairs={{0,1},{1,0},{2,3},{3,2},{4,5},{5,4},{6,7},{7,6},{8,9},{9,8},{10,11... | collective-permute-start | bytes 4128776 | tf_op jit(solution)/shard_map/ppermute | solution.py:708
  85.2 4.6 %copy-start.14 = (bf16[2560,384]{1,0:T(8,128)(2,1)}, bf16[2560,384]{1,0:T(8,128)(2,1)S(1)}, u32[]{:S(2)}) copy-start(bf16[2560,384]{1,0:T(8,128)(2,1)S(1)} %get-tuple-element.90) | copy-start | bytes 5898244
  85.2 4.6 %copy-start.17 = (f32[16,384]{1,0:T(8,128)}, f32[16,384]{1,0:T(8,128)S(1)}, u32[]{:S(2)}) copy-start(f32[16,384]{1,0:T(8,128)S(1)} %get-tuple-element.94.two_ref) | copy-start | bytes 73732
  85.2 3.2 %collective-permute-start.4 = (bf16[384,1792]{1,0:T(8,128)(2,1)S(1)}, bf16[384,1792]{1,0:T(8,128)(2,1)S(1)}, u32[]{:S(2)}, u32[]{:S(2)}) collective-permute-start(bf16[384,1792]{1,0:T(8,128)(2,1)S(1)} %get-tuple-element.88), channel_id=1, source_target_pairs={{0,1},{1,0},{2,3},{3,2},{4,5},{5,4},{6,7},{7,6},{8,9},{9,8},{10,11... | collective-permute-start | bytes 4128776 | tf_op jit(solution)/shard_map/ppermute | solution.py:708
  89.8 27.6 %all-to-all-start.2 = ((bf16[8,2,24,1792]{3,2,1,0:T(8,128)(2,1)}), bf16[8,2,24,1792]{3,2,1,0:T(8,128)(2,1)S(1)}, u32[]{:S(2)}, u32[]{:S(2)}) async-start(bf16[8,2,24,1792]{3,2,1,0:T(8,128)(2,1)} %add_rest.1), calls=%async_computation.2 | async-start | bytes 2752512 | tf_op jit(solution)/shard_map/all_to_all | solution.py:773
  114.8 4.4 %collective-permute-start.5 = (bf16[384,640]{1,0:T(8,128)(2,1)S(1)}, bf16[384,640]{1,0:T(8,128)(2,1)S(1)}, u32[]{:S(2)}, u32[]{:S(2)}) collective-permute-start(bf16[384,640]{1,0:T(8,128)(2,1)S(1)} %get-tuple-element.104), channel_id=1, source_target_pairs={{0,1},{1,0},{2,3},{3,2},{4,5},{5,4},{6,7},{7,6},{8,9},{9,8},{10,11... | collective-permute-start | bytes 1474568 | tf_op jit(solution)/shard_map/ppermute | solution.py:708
  117.6 24.7 %collective-permute-start.6 = (bf16[24,1792]{1,0:T(8,128)(2,1)S(1)}, bf16[24,1792]{1,0:T(8,128)(2,1)S(1)}, u32[]{:S(2)}, u32[]{:S(2)}) collective-permute-start(bf16[24,1792]{1,0:T(8,128)(2,1)S(1)} %get-tuple-element.107), channel_id=1, source_target_pairs={{0,16},{2,18},{4,20},{6,22},{8,24},{10,26},{12,28},{14,30},{16,0},... | collective-permute-start | bytes 258056 | tf_op jit(solution)/shard_map/ppermute | solution.py:785
  120.1 22.2 %all-to-all-start.3 = ((bf16[16,24,640]{2,1,0:T(8,128)(2,1)}), bf16[16,24,640]{2,1,0:T(8,128)(2,1)S(1)}, u32[]{:S(2)}, u32[]{:S(2)}) async-start(bf16[16,24,640]{2,1,0:T(8,128)(2,1)} %bitcast.15), calls=%async_computation.3 | async-start | bytes 983040 | tf_op jit(solution)/shard_map/all_to_all | solution.py:781
  143.0 14.8 %copy-start = (f32[2,24,3,192]{3,1,2,0:T(8,128)S(1)}, f32[2,24,3,192]{3,1,2,0:T(8,128)}, u32[]{:S(2)}) copy-start(f32[2,24,3,192]{3,1,2,0:T(8,128)} %param.23) | copy-start | bytes 331780
  143.0 14.8 %copy-start.1 = (f32[2,24,768]{2,1,0:T(8,128)S(1)}, f32[2,24,768]{2,1,0:T(8,128)}, u32[]{:S(2)}) copy-start(f32[2,24,768]{2,1,0:T(8,128)} %up_m_ref.1) | copy-start | bytes 442372
  143.0 14.9 %copy-start.2 = (f32[2,768,24]{1,2,0:T(8,128)S(1)}, f32[2,768,24]{1,2,0:T(8,128)}, u32[]{:S(2)}) copy-start(f32[2,768,24]{1,2,0:T(8,128)} %param.26) | copy-start | bytes 442372
  143.0 14.9 %copy-start.4 = (f32[24,3,192]{2,0,1:T(8,128)S(1)}, f32[24,3,192]{2,0,1:T(8,128)}, u32[]{:S(2)}) copy-start(f32[24,3,192]{2,0,1:T(8,128)} %param.18) | copy-start | bytes 165892
  143.0 14.9 %copy-start.5 = (f32[24,768]{1,0:T(8,128)S(1)}, f32[24,768]{1,0:T(8,128)}, u32[]{:S(2)}) copy-start(f32[24,768]{1,0:T(8,128)} %up_ref.3) | copy-start | bytes 221188
  143.1 14.9 %copy-start.6 = (f32[768,24]{0,1:T(8,128)S(1)}, f32[768,24]{0,1:T(8,128)}, u32[]{:S(2)}) copy-start(f32[768,24]{0,1:T(8,128)} %param.21) | copy-start | bytes 221188
  143.1 14.9 %copy-start.7 = (f32[2,192,24]{1,2,0:T(8,128)S(1)}, f32[2,192,24]{1,2,0:T(8,128)}, u32[]{:S(2)}) copy-start(f32[2,192,24]{1,2,0:T(8,128)} %param.24) | copy-start | bytes 110596
  143.1 14.9 %copy-start.9 = (f32[192,24]{0,1:T(8,128)S(1)}, f32[192,24]{0,1:T(8,128)}, u32[]{:S(2)}) copy-start(f32[192,24]{0,1:T(8,128)} %param.19) | copy-start | bytes 55300
  143.1 14.9 %copy-start.11 = (f32[2,48]{1,0:T(2,128)S(1)}, f32[2,48]{1,0:T(2,128)}, u32[]{:S(2)}) copy-start(f32[2,48]{1,0:T(2,128)} %norm_m_ref.1) | copy-start | bytes 1156
  143.1 14.9 %copy-start.13 = (f32[48]{0:T(128)S(1)}, f32[48]{0:T(128)}, u32[]{:S(2)}) copy-start(f32[48]{0:T(128)} %param.22) | copy-start | bytes 580
  143.2 1.2 collective-permute-start.7
  144.5 3.1 %collective-permute-start.8 = (f32[8,384]{1,0:T(8,128)S(1)}, f32[8,384]{1,0:T(8,128)S(1)}, u32[]{:S(2)}, u32[]{:S(2)}) collective-permute-start(f32[8,384]{1,0:T(8,128)S(1)} %add.20), channel_id=1, source_target_pairs={{0,3},{1,2},{2,1},{3,0},{4,7},{5,6},{6,5},{7,4},{8,11},{9,10},{10,... | collective-permute-start | bytes 36872 | tf_op jit(solution)/shard_map/ppermute | solution.py:799
  147.6 3.1 %collective-permute-start.9 = (f32[8,384]{1,0:T(8,128)S(1)}, f32[8,384]{1,0:T(8,128)S(1)}, u32[]{:S(2)}, u32[]{:S(2)}) collective-permute-start(f32[8,384]{1,0:T(8,128)S(1)} %add.21), channel_id=1, source_target_pairs={{0,5},{1,4},{2,7},{3,6},{4,1},{5,0},{6,3},{7,2},{8,13},{9,12},{10,... | collective-permute-start | bytes 36872 | tf_op jit(solution)/shard_map/ppermute | solution.py:799
  150.7 3.1 %collective-permute-start.10 = (f32[8,384]{1,0:T(8,128)S(1)}, f32[8,384]{1,0:T(8,128)S(1)}, u32[]{:S(2)}, u32[]{:S(2)}) collective-permute-start(f32[8,384]{1,0:T(8,128)S(1)} %add.22), channel_id=1, source_target_pairs={{0,9},{1,8},{2,11},{3,10},{4,13},{5,12},{6,15},{7,14},{8,1},{9,0},... | collective-permute-start | bytes 36872 | tf_op jit(solution)/shard_map/ppermute | solution.py:799
  153.9 4.0 %collective-permute-start.11 = (f32[8,384]{1,0:T(8,128)S(1)}, f32[8,384]{1,0:T(8,128)S(1)}, u32[]{:S(2)}, u32[]{:S(2)}) collective-permute-start(f32[8,384]{1,0:T(8,128)S(1)} %add.23), channel_id=1, source_target_pairs={{0,17},{1,16},{2,19},{3,18},{4,21},{5,20},{6,23},{7,22},{8,25},{9,... | collective-permute-start | bytes 36872 | tf_op jit(solution)/shard_map/ppermute | solution.py:799
  (3 other events, 2.4 us)

commit v11 on v10

--- a/solution.py
+++ b/solution.py
@@ -216,7 +216,7 @@
         if half == 1:
             cols = slice(pair * PAIR, (pair + 1) * PAIR)
             att_ref[sl, cols] = jnp.where(lane < HD, outs[0][0], outs[1][0]).astype(BF16)
-            linv_ref[sl, cols] = jnp.where(lane < HD, outs[0][1], outs[1][1])
+            linv_ref[sl, cols] = jnp.where(lane < HD, outs[0][1], outs[1][1]).astype(BF16)
 
     pending = None
     for pair in range(pairs):
@@ -253,7 +253,7 @@
             shape((seqs, width, rows), BF16),
             shape((seqs, pairs, rows, 3 * PAIR), BF16),
             shape((seqs, rows, width), BF16),
-            shape((seqs, rows, width), F32),
+            shape((seqs, rows, width), BF16),
             shape((seqs, heads, rows, rows), BF16),
             shape((width, 3 * width), BF16),
             shape((4, width), F32),
@@ -332,7 +332,7 @@
     weigh(1)
     gm = gmid.astype(BF16)
     gout_ref[...] += mm(gm, att, TN)
-    gatt_ref[...] = (mm(gm, wo_ref[...]) * linv_ref[...]).astype(BF16)
+    gatt_ref[...] = (mm(gm, wo_ref[...]) * linv_ref[...].astype(F32)).astype(BF16)
 
     @pl.when(step == pl.num_programs(0) - 1)
     def _():

time: 160 us -> 159 us (level)
  starting transfers between devices: 44 us -> 33.7 us
  Pallas kernels: 97 us -> 104 us
  waiting for transfers between devices: 14.9 us -> 17 us
    ppermute x5, starting transfers between devices: 5.53 us -> 0.35 us  [swap(): return lax.ppermute(values, 'head', [(0, 1), (1, 0)])]
    pallas_call x1, Pallas kernels: 19.5 us -> 23.8 us  [backward(): pl.pallas_call(backward_kernel, grid=(seqs,), in_specs=[IN_SMEM, IN_SMEM,...]
    pallas_call x1, Pallas kernels: 18.8 us -> 21.8 us  [forward(): pl.pallas_call(functools.partial(forward_kernel, chips, part), grid=(seqs...]
    ppermute x5, waiting for transfers between devices: 6.68 us -> 8.8 us  [swap(): return lax.ppermute(values, 'head', [(0, 1), (1, 0)])]
    all_to_all x1, starting transfers between devices: 5.46 us -> 3.6 us  [per_device(): lax.all_to_all(rest_sum, 'batch', 0, 0, axis_index_groups=teams)]
    all_to_all x1, starting transfers between devices: 6.85 us -> 5.1 us  [per_device(): lax.all_to_all(lead_sum.reshape(chips, shard_rows, 10 * HD), 'batch', 0, 0)]
  transfers between devices with their start and end apart: 16 -> 16, of which waited for: 8 -> 9; matrix products, arithmetic and copies ran while one was open for 0% -> 0% of each run, Pallas kernels for 39% -> 44%
where the time goes in v11:
time: 159 us; the launch traced here: 158 us
  Pallas kernels  104 us (65%)
  starting transfers between devices  33.7 us (21%)
  waiting for transfers between devices  17 us (11%)
  local copies, waits for them, and re-layouts  2.44 us (2%)
    pallas_call x1, Pallas kernels, middle(): pl.pallas_call(functools.partial(middle_kernel, units), grid=(total // FB...  29.6 us
    pallas_call x1, Pallas kernels, backward(): pl.pallas_call(backward_kernel, grid=(seqs,), in_specs=[IN_SMEM, IN_SMEM,...  23.8 us
    pallas_call x1, Pallas kernels, forward(): pl.pallas_call(functools.partial(forward_kernel, chips, part), grid=(seqs...  21.8 us
    pallas_call x1, Pallas kernels, input_gradient(): pl.pallas_call(input_kernel, grid=(seqs, rows // DB), in_specs=[full, pl....  15.3 us
    ppermute x5, waiting for transfers between devices, swap(): return lax.ppermute(values, 'head', [(0, 1), (1, 0)])  8.8 us
    ppermute x4, starting transfers between devices, per_device(): message = message + lax.ppermute(message, ('batch', 'head'), across)  7.62 us
    pallas_call x8, Pallas kernels, small_call(): pl.pallas_call(kernel, in_specs=[IN_SMEM if a.dtype == jnp.int32 else in_...  7.45 us
    pallas_call x1, Pallas kernels, prepare(): pl.pallas_call(functools.partial(prepare_kernel, seq_rows), grid=(total /...  6.18 us
  transfers between devices with their start and end apart: 16, of which 9 were waited for; matrix products, arithmetic and copies ran while one was open for 0% of the time, Pallas kernels for 44%

profile of v11, /device:TPU:0, one launch (start us, length us, event | category | flops | bytes accessed | tf_op | source)
XLA Modules:
  0.0 158.4 jit_solution(8746227485143319408)
XLA Ops:
  0.6 1.7 %pack_weights.1 = (bf16[24,640]{1,0:T(8,128)(2,1)}, bf16[24,1792]{1,0:T(8,128)(2,1)}) custom-call(f32[3,24,192]{2,1,0:T(8,128)} %bitcast.30, f32[24,192]{1,0:T(8,128)} %bitcast.35, f32[24,768]{1,0:T(8,128)} %up_ref.3, f32[24,768]{1,0:T(8,128)} %bitcast.32, f32[1,48]{1,0:T(1,128)} %bitcast.37), custom_call_target="tpu_custom_call" | custom-call | flops 2000000000 | bytes 1000000 | tf_op jit(solution)/shard_map/pack_weights/pallas_call | solution.py:696
  2.3 4.0 %collective-permute-start = (bf16[24,640]{1,0:T(8,128)(2,1)}, bf16[24,640]{1,0:T(8,128)(2,1)S(1)}, u32[]{:S(2)}, u32[]{:S(2)}) collective-permute-start(bf16[24,640]{1,0:T(8,128)(2,1)} %get-tuple-element.69.own_ref), channel_id=1, source_target_pairs={{0,16},{2,18},{4,20},{6,22},{8,24},{10,26},{12,28},{14,30},{16,0},... | collective-permute-start | bytes 92168 | tf_op jit(solution)/shard_map/ppermute | solution.py:749
  6.4 2.4 %collective-permute-done.far_ref = bf16[24,640]{1,0:T(8,128)(2,1)S(1)} collective-permute-done((bf16[24,640]{1,0:T(8,128)(2,1)}, bf16[24,640]{1,0:T(8,128)(2,1)S(1)}, u32[]{:S(2)}, u32[]{:S(2)}) %collective-permute-start) | collective-permute-done | bytes 30752 | tf_op jit(solution)/shard_map/ppermute | solution.py:749
  8.8 0.8 copy-done.8
  9.5 0.8 pair_lead.1
  10.4 4.7 %all-to-all-start = ((bf16[8,2,24,640]{3,2,1,0:T(8,128)(2,1)}), bf16[8,2,24,640]{3,2,1,0:T(8,128)(2,1)S(1)}, u32[]{:S(2)}, u32[]{:S(2)}) async-start(bf16[8,2,24,640]{3,2,1,0:T(8,128)(2,1)} %pair_lead.1), calls=%async_computation | async-start | bytes 983040 | tf_op jit(solution)/shard_map/all_to_all | solution.py:753
  15.1 2.9 %collective-permute-start.1 = (bf16[24,1792]{1,0:T(8,128)(2,1)S(1)}, bf16[24,1792]{1,0:T(8,128)(2,1)S(1)}, u32[]{:S(2)}, u32[]{:S(2)}) collective-permute-start(bf16[24,1792]{1,0:T(8,128)(2,1)S(1)} %copy-done.3), channel_id=1, source_target_pairs={{0,16},{2,18},{4,20},{6,22},{8,24},{10,26},{12,28},{14,30},{16,0},... | collective-permute-start | bytes 258056 | tf_op jit(solution)/shard_map/ppermute | solution.py:750
  18.0 6.2 %prepare.1 = (f32[2560,384]{1,0:T(8,128)}, bf16[2560,384]{1,0:T(8,128)(2,1)}, bf16[384,2560]{1,0:T(8,128)(2,1)}) custom-call(s32[1]{0:T(128)} %bitcast.side_ref, s32[8]{0:T(128)} %len_ref.5, bf16[2560,384]{1,0:T(8,128)(2,1)} %bitcast.41, bf16[2560,384]{1,0:T(8,128)(2,1)} %bitcast.40), custom_call_target="tpu_custom_call" | custom-call | flops 5000000000 | bytes 1000000 | tf_op jit(solution)/shard_map/prepare/pallas_call | solution.py:123
  24.2 1.2 pair_rest.1
  25.4 5.3 %all-to-all-start.1 = ((bf16[8,2,24,1792]{3,2,1,0:T(8,128)(2,1)}), bf16[8,2,24,1792]{3,2,1,0:T(8,128)(2,1)S(1)}, u32[]{:S(2)}, u32[]{:S(2)}) async-start(bf16[8,2,24,1792]{3,2,1,0:T(8,128)(2,1)} %pair_rest.1), calls=%async_computation.1 | async-start | bytes 2752512 | tf_op jit(solution)/shard_map/all_to_all | solution.py:760
  30.7 21.8 %attention_forward.1 = (bf16[4,384,640]{2,1,0:T(8,128)(2,1)}, bf16[4,3,640,384]{3,2,1,0:T(8,128)(2,1)}, bf16[4,640,384]{2,1,0:T(8,128)(2,1)}, bf16[4,640,384]{2,...) custom-call(s32[1]{0:T(128)} %bitcast.side_ref, ...), custom_call_target="tpu_custom_call" | custom-call | flops 24000000000 | bytes 1000000 | tf_op jit(solution)/shard_map/attention_forward/pallas_call | solution.py:239
  52.5 0.9 copy-done.15
  53.4 3.1 %collective-permute-done.3.other_ref = bf16[8,2,24,1792]{3,2,1,0:T(8,128)(2,1)S(1)} collective-permute-done((bf16[8,2,24,1792]{3,2,1,0:T(8,128)(2,1)S(1)}, bf16[8,2,24,1792]{3,2,1,0:T(8,128)(2,1)S(1)}, u32[]{:S(2)}, u32[]{:S(2)}) %collective-permute-start.3) | collective-permute-done | bytes 1376288 | tf_op jit(solution)/shard_map/ppermute | solution.py:708
  56.5 29.6 %feed_forward.1 = (f32[2560,384]{1,0:T(8,128)}, bf16[2,2560,768]{2,1,0:T(8,128)(2,1)}, f32[2560,384]{1,0:T(8,128)}, bf16[2560,384]{1,0:T(8,128)(2,1)S(1)}, bf16[...) custom-call(bf16[2560,384]{1,0:T(8,128)(2,1)} %bitcast.42, ...), custom_call_target="tpu_custom_call" | custom-call | flops 35999997952 | bytes 1000000 | tf_op jit(solution)/shard_map/feed_forward/pallas_call | solution.py:359
  86.4 3.0 %collective-permute-done.4.right_ref = bf16[384,1792]{1,0:T(8,128)(2,1)S(1)} collective-permute-done((bf16[384,1792]{1,0:T(8,128)(2,1)S(1)}, bf16[384,1792]{1,0:T(8,128)(2,1)S(1)}, u32[]{:S(2)}, u32[]{:S(2)}) %collective-permute-start.4) | collective-permute-done | bytes 1376288 | tf_op jit(solution)/shard_map/ppermute | solution.py:708
  89.4 1.4 add_rest.1
  90.8 3.6 %all-to-all-start.2 = ((bf16[8,2,24,1792]{3,2,1,0:T(8,128)(2,1)}), bf16[8,2,24,1792]{3,2,1,0:T(8,128)(2,1)S(1)}, u32[]{:S(2)}, u32[]{:S(2)}) async-start(bf16[8,2,24,1792]{3,2,1,0:T(8,128)(2,1)} %add_rest.1), calls=%async_computation.2 | async-start | bytes 2752512 | tf_op jit(solution)/shard_map/all_to_all | solution.py:773
  94.3 23.8 %attention_backward.1 = (bf16[4,640,1152]{2,1,0:T(8,128)(2,1)}, bf16[384,640]{1,0:T(8,128)(2,1)S(1)}, bf16[384,640]{1,0:T(8,128)(2,1)S(1)}) custom-call(s32[1]{0:T(128)} %bitcast.side_ref, s32[8]{0:T(128)S(1)} %copy-done.12, bf16[4,384,640]{2,1,0:T(8,128)(2,1)} %get-tuple-element.76.n1t_ref, bf16[4,3,640,384]{3,2,1,0:T(8,128)(2,1)} %get-tuple-element.77.qkv_ref, ...), custom_call_target="tpu_custom_call" | custom-call | flops 27000000512 | bytes 1000000 | tf_op jit(solution)/shard_map/attention_backward/pallas_call | solution.py:497
  118.4 1.6 collective-permute-done.5.right_ref
  120.0 0.9 add_lead.1
  120.9 5.1 %all-to-all-start.3 = ((bf16[16,24,640]{2,1,0:T(8,128)(2,1)}), bf16[16,24,640]{2,1,0:T(8,128)(2,1)S(1)}, u32[]{:S(2)}, u32[]{:S(2)}) async-start(bf16[16,24,640]{2,1,0:T(8,128)(2,1)} %bitcast.15), calls=%async_computation.3 | async-start | bytes 983040 | tf_op jit(solution)/shard_map/all_to_all | solution.py:781
  126.0 15.3 %input_gradient.1 = (f32[4,640,384]{2,1,0:T(8,128)}, f32[8,384]{1,0:T(8,128)}, bf16[4,640,384]{2,1,0:T(8,128)(2,1)}) custom-call(bf16[4,640,384]{2,1,0:T(8,128)(2,1)} %tok_ref.1, bf16[4,640,1152]{2,1,0:T(8,128)(2,1)} %get-tuple-element.91.gp_ref, f32[4,640,384]{2,1,0:T(8,128)} %bitcast.44, bf16[384,1152]{1,0:T(8,128)(2,1)} %copy-done.15, ...), custom_call_target="tpu_custom_call" | custom-call | flops 12999999488 | bytes 1000000 | tf_op jit(solution)/shard_map/input_gradient/pallas_call | solution.py:548
  142.4 1.1 collective-permute-done.7
  143.5 1.7 %collective-permute-start.8 = (f32[8,384]{1,0:T(8,128)S(1)}, f32[8,384]{1,0:T(8,128)S(1)}, u32[]{:S(2)}, u32[]{:S(2)}) collective-permute-start(f32[8,384]{1,0:T(8,128)S(1)} %add.20), channel_id=1, source_target_pairs={{0,3},{1,2},{2,1},{3,0},{4,7},{5,6},{6,5},{7,4},{8,11},{9,10},{10,... | collective-permute-start | bytes 36872 | tf_op jit(solution)/shard_map/ppermute | solution.py:799
  145.2 1.4 collective-permute-done.8
  146.7 1.7 %collective-permute-start.9 = (f32[8,384]{1,0:T(8,128)S(1)}, f32[8,384]{1,0:T(8,128)S(1)}, u32[]{:S(2)}, u32[]{:S(2)}) collective-permute-start(f32[8,384]{1,0:T(8,128)S(1)} %add.21), channel_id=1, source_target_pairs={{0,5},{1,4},{2,7},{3,6},{4,1},{5,0},{6,3},{7,2},{8,13},{9,12},{10,... | collective-permute-start | bytes 36872 | tf_op jit(solution)/shard_map/ppermute | solution.py:799
  148.3 1.4 collective-permute-done.9
  149.8 1.7 %collective-permute-start.10 = (f32[8,384]{1,0:T(8,128)S(1)}, f32[8,384]{1,0:T(8,128)S(1)}, u32[]{:S(2)}, u32[]{:S(2)}) collective-permute-start(f32[8,384]{1,0:T(8,128)S(1)} %add.22), channel_id=1, source_target_pairs={{0,9},{1,8},{2,11},{3,10},{4,13},{5,12},{6,15},{7,14},{8,1},{9,0},... | collective-permute-start | bytes 36872 | tf_op jit(solution)/shard_map/ppermute | solution.py:799
  151.5 1.4 collective-permute-done.10
  152.9 2.6 %collective-permute-start.11 = (f32[8,384]{1,0:T(8,128)S(1)}, f32[8,384]{1,0:T(8,128)S(1)}, u32[]{:S(2)}, u32[]{:S(2)}) collective-permute-start(f32[8,384]{1,0:T(8,128)S(1)} %add.23), channel_id=1, source_target_pairs={{0,17},{1,16},{2,19},{3,18},{4,21},{5,20},{6,23},{7,22},{8,25},{9,... | collective-permute-start | bytes 36872 | tf_op jit(solution)/shard_map/ppermute | solution.py:799
  155.5 1.4 collective-permute-done.11
  157.0 1.2 update_weights.1
  (56 shorter events, 1.5 us)
Async XLA Ops:
  2.3 6.4 %collective-permute-start = (bf16[24,640]{1,0:T(8,128)(2,1)}, bf16[24,640]{1,0:T(8,128)(2,1)S(1)}, u32[]{:S(2)}, u32[]{:S(2)}) collective-permute-start(bf16[24,640]{1,0:T(8,128)(2,1)} %get-tuple-element.69.own_ref), channel_id=1, source_target_pairs={{0,16},{2,18},{4,20},{6,22},{8,24},{10,26},{12,28},{14,30},{16,0},... | collective-permute-start | bytes 92168 | tf_op jit(solution)/shard_map/ppermute | solution.py:749
  9.5 5.6 %copy-start.3 = (bf16[24,1792]{1,0:T(8,128)(2,1)S(1)}, bf16[24,1792]{1,0:T(8,128)(2,1)}, u32[]{:S(2)}) copy-start(bf16[24,1792]{1,0:T(8,128)(2,1)} %get-tuple-element.70.own_ref) | copy-start | bytes 258052
  10.4 15.0 %all-to-all-start = ((bf16[8,2,24,640]{3,2,1,0:T(8,128)(2,1)}), bf16[8,2,24,640]{3,2,1,0:T(8,128)(2,1)S(1)}, u32[]{:S(2)}, u32[]{:S(2)}) async-start(bf16[8,2,24,640]{3,2,1,0:T(8,128)(2,1)} %pair_lead.1), calls=%async_computation | async-start | bytes 983040 | tf_op jit(solution)/shard_map/all_to_all | solution.py:753
  15.1 9.1 %collective-permute-start.1 = (bf16[24,1792]{1,0:T(8,128)(2,1)S(1)}, bf16[24,1792]{1,0:T(8,128)(2,1)S(1)}, u32[]{:S(2)}, u32[]{:S(2)}) collective-permute-start(bf16[24,1792]{1,0:T(8,128)(2,1)S(1)} %copy-done.3), channel_id=1, source_target_pairs={{0,16},{2,18},{4,20},{6,22},{8,24},{10,26},{12,28},{14,30},{16,0},... | collective-permute-start | bytes 258056 | tf_op jit(solution)/shard_map/ppermute | solution.py:750
  25.3 5.3 %copy-start.10 = (s32[8,640]{1,0:T(8,128)S(1)}, s32[8,640]{1,0:T(8,128)}, u32[]{:S(2)}) copy-start(s32[8,640]{1,0:T(8,128)} %mask_ref.1) | copy-start | bytes 61444
  25.3 5.3 %copy-start.12 = (s32[8]{0:T(128)S(1)}, s32[8]{0:T(128)}, u32[]{:S(2)}) copy-start(s32[8]{0:T(128)} %len_ref.5) | copy-start | bytes 100
  25.3 5.3 %collective-permute-start.2 = (bf16[8,2,24,640]{3,2,1,0:T(8,128)(2,1)S(1)}, bf16[8,2,24,640]{3,2,1,0:T(8,128)(2,1)S(1)}, u32[]{:S(2)}, u32[]{:S(2)}) collective-permute-start(bf16[8,2,24,640]{3,2,1,0:T(8,128)(2,1)S(1)} %all-to-all-done.own_ref), channel_id=1, source_target_pairs={{0,1},{1,0},{2,3},{3,2},{4,5},{5,4},{6,7},{7,6},{8,9},{9,8},{10,11... | collective-permute-start | bytes 1474568 | tf_op jit(solution)/shard_map/ppermute | solution.py:708
  25.4 28.0 %all-to-all-start.1 = ((bf16[8,2,24,1792]{3,2,1,0:T(8,128)(2,1)}), bf16[8,2,24,1792]{3,2,1,0:T(8,128)(2,1)S(1)}, u32[]{:S(2)}, u32[]{:S(2)}) async-start(bf16[8,2,24,1792]{3,2,1,0:T(8,128)(2,1)} %pair_rest.1), calls=%async_computation.1 | async-start | bytes 2752512 | tf_op jit(solution)/shard_map/all_to_all | solution.py:760
  53.4 32.7 %copy-start.18 = (f32[4,384]{1,0:T(4,128)}, f32[4,384]{1,0:T(4,128)S(1)}, u32[]{:S(2)}) copy-start(f32[4,384]{1,0:T(4,128)S(1)} %get-tuple-element.86.norms_ref) | copy-start | bytes 18436
  53.4 3.1 %collective-permute-start.3 = (bf16[8,2,24,1792]{3,2,1,0:T(8,128)(2,1)S(1)}, bf16[8,2,24,1792]{3,2,1,0:T(8,128)(2,1)S(1)}, u32[]{:S(2)}, u32[]{:S(2)}) collective-permute-start(bf16[8,2,24,1792]{3,2,1,0:T(8,128)(2,1)S(1)} %all-to-all-done.1.own_ref), channel_id=1, source_target_pairs={{0,1},{1,0},{2,3},{3,2},{4,5},{5,4},{6,7},{7,6},{8,9},{9,8},{10,11... | collective-permute-start | bytes 4128776 | tf_op jit(solution)/shard_map/ppermute | solution.py:708
  86.1 4.6 %copy-start.14 = (bf16[2560,384]{1,0:T(8,128)(2,1)}, bf16[2560,384]{1,0:T(8,128)(2,1)S(1)}, u32[]{:S(2)}) copy-start(bf16[2560,384]{1,0:T(8,128)(2,1)S(1)} %get-tuple-element.90) | copy-start | bytes 5898244
  86.1 4.6 %copy-start.17 = (f32[16,384]{1,0:T(8,128)}, f32[16,384]{1,0:T(8,128)S(1)}, u32[]{:S(2)}) copy-start(f32[16,384]{1,0:T(8,128)S(1)} %get-tuple-element.94.two_ref) | copy-start | bytes 73732
  86.2 3.2 %collective-permute-start.4 = (bf16[384,1792]{1,0:T(8,128)(2,1)S(1)}, bf16[384,1792]{1,0:T(8,128)(2,1)S(1)}, u32[]{:S(2)}, u32[]{:S(2)}) collective-permute-start(bf16[384,1792]{1,0:T(8,128)(2,1)S(1)} %get-tuple-element.88), channel_id=1, source_target_pairs={{0,1},{1,0},{2,3},{3,2},{4,5},{5,4},{6,7},{7,6},{8,9},{9,8},{10,11... | collective-permute-start | bytes 4128776 | tf_op jit(solution)/shard_map/ppermute | solution.py:708
  90.8 27.4 %all-to-all-start.2 = ((bf16[8,2,24,1792]{3,2,1,0:T(8,128)(2,1)}), bf16[8,2,24,1792]{3,2,1,0:T(8,128)(2,1)S(1)}, u32[]{:S(2)}, u32[]{:S(2)}) async-start(bf16[8,2,24,1792]{3,2,1,0:T(8,128)(2,1)} %add_rest.1), calls=%async_computation.2 | async-start | bytes 2752512 | tf_op jit(solution)/shard_map/all_to_all | solution.py:773
  118.2 1.9 %collective-permute-start.5 = (bf16[384,640]{1,0:T(8,128)(2,1)S(1)}, bf16[384,640]{1,0:T(8,128)(2,1)S(1)}, u32[]{:S(2)}, u32[]{:S(2)}) collective-permute-start(bf16[384,640]{1,0:T(8,128)(2,1)S(1)} %get-tuple-element.104), channel_id=1, source_target_pairs={{0,1},{1,0},{2,3},{3,2},{4,5},{5,4},{6,7},{7,6},{8,9},{9,8},{10,11... | collective-permute-start | bytes 1474568 | tf_op jit(solution)/shard_map/ppermute | solution.py:708
  118.4 23.0 %collective-permute-start.6 = (bf16[24,1792]{1,0:T(8,128)(2,1)S(1)}, bf16[24,1792]{1,0:T(8,128)(2,1)S(1)}, u32[]{:S(2)}, u32[]{:S(2)}) collective-permute-start(bf16[24,1792]{1,0:T(8,128)(2,1)S(1)} %get-tuple-element.107), channel_id=1, source_target_pairs={{0,16},{2,18},{4,20},{6,22},{8,24},{10,26},{12,28},{14,30},{16,0},... | collective-permute-start | bytes 258056 | tf_op jit(solution)/shard_map/ppermute | solution.py:785
  120.9 20.5 %all-to-all-start.3 = ((bf16[16,24,640]{2,1,0:T(8,128)(2,1)}), bf16[16,24,640]{2,1,0:T(8,128)(2,1)S(1)}, u32[]{:S(2)}, u32[]{:S(2)}) async-start(bf16[16,24,640]{2,1,0:T(8,128)(2,1)} %bitcast.15), calls=%async_computation.3 | async-start | bytes 983040 | tf_op jit(solution)/shard_map/all_to_all | solution.py:781
  142.1 14.8 %copy-start = (f32[2,24,3,192]{3,1,2,0:T(8,128)S(1)}, f32[2,24,3,192]{3,1,2,0:T(8,128)}, u32[]{:S(2)}) copy-start(f32[2,24,3,192]{3,1,2,0:T(8,128)} %param.23) | copy-start | bytes 331780
  142.1 14.8 %copy-start.1 = (f32[2,24,768]{2,1,0:T(8,128)S(1)}, f32[2,24,768]{2,1,0:T(8,128)}, u32[]{:S(2)}) copy-start(f32[2,24,768]{2,1,0:T(8,128)} %up_m_ref.1) | copy-start | bytes 442372
  142.1 14.9 %copy-start.2 = (f32[2,768,24]{1,2,0:T(8,128)S(1)}, f32[2,768,24]{1,2,0:T(8,128)}, u32[]{:S(2)}) copy-start(f32[2,768,24]{1,2,0:T(8,128)} %param.26) | copy-start | bytes 442372
  142.1 14.9 %copy-start.4 = (f32[24,3,192]{2,0,1:T(8,128)S(1)}, f32[24,3,192]{2,0,1:T(8,128)}, u32[]{:S(2)}) copy-start(f32[24,3,192]{2,0,1:T(8,128)} %param.18) | copy-start | bytes 165892
  142.1 14.9 %copy-start.5 = (f32[24,768]{1,0:T(8,128)S(1)}, f32[24,768]{1,0:T(8,128)}, u32[]{:S(2)}) copy-start(f32[24,768]{1,0:T(8,128)} %up_ref.3) | copy-start | bytes 221188
  142.1 14.9 %copy-start.6 = (f32[768,24]{0,1:T(8,128)S(1)}, f32[768,24]{0,1:T(8,128)}, u32[]{:S(2)}) copy-start(f32[768,24]{0,1:T(8,128)} %param.21) | copy-start | bytes 221188
  142.1 14.9 %copy-start.7 = (f32[2,192,24]{1,2,0:T(8,128)S(1)}, f32[2,192,24]{1,2,0:T(8,128)}, u32[]{:S(2)}) copy-start(f32[2,192,24]{1,2,0:T(8,128)} %param.24) | copy-start | bytes 110596
  142.1 14.9 %copy-start.9 = (f32[192,24]{0,1:T(8,128)S(1)}, f32[192,24]{0,1:T(8,128)}, u32[]{:S(2)}) copy-start(f32[192,24]{0,1:T(8,128)} %param.19) | copy-start | bytes 55300
  142.2 14.9 %copy-start.11 = (f32[2,48]{1,0:T(2,128)S(1)}, f32[2,48]{1,0:T(2,128)}, u32[]{:S(2)}) copy-start(f32[2,48]{1,0:T(2,128)} %norm_m_ref.1) | copy-start | bytes 1156
  142.2 14.9 %copy-start.13 = (f32[48]{0:T(128)S(1)}, f32[48]{0:T(128)}, u32[]{:S(2)}) copy-start(f32[48]{0:T(128)} %param.22) | copy-start | bytes 580
  142.3 1.2 collective-permute-start.7
  143.5 3.1 %collective-permute-start.8 = (f32[8,384]{1,0:T(8,128)S(1)}, f32[8,384]{1,0:T(8,128)S(1)}, u32[]{:S(2)}, u32[]{:S(2)}) collective-permute-start(f32[8,384]{1,0:T(8,128)S(1)} %add.20), channel_id=1, source_target_pairs={{0,3},{1,2},{2,1},{3,0},{4,7},{5,6},{6,5},{7,4},{8,11},{9,10},{10,... | collective-permute-start | bytes 36872 | tf_op jit(solution)/shard_map/ppermute | solution.py:799
  146.7 3.1 %collective-permute-start.9 = (f32[8,384]{1,0:T(8,128)S(1)}, f32[8,384]{1,0:T(8,128)S(1)}, u32[]{:S(2)}, u32[]{:S(2)}) collective-permute-start(f32[8,384]{1,0:T(8,128)S(1)} %add.21), channel_id=1, source_target_pairs={{0,5},{1,4},{2,7},{3,6},{4,1},{5,0},{6,3},{7,2},{8,13},{9,12},{10,... | collective-permute-start | bytes 36872 | tf_op jit(solution)/shard_map/ppermute | solution.py:799
  149.8 3.1 %collective-permute-start.10 = (f32[8,384]{1,0:T(8,128)S(1)}, f32[8,384]{1,0:T(8,128)S(1)}, u32[]{:S(2)}, u32[]{:S(2)}) collective-permute-start(f32[8,384]{1,0:T(8,128)S(1)} %add.22), channel_id=1, source_target_pairs={{0,9},{1,8},{2,11},{3,10},{4,13},{5,12},{6,15},{7,14},{8,1},{9,0},... | collective-permute-start | bytes 36872 | tf_op jit(solution)/shard_map/ppermute | solution.py:799
  152.9 4.0 %collective-permute-start.11 = (f32[8,384]{1,0:T(8,128)S(1)}, f32[8,384]{1,0:T(8,128)S(1)}, u32[]{:S(2)}, u32[]{:S(2)}) collective-permute-start(f32[8,384]{1,0:T(8,128)S(1)} %add.23), channel_id=1, source_target_pairs={{0,17},{1,16},{2,19},{3,18},{4,21},{5,20},{6,23},{7,22},{8,25},{9,... | collective-permute-start | bytes 36872 | tf_op jit(solution)/shard_map/ppermute | solution.py:799
  (3 other events, 2.4 us)
